TPU v7x, 32 devices: a whole 2x2x4 slice. The times are simulated.
32 devices in a mesh: dp: 2 (over x), blk: 8 (over z, core), ulysses: 2 (over y).
Axes of the slice: x: 2, y: 2, z: 4, core: 2. Of those that a mesh axis runs over, the one named last changes fastest.
Arguments:
- x_in: bfloat16 [2, 2048, 768], P('dp', ('blk', 'ulysses')), may hold values from -6 to 6
- block_ids: int32 [2, 2048], P('dp'), may hold values from 0 to 15, never falling along the last dimension, each value on 1 to 256 neighbouring positions
- expert_ids: int32 [2, 2048, 2], P('dp', ('blk', 'ulysses')), may hold values from 0 to 15, all different within a row; in each aligned block of 128 rows (0 to 127, 128 to 255, ..., all dimensions but the last counted through in order) at most 21 rows name the same one
- cotangent: bfloat16 [2, 2048, 768], P('dp', ('blk', 'ulysses')), may hold values from -6 to 6
- gain_attn: bfloat16 [2, 768], P(None, ('dp', 'blk', 'ulysses')), may hold values from 0.5 to 1.5
- w_qkv: bfloat16 [2, 768, 2304], P(None, ('dp', 'blk', 'ulysses')), may hold values from -0.21875 to 0.21875
- w_out: bfloat16 [2, 768, 768], P(None, ('dp', 'blk', 'ulysses')), may hold values from -2 to 2
- gain_ffn: bfloat16 [2, 768], P(None, ('dp', 'blk', 'ulysses')), may hold values from 0.5 to 1.5
- w_router: bfloat16 [2, 768, 16], P(None, ('dp', 'blk', 'ulysses')), may hold values from -0.15625 to 0.15625
- shared_gate_up: bfloat16 [2, 768, 4096], P(None, ('dp', 'blk', 'ulysses')), may hold values from -0.21875 to 0.21875
- shared_down: bfloat16 [2, 2048, 768], P(None, ('dp', 'blk', 'ulysses')), may hold values from -0.125 to 0.125
- expert_gate_up: bfloat16 [2, 16, 768, 4096], P(None, ('blk', 'ulysses')), may hold values from -0.21875 to 0.21875
- expert_down: bfloat16 [2, 16, 2048, 768], P(None, ('blk', 'ulysses')), may hold values from -0.125 to 0.125
Outputs:
- y_out: bfloat16 [2, 2048, 768], P('dp', ('blk', 'ulysses'))
- grad_x: bfloat16 [2, 2048, 768], P('dp', ('blk', 'ulysses'))
- grad_gain_attn: float32 [2, 768], P(None, ('dp', 'blk', 'ulysses'))
- grad_qkv: float32 [2, 768, 2304], P(None, ('dp', 'blk', 'ulysses'))
- grad_out: float32 [2, 768, 768], P(None, ('dp', 'blk', 'ulysses'))
- grad_gain_ffn: float32 [2, 768], P(None, ('dp', 'blk', 'ulysses'))
- grad_router: float32 [2, 768, 16], P(None, ('dp', 'blk', 'ulysses'))
- grad_shared_gate_up: float32 [2, 768, 4096], P(None, ('dp', 'blk', 'ulysses'))
- grad_shared_down: float32 [2, 2048, 768], P(None, ('dp', 'blk', 'ulysses'))
- grad_expert_gate_up: float32 [2, 16, 768, 4096], P(None, ('blk', 'ulysses'))
- grad_expert_down: float32 [2, 16, 2048, 768], P(None, ('blk', 'ulysses'))
Inputs may be any that keep to these rules, and one draw needn't show every extreme that they name: `block_ids`: block numbers never fall along a sequence; each block is 1 to 256 positions long and some block is exactly 256 long. `expert_ids`: the two experts of a position differ. Within each aligned run of 128 positions of one sequence (the rows of one device) no expert is named more than 21 times, a bound that some block reaches.
All inputs are finite; a program needn't handle non-finite values.
Results may differ from a plain program's by a relative error of at most 0.023.
Values may be sent and summed in bfloat16 or wider, within the bound.
No kernel may reach another device: no remote copies, remote signals or barrier semaphores. Data moves between devices by JAX's collectives and lax.ppermute only.
A program may use at most 320 MiB of HBM per device.

v0:
```python
import math

import jax
import jax.numpy as jnp
from jax import lax
from jax.sharding import PartitionSpec as P

D = 768
HEADS = 12
HEAD = 64
FF = 2048
EXPERTS = 16
LAYERS = 2
MOST = 21


NORM_EPS = 1e-06
NEG_BIG = -1e30
PRECISE = lax.Precision.HIGHEST


def rms_factor(stream):
    return lax.rsqrt(jnp.mean(stream * stream, axis=-1, keepdims=True) + NORM_EPS)


def norm_back(stream, gain, factor, upstream):
    weighted = upstream * gain
    inner_mean = jnp.mean(weighted * stream, axis=-1, keepdims=True)
    grad_stream = factor * weighted - stream * factor * factor * factor * inner_mean
    grad_gain = jnp.sum(upstream * stream * factor, axis=0)
    return (grad_stream, grad_gain)


def rope_tables(positions):
    half_size = HEAD // 2
    spacing = 10000.0 ** (-jnp.arange(half_size).astype(jnp.float32) * 2.0 / HEAD)
    angles = positions.astype(jnp.float32)[:, None] * spacing[None, :]
    return (jnp.cos(angles)[:, None, :], jnp.sin(angles)[:, None, :])


def rotate(vectors, cosine, sine_part, direction):
    half_size = vectors.shape[-1] // 2
    leading = vectors[..., :half_size]
    trailing = vectors[..., half_size:]
    return jnp.concatenate(
        [
            leading * cosine - direction * (trailing * sine_part),
            trailing * cosine + direction * (leading * sine_part),
        ],
        axis=-1,
    )


def swiglu_back(gate_pre, up_pre, hidden_grad):
    sigmoid_gate = jax.nn.sigmoid(gate_pre)
    silu_gate = gate_pre * sigmoid_gate
    gate_grad = hidden_grad * up_pre * (sigmoid_gate + silu_gate * (1.0 - sigmoid_gate))
    up_grad = hidden_grad * silu_gate
    return jnp.concatenate([gate_grad.astype(jnp.bfloat16), up_grad.astype(jnp.bfloat16)], axis=1)


def score_block(query_heads, key_block, offset, query_ids, block_row):
    key_count = key_block.shape[0]
    key_heads = key_block.reshape(key_count, query_heads.shape[1], query_heads.shape[2])
    scores = jnp.einsum(
        "qhd,khd->hqk", query_heads, key_heads, preferred_element_type=jnp.float32
    ) * HEAD ** (-0.5)
    key_ids = lax.dynamic_slice_in_dim(block_row, offset, key_count)
    allowed = key_ids[None, None, :] <= query_ids[None, :, None]
    return (scores, allowed)


def over_blocks(total_rows, update, carry):
    block_span = math.gcd(total_rows, 512)

    def advance(state, block_index):
        return (update(state, block_index * block_span, block_span), None)

    return lax.scan(advance, carry, jnp.arange(total_rows // block_span, dtype=jnp.int32))[0]


def norm_pass(query_heads, query_ids, block_row, carry, pieces, start):
    key_rows = pieces[0]

    def update(state, offset, key_count):
        highest, totals = state
        key_block = lax.dynamic_slice_in_dim(key_rows, offset, key_count)
        scores, allowed = score_block(query_heads, key_block, start + offset, query_ids, block_row)
        raised = jnp.maximum(highest, jnp.max(jnp.where(allowed, scores, NEG_BIG), axis=2))
        kept_terms = jnp.where(allowed, jnp.exp(scores - raised[:, :, None]), 0.0)
        return (raised, totals * jnp.exp(highest - raised) + jnp.sum(kept_terms, axis=2))

    return over_blocks(key_rows.shape[0], update, carry)


def value_pass(query_heads, query_ids, block_row, log_sum, carry, pieces, start):
    local_heads = query_heads.shape[1]
    key_rows, value_rows = pieces

    def update(running, offset, key_count):
        key_block = lax.dynamic_slice_in_dim(key_rows, offset, key_count)
        value_block = lax.dynamic_slice_in_dim(value_rows, offset, key_count)
        scores, allowed = score_block(query_heads, key_block, start + offset, query_ids, block_row)
        attn_probs = jnp.where(allowed, jnp.exp(scores - log_sum[:, :, None]), 0.0).astype(
            jnp.bfloat16
        )
        return running + jnp.einsum(
            "hqk,khd->qhd",
            attn_probs,
            value_block.reshape(key_count, local_heads, HEAD),
            preferred_element_type=jnp.float32,
        )

    return over_blocks(key_rows.shape[0], update, carry)


def send_back(partial_out):
    return lax.all_to_all(
        partial_out.astype(jnp.bfloat16),
        ("blk", "ulysses"),
        split_axis=0,
        concat_axis=0,
        tiled=True,
    ).astype(partial_out.dtype)


def route_tables(route_ids):
    stretch_rows = route_ids.shape[0]
    experts_row = jnp.arange(EXPERTS, dtype=jnp.int32)
    route_hits = (route_ids[:, :, None] == experts_row[None, None, :]).astype(jnp.int32)
    running = (
        jnp.cumsum(route_hits.reshape(2 * stretch_rows, EXPERTS), axis=0).reshape(
            stretch_rows, 2, EXPERTS
        )
        - 1
    )
    slot_index = jnp.sum(route_hits * running, axis=2)
    route_rows = (route_ids * MOST + slot_index).reshape(2 * stretch_rows)
    all_rows = jnp.arange(EXPERTS * MOST, dtype=jnp.int32)
    route_table = (route_rows[:, None] == all_rows[None, :]).astype(jnp.bfloat16)
    return (route_rows, route_table, route_hits.astype(jnp.float32))


def forward_layer(stream, weights, local_experts, context):
    gain_one, qkv_weight, out_weight, gain_two, router_weight, joint_weight, down_weight = weights
    expert_joint, expert_down = local_experts
    cosine, sine_part, query_ids, block_row, route_rows, route_table, route_hits, split_count = (
        context
    )
    stretch_rows = stream.shape[0]
    slot_count = route_table.shape[1] // EXPERTS
    factor_one = rms_factor(stream)
    normed_attn = (stream * factor_one * gain_one.astype(jnp.float32)).astype(jnp.bfloat16)
    projected = jnp.dot(normed_attn, qkv_weight, preferred_element_type=jnp.float32)
    queries = (
        rotate(projected[:, :D].reshape(stretch_rows, HEADS, HEAD), cosine, sine_part, 1.0)
        .astype(jnp.bfloat16)
        .reshape(stretch_rows, D)
    )
    key_rows = (
        rotate(projected[:, D : 2 * D].reshape(stretch_rows, HEADS, HEAD), cosine, sine_part, 1.0)
        .astype(jnp.bfloat16)
        .reshape(stretch_rows, D)
    )
    values = projected[:, 2 * D :].astype(jnp.bfloat16)
    query_flat, key_heads, value_heads = (
        lax.all_to_all(queries, "ulysses", split_axis=1, concat_axis=0, tiled=True),
        lax.all_to_all(key_rows, "ulysses", split_axis=1, concat_axis=0, tiled=True),
        lax.all_to_all(values, "ulysses", split_axis=1, concat_axis=0, tiled=True),
    )
    query_count = query_flat.shape[0]
    local_heads = query_flat.shape[1] // HEAD
    query_heads = query_flat.reshape(query_count, local_heads, HEAD)
    start_state = (
        jnp.full((local_heads, query_count), NEG_BIG, jnp.float32),
        jnp.zeros((local_heads, query_count), jnp.float32),
    )
    empty_sum = jnp.zeros((query_count, local_heads, HEAD), jnp.float32)
    whole_keys = (
        lax.all_gather(key_heads, "blk", axis=0, tiled=True),
        lax.all_gather(value_heads, "blk", axis=0, tiled=True),
    )
    highest, totals = norm_pass(query_heads, query_ids, block_row, start_state, (whole_keys[0],), 0)
    log_sum = highest + jnp.log(totals)
    attended = value_pass(query_heads, query_ids, block_row, log_sum, empty_sum, whole_keys, 0)
    mixed_tokens = lax.all_to_all(
        attended.astype(jnp.bfloat16).reshape(query_count, local_heads * HEAD),
        "ulysses",
        split_axis=0,
        concat_axis=1,
        tiled=True,
    )
    middle = stream + jnp.dot(mixed_tokens, out_weight, preferred_element_type=jnp.float32)
    factor_two = rms_factor(middle)
    normed_ffn = (middle * factor_two * gain_two.astype(jnp.float32)).astype(jnp.bfloat16)
    logits = jnp.dot(normed_ffn, router_weight, preferred_element_type=jnp.float32)
    picked = jnp.sum(logits[:, None, :] * route_hits, axis=2)
    gate_values = jax.nn.softmax(picked, axis=1)
    shared_joint = jnp.dot(normed_ffn, joint_weight, preferred_element_type=jnp.float32)
    shared_hidden = (jax.nn.silu(shared_joint[:, :FF]) * shared_joint[:, FF:]).astype(jnp.bfloat16)
    shared_out = jnp.dot(shared_hidden, down_weight, preferred_element_type=jnp.float32)
    paired = jnp.broadcast_to(normed_ffn[:, None, :], (stretch_rows, 2, D)).reshape(
        2 * stretch_rows, D
    )
    outgoing = jnp.dot(route_table.T, paired, preferred_element_type=jnp.float32).astype(
        jnp.bfloat16
    )
    outgoing = jnp.repeat(outgoing.reshape(EXPERTS, slot_count, D), split_count, axis=0)
    arrived = lax.all_to_all(outgoing, ("blk", "ulysses"), split_axis=0, concat_axis=0, tiled=True)
    senders = arrived.shape[0]
    slots = arrived.shape[1]
    flat_rows = arrived.reshape(senders * slots, D)
    expert_pre = jnp.dot(flat_rows, expert_joint, preferred_element_type=jnp.float32)
    half_width = expert_pre.shape[1] // 2
    expert_hidden = (jax.nn.silu(expert_pre[:, :half_width]) * expert_pre[:, half_width:]).astype(
        jnp.bfloat16
    )
    partial_out = jnp.dot(expert_hidden, expert_down, preferred_element_type=jnp.float32).reshape(
        senders, slots, D
    )
    returned, arrived_rows, expert_pre = (
        send_back(partial_out),
        arrived,
        expert_pre.reshape(senders, slots, 2 * half_width),
    )
    expert_rows = (
        returned.reshape(EXPERTS, split_count, slot_count, D)
        .sum(axis=1)
        .reshape(EXPERTS * slot_count, D)
    )
    per_choice = jnp.take(expert_rows, route_rows, axis=0).reshape(stretch_rows, 2, D)
    routed_out = jnp.sum(gate_values[:, :, None] * per_choice, axis=1)
    output = middle + shared_out + routed_out
    saved = (
        stream,
        factor_one,
        normed_attn,
        query_heads,
        key_heads,
        value_heads,
        whole_keys,
        log_sum,
        attended,
        mixed_tokens,
        middle,
        factor_two,
        normed_ffn,
        gate_values,
        shared_joint,
        shared_hidden,
        per_choice,
        arrived_rows,
        expert_pre,
    )
    return (output, saved)


def backward_layer(upstream, weights, local_experts, context, saved):
    gain_one, qkv_weight, out_weight, gain_two, router_weight, joint_weight, down_weight = weights
    expert_joint, expert_down = local_experts
    cosine, sine_part, query_ids, block_row, route_rows, route_table, route_hits, split_count = (
        context
    )
    (
        stream,
        factor_one,
        normed_attn,
        query_heads,
        key_heads,
        value_heads,
        whole_keys,
        log_sum,
        attended,
        mixed_tokens,
        middle,
        factor_two,
        normed_ffn,
        gate_values,
        shared_joint,
        shared_hidden,
        per_choice,
        arrived_rows,
        expert_pre,
    ) = saved
    stretch_rows = upstream.shape[0]
    slot_count = route_table.shape[1] // EXPERTS
    branch_grad = upstream.astype(jnp.bfloat16)
    shared_hidden_grad = (
        jnp.dot(branch_grad, down_weight.T, preferred_element_type=jnp.float32)
        .astype(jnp.bfloat16)
        .astype(jnp.float32)
    )
    shared_joint_grad = swiglu_back(shared_joint[:, :FF], shared_joint[:, FF:], shared_hidden_grad)
    grad_shared_down = jnp.dot(shared_hidden.T, branch_grad, preferred_element_type=jnp.float32)
    grad_shared_joint = jnp.dot(normed_ffn.T, shared_joint_grad, preferred_element_type=jnp.float32)
    normed_grad = jnp.dot(shared_joint_grad, joint_weight.T, preferred_element_type=jnp.float32)
    choice_grad = (gate_values[:, :, None] * upstream[:, None, :]).astype(jnp.bfloat16)
    gate_grad = jnp.sum(per_choice * upstream[:, None, :], axis=2)
    outgoing = jnp.dot(
        route_table.T, choice_grad.reshape(2 * stretch_rows, D), preferred_element_type=jnp.float32
    ).astype(jnp.bfloat16)
    outgoing = jnp.repeat(outgoing.reshape(EXPERTS, slot_count, D), split_count, axis=0)
    arrived_grad = lax.all_to_all(
        outgoing, ("blk", "ulysses"), split_axis=0, concat_axis=0, tiled=True
    )
    senders, slots = (arrived_grad.shape[0], arrived_grad.shape[1])
    flat_grad = arrived_grad.reshape(senders * slots, D)
    flat_rows = arrived_rows.reshape(senders * slots, D)
    flat_pre = expert_pre.reshape(senders * slots, expert_pre.shape[2])
    half_width = flat_pre.shape[1] // 2
    hidden_grad = (
        jnp.dot(flat_grad, expert_down.T, preferred_element_type=jnp.float32)
        .astype(jnp.bfloat16)
        .astype(jnp.float32)
    )
    expert_hidden = (jax.nn.silu(flat_pre[:, :half_width]) * flat_pre[:, half_width:]).astype(
        jnp.bfloat16
    )
    expert_joint_grad = swiglu_back(flat_pre[:, :half_width], flat_pre[:, half_width:], hidden_grad)
    grad_expert_down = jnp.dot(expert_hidden.T, flat_grad, preferred_element_type=jnp.float32)
    grad_expert_joint = jnp.dot(flat_rows.T, expert_joint_grad, preferred_element_type=jnp.float32)
    returned_grad = send_back(
        jnp.dot(expert_joint_grad, expert_joint.T, preferred_element_type=jnp.float32).reshape(
            senders, slots, D
        )
    )
    row_grad = (
        returned_grad.reshape(EXPERTS, split_count, slot_count, D)
        .sum(axis=1)
        .reshape(EXPERTS * slot_count, D)
    )
    normed_grad = normed_grad + jnp.sum(
        jnp.take(row_grad, route_rows, axis=0).reshape(stretch_rows, 2, D), axis=1
    )
    lead_grad = gate_values[:, 0] * gate_values[:, 1] * (gate_grad[:, 0] - gate_grad[:, 1])
    logit_grad = lead_grad[:, None] * (route_hits[:, 0, :] - route_hits[:, 1, :])
    grad_router = jnp.dot(normed_ffn.astype(jnp.float32).T, logit_grad, precision=PRECISE)
    normed_grad = normed_grad + jnp.dot(
        logit_grad, router_weight.astype(jnp.float32).T, precision=PRECISE
    )
    norm_grad_two, grad_gain_two = norm_back(
        middle, gain_two.astype(jnp.float32), factor_two, normed_grad
    )
    middle_grad = upstream + norm_grad_two
    attn_grad = middle_grad.astype(jnp.bfloat16)
    grad_out = jnp.dot(mixed_tokens.T, attn_grad, preferred_element_type=jnp.float32)
    mixed_grad = jnp.dot(attn_grad, out_weight.T, preferred_element_type=jnp.float32).astype(
        jnp.bfloat16
    )
    head_grad = lax.all_to_all(mixed_grad, "ulysses", split_axis=1, concat_axis=0, tiled=True)
    query_count, local_heads = (query_heads.shape[0], query_heads.shape[1])
    grad_heads = head_grad.reshape(query_count, local_heads, HEAD)
    key_all, value_all = whole_keys
    total_keys = key_all.shape[0]
    block_span = math.gcd(total_keys, 512)
    score_scale = HEAD ** (-0.5)
    delta_rows = jnp.transpose(jnp.sum(grad_heads.astype(jnp.float32) * attended, axis=2))
    query_start = jnp.zeros((query_count, local_heads, HEAD), jnp.float32)

    def sweep(query_grad, block_index):
        offset = block_index * block_span
        key_block = lax.dynamic_slice_in_dim(key_all, offset, block_span)
        value_block = lax.dynamic_slice_in_dim(value_all, offset, block_span)
        scores, allowed = score_block(query_heads, key_block, offset, query_ids, block_row)
        attn_probs = jnp.where(allowed, jnp.exp(scores - log_sum[:, :, None]), 0.0)
        value_grad = jnp.einsum(
            "hqk,qhd->khd",
            attn_probs.astype(jnp.bfloat16),
            grad_heads,
            preferred_element_type=jnp.float32,
        )
        prob_grad = jnp.einsum(
            "qhd,khd->hqk",
            grad_heads,
            value_block.reshape(block_span, local_heads, HEAD),
            preferred_element_type=jnp.float32,
        )
        score_grad = (attn_probs * (prob_grad - delta_rows[:, :, None])).astype(jnp.bfloat16)
        query_grad = (
            query_grad
            + jnp.einsum(
                "hqk,khd->qhd",
                score_grad,
                key_block.reshape(block_span, local_heads, HEAD),
                preferred_element_type=jnp.float32,
            )
            * score_scale
        )
        key_grad = (
            jnp.einsum("hqk,qhd->khd", score_grad, query_heads, preferred_element_type=jnp.float32)
            * score_scale
        )
        return (
            query_grad,
            (
                key_grad.reshape(block_span, local_heads * HEAD),
                value_grad.reshape(block_span, local_heads * HEAD),
            ),
        )

    query_grad, (key_terms, value_terms) = lax.scan(
        sweep, query_start, jnp.arange(total_keys // block_span, dtype=jnp.int32)
    )
    own_keys, own_values = (
        lax.psum_scatter(
            key_terms.reshape(total_keys, local_heads * HEAD).astype(jnp.bfloat16),
            "blk",
            scatter_dimension=0,
            tiled=True,
        ).astype(jnp.float32),
        lax.psum_scatter(
            value_terms.reshape(total_keys, local_heads * HEAD).astype(jnp.bfloat16),
            "blk",
            scatter_dimension=0,
            tiled=True,
        ).astype(jnp.float32),
    )
    query_tok, key_tok, value_tok = (
        lax.all_to_all(
            query_grad.reshape(query_count, local_heads * HEAD).astype(jnp.bfloat16),
            "ulysses",
            split_axis=0,
            concat_axis=1,
            tiled=True,
        ),
        lax.all_to_all(
            own_keys.astype(jnp.bfloat16), "ulysses", split_axis=0, concat_axis=1, tiled=True
        ),
        lax.all_to_all(
            own_values.astype(jnp.bfloat16), "ulysses", split_axis=0, concat_axis=1, tiled=True
        ),
    )
    query_pre = (
        rotate(
            query_tok.astype(jnp.float32).reshape(stretch_rows, HEADS, HEAD),
            cosine,
            sine_part,
            -1.0,
        )
        .astype(jnp.bfloat16)
        .reshape(stretch_rows, D)
    )
    key_pre = (
        rotate(
            key_tok.astype(jnp.float32).reshape(stretch_rows, HEADS, HEAD), cosine, sine_part, -1.0
        )
        .astype(jnp.bfloat16)
        .reshape(stretch_rows, D)
    )
    projected_grad = jnp.concatenate([query_pre, key_pre, value_tok], axis=1)
    grad_qkv = jnp.dot(normed_attn.T, projected_grad, preferred_element_type=jnp.float32)
    normed_attn_grad = jnp.dot(projected_grad, qkv_weight.T, preferred_element_type=jnp.float32)
    norm_grad_one, grad_gain_one = norm_back(
        stream, gain_one.astype(jnp.float32), factor_one, normed_attn_grad
    )
    dense_terms = (
        grad_gain_one,
        grad_qkv,
        grad_out,
        grad_gain_two,
        grad_router,
        grad_shared_joint,
        grad_shared_down,
    )
    return (middle_grad + norm_grad_one, dense_terms, (grad_expert_joint, grad_expert_down))


def local(
    x_in,
    block_ids,
    expert_ids,
    cotangent,
    gain_attn,
    w_qkv,
    w_out,
    gain_ffn,
    w_router,
    shared_gate_up,
    shared_down,
    expert_gate_up,
    expert_down,
):
    ulysses_size = lax.axis_size("ulysses")
    group_size = lax.axis_size("blk") * ulysses_size
    split_count = group_size // EXPERTS
    stretch_rows = x_in.shape[1]
    placement = lax.axis_index("blk") * ulysses_size + lax.axis_index("ulysses")
    positions = placement * stretch_rows + jnp.arange(stretch_rows, dtype=jnp.int32)
    cosine, sine_part = rope_tables(positions)
    block_row = block_ids[0]
    query_ids = lax.dynamic_slice_in_dim(
        block_row, lax.axis_index("blk") * ulysses_size * stretch_rows, ulysses_size * stretch_rows
    )
    route_rows, route_table, route_hits = route_tables(expert_ids[0])
    context = (
        cosine,
        sine_part,
        query_ids,
        block_row,
        route_rows,
        route_table,
        route_hits,
        split_count,
    )
    stream = x_in[0].astype(jnp.float32)
    records = []
    for layer_index in range(LAYERS):
        weights = (
            lax.all_gather(gain_attn[layer_index], ("dp", "blk", "ulysses"), axis=0, tiled=True),
            lax.all_gather(w_qkv[layer_index], ("dp", "blk", "ulysses"), axis=0, tiled=True),
            lax.all_gather(w_out[layer_index], ("dp", "blk", "ulysses"), axis=0, tiled=True),
            lax.all_gather(gain_ffn[layer_index], ("dp", "blk", "ulysses"), axis=0, tiled=True),
            lax.all_gather(w_router[layer_index], ("dp", "blk", "ulysses"), axis=0, tiled=True),
            lax.all_gather(
                shared_gate_up[layer_index], ("dp", "blk", "ulysses"), axis=0, tiled=True
            ),
            lax.all_gather(shared_down[layer_index], ("dp", "blk", "ulysses"), axis=0, tiled=True),
        )
        local_experts = (expert_gate_up[layer_index, 0], expert_down[layer_index, 0])
        stream, saved = forward_layer(stream, weights, local_experts, context)
        records.append((weights, local_experts, saved))
    upstream = cotangent[0].astype(jnp.float32)
    dense_grads = []
    expert_grads = []
    for layer_index in reversed(range(LAYERS)):
        weights, local_experts, saved = records[layer_index]
        upstream, dense_terms, expert_terms = backward_layer(
            upstream, weights, local_experts, context, saved
        )
        gain_one_term, qkv_term, out_term, gain_two_term, router_term, joint_term, down_term = (
            dense_terms
        )
        dense_grads.insert(
            0,
            (
                lax.psum_scatter(
                    gain_one_term, ("dp", "blk", "ulysses"), scatter_dimension=0, tiled=True
                ),
                lax.psum_scatter(
                    qkv_term, ("dp", "blk", "ulysses"), scatter_dimension=0, tiled=True
                ),
                lax.psum_scatter(
                    out_term, ("dp", "blk", "ulysses"), scatter_dimension=0, tiled=True
                ),
                lax.psum_scatter(
                    gain_two_term, ("dp", "blk", "ulysses"), scatter_dimension=0, tiled=True
                ),
                lax.psum_scatter(
                    router_term, ("dp", "blk", "ulysses"), scatter_dimension=0, tiled=True
                ),
                lax.psum_scatter(
                    joint_term, ("dp", "blk", "ulysses"), scatter_dimension=0, tiled=True
                ),
                lax.psum_scatter(
                    down_term, ("dp", "blk", "ulysses"), scatter_dimension=0, tiled=True
                ),
            ),
        )
        joint_expert, down_expert = expert_terms
        expert_grads.insert(
            0,
            (
                lax.psum(joint_expert.astype(jnp.bfloat16), "dp").astype(jnp.float32),
                lax.psum(down_expert.astype(jnp.bfloat16), "dp").astype(jnp.float32),
            ),
        )
    stacked_dense = [jnp.stack([entry[member] for entry in dense_grads]) for member in range(7)]
    stacked_joint = jnp.stack([entry[0] for entry in expert_grads])[:, None]
    stacked_down = jnp.stack([entry[1] for entry in expert_grads])[:, None]
    return (
        stream.astype(jnp.bfloat16)[None],
        upstream.astype(jnp.bfloat16)[None],
        stacked_dense[0],
        stacked_dense[1],
        stacked_dense[2],
        stacked_dense[3],
        stacked_dense[4],
        stacked_dense[5],
        stacked_dense[6],
        stacked_joint,
        stacked_down,
    )


def solution(mesh):
    in_specs = (
        P("dp", ("blk", "ulysses"), None),
        P("dp", None),
        P("dp", ("blk", "ulysses"), None),
        P("dp", ("blk", "ulysses"), None),
        P(None, ("dp", "blk", "ulysses")),
        P(None, ("dp", "blk", "ulysses"), None),
        P(None, ("dp", "blk", "ulysses"), None),
        P(None, ("dp", "blk", "ulysses")),
        P(None, ("dp", "blk", "ulysses"), None),
        P(None, ("dp", "blk", "ulysses"), None),
        P(None, ("dp", "blk", "ulysses"), None),
        P(None, ("blk", "ulysses"), None, None),
        P(None, ("blk", "ulysses"), None, None),
    )
    out_specs = (
        P("dp", ("blk", "ulysses"), None),
        P("dp", ("blk", "ulysses"), None),
        P(None, ("dp", "blk", "ulysses")),
        P(None, ("dp", "blk", "ulysses"), None),
        P(None, ("dp", "blk", "ulysses"), None),
        P(None, ("dp", "blk", "ulysses")),
        P(None, ("dp", "blk", "ulysses"), None),
        P(None, ("dp", "blk", "ulysses"), None),
        P(None, ("dp", "blk", "ulysses"), None),
        P(None, ("blk", "ulysses"), None, None),
        P(None, ("blk", "ulysses"), None, None),
    )
    return jax.shard_map(local, mesh=mesh, in_specs=in_specs, out_specs=out_specs, check_vma=False)
```

profile of v0, /device:TPU:0, one launch (start us, length us, event | category | flops | bytes accessed | tf_op | source)
XLA Modules:
  0.0 2658.4 jit_solution(15844135569221766464)
XLA Ops:
  11.3 42.1 %all-reduce.11 = (bf16[768]{0:T(1024)(128)(2,1)S(1)}, bf16[768]{0:T(1024)(128)(2,1)}, bf16[768]{0:T(1024)(128)(2,1)}, bf16[768]{0:T(1024)(128)(2,1)}) all-reduce(bf16[768]{0:T(1024)(128)(2,1)S(1)} %dynamic-update-slice, bf16[768]{0:T(1024)(128)(2,1)S(1)} %dynamic-update-slice.1, ...), channel_id=2, replica_groups=mesh['dp'=2,'blk'=8,'ulysses'=2] {'dp','blk','ulysses'}, use_global_device_ids=true, to_apply=%add | all-reduce | flops 3072 | bytes 12288
  54.6 19.9 all-gather.35.cloned.1.call-done
  112.9 15.8 while.78
  139.1 20.8 while.79
  165.3 30.5 %all-gather.37.cloned.1.call-done = bf16[1,768,768]{2,1,0:T(8,128)(2,1)} async-done(((bf16[1,24,768]{2,1,0:T(8,128)(2,1)}), bf16[1,768,768]{2,1,0:T(8,128)(2,1)}) %all-gather.37.cloned.1.call-update) | async-done | bytes 1179664 | tf_op jit(solution)/shard_map/all_gather | solution.py:511
  204.9 79.1 %all-gather.6 = bf16[1,768,16]{2,0,1:T(2,128)(2,1)S(1)} all-gather(bf16[1,24,16]{2,0,1:T(2,128)(2,1)S(1)} %copy.316), channel_id=8, replica_groups=mesh['dp'=2,'blk'=8,'ulysses'=2] {'dp','blk','ulysses'}, dimensions={1}, use_global_device_ids=true | all-gather | bytes 25344 | tf_op jit(solution)/shard_map/all_gather | solution.py:513
  303.8 16.8 all-to-all-done.5
  337.7 59.8 %all-gather.43.cloned.1.call-done = bf16[1,768,2304]{2,1,0:T(8,128)(2,1)} async-done(((bf16[1,24,2304]{2,1,0:T(8,128)(2,1)}), bf16[1,768,2304]{2,1,0:T(8,128)(2,1)}) %all-gather.43.cloned.1.call-update) | async-done | bytes 3538960 | tf_op jit(solution)/shard_map/all_gather | solution.py:510
  435.8 15.8 while.80
  451.6 10.5 all-gather.31.cloned.1.call-done
  462.1 20.8 while.81
  489.3 28.9 %all-gather.45.cloned.1.call-done = bf16[1,768,768]{2,1,0:T(8,128)(2,1)} async-done(((bf16[1,24,768]{2,1,0:T(8,128)(2,1)}), bf16[1,768,768]{2,1,0:T(8,128)(2,1)}) %all-gather.45.cloned.1.call-update) | async-done | bytes 1179664 | tf_op jit(solution)/shard_map/all_gather | solution.py:511
  528.2 78.0 %all-gather.13 = bf16[1,768,16]{2,0,1:T(2,128)(2,1)S(1)} all-gather(bf16[1,24,16]{2,0,1:T(2,128)(2,1)S(1)} %copy.317), channel_id=15, replica_groups=mesh['dp'=2,'blk'=8,'ulysses'=2] {'dp','blk','ulysses'}, dimensions={1}, use_global_device_ids=true | all-gather | bytes 25344 | tf_op jit(solution)/shard_map/all_gather | solution.py:513
  615.1 16.1 all-to-all-done.12
  719.8 49.7 %while.82 = (s32[]{:T(128)}, f32[256,6,64]{0,2,1:T(8,128)S(1)}, bf16[4,512,384]{2,1,0:T(8,128)(2,1)}, bf16[4,512,384]{2,1,0:T(8,128)(2,1)}, s32[4]{0:T(128)}, /*...) while((s32[]{:T(128)}, f32[256,6,64]{0,2,1:T(8,128)S(1)}, ...), condition=%wide.region_32.34_spmd.clone, body=%wide.region_31.33_spmd.clone.sunk | while | flops 512000000 | bytes 35988840 | solution.py:401
  777.4 24.8 reduce-scatter.17.cloned.1.call-done
  805.7 31.0 %reduce-scatter.15.cloned.1.call-done = bf16[256,384]{1,0:T(8,128)(2,1)} async-done(((bf16[2048,384]{1,0:T(8,128)(2,1)}), bf16[256,384]{1,0:T(8,128)(2,1)}) %reduce-scatter.15.cloned.1.call-update) | async-done | bytes 196624 | tf_op jit(solution)/shard_map/reduce_scatter | solution.py:405
  852.0 20.0 all_to_all.296
  935.6 49.8 %while.83 = (s32[]{:T(128)}, f32[256,6,64]{0,2,1:T(8,128)S(1)}, bf16[4,512,384]{2,1,0:T(8,128)(2,1)}, bf16[4,512,384]{2,1,0:T(8,128)(2,1)}, s32[4]{0:T(128)}, /*...) while((s32[]{:T(128)}, f32[256,6,64]{0,2,1:T(8,128)S(1)}, ...), condition=%wide.region_41.43_spmd.clone, body=%wide.region_40.42_spmd.clone.sunk | while | flops 512000000 | bytes 35988840 | solution.py:401
  997.8 20.7 reduce-scatter.21.cloned.1.call-done
  1022.8 30.3 %reduce-scatter.19.cloned.1.call-done = bf16[256,384]{1,0:T(8,128)(2,1)} async-done(((bf16[2048,384]{1,0:T(8,128)(2,1)}), bf16[256,384]{1,0:T(8,128)(2,1)}) %reduce-scatter.19.cloned.1.call-update) | async-done | bytes 196624 | tf_op jit(solution)/shard_map/reduce_scatter | solution.py:405
  1127.7 27.8 %reduce-scatter.29.cloned.1.call-done = f32[24,768]{1,0:T(8,128)} async-done(((f32[768,768]{1,0:T(8,128)}), f32[24,768]{1,0:T(8,128)}) %reduce-scatter.29.cloned.1.call-update) | async-done | bytes 73744 | tf_op jit(solution)/shard_map/reduce_scatter | solution.py:542
  1155.5 104.0 %reduce-scatter.27.cloned.1.call-done = f32[24,768]{1,0:T(8,128)} async-done(((f32[768,768]{1,0:T(8,128)}), f32[24,768]{1,0:T(8,128)}) %reduce-scatter.27.cloned.1.call-update) | async-done | bytes 73744 | tf_op jit(solution)/shard_map/reduce_scatter | solution.py:542
  1262.0 127.5 %all-reduce.16.cloned.1.call-done = (f32[768]{0:T(1024)}, f32[768]{0:T(1024)}, f32[768]{0:T(1024)}, f32[768]{0:T(1024)}, f32[768,16]{0,1:T(8,128)}, /*index=5*/f32[768,16]{0,1:T(8,128)}) async-done(((f32[768]{0:T(1024)}, f32[768]{0:T(1024)}, f32[768]{0:T(1024)}, f32[768]{0:T(1024)}, f32[768,16]{0,1:T(8,128)}, /*index=5*/f32[768,16]{0,1:T(8,128)}), (f32[768]{0:T(1024)}, f32[768]{0:T(1024)}, f32[768]{0:T(1024)}, ...) | async-done | bytes 110608
  1395.8 114.3 %reduce-scatter.37.cloned.1.call-done = f32[64,768]{1,0:T(8,128)} async-done(((f32[2048,768]{1,0:T(8,128)}), f32[64,768]{1,0:T(8,128)}) %reduce-scatter.37.cloned.1.call-update) | async-done | bytes 196624 | tf_op jit(solution)/shard_map/reduce_scatter | solution.py:554
  1510.2 120.5 %reduce-scatter.35.cloned.1.call-done = f32[64,768]{1,0:T(8,128)} async-done(((f32[2048,768]{1,0:T(8,128)}), f32[64,768]{1,0:T(8,128)}) %reduce-scatter.35.cloned.1.call-update) | async-done | bytes 196624 | tf_op jit(solution)/shard_map/reduce_scatter | solution.py:554
  1632.4 122.3 %reduce-scatter.25.cloned.1.call-done = f32[24,2304]{1,0:T(8,128)} async-done(((f32[768,2304]{1,0:T(8,128)}), f32[24,2304]{1,0:T(8,128)}) %reduce-scatter.25.cloned.1.call-update) | async-done | bytes 221200 | tf_op jit(solution)/shard_map/reduce_scatter | solution.py:539
  1754.7 125.1 %reduce-scatter.23.cloned.1.call-done = f32[24,2304]{1,0:T(8,128)} async-done(((f32[768,2304]{1,0:T(8,128)}), f32[24,2304]{1,0:T(8,128)}) %reduce-scatter.23.cloned.1.call-update) | async-done | bytes 221200 | tf_op jit(solution)/shard_map/reduce_scatter | solution.py:539
  1881.6 159.3 %reduce-scatter.33.cloned.1.call-done = f32[24,4096]{1,0:T(8,128)} async-done(((f32[768,4096]{1,0:T(8,128)}), f32[24,4096]{1,0:T(8,128)}) %reduce-scatter.33.cloned.1.call-update) | async-done | bytes 393232 | tf_op jit(solution)/shard_map/reduce_scatter | solution.py:551
  2040.9 162.1 %reduce-scatter.31.cloned.1.call-done = f32[24,4096]{1,0:T(8,128)} async-done(((f32[768,4096]{1,0:T(8,128)}), f32[24,4096]{1,0:T(8,128)}) %reduce-scatter.31.cloned.1.call-update) | async-done | bytes 393232 | tf_op jit(solution)/shard_map/reduce_scatter | solution.py:551
  2205.1 425.3 %all-reduce.18.cloned.1.call-done = (bf16[1,768,4096]{2,1,0:T(8,128)(2,1)}, bf16[1,768,4096]{2,1,0:T(8,128)(2,1)}, bf16[1,2048,768]{2,1,0:T(8,128)(2,1)}, bf16[1,2048,768]{2,1,0:T(8,128)(2,1)}) async-done(((bf16[1,768,4096]{2,1,0:T(8,128)(2,1)}, bf16[1,768,4096]{2,1,0:T(8,128)(2,1)}, bf16[1,2048,768]{2,1,0:T(8,128)(2,1)}, bf16[1,2048,768]{2,1,0:T(8,128)(2,1)}), (bf16[1,768,4096]{2,1,0:T(8,128)(2,1)}, ...) | async-done | bytes 18874384 | tf_op jit(solution)/shard_map/psum | solution.py:563
  2630.3 15.5 fusion.46
  (913 shorter events, 612.0 us)
Async XLA Ops:
  7.2 67.3 %all-gather.35.cloned.1.call-start = ((), (), s32[]{:S(2)}) async-start(), calls=%async_computation.52 | async-start | bytes 3649536 | tf_op jit(solution)/shard_map/all_gather | solution.py:510
  8.9 101.4 %all-gather.29.cloned.1.call-start = ((), (), s32[]{:S(2)}) async-start(), calls=%async_computation.37 | async-start | bytes 1769472 | tf_op jit(solution)/shard_map/all_gather | solution.py:180
  86.3 52.8 %all-gather.27.cloned.1.call-start = ((), (), s32[]{:S(2)}) async-start(), calls=%async_computation.36 | async-start | bytes 1769472 | tf_op jit(solution)/shard_map/all_gather | solution.py:181
  94.5 101.3 %all-gather.37.cloned.1.call-start = ((), (), s32[]{:S(2)}) async-start(), calls=%async_computation.53 | async-start | bytes 1216512 | tf_op jit(solution)/shard_map/all_gather | solution.py:511
  95.2 228.3 %all-gather.39.cloned.1.call-start = ((), (), s32[]{:S(2)}) async-start(), calls=%async_computation.54 | async-start | bytes 6488064 | tf_op jit(solution)/shard_map/all_gather | solution.py:514
  96.0 239.1 %all-gather.41.cloned.1.call-start = ((), (), s32[]{:S(2)}) async-start(), calls=%async_computation.55 | async-start | bytes 3244032 | tf_op jit(solution)/shard_map/all_gather | solution.py:517
  96.8 300.7 %all-gather.43.cloned.1.call-start = ((), (), s32[]{:S(2)}) async-start(), calls=%async_computation.56 | async-start | bytes 3649536 | tf_op jit(solution)/shard_map/all_gather | solution.py:510
  161.8 34.0 %all-to-all-start.3 = ((bf16[2,128,384]{1,2,0:T(8,128)(2,1)}), bf16[2,128,384]{1,2,0:T(8,128)(2,1)S(1)}, u32[]{:S(2)}, u32[]{:S(2)}) async-start(bf16[2,128,384]{1,2,0:T(8,128)(2,1)} %copy.253), calls=%async_computation.3 | async-start | bytes 393216 | tf_op jit(solution)/shard_map/all_to_all | solution.py:186
  199.6 84.6 %all-to-all-start.4 = ((bf16[16,21,768]{2,1,0:T(8,128)(2,1)}), bf16[16,21,768]{2,1,0:T(8,128)(2,1)S(1)}, u32[]{:S(2)}, u32[]{:S(2)}) async-start(bf16[16,21,768]{2,1,0:T(8,128)(2,1)} %reshape_broadcast_in_dim_reshape.12), calls=%async_computation.4 | async-start | bytes 1179648 | tf_op jit(solution)/shard_map/all_to_all | solution.py:209
  303.3 129.8 %all-gather.33.cloned.1.call-start = ((), (), s32[]{:S(2)}) async-start(), calls=%async_computation.39 | async-start | bytes 1769472 | tf_op jit(solution)/shard_map/all_gather | solution.py:180
  409.2 52.9 %all-gather.31.cloned.1.call-start = ((), (), s32[]{:S(2)}) async-start(), calls=%async_computation.38 | async-start | bytes 1769472 | tf_op jit(solution)/shard_map/all_gather | solution.py:181
  417.4 100.8 %all-gather.45.cloned.1.call-start = ((), (), s32[]{:S(2)}) async-start(), calls=%async_computation.57 | async-start | bytes 1216512 | tf_op jit(solution)/shard_map/all_gather | solution.py:511
  418.0 257.0 %all-gather.47.cloned.1.call-start = ((), (), s32[]{:S(2)}) async-start(), calls=%async_computation.58 | async-start | bytes 6488064 | tf_op jit(solution)/shard_map/all_gather | solution.py:514
  485.2 32.9 %all-to-all-start.9 = ((bf16[2,128,384]{1,2,0:T(8,128)(2,1)}), bf16[2,128,384]{1,2,0:T(8,128)(2,1)S(1)}, u32[]{:S(2)}, u32[]{:S(2)}) async-start(bf16[2,128,384]{1,2,0:T(8,128)(2,1)} %copy.268), calls=%async_computation.9 | async-start | bytes 393216 | tf_op jit(solution)/shard_map/all_to_all | solution.py:186
  488.7 191.4 %all-gather.49.cloned.1.call-start = ((), (), s32[]{:S(2)}) async-start(), calls=%async_computation.59 | async-start | bytes 3244032 | tf_op jit(solution)/shard_map/all_gather | solution.py:517
  521.9 87.9 %all-to-all-start.10 = ((bf16[16,21,768]{2,1,0:T(8,128)(2,1)}), bf16[16,21,768]{2,1,0:T(8,128)(2,1)S(1)}, u32[]{:S(2)}, u32[]{:S(2)}) async-start(bf16[16,21,768]{2,1,0:T(8,128)(2,1)} %reshape_broadcast_in_dim_reshape.13), calls=%async_computation.10 | async-start | bytes 1179648 | tf_op jit(solution)/shard_map/all_to_all | solution.py:209
  708.5 93.8 %reduce-scatter.17.cloned.1.call-start = ((), (), s32[]{:S(2)}) async-start(), calls=%async_computation.41 | async-start | bytes 1769472 | tf_op jit(solution)/shard_map/reduce_scatter | solution.py:411
  769.5 67.1 %reduce-scatter.15.cloned.1.call-start = ((), (), s32[]{:S(2)}) async-start(), calls=%async_computation.40 | async-start | bytes 1769472 | tf_op jit(solution)/shard_map/reduce_scatter | solution.py:405
  802.2 34.4 %all-to-all-start.17 = ((bf16[2,128,384]{2,1,0:T(8,128)(2,1)}), bf16[2,128,384]{2,1,0:T(8,128)(2,1)S(1)}, u32[]{:S(2)}, u32[]{:S(2)}) async-start(bf16[2,128,384]{2,1,0:T(8,128)(2,1)} %bitcast.703), calls=%async_computation.19 | async-start | bytes 393216 | tf_op jit(solution)/shard_map/all_to_all | solution.py:429
  924.5 94.1 %reduce-scatter.21.cloned.1.call-start = ((), (), s32[]{:S(2)}) async-start(), calls=%async_computation.43 | async-start | bytes 1769472 | tf_op jit(solution)/shard_map/reduce_scatter | solution.py:411
  985.4 67.8 %reduce-scatter.19.cloned.1.call-start = ((), (), s32[]{:S(2)}) async-start(), calls=%async_computation.42 | async-start | bytes 1769472 | tf_op jit(solution)/shard_map/reduce_scatter | solution.py:405
  986.0 169.5 %reduce-scatter.29.cloned.1.call-start = ((), (), s32[]{:S(2)}) async-start(), calls=%async_computation.47 | async-start | bytes 2433024 | tf_op jit(solution)/shard_map/reduce_scatter | solution.py:542
  988.4 271.2 %reduce-scatter.27.cloned.1.call-start = ((), (), s32[]{:S(2)}) async-start(), calls=%async_computation.46 | async-start | bytes 2433024 | tf_op jit(solution)/shard_map/reduce_scatter | solution.py:542
  1018.6 34.6 %all-to-all-start.23 = ((bf16[2,128,384]{2,1,0:T(8,128)(2,1)}), bf16[2,128,384]{2,1,0:T(8,128)(2,1)S(1)}, u32[]{:S(2)}, u32[]{:S(2)}) async-start(bf16[2,128,384]{2,1,0:T(8,128)(2,1)} %bitcast.701), calls=%async_computation.27 | async-start | bytes 393216 | tf_op jit(solution)/shard_map/all_to_all | solution.py:429
  1056.6 332.9 %all-reduce.16.cloned.1.call-start = ((), (), s32[]{:S(2)}) async-start(), calls=%async_computation.60 | async-start | bytes 229376
  1066.8 443.4 %reduce-scatter.37.cloned.1.call-start = ((), (), s32[]{:S(2)}) async-start(), calls=%async_computation.51 | async-start | bytes 6488064 | tf_op jit(solution)/shard_map/reduce_scatter | solution.py:554
  1070.5 560.1 %reduce-scatter.35.cloned.1.call-start = ((), (), s32[]{:S(2)}) async-start(), calls=%async_computation.50 | async-start | bytes 6488064 | tf_op jit(solution)/shard_map/reduce_scatter | solution.py:554
  1075.3 679.4 %reduce-scatter.25.cloned.1.call-start = ((), (), s32[]{:S(2)}) async-start(), calls=%async_computation.45 | async-start | bytes 7299072 | tf_op jit(solution)/shard_map/reduce_scatter | solution.py:539
  1080.6 799.2 %reduce-scatter.23.cloned.1.call-start = ((), (), s32[]{:S(2)}) async-start(), calls=%async_computation.44 | async-start | bytes 7299072 | tf_op jit(solution)/shard_map/reduce_scatter | solution.py:539
  1085.6 955.3 %reduce-scatter.33.cloned.1.call-start = ((), (), s32[]{:S(2)}) async-start(), calls=%async_computation.49 | async-start | bytes 12976128 | tf_op jit(solution)/shard_map/reduce_scatter | solution.py:551
  1093.4 1109.6 %reduce-scatter.31.cloned.1.call-start = ((), (), s32[]{:S(2)}) async-start(), calls=%async_computation.48 | async-start | bytes 12976128 | tf_op jit(solution)/shard_map/reduce_scatter | solution.py:551
  1101.2 1529.1 %all-reduce.18.cloned.1.call-start = ((), (), s32[]{:S(2)}) async-start(), calls=%async_computation.61 | async-start | bytes 37748736 | tf_op jit(solution)/shard_map/psum | solution.py:563
  (180 other events, 4329.6 us)
Sparse Core Ops, SparseCore 0:
  11.5 62.9 all-gather.34
  86.4 23.8 all-gather.28
  112.5 26.6 all-gather.26
  142.5 53.2 all-gather.36
  198.7 73.6 all-gather.38
  275.2 59.8 all-gather.40
  338.6 58.8 all-gather.42
  409.3 23.7 all-gather.32
  435.3 26.6 all-gather.30
  464.8 53.2 all-gather.44
  521.2 73.7 all-gather.46
  597.8 58.9 all-gather.48
  769.6 32.5 reduce-scatter.16
  804.4 32.1 reduce-scatter.14
  985.5 32.9 reduce-scatter.20
  1021.3 31.8 reduce-scatter.18
  1058.3 97.1 reduce-scatter.28
  1161.5 97.9 reduce-scatter.26
  1266.5 122.9 all-reduce.15
  1395.0 115.1 reduce-scatter.36
  1516.8 113.8 reduce-scatter.34
  1636.3 118.3 reduce-scatter.24
  1761.4 118.3 reduce-scatter.22
  1886.2 154.6 reduce-scatter.32
  2048.5 154.4 reduce-scatter.30
  2205.5 424.7 all-reduce.17
where the time goes:
time: 2670 us; the launch traced here: 2660 us
  waiting for transfers between devices  1850 us (69%)
  blocking collectives  263 us (10%)
  matrix products  234 us (9%)
  local copies, waits for them, and re-layouts  146 us (5%)
  starting transfers between devices  68.1 us (3%)
  other arithmetic  62.9 us (2%)
    psum x1, waiting for transfers between devices, local(): lax.psum(joint_expert.astype(jnp.bfloat16), 'dp').astype(jnp.float32)  425 us
    reduce_scatter x2, waiting for transfers between devices, local(): lax.psum_scatter(joint_term, ('dp', 'blk', 'ulysses'), scatter_dimension=...  321 us
    reduce_scatter x2, waiting for transfers between devices, local(): lax.psum_scatter(qkv_term, ('dp', 'blk', 'ulysses'), scatter_dimension=0,...  247 us
    reduce_scatter x2, waiting for transfers between devices, local(): lax.psum_scatter(down_term, ('dp', 'blk', 'ulysses'), scatter_dimension=0...  235 us
    all_gather x2, blocking collectives, local(): lax.all_gather(w_router[layer_index], ('dp', 'blk', 'ulysses'), axis=0, t...  157 us
    reduce_scatter x2, waiting for transfers between devices, local(): lax.psum_scatter(out_term, ('dp', 'blk', 'ulysses'), scatter_dimension=0,...  132 us
    unnamed x27, waiting for transfers between devices  131 us
    all_gather x2, waiting for transfers between devices, local(): lax.all_gather(w_qkv[layer_index], ('dp', 'blk', 'ulysses'), axis=0, tile...  79.7 us
  transfers between devices with their start and end apart: 43, of which 34 were waited for; matrix products, arithmetic and copies ran while one was open for 9% of the time, Pallas kernels for 0%

commit v1 on v0

v1 whole, which is shorter than its diff:
```python
import functools

import jax
import jax.numpy as jnp
from jax import lax
from jax.experimental import pallas as pl
from jax.experimental.pallas import tpu as pltpu
from jax.sharding import Mesh
from jax.sharding import PartitionSpec as P

D = 768
HEADS = 12
HEAD = 64
FF = 2048
EXPERTS = 16
LAYERS = 2
MOST = 21
TEAM_SIZE = 4
TEAM_HEADS = HEADS // TEAM_SIZE

ALL = ("dp", "z", "core", "ulysses")
SEQ = ("z", "core", "ulysses")
TEAM = ("core", "ulysses")
REST = ("dp", "z")

NORM_EPS = 1e-06
NEG_BIG = -1e30
PRECISE = lax.Precision.HIGHEST
F32 = jnp.float32
BF16 = jnp.bfloat16
QUERY_TILE = 256
VMEM_LIMIT = 48 * 1024 * 1024


def contract(left, right, left_dim, right_dim):
    return lax.dot_general(
        left, right, (((left_dim,), (right_dim,)), ((), ())), preferred_element_type=F32
    )


def exchange(rows, axes):
    return lax.all_to_all(rows, axes, split_axis=0, concat_axis=0, tiled=True)


SWAP = [(0, 1), (1, 0)]


def from_member(rows, turn):
    if turn == 1:
        return lax.ppermute(rows, "ulysses", SWAP)
    if turn == 2:
        return lax.ppermute(rows, "core", SWAP)
    return lax.ppermute(rows, TEAM, [(i, 3 - i) for i in range(4)])


def team_gather(rows):
    return jnp.stack([rows] + [from_member(rows, turn) for turn in (1, 2, 3)])


def in_order(stacked, member):
    turns = [jnp.equal(member, i) for i in range(4)]
    pieces = []
    for k in range(4):
        piece = stacked[k ^ 3]
        for i in range(3):
            piece = jnp.where(turns[i], stacked[k ^ i], piece)
        pieces.append(piece)
    return jnp.stack(pieces)


def team_sum(parts):
    total = parts[0].astype(F32)
    for turn in (1, 2, 3):
        total = total + from_member(parts[turn].astype(BF16), turn).astype(F32)
    return total


def rms_factor(stream):
    return lax.rsqrt(jnp.mean(stream * stream, axis=-1, keepdims=True) + NORM_EPS)


def norm_back(stream, gain, factor, upstream):
    weighted = upstream * gain
    inner_mean = jnp.mean(weighted * stream, axis=-1, keepdims=True)
    grad_stream = factor * weighted - stream * factor * factor * factor * inner_mean
    grad_gain = jnp.sum(upstream * stream * factor, axis=0)
    return (grad_stream, grad_gain)


def attention_kernel(full_ref, some_ref, base_ref, rows_ref, limit_ref, out_ref, wide_ref, log_ref, keys):
    span = rows_ref.shape[2]
    step = pl.program_id(0)
    per_block = span // QUERY_TILE

    @pl.when(step == 0)
    def _():
        for s in range(rows_ref.shape[0]):
            keys[s] = rows_ref[s, HEAD : 2 * HEAD, :].T

    tile = base_ref[0] + step
    lanes = pl.ds(pl.multiple_of((tile % per_block) * QUERY_TILE, QUERY_TILE), QUERY_TILE)
    queries = rows_ref[tile // per_block, 0:HEAD, lanes] * BF16(HEAD**-0.5)
    limit = limit_ref[...]
    key_index = lax.broadcasted_iota(jnp.int32, (span, QUERY_TILE), 0)

    def sweep(s, state, masked):
        highest, total, running = state
        scores = jnp.dot(keys[s], queries, preferred_element_type=F32)
        if masked:
            scores = jnp.where(key_index < limit - s * span, scores, NEG_BIG)
        raised = jnp.maximum(highest, jnp.max(scores, axis=0, keepdims=True))
        terms = jnp.exp(scores - raised)
        shrink = jnp.exp(highest - raised)
        total = total * shrink + jnp.sum(terms, axis=0, keepdims=True)
        running = running * shrink + jnp.dot(
            rows_ref[s, 2 * HEAD :, :], terms.astype(BF16), preferred_element_type=F32
        )
        return (raised, total, running)

    state = (
        jnp.full((1, QUERY_TILE), NEG_BIG, F32),
        jnp.zeros((1, QUERY_TILE), F32),
        jnp.zeros((HEAD, QUERY_TILE), F32),
    )
    state = lax.fori_loop(0, full_ref[step], lambda s, c: sweep(s, c, False), state)
    state = lax.fori_loop(full_ref[step], some_ref[step], lambda s, c: sweep(s, c, True), state)
    highest, total, running = state
    result = running / total
    log_ref[...] = highest + jnp.log(total)
    wide_ref[...] = result
    stretch = out_ref.shape[2]
    for i in range(QUERY_TILE // stretch):
        out_ref[i] = result[:, i * stretch : (i + 1) * stretch].astype(BF16)


def attention_back_kernel(
    full_ref, some_ref, base_ref, rows_ref, limit_ref, grad_ref, wide_ref, log_ref, out_ref, keys, values, key_sum, value_sum
):
    span = rows_ref.shape[2]
    blocks = rows_ref.shape[0]
    step = pl.program_id(0)
    per_block = span // QUERY_TILE

    @pl.when(step == 0)
    def _():
        for s in range(blocks):
            keys[s] = rows_ref[s, HEAD : 2 * HEAD, :].T
            values[s] = rows_ref[s, 2 * HEAD :, :].T
        key_sum[...] = jnp.zeros_like(key_sum)
        value_sum[...] = jnp.zeros_like(value_sum)
        out_ref[...] = jnp.zeros_like(out_ref)

    tile = base_ref[0] + step
    lanes = pl.ds(pl.multiple_of((tile % per_block) * QUERY_TILE, QUERY_TILE), QUERY_TILE)
    queries = rows_ref[tile // per_block, 0:HEAD, lanes] * BF16(HEAD**-0.5)
    limit = limit_ref[...]
    key_index = lax.broadcasted_iota(jnp.int32, (span, QUERY_TILE), 0)
    grads = jnp.concatenate([grad_ref[i] for i in range(grad_ref.shape[0])], axis=1)
    delta = jnp.sum(grads.astype(F32) * wide_ref[...], axis=0, keepdims=True)
    logs = log_ref[...]

    def sweep(s, query_grad, masked):
        scores = jnp.dot(keys[s], queries, preferred_element_type=F32)
        probs = jnp.exp(scores - logs)
        if masked:
            probs = jnp.where(key_index < limit - s * span, probs, 0.0)
        prob_grad = jnp.dot(values[s], grads, preferred_element_type=F32)
        score_grad = (probs * (prob_grad - delta)).astype(BF16)
        value_sum[s] += contract(grads, probs.astype(BF16), 1, 1)
        key_sum[s] += contract(queries, score_grad, 1, 1)
        return query_grad + jnp.dot(
            rows_ref[s, HEAD : 2 * HEAD, :], score_grad, preferred_element_type=F32
        )

    query_grad = jnp.zeros((HEAD, QUERY_TILE), F32)
    query_grad = lax.fori_loop(0, full_ref[step], lambda s, c: sweep(s, c, False), query_grad)
    query_grad = lax.fori_loop(
        full_ref[step], some_ref[step], lambda s, c: sweep(s, c, True), query_grad
    )
    out_ref[tile // per_block, 0:HEAD, lanes] = (query_grad * HEAD**-0.5).astype(BF16)

    @pl.when(step == pl.num_programs(0) - 1)
    def _():
        out_ref[:, HEAD : 2 * HEAD, :] = key_sum[...].astype(BF16)
        out_ref[:, 2 * HEAD :, :] = value_sum[...].astype(BF16)


def whole(shape):
    return pl.BlockSpec(shape, lambda step, *_: (0,) * len(shape))


def tile_at(step, full, some, base):
    return (0, base[0] + step)


def attention_cost(rows, tiles, dots):
    span = rows.shape[0] * rows.shape[2]
    return pl.CostEstimate(
        flops=dots * 4 * tiles * QUERY_TILE * span * HEAD,
        bytes_accessed=rows.size * 4,
        transcendentals=tiles * QUERY_TILE * span,
    )


def attention(rows, spans, stretch):
    full, some, base, limit, tiles = spans
    blocks, _, span = rows.shape
    length = tiles * QUERY_TILE
    return pl.pallas_call(
        attention_kernel,
        grid_spec=pltpu.PrefetchScalarGridSpec(
            num_scalar_prefetch=3,
            grid=(tiles,),
            in_specs=[whole(rows.shape), pl.BlockSpec((1, QUERY_TILE), tile_at)],
            out_specs=[
                pl.BlockSpec((QUERY_TILE // stretch, HEAD, stretch), lambda step, *_: (step, 0, 0)),
                pl.BlockSpec((HEAD, QUERY_TILE), lambda step, *_: (0, step)),
                pl.BlockSpec((1, QUERY_TILE), lambda step, *_: (0, step)),
            ],
            scratch_shapes=[pltpu.VMEM((blocks, span, HEAD), BF16)],
        ),
        out_shape=[
            jax.ShapeDtypeStruct((length // stretch, HEAD, stretch), BF16),
            jax.ShapeDtypeStruct((HEAD, length), F32),
            jax.ShapeDtypeStruct((1, length), F32),
        ],
        compiler_params=pltpu.CompilerParams(vmem_limit_bytes=VMEM_LIMIT),
        cost_estimate=attention_cost(rows, tiles, 1),
        name="attend",
    )(full, some, base, rows, limit)


def attention_back(rows, spans, grads, wide, logs):
    full, some, base, limit, tiles = spans
    blocks, _, span = rows.shape
    stretch = grads.shape[2]
    return pl.pallas_call(
        attention_back_kernel,
        grid_spec=pltpu.PrefetchScalarGridSpec(
            num_scalar_prefetch=3,
            grid=(tiles,),
            in_specs=[
                whole(rows.shape),
                pl.BlockSpec((1, QUERY_TILE), tile_at),
                pl.BlockSpec((QUERY_TILE // stretch, HEAD, stretch), lambda step, *_: (step, 0, 0)),
                pl.BlockSpec((HEAD, QUERY_TILE), lambda step, *_: (0, step)),
                pl.BlockSpec((1, QUERY_TILE), lambda step, *_: (0, step)),
            ],
            out_specs=whole(rows.shape),
            scratch_shapes=[
                pltpu.VMEM((blocks, span, HEAD), BF16),
                pltpu.VMEM((blocks, span, HEAD), BF16),
                pltpu.VMEM((blocks, HEAD, span), F32),
                pltpu.VMEM((blocks, HEAD, span), F32),
            ],
        ),
        out_shape=jax.ShapeDtypeStruct(rows.shape, BF16),
        compiler_params=pltpu.CompilerParams(vmem_limit_bytes=VMEM_LIMIT),
        cost_estimate=attention_cost(rows, tiles, 3),
        name="attend_back",
    )(full, some, base, rows, limit, grads, wide, logs)


def turn_heads(parts, cosine, sine, direction):
    first, second = parts[:, :2, 0], parts[:, :2, 1]
    turned = jnp.stack(
        [
            first * cosine - direction * (second * sine),
            second * cosine + direction * (first * sine),
        ],
        axis=2,
    )
    return jnp.concatenate([turned, parts[:, 2:]], axis=1)


def swiglu_back(gate_pre, up_pre, hidden_grad):
    sigmoid_gate = jax.nn.sigmoid(gate_pre)
    silu_gate = gate_pre * sigmoid_gate
    gate_grad = hidden_grad * up_pre * (sigmoid_gate + silu_gate * (1.0 - sigmoid_gate))
    up_grad = hidden_grad * silu_gate
    return (gate_grad.astype(BF16), up_grad.astype(BF16))


def expert_grad_kernel(has_before, rows_ref, grads_ref, gate_ref, up_ref, down_ref, *refs):
    joint_out, down_out, up_hold = refs[-3:]

    @pl.when(pl.program_id(1) == 0)
    def _():
        rows = rows_ref[...]
        grads = grads_ref[...]
        gate_pre = jnp.dot(rows, gate_ref[0, 0], preferred_element_type=F32)
        up_pre = jnp.dot(rows, up_ref[0, 0], preferred_element_type=F32)
        hidden_grad = contract(grads, down_ref[0, 0], 1, 1).astype(BF16).astype(F32)
        hidden = (gate_pre * jax.nn.sigmoid(gate_pre) * up_pre).astype(BF16)
        gate_grad, up_grad = swiglu_back(gate_pre, up_pre, hidden_grad)
        up_hold[...] = up_grad
        down_out[0, 0] = contract(hidden, grads, 0, 0)
        joint_out[0, 0] = contract(rows, gate_grad, 0, 0)

    @pl.when(pl.program_id(1) == 1)
    def _():
        joint_out[0, 0] = contract(rows_ref[...], up_hold[...], 0, 0)


def expert_grads(layer, rows, grads, joint, down, before):
    half = joint.shape[3] // 2
    chunk = min(512, half)
    chunks = half // chunk
    count = rows.shape[0]
    in_specs = [
        pl.BlockSpec((count, D), lambda i, h: (0, 0)),
        pl.BlockSpec((count, D), lambda i, h: (0, 0)),
        pl.BlockSpec((1, 1, D, chunk), lambda i, h: (layer, 0, 0, i)),
        pl.BlockSpec((1, 1, D, chunk), lambda i, h: (layer, 0, 0, chunks + i)),
        pl.BlockSpec((1, 1, chunk, D), lambda i, h: (layer, 0, i, 0)),
    ]
    operands = [rows, grads, joint, joint, down]
    aliases = {}
    if before is not None:
        in_specs += [pl.BlockSpec(memory_space=pl.ANY)] * 2
        operands += list(before)
        aliases = {5: 0, 6: 1}
    return pl.pallas_call(
        functools.partial(expert_grad_kernel, before is not None),
        grid=(chunks, 2),
        in_specs=in_specs,
        out_specs=[
            pl.BlockSpec((1, 1, D, chunk), lambda i, h: (layer, 0, 0, h * chunks + i)),
            pl.BlockSpec((1, 1, chunk, D), lambda i, h: (layer, 0, i, 0)),
        ],
        out_shape=[
            jax.ShapeDtypeStruct(joint.shape, F32),
            jax.ShapeDtypeStruct(down.shape, F32),
        ],
        scratch_shapes=[pltpu.VMEM((count, chunk), BF16)],
        input_output_aliases=aliases,
        compiler_params=pltpu.CompilerParams(vmem_limit_bytes=VMEM_LIMIT),
        cost_estimate=pl.CostEstimate(
            flops=12 * count * D * half,
            bytes_accessed=18 * D * half,
            transcendentals=count * half,
        ),
        name="expert_grads",
    )(*operands)


def route_tables(route_ids):
    stretch_rows = route_ids.shape[0]
    experts_row = jnp.arange(EXPERTS, dtype=jnp.int32)
    route_hits = (route_ids[:, :, None] == experts_row[None, None, :]).astype(jnp.int32)
    running = (
        jnp.cumsum(route_hits.reshape(2 * stretch_rows, EXPERTS), axis=0).reshape(
            stretch_rows, 2, EXPERTS
        )
        - 1
    )
    slot_index = jnp.sum(route_hits * running, axis=2)
    route_rows = route_ids * MOST + slot_index
    all_rows = jnp.arange(EXPERTS * MOST, dtype=jnp.int32)
    tables = [
        (route_rows[:, c, None] == all_rows[None, :]).astype(BF16) for c in range(2)
    ]
    return (tables, route_hits.astype(F32))


def send_rows(outgoing, split_count):
    outgoing = outgoing.reshape(EXPERTS, MOST, D)
    if split_count > 1:
        outgoing = jnp.repeat(outgoing, split_count, axis=0)
    arrived = exchange(outgoing, SEQ)
    return arrived.reshape(-1, D)


def return_rows(rows, split_count):
    returned = exchange(rows.astype(BF16).reshape(-1, MOST, D), SEQ)
    if split_count > 1:
        returned = (
            returned.reshape(EXPERTS, split_count, MOST, D).astype(F32).sum(axis=1)
        ).astype(BF16)
    return returned.reshape(EXPERTS * MOST, D)


def forward_layer(layer, stream, first_rows, weights, experts, context):
    gain_one, qkv_weight, out_weight, gain_two, router_weight, joint_weight, down_weight = weights
    expert_joint, expert_down = experts
    stretch = stream.shape[0]
    group = TEAM_SIZE * stretch
    member = context["member"]
    factor_one = rms_factor(stream)
    if first_rows is not None:
        wide_rows = first_rows.astype(F32)
        normed_team = (wide_rows * rms_factor(wide_rows) * gain_one).astype(BF16)
    else:
        normed = (stream * factor_one * gain_one).astype(BF16)
        normed_team = in_order(team_gather(normed), member).reshape(group, D)
    projected = contract(qkv_weight, normed_team, 0, 1)
    turned = turn_heads(
        projected.reshape(TEAM_HEADS, 3, 2, HEAD // 2, group),
        context["cosine"],
        context["sine"],
        1.0,
    )
    heads = turned.astype(BF16).reshape(TEAM_HEADS, 3 * HEAD, group)
    heads = jnp.concatenate([heads, jnp.zeros((1,) + heads.shape[1:], BF16)], axis=0)
    parts = context["parts"]
    if parts > 1:
        heads = jnp.repeat(heads, parts, axis=0)
    head_rows = exchange(heads, "z")
    attended, wide, logs = attention(head_rows, context["spans"], stretch)
    pieces = context["pieces"]
    if parts > 1:
        attended = lax.dynamic_update_slice_in_dim(
            jnp.zeros((pieces, HEAD, stretch), BF16),
            attended,
            context["part"] * (pieces // parts),
            0,
        )
    back = exchange(attended, SEQ)
    if parts > 1:
        back = (
            back.reshape(TEAM_SIZE, parts, TEAM_SIZE, HEAD, stretch).astype(F32).sum(axis=1)
        ).astype(BF16)
    back = back.reshape(TEAM_SIZE, TEAM_SIZE, HEAD, stretch)[:TEAM_HEADS]
    mixed = back.transpose(1, 0, 2, 3).reshape(D, stretch)
    middle = stream + contract(mixed, out_weight, 0, 0)
    factor_two = rms_factor(middle)
    normed_ffn = (middle * factor_two * gain_two).astype(BF16)

    table_one, table_two = context["tables"]
    table = table_one + table_two
    split_count = context["split_count"]
    arrived = send_rows(contract(table, normed_ffn, 0, 0).astype(BF16), split_count)
    ffn_team = team_gather(normed_ffn).reshape(group, D)
    logits = jnp.dot(normed_ffn, router_weight, preferred_element_type=F32)
    picked = jnp.sum(logits[:, None, :] * context["hits"], axis=2)
    gate_values = jax.nn.softmax(picked, axis=1)

    shared_joint = jnp.dot(ffn_team, joint_weight, preferred_element_type=F32)
    half = shared_joint.shape[1] // 2
    shared_hidden = (jax.nn.silu(shared_joint[:, :half]) * shared_joint[:, half:]).astype(BF16)
    shared_out = team_sum(
        jnp.dot(shared_hidden, down_weight, preferred_element_type=F32).reshape(
            TEAM_SIZE, stretch, D
        )
    )

    joint_pre = jnp.dot(arrived, expert_joint[layer, 0], preferred_element_type=F32)
    part_width = joint_pre.shape[1] // 2
    hidden = (jax.nn.silu(joint_pre[:, :part_width]) * joint_pre[:, part_width:]).astype(BF16)
    partial_out = jnp.dot(hidden, expert_down[layer, 0], preferred_element_type=F32)
    returned = return_rows(partial_out, split_count)
    choice_one = jnp.dot(table_one, returned, preferred_element_type=F32)
    choice_two = jnp.dot(table_two, returned, preferred_element_type=F32)
    output = (
        middle
        + shared_out
        + gate_values[:, 0:1] * choice_one
        + gate_values[:, 1:2] * choice_two
    )
    saved = dict(
        stream=stream,
        factor_one=factor_one,
        normed_team=normed_team,
        head_rows=head_rows,
        wide=wide,
        logs=logs,
        mixed=mixed,
        middle=middle,
        factor_two=factor_two,
        normed_ffn=normed_ffn,
        ffn_team=ffn_team,
        gate_values=gate_values,
        shared_joint=shared_joint,
        shared_hidden=shared_hidden,
        choices=(choice_one, choice_two),
        arrived=arrived,
        joint_pre=joint_pre,
    )
    return (output, saved)


def both_halves(rows):
    other = lax.ppermute(rows, "dp", SWAP)
    first = lax.axis_index("dp") == 0
    return jnp.concatenate([jnp.where(first, rows, other), jnp.where(first, other, rows)], axis=0)


def backward_layer(layer, upstream, weights, experts, context, saved, before):
    gain_one, qkv_weight, out_weight, gain_two, router_weight, joint_weight, down_weight = weights
    expert_joint, expert_down = experts
    stretch = upstream.shape[0]
    group = TEAM_SIZE * stretch
    member = context["member"]
    split_count = context["split_count"]
    table_one, table_two = context["tables"]
    gate_values = saved["gate_values"]

    outgoing = contract(table_one, (gate_values[:, 0:1] * upstream).astype(BF16), 0, 0) + contract(
        table_two, (gate_values[:, 1:2] * upstream).astype(BF16), 0, 0
    )
    arrived_grad = send_rows(outgoing.astype(BF16), split_count)
    joint_pre = saved["joint_pre"]
    part_width = joint_pre.shape[1] // 2
    hidden_grad = (
        contract(arrived_grad, expert_down[layer, 0], 1, 1).astype(BF16).astype(F32)
    )
    pre_grad = jnp.concatenate(
        swiglu_back(joint_pre[:, :part_width], joint_pre[:, part_width:], hidden_grad), axis=1
    )
    returned_grad = return_rows(contract(pre_grad, expert_joint[layer, 0], 1, 1), split_count)

    grad_team = team_gather(upstream.astype(BF16)).reshape(group, D)
    shared_joint = saved["shared_joint"]
    half = shared_joint.shape[1] // 2
    shared_hidden_grad = contract(grad_team, down_weight, 1, 1).astype(BF16).astype(F32)
    shared_joint_grad = jnp.concatenate(
        swiglu_back(shared_joint[:, :half], shared_joint[:, half:], shared_hidden_grad), axis=1
    )
    normed_grad = team_sum(
        contract(shared_joint_grad, joint_weight, 1, 1).reshape(TEAM_SIZE, stretch, D)
    )
    grad_down = contract(saved["shared_hidden"], grad_team, 0, 0).astype(BF16)
    grad_joint = contract(saved["ffn_team"], shared_joint_grad, 0, 0).astype(BF16)

    choice_one, choice_two = saved["choices"]
    lead_grad = (
        gate_values[:, 0:1]
        * gate_values[:, 1:2]
        * jnp.sum((choice_one - choice_two) * upstream, axis=1, keepdims=True)
    )
    hits = context["hits"]
    logit_grad = lead_grad * (hits[:, 0, :] - hits[:, 1, :])
    grad_router = jnp.dot(saved["normed_ffn"].astype(F32).T, logit_grad, precision=PRECISE)
    normed_grad = (
        normed_grad
        + jnp.dot(logit_grad, router_weight.astype(F32).T, precision=PRECISE)
        + jnp.dot(table_one + table_two, returned_grad, preferred_element_type=F32)
    )
    norm_grad_two, grad_gain_two = norm_back(
        saved["middle"], gain_two, saved["factor_two"], normed_grad
    )
    middle_grad = upstream + norm_grad_two

    attn_grad = middle_grad.astype(BF16)
    grad_out = jnp.dot(saved["mixed"], attn_grad, preferred_element_type=F32).astype(BF16)
    mixed_grad = contract(out_weight, attn_grad, 1, 1).astype(BF16)
    mixed_grad = mixed_grad.reshape(TEAM_SIZE, TEAM_HEADS, HEAD, stretch).transpose(1, 0, 2, 3)
    mixed_grad = jnp.concatenate(
        [mixed_grad, jnp.zeros((1,) + mixed_grad.shape[1:], BF16)], axis=0
    )
    parts = context["parts"]
    if parts > 1:
        mixed_grad = jnp.repeat(mixed_grad, parts, axis=0)
    pieces = context["pieces"]
    head_grad = exchange(mixed_grad.reshape(-1, HEAD, stretch), SEQ)
    if parts > 1:
        head_grad = lax.dynamic_slice_in_dim(
            head_grad, context["part"] * (pieces // parts), pieces // parts, 0
        )
    rows_grad = attention_back(
        saved["head_rows"], context["spans"], head_grad, saved["wide"], saved["logs"]
    )
    team_grad = exchange(rows_grad, "z")
    if parts > 1:
        team_grad = team_grad.reshape(TEAM_SIZE, parts, 3 * HEAD, group).astype(F32).sum(axis=1)
        team_grad = team_grad.astype(BF16)
    projected_grad = turn_heads(
        team_grad[:TEAM_HEADS].astype(F32).reshape(TEAM_HEADS, 3, 2, HEAD // 2, group),
        context["cosine"],
        context["sine"],
        -1.0,
    )
    projected_grad = projected_grad.astype(BF16).reshape(TEAM_HEADS * 3 * HEAD, group)
    grad_qkv = contract(saved["normed_team"], projected_grad, 0, 1).astype(BF16)
    team_part = contract(projected_grad, qkv_weight, 0, 1).astype(BF16)
    team_part = in_order(team_part.reshape(TEAM_SIZE, stretch, D), member)
    norm_grad_one, grad_gain_one = norm_back(
        saved["stream"], gain_one, saved["factor_one"], team_sum(team_part)
    )
    small = jnp.concatenate([grad_gain_one[:, None], grad_gain_two[:, None], grad_router], axis=1)

    expert_terms = expert_grads(
        layer,
        both_halves(saved["arrived"]),
        both_halves(arrived_grad),
        expert_joint,
        expert_down,
        before,
    )
    dense = dense_sums(grad_qkv, small, grad_out, grad_joint, grad_down)
    return (middle_grad + norm_grad_one, dense, expert_terms)


def dense_sums(grad_qkv, small, grad_out, grad_joint, grad_down):
    total = lax.axis_size(ALL)
    rest = total // TEAM_SIZE
    width = D // total
    qkv_width = grad_qkv.shape[1]
    packed = jnp.concatenate([grad_qkv, small.astype(BF16)], axis=1)
    packed = exchange(packed.reshape(total, width, -1), ALL).astype(F32)
    small_sum = packed[:, :, qkv_width:].sum(axis=0)
    qkv_sum = packed[:, :, :qkv_width].reshape(rest, TEAM_SIZE, width, qkv_width).sum(axis=0)
    qkv_sum = (
        qkv_sum.reshape(TEAM_SIZE, width, TEAM_HEADS, 3, HEAD)
        .transpose(1, 3, 0, 2, 4)
        .reshape(width, 3 * D)
    )
    out_sum = exchange(grad_out.reshape(total, width, D), ALL).astype(F32).sum(axis=0)
    joint_sum = exchange(grad_joint.reshape(total, width, -1), ALL).astype(F32)
    joint_sum = joint_sum.reshape(rest, TEAM_SIZE, width, -1).sum(axis=0)
    joint_sum = (
        joint_sum.reshape(TEAM_SIZE, width, 2, rest, FF // total)
        .transpose(1, 2, 3, 0, 4)
        .reshape(width, 2 * FF)
    )
    down_sum = exchange(grad_down.reshape(rest, FF // total, D), REST).astype(F32).sum(axis=0)
    return (
        small_sum[:, 0],
        qkv_sum,
        out_sum,
        small_sum[:, 1],
        small_sum[:, 2:],
        joint_sum,
        down_sum,
    )


def spread(rows):
    return lax.all_gather(rows, REST, axis=0, tiled=True)


def dense_weights(gain_attn, w_qkv, w_out, gain_ffn, w_router, shared_gate_up, shared_down):
    total = lax.axis_size(ALL)
    rest = total // TEAM_SIZE
    width = w_qkv.shape[1]
    small = jnp.concatenate(
        [gain_attn.T, gain_ffn.T, w_router.transpose(1, 0, 2).reshape(width, -1)], axis=1
    )
    small = jnp.broadcast_to(small[None], (TEAM_SIZE,) + small.shape)

    def qkv_columns(layer):
        blocks = w_qkv[layer].reshape(width, 3, TEAM_SIZE, TEAM_HEADS, HEAD)
        return blocks.transpose(2, 0, 3, 1, 4).reshape(TEAM_SIZE, width, -1)

    def joint_columns(layer):
        blocks = shared_gate_up[layer].reshape(width, 2, rest, TEAM_SIZE, FF // total)
        return blocks.transpose(3, 0, 1, 2, 4).reshape(TEAM_SIZE, width, -1)

    qkv_width = 3 * D // TEAM_SIZE
    first = exchange(jnp.concatenate([qkv_columns(0), small], axis=2), TEAM)
    first = spread(first.reshape(TEAM_SIZE * width, -1))
    qkv = [first[:, :qkv_width]]
    smalls = first[:, qkv_width:].astype(F32)
    out, joint, down = [], [], []
    for layer in range(LAYERS):
        if layer > 0:
            columns = exchange(qkv_columns(layer), TEAM)
            qkv.append(spread(columns.reshape(TEAM_SIZE * width, -1)))
        out.append(lax.all_gather(w_out[layer], ALL, axis=0, tiled=True))
        columns = exchange(joint_columns(layer), TEAM)
        joint.append(spread(columns.reshape(TEAM_SIZE * width, -1)))
        down.append(spread(shared_down[layer]))
    weights = []
    for layer in range(LAYERS):
        router = smalls[:, 2 * LAYERS + layer * EXPERTS : 2 * LAYERS + (layer + 1) * EXPERTS]
        weights.append(
            (
                smalls[:, layer],
                qkv[layer],
                out[layer],
                smalls[:, LAYERS + layer],
                router.astype(BF16),
                joint[layer],
                down[layer],
            )
        )
    return weights


def query_spans(block_row, group, part, parts):
    length = block_row.shape[0]
    limit = jnp.sum((block_row[None, :] <= block_row[:, None]).astype(jnp.int32), axis=1)
    tiles = length // QUERY_TILE // parts
    base = part * tiles
    ends = lax.dynamic_slice_in_dim(limit.reshape(-1, QUERY_TILE), base, tiles, 0)
    full = ends[:, 0] // group
    some = (ends[:, -1] + group - 1) // group
    base = jnp.full((1,), base, jnp.int32)
    return (full, some, base, limit[None, :], tiles)


def local(
    x_in,
    block_ids,
    expert_ids,
    cotangent,
    gain_attn,
    w_qkv,
    w_out,
    gain_ffn,
    w_router,
    shared_gate_up,
    shared_down,
    expert_gate_up,
    expert_down,
):
    stretch = x_in.shape[1]
    group = TEAM_SIZE * stretch
    deep = lax.axis_size("z")
    parts = max(1, deep // TEAM_SIZE)
    at = lax.axis_index("z")
    member = lax.axis_index("core") * lax.axis_size("ulysses") + lax.axis_index("ulysses")
    half_size = HEAD // 2
    spacing = 10000.0 ** (-jnp.arange(half_size).astype(F32) * 2.0 / HEAD)
    positions = (at * group + jnp.arange(group, dtype=jnp.int32)).astype(F32)
    angles = spacing[:, None] * positions[None, :]
    tables, hits = route_tables(expert_ids[0])
    part = at % parts
    context = dict(
        member=member,
        cosine=jnp.cos(angles),
        sine=jnp.sin(angles),
        tables=tables,
        hits=hits,
        parts=parts,
        part=part,
        pieces=deep * TEAM_SIZE,
        split_count=deep * TEAM_SIZE // EXPERTS,
        spans=query_spans(block_ids[0], group, part, parts),
    )
    experts = (expert_gate_up, expert_down)
    first_rows = in_order(team_gather(x_in[0]), member).reshape(group, D)
    weights = dense_weights(
        gain_attn, w_qkv, w_out, gain_ffn, w_router, shared_gate_up, shared_down
    )
    stream = x_in[0].astype(F32)
    records = []
    for layer in range(LAYERS):
        stream, saved = forward_layer(
            layer, stream, first_rows if layer == 0 else None, weights[layer], experts, context
        )
        records.append(saved)
    upstream = cotangent[0].astype(F32)
    dense = [None] * LAYERS
    expert_terms = None
    for layer in reversed(range(LAYERS)):
        upstream, dense[layer], expert_terms = backward_layer(
            layer, upstream, weights[layer], experts, context, records[layer], expert_terms
        )
    stacked = [jnp.stack([dense[layer][i] for layer in range(LAYERS)]) for i in range(7)]
    return (
        stream.astype(BF16)[None],
        upstream.astype(BF16)[None],
        *stacked,
        *expert_terms,
    )


def solution(mesh):
    dp, blk, ulysses = mesh.devices.shape
    grid = Mesh(mesh.devices.reshape(dp, blk // 2, 2, ulysses), ALL)
    rows = P("dp", SEQ, None)
    in_specs = (
        rows,
        P("dp", None),
        rows,
        rows,
        P(None, ALL),
        P(None, ALL, None),
        P(None, ALL, None),
        P(None, ALL),
        P(None, ALL, None),
        P(None, ALL, None),
        P(None, ALL, None),
        P(None, SEQ, None, None),
        P(None, SEQ, None, None),
    )
    out_specs = (
        rows,
        rows,
        P(None, ALL),
        P(None, ALL, None),
        P(None, ALL, None),
        P(None, ALL),
        P(None, ALL, None),
        P(None, ALL, None),
        P(None, ALL, None),
        P(None, SEQ, None, None),
        P(None, SEQ, None, None),
    )
    return jax.shard_map(local, mesh=grid, in_specs=in_specs, out_specs=out_specs, check_vma=False)
```

time: 2670 us -> 976 us (0.37)
  waiting for transfers between devices: 1850 us -> 288 us
  matrix products: 234 us -> 122 us
  Pallas kernels: 0 us -> 110 us
  blocking collectives: 263 us -> 155 us
  starting transfers between devices: 68.1 us -> 145 us
  local copies, waits for them, and re-layouts: 146 us -> 81.5 us
    reduce_scatter x12 -> x0, waiting for transfers between devices: 1040 us -> none  [the longest x2 321 us: local(): lax.psum_scatter(joint_term, ('dp', 'blk', 'ulysses'), scatter_dimension=...]
    psum x1 -> x0, waiting for transfers between devices: 425 us -> none  [local(): lax.psum(joint_expert.astype(jnp.bfloat16), 'dp').astype(jnp.float32)]
    all_gather x12 -> x4, waiting for transfers between devices: 173 us -> 20.6 us  [the longest x2 20.6 us: spread(): return lax.all_gather(rows, REST, axis=0, tiled=True)]
    unnamed x27 -> x4, waiting for transfers between devices: 131 us -> 0.99 us
    dot_general x102 -> x50, matrix products: 234 us -> 122 us  [the longest x28 67.5 us: contract(): lax.dot_general(left, right, (((left_dim,), (right_dim,)), ((), ())), pre...]
    pallas_call x0 -> x6, Pallas kernels: none -> 110 us  [the longest x2 54.8 us: expert_grads(): pl.pallas_call(functools.partial(expert_grad_kernel, before is not None),...]
    ppermute x0 -> x40, waiting for transfers between devices: none -> 100 us  [the longest x12 41.1 us: from_member(): return lax.ppermute(rows, 'ulysses', SWAP)]
    all_to_all x17 -> x27, waiting for transfers between devices: 77.9 us -> 167 us  [exchange(): return lax.all_to_all(rows, axes, split_axis=0, concat_axis=0, tiled=True)]
  transfers between devices with their start and end apart: 43 -> 71, of which waited for: 34 -> 37; matrix products, arithmetic and copies ran while one was open for 9% -> 22% of each run, Pallas kernels for 0% -> 11%
where the time goes in v1:
time: 976 us; the launch traced here: 962 us
  waiting for transfers between devices  288 us (30%)
  blocking collectives  155 us (16%)
  starting transfers between devices  145 us (15%)
  matrix products  122 us (12%)
  Pallas kernels  110 us (11%)
  local copies, waits for them, and re-layouts  81.5 us (8%)
  other arithmetic  44.3 us (5%)
  between operations  16.1 us (2%)
    all_to_all x27, waiting for transfers between devices, exchange(): return lax.all_to_all(rows, axes, split_axis=0, concat_axis=0, tiled=True)  167 us
    all_gather x4, blocking collectives, spread(): return lax.all_gather(rows, REST, axis=0, tiled=True)  145 us
    all_to_all x27, starting transfers between devices, exchange(): return lax.all_to_all(rows, axes, split_axis=0, concat_axis=0, tiled=True)  114 us
    dot_general x28, matrix products, contract(): lax.dot_general(left, right, (((left_dim,), (right_dim,)), ((), ())), pre...  67.5 us
    pallas_call x2, Pallas kernels, expert_grads(): pl.pallas_call(functools.partial(expert_grad_kernel, before is not None),...  54.8 us
    ppermute x12, waiting for transfers between devices, from_member(): return lax.ppermute(rows, 'ulysses', SWAP)  41.1 us
    ppermute x4, waiting for transfers between devices, both_halves(): other = lax.ppermute(rows, 'dp', SWAP)  35.2 us
    pallas_call x2, Pallas kernels, attention_back(): pl.pallas_call(attention_back_kernel, grid_spec=pltpu.PrefetchScalarGridS...  28.9 us
  transfers between devices with their start and end apart: 71, of which 37 were waited for; matrix products, arithmetic and copies ran while one was open for 22% of the time, Pallas kernels for 11%

profile of v1, /device:TPU:0, one launch (start us, length us, event | category | flops | bytes accessed | tf_op | source)
XLA Modules:
  0.0 962.4 jit_solution(14713943806617399296)
XLA Ops:
  11.4 9.5 all_to_all.140
  33.3 37.5 %all_gather.24 = bf16[768,612]{1,0:T(8,128)(2,1)S(1)} all-gather(bf16[96,612]{1,0:T(8,128)(2,1)S(1)} %bitcast.386), channel_id=1, replica_groups=mesh['dp'=2,'z'=4,'core'=2,'ulysses'=2] {'dp','z'}, dimensions={0}, use_global_device_ids=true | all-gather | bytes 1057536 | tf_op jit(solution)/shard_map/all_gather | solution.py:629
  86.2 17.7 %all-to-all-done.1.rows_ref = bf16[4,192,512]{2,1,0:T(8,128)(2,1)S(1)} async-done(((bf16[4,192,512]{2,1,0:T(8,128)(2,1)}), bf16[4,192,512]{2,1,0:T(8,128)(2,1)S(1)}, u32[]{:S(2)}, u32[]{:S(2)}) %all-to-all-start.1) | async-done | bytes 786464 | tf_op jit(solution)/shard_map/all_to_all | solution.py:42
  103.8 13.3 %attend.2 = (bf16[16,64,128]{2,1,0:T(8,128)(2,1)}, f32[64,2048]{1,0:T(8,128)S(1)}, f32[1,2048]{1,0:T(1,128)S(1)}) custom-call(s32[8]{0:T(128)S(1)} %get-tuple-element.173.full_ref, s32[8]{0:T(128)S(1)} %get-tuple-element.172.some_ref, s32[1]{0:T(128)} %constant.92.clone.1.base_ref, bf16[4,192,512]{2,1,0:T(8,128)(2,1)S(1)} %all-to-all-done.1.rows_ref, ...), custom_call_target="tpu_custom_call" | custom-call | flops 1073741824 | bytes 1572864 | tf_op jit(solution)/shard_map/attend/pallas_call | solution.py:209
  122.9 36.8 %all-gather.1 = bf16[1,512,768]{2,1,0:T(8,128)(2,1)} all-gather(bf16[1,64,768]{2,1,0:T(8,128)(2,1)} %get-tuple-element.148), channel_id=3, replica_groups=mesh['dp'=2,'z'=4,'core'=2,'ulysses'=2] {'dp','z'}, dimensions={1}, use_global_device_ids=true | all-gather | bytes 884736 | tf_op jit(solution)/shard_map/all_gather | solution.py:629
  178.5 9.2 all-to-all-done.4
  215.7 7.0 all-to-all-done.5
  232.9 35.5 %all_gather.28 = bf16[768,576]{1,0:T(8,128)(2,1)S(1)} all-gather(bf16[96,576]{1,0:T(8,128)(2,1)} %bitcast.43), channel_id=1, replica_groups=mesh['dp'=2,'z'=4,'core'=2,'ulysses'=2] {'dp','z'}, dimensions={0}, use_global_device_ids=true | all-gather | bytes 995328 | tf_op jit(solution)/shard_map/all_gather | solution.py:629
  280.9 9.7 %all-to-all-done.7.rows_ref = bf16[4,192,512]{2,1,0:T(8,128)(2,1)S(1)} async-done(((bf16[4,192,512]{2,1,0:T(8,128)(2,1)}), bf16[4,192,512]{2,1,0:T(8,128)(2,1)S(1)}, u32[]{:S(2)}, u32[]{:S(2)}) %all-to-all-start.7) | async-done | bytes 786464 | tf_op jit(solution)/shard_map/all_to_all | solution.py:42
  294.0 35.7 %all-gather.3 = bf16[1,512,768]{2,1,0:T(8,128)(2,1)} all-gather(bf16[1,64,768]{2,1,0:T(8,128)(2,1)S(1)} %copy-done.52), channel_id=5, replica_groups=mesh['dp'=2,'z'=4,'core'=2,'ulysses'=2] {'dp','z'}, dimensions={1}, use_global_device_ids=true | all-gather | bytes 884736 | tf_op jit(solution)/shard_map/all_gather | solution.py:629
  329.7 13.4 %attend.3 = (bf16[16,64,128]{2,1,0:T(8,128)(2,1)}, f32[64,2048]{1,0:T(8,128)S(1)}, f32[1,2048]{1,0:T(1,128)S(1)}) custom-call(s32[8]{0:T(128)S(1)} %get-tuple-element.173.full_ref, s32[8]{0:T(128)S(1)} %get-tuple-element.172.some_ref, s32[1]{0:T(128)} %constant.92.clone.1.base_ref, bf16[4,192,512]{2,1,0:T(8,128)(2,1)S(1)} %all-to-all-done.7.rows_ref, ...), custom_call_target="tpu_custom_call" | custom-call | flops 1073741824 | bytes 1572864 | tf_op jit(solution)/shard_map/attend/pallas_call | solution.py:209
  350.3 7.3 all-to-all-done.8
  383.0 20.6 %all-gather.11.cloned.1.call-done = bf16[768,1024]{1,0:T(8,128)(2,1)} async-done(((bf16[96,1024]{1,0:T(8,128)(2,1)}), bf16[768,1024]{1,0:T(8,128)(2,1)}) %all-gather.11.cloned.1.call-update) | async-done | bytes 1572880 | tf_op jit(solution)/shard_map/all_gather | solution.py:629
  417.9 7.7 fusion.2
  509.1 7.2 all-to-all-done.14.grad_ref
  520.5 14.4 %attend_back.2 = bf16[4,192,512]{2,1,0:T(8,128)(2,1)} custom-call(s32[8]{0:T(128)S(1)} %get-tuple-element.173.full_ref, s32[8]{0:T(128)S(1)} %get-tuple-element.172.some_ref, s32[1]{0:T(128)} %constant.92.clone.1.base_ref, bf16[4,192,512]{2,1,0:T(8,128)(2,1)S(1)} %all-to-all-done.7.rows_ref, s32[1,2048]{1,0:T(1,128)S(1)} %bitcast.320, ...), custom_call_target="tpu_custom_call" | custom-call | flops 3221225472 | bytes 1572864 | tf_op jit(solution)/shard_map/attend_back/pallas_call | solution.py:237
  534.9 7.1 all-to-all-done.27
  549.2 16.2 %all-to-all-done.15 = bf16[4,192,512]{2,1,0:T(8,128)(2,1)S(1)} async-done(((bf16[4,192,512]{2,1,0:T(8,128)(2,1)}), bf16[4,192,512]{2,1,0:T(8,128)(2,1)S(1)}, u32[]{:S(2)}, u32[]{:S(2)}) %all-to-all-start.15) | async-done | bytes 786464 | tf_op jit(solution)/shard_map/all_to_all | solution.py:42
  573.8 12.3 %collective-permute-done.24 = bf16[128,768]{1,0:T(8,128)(2,1)S(1)} collective-permute-done((bf16[128,768]{1,0:T(8,128)(2,1)S(1)}, bf16[128,768]{1,0:T(8,128)(2,1)S(1)}, u32[]{:S(2)}, u32[]{:S(2)}) %collective-permute-start.24) | collective-permute-done | bytes 196640 | tf_op jit(solution)/shard_map/ppermute | solution.py:50
  593.0 14.3 %all-to-all-done.25 = bf16[32,24,1024]{2,1,0:T(8,128)(2,1)} async-done(((bf16[32,24,1024]{2,1,0:T(8,128)(2,1)}), bf16[32,24,1024]{2,1,0:T(8,128)(2,1)}, u32[]{:S(2)}, u32[]{:S(2)}) %all-to-all-start.25) | async-done | bytes 1572896 | tf_op jit(solution)/shard_map/all_to_all | solution.py:42
  612.5 14.2 %all-to-all-done.16 = bf16[16,21,768]{2,1,0:T(8,128)(2,1)S(1)} async-done(((bf16[16,21,768]{2,1,0:T(8,128)(2,1)}), bf16[16,21,768]{2,1,0:T(8,128)(2,1)S(1)}, u32[]{:S(2)}, u32[]{:S(2)}) %all-to-all-start.16) | async-done | bytes 516128 | tf_op jit(solution)/shard_map/all_to_all | solution.py:42
  634.4 11.5 %collective-permute-done.27 = bf16[128,768]{1,0:T(8,128)(2,1)S(1)} collective-permute-done((bf16[128,768]{1,0:T(8,128)(2,1)S(1)}, bf16[128,768]{1,0:T(8,128)(2,1)S(1)}, u32[]{:S(2)}, u32[]{:S(2)}) %collective-permute-start.27) | collective-permute-done | bytes 196640 | tf_op jit(solution)/shard_map/ppermute | solution.py:50
  679.0 7.4 all-to-all-done.26
  697.7 8.7 all-to-all-done.17
  723.9 7.0 collective-permute-done.32
  760.2 16.4 %collective-permute-done.38 = bf16[336,768]{1,0:T(8,128)(2,1)} collective-permute-done((bf16[336,768]{1,0:T(8,128)(2,1)}, bf16[336,768]{1,0:T(8,128)(2,1)}, u32[]{:S(2)}, u32[]{:S(2)}) %collective-permute-start.38) | collective-permute-done | bytes 516128 | tf_op jit(solution)/shard_map/ppermute | solution.py:483
  777.9 17.8 %collective-permute-done.39 = bf16[336,768]{1,0:T(8,128)(2,1)S(1)} collective-permute-done((bf16[336,768]{1,0:T(8,128)(2,1)S(1)}, bf16[336,768]{1,0:T(8,128)(2,1)S(1)}, u32[]{:S(2)}, u32[]{:S(2)}) %collective-permute-start.39) | collective-permute-done | bytes 516128 | tf_op jit(solution)/shard_map/ppermute | solution.py:483
  795.9 27.6 %expert_grads.2 = (f32[2,1,768,4096]{3,2,1,0:T(8,128)}, f32[2,1,2048,768]{3,2,1,0:T(8,128)}) custom-call(bf16[672,768]{1,0:T(8,128)(2,1)S(1)} %pad_maximum_fusion.4.rows_ref, bf16[672,768]{1,0:T(8,128)(2,1)S(1)} %pad_maximum_fusion.5.grads_ref, bf16[2,1,768,4096]{3,2,1,0:T(8,128)(2,1)} %up_ref.3, bf16[2,1,768,4096]{3,2,1,0:T(8,128)(2,1)} %up_ref.3, ...), custom_call_target="tpu_custom_call" | custom-call | flops 12683575296 | bytes 28311552 | tf_op jit(solution)/shard_map/expert_grads/pallas_call | solution.py:323
  827.0 14.4 %attend_back.3 = bf16[4,192,512]{2,1,0:T(8,128)(2,1)} custom-call(s32[8]{0:T(128)S(1)} %get-tuple-element.173.full_ref, s32[8]{0:T(128)S(1)} %get-tuple-element.172.some_ref, s32[1]{0:T(128)} %constant.92.clone.1.base_ref, bf16[4,192,512]{2,1,0:T(8,128)(2,1)S(1)} %all-to-all-done.1.rows_ref, s32[1,2048]{1,0:T(1,128)S(1)} %bitcast.321, ...), custom_call_target="tpu_custom_call" | custom-call | flops 3221225472 | bytes 1572864 | tf_op jit(solution)/shard_map/attend_back/pallas_call | solution.py:237
  857.5 8.4 all-to-all-done.19
  869.5 27.2 %expert_grads.3 = (f32[2,1,768,4096]{3,2,1,0:T(8,128)}, f32[2,1,2048,768]{3,2,1,0:T(8,128)}) custom-call(bf16[672,768]{1,0:T(8,128)(2,1)S(1)} %pad_maximum_fusion.2.rows_ref, bf16[672,768]{1,0:T(8,128)(2,1)S(1)} %pad_maximum_fusion.3.grads_ref, bf16[2,1,768,4096]{3,2,1,0:T(8,128)(2,1)} %up_ref.3, ...), custom_call_target="tpu_custom_call", output_to_operand_aliasing={{0}: (5, {}), {1}: (6, {})} | custom-call | flops 12683575296 | bytes 28311552 | tf_op jit(solution)/shard_map/expert_grads/pallas_call | solution.py:323
  936.6 11.7 %all-to-all-done.20 = bf16[32,24,594]{2,1,0:T(8,128)(2,1)S(1)} async-done(((bf16[32,24,594]{2,1,0:T(8,128)(2,1)}), bf16[32,24,594]{2,1,0:T(8,128)(2,1)S(1)}, u32[]{:S(2)}, u32[]{:S(2)}) %all-to-all-start.20) | async-done | bytes 912416 | tf_op jit(solution)/shard_map/all_to_all | solution.py:42
  (520 shorter events, 441.8 us)
Async XLA Ops:
  7.2 153.5 %all-gather.13.cloned.1.call-start = ((), (), s32[]{:S(2)}) async-start(), calls=%async_computation.30 | async-start | bytes 1216512 | tf_op jit(solution)/shard_map/all_gather | solution.py:659
  8.9 198.1 %all-gather.9.cloned.1.call-start = ((), (), s32[]{:S(2)}) async-start(), calls=%async_computation.28 | async-start | bytes 1769472 | tf_op jit(solution)/shard_map/all_gather | solution.py:629
  20.9 54.2 %collective-permute-start.1 = (bf16[128,768]{1,0:T(8,128)(2,1)S(1)}, bf16[128,768]{1,0:T(8,128)(2,1)S(1)}, u32[]{:S(2)}, u32[]{:S(2)}) collective-permute-start(bf16[128,768]{1,0:T(8,128)(2,1)S(1)} %bitcast.327), channel_id=1, source_target_pairs={{0,1},{1,0},{2,3},{3,2},{4,5},{5,4},{6,7},{7,6},{8,9},{9,8},{10,11... | collective-permute-start | bytes 589832 | tf_op jit(solution)/shard_map/ppermute | solution.py:50
  21.1 54.0 %collective-permute-start = (bf16[128,768]{1,0:T(8,128)(2,1)S(1)}, bf16[128,768]{1,0:T(8,128)(2,1)S(1)}, u32[]{:S(2)}, u32[]{:S(2)}) collective-permute-start(bf16[128,768]{1,0:T(8,128)(2,1)S(1)} %bitcast.328), channel_id=1, source_target_pairs={{0,2},{2,0},{1,3},{3,1},{4,6},{6,4},{5,7},{7,5},{8,10},{10,8},{9,1... | collective-permute-start | bytes 589832 | tf_op jit(solution)/shard_map/ppermute | solution.py:52
  21.1 54.0 %collective-permute-start.2 = (bf16[128,768]{1,0:T(8,128)(2,1)S(1)}, bf16[128,768]{1,0:T(8,128)(2,1)}, u32[]{:S(2)}, u32[]{:S(2)}) collective-permute-start(bf16[128,768]{1,0:T(8,128)(2,1)S(1)} %bitcast.329), channel_id=1, source_target_pairs={{0,3},{1,2},{2,1},{3,0},{4,7},{5,6},{6,5},{7,4},{8,11},{9,10},{10,... | collective-permute-start | bytes 589832 | tf_op jit(solution)/shard_map/ppermute | solution.py:53
  28.1 331.1 %all-gather.15.cloned.1.call-start = ((), (), s32[]{:S(2)}) async-start(), calls=%async_computation.31 | async-start | bytes 1216512 | tf_op jit(solution)/shard_map/all_gather | solution.py:659
  78.7 25.2 %all-to-all-start.1 = ((bf16[4,192,512]{2,1,0:T(8,128)(2,1)}), bf16[4,192,512]{2,1,0:T(8,128)(2,1)S(1)}, u32[]{:S(2)}, u32[]{:S(2)}) async-start(bf16[4,192,512]{2,1,0:T(8,128)(2,1)} %concatenate.71), calls=%async_computation.1 | async-start | bytes 1572864 | tf_op jit(solution)/shard_map/all_to_all | solution.py:42
  117.2 42.5 %all-to-all-start.2 = ((bf16[16,64,128]{2,1,0:T(8,128)(2,1)}), bf16[16,64,128]{2,1,0:T(8,128)(2,1)}, u32[]{:S(2)}, u32[]{:S(2)}) async-start(bf16[16,64,128]{2,1,0:T(8,128)(2,1)} %get-tuple-element.21), calls=%async_computation.2 | async-start | bytes 524288 | tf_op jit(solution)/shard_map/all_to_all | solution.py:42
  230.9 37.4 %collective-permute-start.11 = (bf16[128,768]{1,0:T(8,128)(2,1)S(1)}, bf16[128,768]{1,0:T(8,128)(2,1)S(1)}, u32[]{:S(2)}, u32[]{:S(2)}) collective-permute-start(bf16[128,768]{1,0:T(8,128)(2,1)S(1)} %multiply_convert_fusion.13), channel_id=1, source_target_pairs={{0,3},{1,2},{2,1},{3,0},{4,7},{5,6},{6,5},{7,4},{8,11},{9,10},{10,... | collective-permute-start | bytes 589832 | tf_op jit(solution)/shard_map/ppermute | solution.py:53
  231.6 36.8 %collective-permute-start.10 = (bf16[128,768]{1,0:T(8,128)(2,1)S(1)}, bf16[128,768]{1,0:T(8,128)(2,1)S(1)}, u32[]{:S(2)}, u32[]{:S(2)}) collective-permute-start(bf16[128,768]{1,0:T(8,128)(2,1)S(1)} %multiply_convert_fusion.13), channel_id=1, source_target_pairs={{0,1},{1,0},{2,3},{3,2},{4,5},{5,4},{6,7},{7,6},{8,9},{9,8},{10,11... | collective-permute-start | bytes 589832 | tf_op jit(solution)/shard_map/ppermute | solution.py:50
  232.7 35.6 %collective-permute-start.9 = (bf16[128,768]{1,0:T(8,128)(2,1)S(1)}, bf16[128,768]{1,0:T(8,128)(2,1)S(1)}, u32[]{:S(2)}, u32[]{:S(2)}) collective-permute-start(bf16[128,768]{1,0:T(8,128)(2,1)S(1)} %multiply_convert_fusion.13), channel_id=1, source_target_pairs={{0,2},{2,0},{1,3},{3,1},{4,6},{6,4},{5,7},{7,5},{8,10},{10,8},{9,1... | collective-permute-start | bytes 589832 | tf_op jit(solution)/shard_map/ppermute | solution.py:52
  274.9 73.2 %collective-permute-start.19 = (bf16[128,768]{1,0:T(8,128)(2,1)S(1)}, bf16[128,768]{1,0:T(8,128)(2,1)}, u32[]{:S(2)}, u32[]{:S(2)}) collective-permute-start(bf16[128,768]{1,0:T(8,128)(2,1)S(1)} %bitcast.324), channel_id=1, source_target_pairs={{0,2},{2,0},{1,3},{3,1},{4,6},{6,4},{5,7},{7,5},{8,10},{10,8},{9,1... | collective-permute-start | bytes 589832 | tf_op jit(solution)/shard_map/ppermute | solution.py:52
  274.9 73.2 %collective-permute-start.18 = (bf16[128,768]{1,0:T(8,128)(2,1)S(1)}, bf16[128,768]{1,0:T(8,128)(2,1)}, u32[]{:S(2)}, u32[]{:S(2)}) collective-permute-start(bf16[128,768]{1,0:T(8,128)(2,1)S(1)} %bitcast.325), channel_id=1, source_target_pairs={{0,1},{1,0},{2,3},{3,2},{4,5},{5,4},{6,7},{7,6},{8,9},{9,8},{10,11... | collective-permute-start | bytes 589832 | tf_op jit(solution)/shard_map/ppermute | solution.py:50
  276.3 71.9 %collective-permute-start.20 = (bf16[128,768]{1,0:T(8,128)(2,1)S(1)}, bf16[128,768]{1,0:T(8,128)(2,1)}, u32[]{:S(2)}, u32[]{:S(2)}) collective-permute-start(bf16[128,768]{1,0:T(8,128)(2,1)S(1)} %bitcast.326), channel_id=1, source_target_pairs={{0,3},{1,2},{2,1},{3,0},{4,7},{5,6},{6,5},{7,4},{8,11},{9,10},{10,... | collective-permute-start | bytes 589832 | tf_op jit(solution)/shard_map/ppermute | solution.py:53
  290.6 52.4 %all-to-all-start.9 = ((bf16[4,24,1024]{2,1,0:T(8,128)(2,1)}), bf16[4,24,1024]{2,1,0:T(8,128)(2,1)S(1)}, u32[]{:S(2)}, u32[]{:S(2)}) async-start(bf16[4,24,1024]{2,1,0:T(8,128)(2,1)} %reshape.568), calls=%async_computation.9 | async-start | bytes 393216 | tf_op jit(solution)/shard_map/all_to_all | solution.py:42
  347.5 56.0 %all-gather.11.cloned.1.call-start = ((), (), s32[]{:S(2)}) async-start(), calls=%async_computation.29 | async-start | bytes 1769472 | tf_op jit(solution)/shard_map/all_gather | solution.py:629
  369.6 38.0 %all-to-all-start.10 = ((bf16[16,21,768]{2,1,0:T(8,128)(2,1)}), bf16[16,21,768]{2,1,0:T(8,128)(2,1)}, u32[]{:S(2)}, u32[]{:S(2)}) async-start(bf16[16,21,768]{2,1,0:T(8,128)(2,1)} %reshape.570), calls=%async_computation.10 | async-start | bytes 1179648 | tf_op jit(solution)/shard_map/all_to_all | solution.py:42
  470.0 27.1 %collective-permute-start.21 = (bf16[128,768]{1,0:T(8,128)(2,1)}, bf16[128,768]{1,0:T(8,128)(2,1)}, u32[]{:S(2)}, u32[]{:S(2)}) collective-permute-start(bf16[128,768]{1,0:T(8,128)(2,1)} %get-tuple-element.126), channel_id=1, source_target_pairs={{0,1},{1,0},{2,3},{3,2},{4,5},{5,4},{6,7},{7,6},{8,9},{9,8},{10,11... | collective-permute-start | bytes 589832 | tf_op jit(solution)/shard_map/ppermute | solution.py:50
  471.8 25.3 %collective-permute-start.23 = (bf16[128,768]{1,0:T(8,128)(2,1)}, bf16[128,768]{1,0:T(8,128)(2,1)}, u32[]{:S(2)}, u32[]{:S(2)}) collective-permute-start(bf16[128,768]{1,0:T(8,128)(2,1)} %get-tuple-element.127), channel_id=1, source_target_pairs={{0,3},{1,2},{2,1},{3,0},{4,7},{5,6},{6,5},{7,4},{8,11},{9,10},{10,... | collective-permute-start | bytes 589832 | tf_op jit(solution)/shard_map/ppermute | solution.py:53
  516.3 25.8 %all-to-all-start.27 = ((bf16[8,64,768]{2,1,0:T(8,128)(2,1)}), bf16[8,64,768]{2,1,0:T(8,128)(2,1)}, u32[]{:S(2)}, u32[]{:S(2)}) async-start(bf16[8,64,768]{2,1,0:T(8,128)(2,1)} %bitcast.373), calls=%async_computation.27 | async-start | bytes 1572864 | tf_op jit(solution)/shard_map/all_to_all | solution.py:42
  542.1 23.3 %all-to-all-start.15 = ((bf16[4,192,512]{2,1,0:T(8,128)(2,1)}), bf16[4,192,512]{2,1,0:T(8,128)(2,1)S(1)}, u32[]{:S(2)}, u32[]{:S(2)}) async-start(bf16[4,192,512]{2,1,0:T(8,128)(2,1)} %attend_back.2), calls=%async_computation.15 | async-start | bytes 1572864 | tf_op jit(solution)/shard_map/all_to_all | solution.py:42
  565.4 41.9 %all-to-all-start.25 = ((bf16[32,24,1024]{2,1,0:T(8,128)(2,1)}), bf16[32,24,1024]{2,1,0:T(8,128)(2,1)}, u32[]{:S(2)}, u32[]{:S(2)}) async-start(bf16[32,24,1024]{2,1,0:T(8,128)(2,1)} %bitcast.357), calls=%async_computation.25 | async-start | bytes 3145728 | tf_op jit(solution)/shard_map/all_to_all | solution.py:42
  627.5 33.6 %all-to-all-start.23 = ((bf16[32,24,768]{2,1,0:T(8,128)(2,1)}), bf16[32,24,768]{2,1,0:T(8,128)(2,1)S(1)}, u32[]{:S(2)}, u32[]{:S(2)}) async-start(bf16[32,24,768]{2,1,0:T(8,128)(2,1)} %bitcast.331), calls=%async_computation.23 | async-start | bytes 2359296 | tf_op jit(solution)/shard_map/all_to_all | solution.py:42
  661.1 25.3 %all-to-all-start.26 = ((bf16[8,64,768]{2,1,0:T(8,128)(2,1)}), bf16[8,64,768]{2,1,0:T(8,128)(2,1)}, u32[]{:S(2)}, u32[]{:S(2)}) async-start(bf16[8,64,768]{2,1,0:T(8,128)(2,1)} %bitcast.372), calls=%async_computation.26 | async-start | bytes 1572864 | tf_op jit(solution)/shard_map/all_to_all | solution.py:42
  706.4 30.4 %all-to-all-start.21 = ((bf16[32,24,594]{2,1,0:T(8,128)(2,1)}), bf16[32,24,594]{2,1,0:T(8,128)(2,1)S(1)}, u32[]{:S(2)}, u32[]{:S(2)}) async-start(bf16[32,24,594]{2,1,0:T(8,128)(2,1)} %bitcast.334), calls=%async_computation.21 | async-start | bytes 1966080 | tf_op jit(solution)/shard_map/all_to_all | solution.py:42
  744.4 32.2 %collective-permute-start.38 = (bf16[336,768]{1,0:T(8,128)(2,1)}, bf16[336,768]{1,0:T(8,128)(2,1)}, u32[]{:S(2)}, u32[]{:S(2)}) collective-permute-start(bf16[336,768]{1,0:T(8,128)(2,1)} %reshape.571), channel_id=1, source_target_pairs={{0,16},{16,0},{1,17},{17,1},{2,18},{18,2},{3,19},{19,3},{4,20},{20... | collective-permute-start | bytes 1548296 | tf_op jit(solution)/shard_map/ppermute | solution.py:483
  752.6 88.8 %all-to-all-start.24 = ((bf16[32,24,1024]{2,1,0:T(8,128)(2,1)}), bf16[32,24,1024]{2,1,0:T(8,128)(2,1)}, u32[]{:S(2)}, u32[]{:S(2)}) async-start(bf16[32,24,1024]{2,1,0:T(8,128)(2,1)} %bitcast.356), calls=%async_computation.24 | async-start | bytes 3145728 | tf_op jit(solution)/shard_map/all_to_all | solution.py:42
  758.5 37.3 %collective-permute-start.39 = (bf16[336,768]{1,0:T(8,128)(2,1)S(1)}, bf16[336,768]{1,0:T(8,128)(2,1)S(1)}, u32[]{:S(2)}, u32[]{:S(2)}) collective-permute-start(bf16[336,768]{1,0:T(8,128)(2,1)S(1)} %copy-done.37), channel_id=1, source_target_pairs={{0,16},{16,0},{1,17},{17,1},{2,18},{18,2},{3,19},{19,3},{4,20},{20... | collective-permute-start | bytes 1548296 | tf_op jit(solution)/shard_map/ppermute | solution.py:483
  825.4 29.1 %collective-permute-start.37 = (bf16[336,768]{1,0:T(8,128)(2,1)}, bf16[336,768]{1,0:T(8,128)(2,1)}, u32[]{:S(2)}, u32[]{:S(2)}) collective-permute-start(bf16[336,768]{1,0:T(8,128)(2,1)} %reshape.585), channel_id=1, source_target_pairs={{0,16},{16,0},{1,17},{17,1},{2,18},{18,2},{3,19},{19,3},{4,20},{20... | collective-permute-start | bytes 1548296 | tf_op jit(solution)/shard_map/ppermute | solution.py:483
  841.4 24.4 %all-to-all-start.19 = ((bf16[4,192,512]{2,1,0:T(8,128)(2,1)}), bf16[4,192,512]{2,1,0:T(8,128)(2,1)}, u32[]{:S(2)}, u32[]{:S(2)}) async-start(bf16[4,192,512]{2,1,0:T(8,128)(2,1)} %attend_back.3), calls=%async_computation.19 | async-start | bytes 1572864 | tf_op jit(solution)/shard_map/all_to_all | solution.py:42
  865.9 50.8 %all-to-all-start.22 = ((bf16[32,24,768]{2,1,0:T(8,128)(2,1)}), bf16[32,24,768]{2,1,0:T(8,128)(2,1)}, u32[]{:S(2)}, u32[]{:S(2)}) async-start(bf16[32,24,768]{2,1,0:T(8,128)(2,1)} %bitcast.330), calls=%async_computation.22 | async-start | bytes 2359296 | tf_op jit(solution)/shard_map/all_to_all | solution.py:42
  916.6 31.7 %all-to-all-start.20 = ((bf16[32,24,594]{2,1,0:T(8,128)(2,1)}), bf16[32,24,594]{2,1,0:T(8,128)(2,1)S(1)}, u32[]{:S(2)}, u32[]{:S(2)}) async-start(bf16[32,24,594]{2,1,0:T(8,128)(2,1)} %bitcast.335), calls=%async_computation.20 | async-start | bytes 1966080 | tf_op jit(solution)/shard_map/all_to_all | solution.py:42
  (113 other events, 1633.1 us)
Sparse Core Ops, SparseCore 0:
  11.6 58.0 all-gather.12
  71.8 50.5 all-gather.8
  125.3 56.6 all-gather.14
  350.7 52.8 all-gather.10

commit v2 on v1

v2 whole, which is shorter than its diff:
```python
import functools

import jax
import jax.numpy as jnp
from jax import lax
from jax.experimental import pallas as pl
from jax.experimental.pallas import tpu as pltpu
from jax.sharding import Mesh
from jax.sharding import PartitionSpec as P

D = 768
HEADS = 12
HEAD = 64
FF = 2048
EXPERTS = 16
LAYERS = 2
MOST = 21
SLOTS = -(-MOST // 8) * 8
TEAM_SIZE = 4
TEAM_HEADS = HEADS // TEAM_SIZE

ALL = ("dp", "z", "core", "ulysses")
SEQ = ("z", "core", "ulysses")
TEAM = ("core", "ulysses")
REST = ("dp", "z")

NORM_EPS = 1e-06
NEG_BIG = -1e30
PRECISE = lax.Precision.HIGHEST
F32 = jnp.float32
BF16 = jnp.bfloat16
QUERY_TILE = 256
VMEM_LIMIT = 48 * 1024 * 1024


def cost(flops, moved, steps=0):
    return pl.CostEstimate(flops=flops, bytes_accessed=moved, transcendentals=steps)


def contract(left, right, left_dim, right_dim):
    return lax.dot_general(
        left, right, (((left_dim,), (right_dim,)), ((), ())), preferred_element_type=F32
    )


def exchange(rows, axes):
    return lax.all_to_all(rows, axes, split_axis=0, concat_axis=0, tiled=True)


SWAP = [(0, 1), (1, 0)]


def from_member(rows, turn):
    if turn == 1:
        return lax.ppermute(rows, "ulysses", SWAP)
    if turn == 2:
        return lax.ppermute(rows, "core", SWAP)
    return lax.ppermute(rows, TEAM, [(i, 3 - i) for i in range(4)])


def team_gather(rows):
    return jnp.stack([rows] + [from_member(rows, turn) for turn in (1, 2, 3)])


def in_order(stacked, member):
    turns = [jnp.equal(member, i) for i in range(4)]
    pieces = []
    for k in range(4):
        piece = stacked[k ^ 3]
        for i in range(3):
            piece = jnp.where(turns[i], stacked[k ^ i], piece)
        pieces.append(piece)
    return jnp.stack(pieces)


def team_sum(parts):
    total = parts[0].astype(F32)
    for turn in (1, 2, 3):
        total = total + from_member(parts[turn].astype(BF16), turn).astype(F32)
    return total


def rms_factor(stream):
    return lax.rsqrt(jnp.mean(stream * stream, axis=-1, keepdims=True) + NORM_EPS)


def norm_back(stream, gain, factor, upstream):
    weighted = upstream * gain
    inner_mean = jnp.mean(weighted * stream, axis=-1, keepdims=True)
    grad_stream = factor * weighted - stream * factor * factor * factor * inner_mean
    grad_gain = jnp.sum(upstream * stream * factor, axis=0)
    return (grad_stream, grad_gain)


def attention_kernel(full_ref, some_ref, base_ref, rows_ref, limit_ref, out_ref, wide_ref, log_ref, keys):
    span = rows_ref.shape[2]
    step = pl.program_id(0)
    per_block = span // QUERY_TILE

    @pl.when(step == 0)
    def _():
        for s in range(rows_ref.shape[0]):
            keys[s] = rows_ref[s, HEAD : 2 * HEAD, :].T

    tile = base_ref[0] + step
    lanes = pl.ds(pl.multiple_of((tile % per_block) * QUERY_TILE, QUERY_TILE), QUERY_TILE)
    queries = rows_ref[tile // per_block, 0:HEAD, lanes] * BF16(HEAD**-0.5)
    limit = limit_ref[...]
    key_index = lax.broadcasted_iota(jnp.int32, (span, QUERY_TILE), 0)

    def sweep(s, state, masked):
        highest, total, running = state
        scores = jnp.dot(keys[s], queries, preferred_element_type=F32)
        if masked:
            scores = jnp.where(key_index < limit - s * span, scores, NEG_BIG)
        raised = jnp.maximum(highest, jnp.max(scores, axis=0, keepdims=True))
        terms = jnp.exp(scores - raised)
        shrink = jnp.exp(highest - raised)
        total = total * shrink + jnp.sum(terms, axis=0, keepdims=True)
        running = running * shrink + jnp.dot(
            rows_ref[s, 2 * HEAD :, :], terms.astype(BF16), preferred_element_type=F32
        )
        return (raised, total, running)

    state = (
        jnp.full((1, QUERY_TILE), NEG_BIG, F32),
        jnp.zeros((1, QUERY_TILE), F32),
        jnp.zeros((HEAD, QUERY_TILE), F32),
    )
    state = lax.fori_loop(0, full_ref[step], lambda s, c: sweep(s, c, False), state)
    state = lax.fori_loop(full_ref[step], some_ref[step], lambda s, c: sweep(s, c, True), state)
    highest, total, running = state
    result = running / total
    log_ref[...] = highest + jnp.log(total)
    wide_ref[...] = result
    stretch = out_ref.shape[2]
    for i in range(QUERY_TILE // stretch):
        out_ref[i] = result[:, i * stretch : (i + 1) * stretch].astype(BF16)


def attention_back_kernel(
    full_ref, some_ref, base_ref, rows_ref, limit_ref, grad_ref, wide_ref, log_ref, *refs
):
    out_ref, keys, values, key_sum, value_sum = refs[-5:]
    span = rows_ref.shape[2]
    blocks = rows_ref.shape[0]
    step = pl.program_id(0)
    per_block = span // QUERY_TILE

    @pl.when(step == 0)
    def _():
        for s in range(blocks):
            keys[s] = rows_ref[s, HEAD : 2 * HEAD, :].T
            values[s] = rows_ref[s, 2 * HEAD :, :].T
        key_sum[...] = jnp.zeros_like(key_sum)
        value_sum[...] = jnp.zeros_like(value_sum)
        out_ref[...] = jnp.zeros_like(out_ref)

    tile = base_ref[0] + step
    lanes = pl.ds(pl.multiple_of((tile % per_block) * QUERY_TILE, QUERY_TILE), QUERY_TILE)
    queries = rows_ref[tile // per_block, 0:HEAD, lanes] * BF16(HEAD**-0.5)
    limit = limit_ref[...]
    key_index = lax.broadcasted_iota(jnp.int32, (span, QUERY_TILE), 0)
    grads = jnp.concatenate([grad_ref[i] for i in range(grad_ref.shape[0])], axis=1)
    delta = jnp.sum(grads.astype(F32) * wide_ref[...], axis=0, keepdims=True)
    logs = log_ref[...]

    def sweep(s, query_grad, masked):
        scores = jnp.dot(keys[s], queries, preferred_element_type=F32)
        probs = jnp.exp(scores - logs)
        if masked:
            probs = jnp.where(key_index < limit - s * span, probs, 0.0)
        prob_grad = jnp.dot(values[s], grads, preferred_element_type=F32)
        score_grad = (probs * (prob_grad - delta)).astype(BF16)
        value_sum[s] += contract(grads, probs.astype(BF16), 1, 1)
        key_sum[s] += contract(queries, score_grad, 1, 1)
        return query_grad + jnp.dot(
            rows_ref[s, HEAD : 2 * HEAD, :], score_grad, preferred_element_type=F32
        )

    query_grad = jnp.zeros((HEAD, QUERY_TILE), F32)
    query_grad = lax.fori_loop(0, full_ref[step], lambda s, c: sweep(s, c, False), query_grad)
    query_grad = lax.fori_loop(
        full_ref[step], some_ref[step], lambda s, c: sweep(s, c, True), query_grad
    )
    out_ref[tile // per_block, 0:HEAD, lanes] = (query_grad * HEAD**-0.5).astype(BF16)

    @pl.when(step == pl.num_programs(0) - 1)
    def _():
        out_ref[:, HEAD : 2 * HEAD, :] = key_sum[...].astype(BF16)
        out_ref[:, 2 * HEAD :, :] = value_sum[...].astype(BF16)


def fixed_attention_kernel(rows_ref, limit_ref, out_ref, wide_ref, log_ref, keys, values):
    blocks, _, span = rows_ref.shape
    length = blocks * span
    stretch = out_ref.shape[2]
    for s in range(blocks):
        keys[s * span : (s + 1) * span, :] = rows_ref[s, HEAD : 2 * HEAD, :].T
        values[:, s * span : (s + 1) * span] = rows_ref[s, 2 * HEAD :, :]
    key_index = lax.broadcasted_iota(jnp.int32, (2 * QUERY_TILE, QUERY_TILE), 0)
    for tile in range(length // QUERY_TILE):
        start = tile * QUERY_TILE
        end = min(start + 2 * QUERY_TILE, length)
        lanes = slice(start % span, start % span + QUERY_TILE)
        queries = rows_ref[start // span, 0:HEAD, lanes] * BF16(HEAD**-0.5)
        scores = jnp.dot(keys[start:end, :], queries, preferred_element_type=F32)
        limit = limit_ref[:, start : start + QUERY_TILE] - start
        scores = jnp.where(key_index[: end - start] < limit, scores, NEG_BIG)
        highest = jnp.max(scores, axis=0, keepdims=True)
        if start > 0:
            before = jnp.dot(keys[:start, :], queries, preferred_element_type=F32)
            highest = jnp.maximum(highest, jnp.max(before, axis=0, keepdims=True))
        terms = jnp.exp(scores - highest)
        total = jnp.sum(terms, axis=0, keepdims=True)
        result = jnp.dot(values[:, start:end], terms.astype(BF16), preferred_element_type=F32)
        if start > 0:
            terms = jnp.exp(before - highest)
            total = total + jnp.sum(terms, axis=0, keepdims=True)
            result = result + jnp.dot(
                values[:, :start], terms.astype(BF16), preferred_element_type=F32
            )
        result = result / total
        log_ref[:, start : start + QUERY_TILE] = highest + jnp.log(total)
        wide_ref[:, start : start + QUERY_TILE] = result
        for i in range(QUERY_TILE // stretch):
            out_ref[start // stretch + i] = result[:, i * stretch : (i + 1) * stretch].astype(BF16)


def fixed_attention_back_kernel(rows_ref, limit_ref, grad_ref, wide_ref, log_ref, *refs):
    out_ref, keys, values, key_sum, value_sum = refs[-5:]
    blocks, _, span = rows_ref.shape
    length = blocks * span
    stretch = grad_ref.shape[2]
    for s in range(blocks):
        keys[s * span : (s + 1) * span, :] = rows_ref[s, HEAD : 2 * HEAD, :].T
        values[s * span : (s + 1) * span, :] = rows_ref[s, 2 * HEAD :, :].T
    key_sum[...] = jnp.zeros_like(key_sum)
    value_sum[...] = jnp.zeros_like(value_sum)
    key_index = lax.broadcasted_iota(jnp.int32, (2 * QUERY_TILE, QUERY_TILE), 0)
    for tile in range(length // QUERY_TILE):
        start = tile * QUERY_TILE
        end = min(start + 2 * QUERY_TILE, length)
        lanes = slice(start % span, start % span + QUERY_TILE)
        queries = rows_ref[start // span, 0:HEAD, lanes] * BF16(HEAD**-0.5)
        pieces = QUERY_TILE // stretch
        grads = jnp.concatenate([grad_ref[tile * pieces + i] for i in range(pieces)], axis=1)
        wide = wide_ref[:, start : start + QUERY_TILE]
        delta = jnp.sum(grads.astype(F32) * wide, axis=0, keepdims=True)
        logs = log_ref[:, start : start + QUERY_TILE]
        limit = limit_ref[:, start : start + QUERY_TILE] - start
        query_grad = jnp.zeros((HEAD, QUERY_TILE), F32)
        for low, high in ((0, start), (start, end)):
            if low == high:
                continue
            scores = jnp.dot(keys[low:high, :], queries, preferred_element_type=F32)
            probs = jnp.exp(scores - logs)
            if low == start:
                probs = jnp.where(key_index[: high - low] < limit, probs, 0.0)
            prob_grad = jnp.dot(values[low:high, :], grads, preferred_element_type=F32)
            score_grad = (probs * (prob_grad - delta)).astype(BF16)
            value_sum[:, low:high] += contract(grads, probs.astype(BF16), 1, 1)
            key_sum[:, low:high] += contract(queries, score_grad, 1, 1)
            query_grad = query_grad + contract(keys[low:high, :], score_grad, 0, 0)
        out_ref[start // span, 0:HEAD, lanes] = (query_grad * HEAD**-0.5).astype(BF16)
    for s in range(blocks):
        out_ref[s, HEAD : 2 * HEAD, :] = key_sum[:, s * span : (s + 1) * span].astype(BF16)
        out_ref[s, 2 * HEAD :, :] = value_sum[:, s * span : (s + 1) * span].astype(BF16)


IN_VMEM = pl.BlockSpec(memory_space=pltpu.VMEM)
ANYWHERE = pl.BlockSpec(memory_space=pl.ANY)


def fixed_attention(rows, limit, stretch):
    blocks, _, span = rows.shape
    length = blocks * span
    return pl.pallas_call(
        fixed_attention_kernel,
        in_specs=[IN_VMEM] * 2,
        out_specs=[IN_VMEM] * 3,
        out_shape=[
            jax.ShapeDtypeStruct((length // stretch, HEAD, stretch), BF16),
            jax.ShapeDtypeStruct((HEAD, length), F32),
            jax.ShapeDtypeStruct((1, length), F32),
        ],
        scratch_shapes=[pltpu.VMEM((length, HEAD), BF16), pltpu.VMEM((HEAD, length), BF16)],
        compiler_params=pltpu.CompilerParams(vmem_limit_bytes=VMEM_LIMIT),
        cost_estimate=cost(rows.size * length // 48, rows.size * 4, length * length),
        name="attend",
    )(rows, limit)


def fixed_attention_back(rows, limit, grads, wide, logs, later_than):
    blocks, _, span = rows.shape
    length = blocks * span
    return pl.pallas_call(
        fixed_attention_back_kernel,
        in_specs=[IN_VMEM] * 5 + [ANYWHERE] * len(later_than),
        out_specs=IN_VMEM,
        out_shape=jax.ShapeDtypeStruct(rows.shape, BF16),
        scratch_shapes=[
            pltpu.VMEM((length, HEAD), BF16),
            pltpu.VMEM((length, HEAD), BF16),
            pltpu.VMEM((HEAD, length), F32),
            pltpu.VMEM((HEAD, length), F32),
        ],
        compiler_params=pltpu.CompilerParams(vmem_limit_bytes=VMEM_LIMIT),
        cost_estimate=cost(rows.size * length // 16, rows.size * 4, length * length),
        name="attend_back",
    )(rows, limit, grads, wide, logs, *later_than)


def whole(shape):
    return pl.BlockSpec(shape, lambda step, *_: (0,) * len(shape))


def tile_at(step, full, some, base):
    return (0, base[0] + step)


def attention(rows, spans, stretch):
    full, some, base, limit, tiles, parts = spans
    if parts == 1:
        return fixed_attention(rows, limit, stretch)
    blocks, _, span = rows.shape
    length = tiles * QUERY_TILE
    return pl.pallas_call(
        attention_kernel,
        grid_spec=pltpu.PrefetchScalarGridSpec(
            num_scalar_prefetch=3,
            grid=(tiles,),
            in_specs=[whole(rows.shape), pl.BlockSpec((1, QUERY_TILE), tile_at)],
            out_specs=[
                pl.BlockSpec((QUERY_TILE // stretch, HEAD, stretch), lambda step, *_: (step, 0, 0)),
                pl.BlockSpec((HEAD, QUERY_TILE), lambda step, *_: (0, step)),
                pl.BlockSpec((1, QUERY_TILE), lambda step, *_: (0, step)),
            ],
            scratch_shapes=[pltpu.VMEM((blocks, span, HEAD), BF16)],
        ),
        out_shape=[
            jax.ShapeDtypeStruct((length // stretch, HEAD, stretch), BF16),
            jax.ShapeDtypeStruct((HEAD, length), F32),
            jax.ShapeDtypeStruct((1, length), F32),
        ],
        compiler_params=pltpu.CompilerParams(vmem_limit_bytes=VMEM_LIMIT),
        cost_estimate=cost(rows.size * length // 48, rows.size * 4, length * length),
        name="attend",
    )(full, some, base, rows, limit)


def attention_back(rows, spans, grads, wide, logs, later_than):
    full, some, base, limit, tiles, parts = spans
    if parts == 1:
        return fixed_attention_back(rows, limit, grads, wide, logs, later_than)
    blocks, _, span = rows.shape
    stretch = grads.shape[2]
    return pl.pallas_call(
        attention_back_kernel,
        grid_spec=pltpu.PrefetchScalarGridSpec(
            num_scalar_prefetch=3,
            grid=(tiles,),
            in_specs=[
                whole(rows.shape),
                pl.BlockSpec((1, QUERY_TILE), tile_at),
                pl.BlockSpec((QUERY_TILE // stretch, HEAD, stretch), lambda step, *_: (step, 0, 0)),
                pl.BlockSpec((HEAD, QUERY_TILE), lambda step, *_: (0, step)),
                pl.BlockSpec((1, QUERY_TILE), lambda step, *_: (0, step)),
                *[pl.BlockSpec(memory_space=pl.ANY)] * len(later_than),
            ],
            out_specs=whole(rows.shape),
            scratch_shapes=[
                pltpu.VMEM((blocks, span, HEAD), BF16),
                pltpu.VMEM((blocks, span, HEAD), BF16),
                pltpu.VMEM((blocks, HEAD, span), F32),
                pltpu.VMEM((blocks, HEAD, span), F32),
            ],
        ),
        out_shape=jax.ShapeDtypeStruct(rows.shape, BF16),
        compiler_params=pltpu.CompilerParams(vmem_limit_bytes=VMEM_LIMIT),
        cost_estimate=cost(rows.size * tiles * QUERY_TILE // 16, rows.size * 4, rows.size),
        name="attend_back",
    )(full, some, base, rows, limit, grads, wide, logs, *later_than)


def turn_heads(parts, cosine, sine, direction):
    first, second = parts[:, :2, 0], parts[:, :2, 1]
    turned = jnp.stack(
        [
            first * cosine - direction * (second * sine),
            second * cosine + direction * (first * sine),
        ],
        axis=2,
    )
    return jnp.concatenate([turned, parts[:, 2:]], axis=1)


def logistic(values):
    return 0.5 * jnp.tanh(0.5 * values) + 0.5


def swiglu_back(gate_pre, up_pre, hidden_grad):
    sigmoid_gate = logistic(gate_pre)
    silu_gate = gate_pre * sigmoid_gate
    gate_grad = hidden_grad * up_pre * (sigmoid_gate + silu_gate * (1.0 - sigmoid_gate))
    up_grad = hidden_grad * silu_gate
    return (gate_grad.astype(BF16), up_grad.astype(BF16))


def swiglu(gate_pre, up_pre):
    return (gate_pre * logistic(gate_pre) * up_pre).astype(BF16)


def expert_kernel(forward, backward, *refs):
    inputs = 1 + backward
    rows_ref, grads_ref = refs[0], refs[inputs - 1]
    gate_ref, up_ref, down_ref, out_ref, total = refs[inputs:]
    step = pl.program_id(0)
    rows = rows_ref[...]
    gate, up, down = gate_ref[0, 0], up_ref[0, 0], down_ref[0, 0]
    gate_pre = jnp.dot(rows, gate, preferred_element_type=F32)
    up_pre = jnp.dot(rows, up, preferred_element_type=F32)
    terms = []
    if forward:
        terms.append(jnp.dot(swiglu(gate_pre, up_pre), down, preferred_element_type=F32))
    if backward:
        hidden_grad = contract(grads_ref[...], down, 1, 1).astype(BF16).astype(F32)
        gate_grad, up_grad = swiglu_back(gate_pre, up_pre, hidden_grad)
        terms.append(contract(gate_grad, gate, 1, 1) + contract(up_grad, up, 1, 1))

    @pl.when(step == 0)
    def _():
        for i, term in enumerate(terms):
            total[:, i * D : (i + 1) * D] = term

    @pl.when(step > 0)
    def _():
        for i, term in enumerate(terms):
            total[:, i * D : (i + 1) * D] += term

    @pl.when(step == pl.num_programs(0) - 1)
    def _():
        out_ref[...] = total[...].astype(BF16)


def run_expert(layer, joint, down, rows, grads, forward):
    half = joint.shape[3] // 2
    chunk = min(512, half)
    chunks = half // chunk
    given = [rows] + ([grads] if grads is not None else [])
    count = rows[0].shape[0]
    width = D * (int(forward) + int(grads is not None))
    return pl.pallas_call(
        functools.partial(expert_kernel, forward, grads is not None),
        grid=(chunks,),
        in_specs=[
            *[pl.BlockSpec((count, D), lambda i, at=at: (0, at)) for _, at in given],
            pl.BlockSpec((1, 1, D, chunk), lambda i: (layer, 0, 0, i)),
            pl.BlockSpec((1, 1, D, chunk), lambda i: (layer, 0, 0, chunks + i)),
            pl.BlockSpec((1, 1, chunk, D), lambda i: (layer, 0, i, 0)),
        ],
        out_specs=pl.BlockSpec((count, width), lambda i: (0, 0)),
        out_shape=jax.ShapeDtypeStruct((count, width), BF16),
        scratch_shapes=[pltpu.VMEM((count, width), F32)],
        compiler_params=pltpu.CompilerParams(vmem_limit_bytes=VMEM_LIMIT),
        cost_estimate=cost(
            2 * count * D * half * (2 + int(forward) + 3 * int(grads is not None)),
            6 * D * half + 4 * count * width,
            count * half,
        ),
        name="expert_forward" if grads is None else "expert_both" if forward else "expert_back",
    )(*[array for array, _ in given], joint, joint, down)


def expert_grad_kernel(slot_ref, own_rows, own_grads, other_rows, other_grads, gate_ref, up_ref, down_ref, *refs):
    joint_out, down_out, rows_all, grads_all, turned, hold = refs[-6:]
    count = own_rows.shape[0]

    @pl.when((pl.program_id(0) == 0) & (pl.program_id(1) == 0))
    def _():
        own = pl.ds(pl.multiple_of(slot_ref[0] * count, count), count)
        other = pl.ds(pl.multiple_of((1 - slot_ref[0]) * count, count), count)
        rows_all[own, :] = own_rows[...]
        rows_all[other, :] = other_rows[...]
        grads_all[own, :] = own_grads[...]
        grads_all[other, :] = other_grads[...]
        turned[...] = rows_all[...].T

    @pl.when(pl.program_id(1) == 0)
    def _():
        rows = rows_all[...]
        grads = grads_all[...]
        gate_pre = jnp.dot(rows, gate_ref[0, 0], preferred_element_type=F32)
        up_pre = jnp.dot(rows, up_ref[0, 0], preferred_element_type=F32)
        hidden_grad = contract(grads, down_ref[0, 0], 1, 1).astype(BF16).astype(F32)
        gate_grad, up_grad = swiglu_back(gate_pre, up_pre, hidden_grad)
        hold[...] = up_grad
        down_out[0, 0] = contract(swiglu(gate_pre, up_pre), grads, 0, 0)
        joint_out[0, 0] = jnp.dot(turned[...], gate_grad, preferred_element_type=F32)

    @pl.when(pl.program_id(1) == 1)
    def _():
        joint_out[0, 0] = jnp.dot(turned[...], hold[...], preferred_element_type=F32)


def expert_grads(layer, own, other, joint, down, before, later_than):
    half = joint.shape[3] // 2
    given = [*own, *other]
    count = given[0][0].shape[0]
    chunk = min(512 if count <= 512 else 128, half)
    chunks = half // chunk
    slot = lax.axis_index("dp").astype(jnp.int32).reshape(1)
    in_specs = [
        pl.BlockSpec(memory_space=pltpu.SMEM),
        *[pl.BlockSpec((count, D), lambda i, h, at=at: (0, at)) for _, at in given],
        pl.BlockSpec((1, 1, D, chunk), lambda i, h: (layer, 0, 0, i)),
        pl.BlockSpec((1, 1, D, chunk), lambda i, h: (layer, 0, 0, chunks + i)),
        pl.BlockSpec((1, 1, chunk, D), lambda i, h: (layer, 0, i, 0)),
    ]
    operands = [slot] + [array for array, _ in given] + [joint, joint, down]
    aliases = {}
    if before is not None:
        aliases = {len(operands): 0, len(operands) + 1: 1}
        operands += list(before)
    operands.append(later_than)
    in_specs += [pl.BlockSpec(memory_space=pl.ANY)] * (len(operands) - len(in_specs))
    return pl.pallas_call(
        expert_grad_kernel,
        grid=(chunks, 2),
        in_specs=in_specs,
        out_specs=[
            pl.BlockSpec((1, 1, D, chunk), lambda i, h: (layer, 0, 0, h * chunks + i)),
            pl.BlockSpec((1, 1, chunk, D), lambda i, h: (layer, 0, i, 0)),
        ],
        out_shape=[
            jax.ShapeDtypeStruct(joint.shape, F32),
            jax.ShapeDtypeStruct(down.shape, F32),
        ],
        scratch_shapes=[
            pltpu.VMEM((2 * count, D), BF16),
            pltpu.VMEM((2 * count, D), BF16),
            pltpu.VMEM((D, 2 * count), BF16),
            pltpu.VMEM((2 * count, chunk), BF16),
        ],
        input_output_aliases=aliases,
        compiler_params=pltpu.CompilerParams(vmem_limit_bytes=VMEM_LIMIT),
        cost_estimate=cost((6 if layer == 0 else 24) * count * D * half, 6 * D * half),
        name="expert_grads",
    )(*operands)


def nothing(*refs):
    pass


def later(rows, *others):
    return pl.pallas_call(
        nothing,
        in_specs=[pl.BlockSpec(memory_space=pl.ANY)] * (1 + len(others)),
        out_specs=pl.BlockSpec(memory_space=pl.ANY),
        out_shape=jax.ShapeDtypeStruct(rows.shape, rows.dtype),
        input_output_aliases={0: 0},
        name="later",
    )(rows, *others)


def route_tables(route_ids):
    stretch_rows = route_ids.shape[0]
    experts_row = jnp.arange(EXPERTS, dtype=jnp.int32)
    route_hits = (route_ids[:, :, None] == experts_row[None, None, :]).astype(jnp.int32)
    running = (
        jnp.cumsum(route_hits.reshape(2 * stretch_rows, EXPERTS), axis=0).reshape(
            stretch_rows, 2, EXPERTS
        )
        - 1
    )
    slot_index = jnp.sum(route_hits * running, axis=2)
    route_rows = route_ids * SLOTS + slot_index
    all_rows = jnp.arange(EXPERTS * SLOTS, dtype=jnp.int32)
    tables = [
        (route_rows[:, c, None] == all_rows[None, :]).astype(BF16) for c in range(2)
    ]
    return (tables, route_hits.astype(F32))


def send_rows(outgoing, split_count):
    width = outgoing.shape[1]
    outgoing = outgoing.reshape(EXPERTS, SLOTS, width)
    if split_count > 1:
        outgoing = jnp.repeat(outgoing, split_count, axis=0)
    return exchange(outgoing, SEQ).reshape(-1, width)


def return_rows(rows, split_count):
    width = rows.shape[1]
    returned = exchange(rows.reshape(-1, SLOTS, width), SEQ)
    if split_count > 1:
        returned = (
            returned.reshape(EXPERTS, split_count, SLOTS, width).astype(F32).sum(axis=1)
        ).astype(BF16)
    return returned.reshape(EXPERTS * SLOTS, width)


def attention_start(stream, first_rows, gain_one, qkv_weight, context):
    stretch = stream.shape[0]
    group = TEAM_SIZE * stretch
    member = context["member"]
    factor_one = rms_factor(stream)
    if first_rows is not None:
        wide_rows = first_rows.astype(F32)
        normed_team = (wide_rows * rms_factor(wide_rows) * gain_one).astype(BF16)
    else:
        normed = (stream * factor_one * gain_one).astype(BF16)
        normed_team = in_order(team_gather(normed), member).reshape(group, D)
    projected = contract(qkv_weight, normed_team, 0, 1)
    turned = turn_heads(
        projected.reshape(TEAM_HEADS, 3, 2, HEAD // 2, group),
        context["cosine"],
        context["sine"],
        1.0,
    )
    heads = turned.astype(BF16).reshape(TEAM_HEADS, 3 * HEAD, group)
    heads = jnp.concatenate([heads, jnp.zeros((1,) + heads.shape[1:], BF16)], axis=0)
    parts = context["parts"]
    if parts > 1:
        heads = jnp.repeat(heads, parts, axis=0)
    head_rows = exchange(heads, "z")
    saved = dict(
        stream=stream, factor_one=factor_one, normed_team=normed_team, head_rows=head_rows
    )
    return (head_rows, saved)


def attend(head_rows, saved, context, stretch):
    attended, wide, logs = attention(head_rows, context["spans"], stretch)
    saved.update(attended=attended, wide=wide, logs=logs)


def attention_end(stream, saved, out_weight, context):
    stretch = stream.shape[0]
    parts = context["parts"]
    attended = saved["attended"]
    pieces = context["pieces"]
    if parts > 1:
        attended = lax.dynamic_update_slice_in_dim(
            jnp.zeros((pieces, HEAD, stretch), BF16),
            attended,
            context["part"] * (pieces // parts),
            0,
        )
    back = exchange(attended, SEQ)
    if parts > 1:
        back = (
            back.reshape(TEAM_SIZE, parts, TEAM_SIZE, HEAD, stretch).astype(F32).sum(axis=1)
        ).astype(BF16)
    back = back.reshape(TEAM_SIZE, TEAM_SIZE, HEAD, stretch)[:TEAM_HEADS]
    mixed = back.transpose(1, 0, 2, 3).reshape(D, stretch)
    middle = stream + contract(mixed, out_weight, 0, 0)
    saved.update(mixed=mixed)
    return middle


def feed_start(middle, weights, context):
    gain_two, router_weight = weights[3:5]
    factor_two = rms_factor(middle)
    normed_ffn = (middle * factor_two * gain_two).astype(BF16)
    logits = jnp.dot(normed_ffn, router_weight, preferred_element_type=F32)
    picked = jnp.sum(logits[:, None, :] * context["hits"], axis=2)
    gate_values = jax.nn.softmax(picked, axis=1)
    return dict(
        middle=middle, factor_two=factor_two, normed_ffn=normed_ffn, gate_values=gate_values
    )


def outgoing_rows(feed, context):
    table_one, table_two = context["tables"]
    return contract(table_one + table_two, feed["normed_ffn"], 0, 0).astype(BF16)


def outgoing_grads(feed, upstream, context):
    table_one, table_two = context["tables"]
    gates = feed["gate_values"]
    return (
        contract(table_one, (gates[:, 0:1] * upstream).astype(BF16), 0, 0)
        + contract(table_two, (gates[:, 1:2] * upstream).astype(BF16), 0, 0)
    ).astype(BF16)


def shared_forward(feed, weights, token):
    joint_weight, down_weight = weights[5:7]
    stretch = feed["normed_ffn"].shape[0]
    ffn_team = team_gather(feed["normed_ffn"]).reshape(TEAM_SIZE * stretch, D)
    ffn_team = later(ffn_team, token)
    shared_joint = jnp.dot(ffn_team, joint_weight, preferred_element_type=F32)
    half = shared_joint.shape[1] // 2
    shared_hidden = swiglu(shared_joint[:, :half], shared_joint[:, half:])
    shared_out = team_sum(
        jnp.dot(shared_hidden, down_weight, preferred_element_type=F32).reshape(
            TEAM_SIZE, stretch, D
        )
    )
    feed.update(ffn_team=ffn_team, shared_joint=shared_joint, shared_hidden=shared_hidden)
    return shared_out


def shared_backward(feed, grad_team, weights):
    joint_weight, down_weight = weights[5:7]
    shared_joint = feed["shared_joint"]
    half = shared_joint.shape[1] // 2
    hidden_grad = contract(grad_team, down_weight, 1, 1).astype(BF16).astype(F32)
    joint_grad = jnp.concatenate(
        swiglu_back(shared_joint[:, :half], shared_joint[:, half:], hidden_grad), axis=1
    )
    normed_grad = team_sum(
        contract(joint_grad, joint_weight, 1, 1).reshape(TEAM_SIZE, -1, D)
    )
    grad_down = contract(feed["shared_hidden"], grad_team, 0, 0).astype(BF16)
    grad_joint = contract(feed["ffn_team"], joint_grad, 0, 0).astype(BF16)
    return (normed_grad, grad_joint, grad_down)


def feed_output(feed, shared_out, returned, context):
    table_one, table_two = context["tables"]
    choices = [
        jnp.dot(table, returned, preferred_element_type=F32) for table in (table_one, table_two)
    ]
    gates = feed["gate_values"]
    feed["choices"] = choices
    return (
        feed["middle"] + shared_out + gates[:, 0:1] * choices[0] + gates[:, 1:2] * choices[1]
    )


def feed_backward(feed, upstream, shared_grad, returned_grad, weights, context):
    gain_two, router_weight = weights[3:5]
    table_one, table_two = context["tables"]
    gates = feed["gate_values"]
    choice_one, choice_two = feed["choices"]
    lead_grad = (
        gates[:, 0:1]
        * gates[:, 1:2]
        * jnp.sum((choice_one - choice_two) * upstream, axis=1, keepdims=True)
    )
    hits = context["hits"]
    logit_grad = lead_grad * (hits[:, 0, :] - hits[:, 1, :])
    grad_router = jnp.dot(feed["normed_ffn"].astype(F32).T, logit_grad, precision=PRECISE)
    normed_grad = (
        shared_grad
        + jnp.dot(logit_grad, router_weight.astype(F32).T, precision=PRECISE)
        + jnp.dot(table_one + table_two, returned_grad, preferred_element_type=F32)
    )
    norm_grad, grad_gain = norm_back(feed["middle"], gain_two, feed["factor_two"], normed_grad)
    return (upstream + norm_grad, grad_gain, grad_router)


def attention_backward(middle_grad, weights, context, saved, later_than, before_end, experts):
    gain_one, qkv_weight, out_weight = weights[:3]
    stretch = middle_grad.shape[0]
    group = TEAM_SIZE * stretch
    member = context["member"]
    attn_grad = middle_grad.astype(BF16)
    mixed_grad = contract(out_weight, attn_grad, 1, 1).astype(BF16)
    mixed_grad = mixed_grad.reshape(TEAM_SIZE, TEAM_HEADS, HEAD, stretch).transpose(1, 0, 2, 3)
    mixed_grad = jnp.concatenate(
        [mixed_grad, jnp.zeros((1,) + mixed_grad.shape[1:], BF16)], axis=0
    )
    parts = context["parts"]
    if parts > 1:
        mixed_grad = jnp.repeat(mixed_grad, parts, axis=0)
    pieces = context["pieces"]
    head_grad = exchange(mixed_grad.reshape(-1, HEAD, stretch), SEQ)
    if parts > 1:
        head_grad = lax.dynamic_slice_in_dim(
            head_grad, context["part"] * (pieces // parts), pieces // parts, 0
        )
    rows_grad = attention_back(
        saved["head_rows"], context["spans"], head_grad, saved["wide"], saved["logs"], later_than
    )
    terms = expert_grads(*experts, rows_grad)
    tokens = [before_end] if experts[0] == 0 else [before_end, terms[1]]
    team_grad = later(exchange(rows_grad, "z"), *tokens)
    if parts > 1:
        team_grad = team_grad.reshape(TEAM_SIZE, parts, 3 * HEAD, group).astype(F32).sum(axis=1)
        team_grad = team_grad.astype(BF16)
    projected_grad = turn_heads(
        team_grad[:TEAM_HEADS].astype(F32).reshape(TEAM_HEADS, 3, 2, HEAD // 2, group),
        context["cosine"],
        context["sine"],
        -1.0,
    )
    projected_grad = projected_grad.astype(BF16).reshape(TEAM_HEADS * 3 * HEAD, group)
    grad_qkv = contract(saved["normed_team"], projected_grad, 0, 1).astype(BF16)
    team_part = contract(projected_grad, qkv_weight, 0, 1).astype(BF16)
    team_part = in_order(team_part.reshape(TEAM_SIZE, stretch, D), member)
    norm_grad, grad_gain = norm_back(
        saved["stream"], gain_one, saved["factor_one"], team_sum(team_part)
    )
    return (middle_grad + norm_grad, grad_gain, grad_qkv, terms)


def team_turn(rows, member):
    pieces = rows.reshape(TEAM_SIZE, -1, rows.shape[1])
    parts = [lax.dynamic_index_in_dim(pieces, member ^ k, 0, keepdims=False) for k in range(4)]
    return in_order(
        jnp.stack([parts[0]] + [from_member(parts[k], k) for k in (1, 2, 3)]), member
    )


def padded_down(grad_down, rest, width):
    blocks = grad_down.reshape(rest, -1, D)
    blocks = jnp.pad(blocks, ((0, 0), (0, TEAM_SIZE * width - blocks.shape[1]), (0, 0)))
    return blocks.reshape(D, D)


def swap_halves(rows):
    halves = rows.reshape(2, -1, rows.shape[1])
    at = lax.axis_index("dp")
    mine = lax.dynamic_index_in_dim(halves, at, 0, keepdims=False)
    other = lax.dynamic_index_in_dim(halves, 1 - at, 0, keepdims=False)
    return (mine, other)


def dp_sum(mine, other, *tokens):
    arrived = lax.ppermute(other, "dp", SWAP)
    if tokens:
        arrived = later(arrived, *tokens)
    return (mine.astype(F32) + arrived.astype(F32)).astype(BF16)


def z_sum(rows):
    return lax.psum_scatter(rows, "z", scatter_dimension=0, tiled=True)


def merge_feed_grads(grad_joint, grad_out, grad_down):
    total = lax.axis_size(ALL)
    rest, width = total // TEAM_SIZE, D // total
    return jnp.concatenate([grad_joint, grad_out, padded_down(grad_down, rest, width)], axis=1)


def feed_sums(mine, member):
    edge = mine.shape[1] - D
    down_sum = mine[: FF // lax.axis_size(ALL), edge:].astype(F32)
    turned = team_turn(mine[:, :edge], member).astype(F32)
    return (turned[:, :, : edge - D], turned[:, :, edge - D :], down_sum)


def qkv_order(columns):
    width = columns.shape[1]
    return (
        columns.reshape(TEAM_SIZE, width, TEAM_HEADS, 3, HEAD)
        .transpose(1, 3, 0, 2, 4)
        .reshape(width, 3 * D)
    )


def joint_order(columns):
    width = columns.shape[1]
    total = lax.axis_size(ALL)
    return (
        columns.reshape(TEAM_SIZE, width, 2, total // TEAM_SIZE, FF // total)
        .transpose(1, 2, 3, 0, 4)
        .reshape(width, 2 * FF)
    )


def pack_small(grad_gain_one, grad_gain_two, grad_router):
    small = jnp.concatenate([grad_gain_one[:, None], grad_gain_two[:, None], grad_router], axis=1)
    return jnp.pad(small, ((0, 0), (0, 64 - small.shape[1]))).astype(BF16)


def qkv_sums(grad_qkv, small):
    total = lax.axis_size(ALL)
    packed = jnp.concatenate([grad_qkv, small], axis=1)
    packed = exchange(packed.reshape(total, D // total, -1), ALL).astype(F32)
    edge = grad_qkv.shape[1]
    small_sum = packed[:, :, edge:].sum(axis=0)
    columns = packed[:, :, :edge].reshape(-1, TEAM_SIZE, D // total, edge).sum(axis=0)
    return (columns, small_sum)


def spread(rows, axes):
    count = lax.axis_size(axes)
    copies = jnp.broadcast_to(rows[None], (count,) + rows.shape)
    return exchange(copies, axes).reshape((-1,) + rows.shape[1:])


def dp_rows(rows):
    other = lax.ppermute(rows, "dp", SWAP)
    first = lax.axis_index("dp") == 0
    return jnp.concatenate([jnp.where(first, rows, other), jnp.where(first, other, rows)], axis=0)


def small_weights(gain_attn, gain_ffn, w_router):
    width = gain_attn.shape[1]
    small = jnp.concatenate(
        [gain_attn.T, gain_ffn.T, w_router.transpose(1, 0, 2).reshape(width, -1)], axis=1
    )
    return jnp.broadcast_to(small[None], (TEAM_SIZE,) + small.shape)


def split_small(smalls):
    smalls = smalls.astype(F32)
    gains, routers = [], []
    for layer in range(LAYERS):
        gains.append((smalls[:, layer], smalls[:, LAYERS + layer]))
        at = 2 * LAYERS + layer * EXPERTS
        routers.append(smalls[:, at : at + EXPERTS].astype(BF16))
    return (gains, routers)


def qkv_columns(w_qkv):
    width = w_qkv.shape[0]
    blocks = w_qkv.reshape(width, 3, TEAM_SIZE, TEAM_HEADS, HEAD)
    return blocks.transpose(2, 0, 3, 1, 4).reshape(TEAM_SIZE, width, -1)


def joint_columns(shared_gate_up):
    total = lax.axis_size(ALL)
    width = shared_gate_up.shape[0]
    blocks = shared_gate_up.reshape(width, 2, total // TEAM_SIZE, TEAM_SIZE, FF // total)
    return blocks.transpose(3, 0, 1, 2, 4).reshape(TEAM_SIZE, width, -1)


def padded_rows(shared_down):
    total = lax.axis_size(ALL)
    return jnp.pad(shared_down, ((0, TEAM_SIZE * D // total - shared_down.shape[0]), (0, 0)))


def down_rows(padded):
    total = lax.axis_size(ALL)
    return padded.reshape(total // TEAM_SIZE, -1, D)[:, : FF // total].reshape(-1, D)


def side_by_side(*arrays):
    return jnp.concatenate(arrays, axis=2)


def copies(rows):
    return jnp.broadcast_to(rows[None], (TEAM_SIZE,) + rows.shape)


def z_gather(rows):
    return lax.all_gather(rows, "z", axis=0, tiled=True)


def rest_gather(rows):
    return lax.all_gather(rows, REST, axis=0, tiled=True)


def dp_gather(rows, edges, token):
    parts = []
    for low, high in zip(edges, edges[1:]):
        token = dp_rows(later(rows[:, low:high], token))
        parts.append(token)
    return parts


def layers(
    x_in,
    cotangent,
    gain_attn,
    w_qkv,
    w_out,
    gain_ffn,
    w_router,
    shared_gate_up,
    shared_down,
    joint,
    down,
    context,
):
    split_count = context["split_count"]
    member = context["member"]
    stretch = x_in.shape[0]
    group = TEAM_SIZE * stretch
    last = LAYERS - 1
    stream = x_in.astype(F32)
    upstream = cotangent.astype(F32)
    grad_team = team_gather(cotangent).reshape(group, D)
    kept, feeds, rows_held = [], [], [None] * LAYERS
    weights = []

    width = w_qkv.shape[1]
    qkv_width, joint_width = 3 * D // TEAM_SIZE, 2 * FF // TEAM_SIZE
    small = small_weights(gain_attn, gain_ffn, w_router)
    first_width = qkv_width + small.shape[2]
    rows = exchange(
        side_by_side(
            qkv_columns(w_qkv[0]), small, copies(w_out[0]), joint_columns(shared_gate_up[0])
        ),
        TEAM,
    ).reshape(TEAM_SIZE * width, -1)
    first_rows = spread(rows[:, :first_width], "z")
    main_rows = z_gather(later(rows[:, first_width:], first_rows))
    following = [padded_rows(shared_down[0])]
    sizes = []
    if LAYERS > 1:
        rows = side_by_side(
            *[qkv_columns(w_qkv[layer]) for layer in range(1, LAYERS)],
            *[copies(w_out[layer]) for layer in range(1, LAYERS)],
            *[joint_columns(shared_gate_up[layer]) for layer in range(1, LAYERS)],
        )
        rows = team_turn(rows.reshape(TEAM_SIZE * width, -1), member)
        rows = rows.reshape(TEAM_SIZE * width, -1)
        edge = (LAYERS - 1) * qkv_width
        following.append(rows[:, :edge])
        last_rows = jnp.concatenate(
            [rows[:, edge:], *[padded_rows(shared_down[layer]) for layer in range(1, LAYERS)]],
            axis=1,
        )
    following = jnp.concatenate(following, axis=1)
    following = jnp.pad(following, ((0, 0), (0, -following.shape[1] % 128)))
    first_rows = spread(first_rows, "dp")
    gains, routers = split_small(first_rows[:, qkv_width:])
    qkv_weights = [first_rows[:, :qkv_width]]

    for layer in range(LAYERS):
        first = None
        if layer == 0:
            first = in_order(team_gather(x_in), member).reshape(group, D)
        head_rows, saved = attention_start(
            stream, first, gains[layer][0], qkv_weights[layer], context
        )
        if layer == 0:
            out_weight, joint_weight = dp_gather(
                main_rows, [0, D, D + joint_width], head_rows
            )
            attend(head_rows, saved, context, stretch)
            following = rest_gather(later(following, head_rows))
            down_weight = following[:, :D]
            for i in range(1, LAYERS):
                qkv_weights.append(following[:, D + (i - 1) * qkv_width : D + i * qkv_width])
            if LAYERS > 1:
                last_rows = rest_gather(later(last_rows, saved["wide"]))
        else:
            count = LAYERS - 1
            at = layer - 1
            starts = [at * D, count * D + at * joint_width, count * (D + joint_width) + at * D]
            out_weight, joint_weight, down_weight = [
                last_rows[:, start : start + size]
                for start, size in zip(starts, [D, joint_width, D])
            ]
            attend(head_rows, saved, context, stretch)
        weights.append(
            (
                gains[layer][0],
                qkv_weights[layer],
                out_weight,
                gains[layer][1],
                routers[layer],
                joint_weight,
                down_rows(down_weight),
            )
        )
        middle = attention_end(stream, saved, out_weight, context)
        kept.append(saved)
        feed = feed_start(middle, weights[layer], context)
        feeds.append(feed)
        outgoing = outgoing_rows(feed, context)
        if layer == last:
            outgoing = jnp.concatenate(
                [outgoing, outgoing_grads(feed, upstream, context)], axis=1
            )
        arrived = send_rows(outgoing, split_count)
        other = lax.ppermute(arrived, "dp", SWAP)
        rows_held[layer] = (arrived, other)
        returned = run_expert(
            layer,
            joint,
            down,
            (arrived, 0),
            (arrived, 1) if layer == last else None,
            True,
        )
        shared_out = shared_forward(feed, weights[layer], returned)
        returned = return_rows(returned, split_count)
        stream = feed_output(feed, shared_out, returned[:, :D], context)
    output = stream
    returned_grad = returned[:, D:]

    sums, feed_parts, head_parts = [None] * LAYERS, [None] * LAYERS, [None] * LAYERS
    terms = None
    for layer in reversed(range(LAYERS)):
        feed = feeds[layer]
        arrived, other = rows_held[layer]
        if layer == last:
            own = ((arrived, 0), (arrived, 1))
            others = ((other, 0), (other, 1))
        else:
            grad_team = team_gather(upstream.astype(BF16)).reshape(group, D)
            arrived_grad = send_rows(outgoing_grads(feed, upstream, context), split_count)
            packed = z_sum(dp_sum(*waiting, arrived_grad))
            packed = team_turn(packed, member).astype(F32)
            edge = 3 * D // TEAM_SIZE
            head_parts[layer + 1] = (packed[:, :, :edge], packed[:, :, edge:].sum(axis=0))
            own = ((arrived, 0), (arrived_grad, 0))
            others = ((other, 0), (lax.ppermute(arrived_grad, "dp", SWAP), 0))
            returned_grad = run_expert(
                layer, joint, down, (arrived, 0), (arrived_grad, 0), False
            )
            returned_grad = return_rows(returned_grad, split_count)
        shared_grad, grad_joint, grad_down = shared_backward(feed, grad_team, weights[layer])
        middle_grad, grad_gain_two, grad_router = feed_backward(
            feed, upstream, shared_grad, returned_grad, weights[layer], context
        )
        attn_grad = middle_grad.astype(BF16)
        grad_out = jnp.dot(kept[layer]["mixed"], attn_grad, preferred_element_type=F32).astype(BF16)
        feed_mine, feed_other = swap_halves(merge_feed_grads(grad_joint, grad_out, grad_down))
        feed_both = dp_sum(feed_mine, feed_other)
        upstream, grad_gain_one, grad_qkv, terms = attention_backward(
            middle_grad,
            weights[layer],
            context,
            kept[layer],
            [feed_other],
            feed_both,
            (layer, own, others, joint, down, terms),
        )
        columns, out_sum, down_sum = feed_sums(z_sum(feed_both), member)
        small = pack_small(grad_gain_one, grad_gain_two, grad_router)
        if layer > 0:
            waiting = swap_halves(jnp.concatenate([grad_qkv, small], axis=1))
        else:
            qkv_sum, small_sum = qkv_sums(grad_qkv, small)
        feed_parts[layer] = (columns, out_sum.sum(axis=0), down_sum)
        if layer == 0:
            head_parts[0] = (qkv_sum, small_sum)
    for layer in range(LAYERS):
        columns, out_sum, down_sum = feed_parts[layer]
        qkv_sum, small_sum = head_parts[layer]
        sums[layer] = (
            small_sum[:, 0],
            qkv_order(qkv_sum),
            out_sum,
            small_sum[:, 1],
            small_sum[:, 2 : 2 + EXPERTS],
            joint_order(columns),
            down_sum,
        )
    return (output, upstream, sums, terms)


def query_spans(block_row, group, part, parts):
    length = block_row.shape[0]
    limit = jnp.sum((block_row[None, :] <= block_row[:, None]).astype(jnp.int32), axis=1)
    tiles = length // QUERY_TILE // parts
    base = part * tiles
    ends = lax.dynamic_slice_in_dim(limit.reshape(-1, QUERY_TILE), base, tiles, 0)
    full = ends[:, 0] // group
    some = (ends[:, -1] + group - 1) // group
    base = jnp.full((1,), base, jnp.int32)
    return (full, some, base, limit[None, :], tiles, parts)


def local(
    x_in,
    block_ids,
    expert_ids,
    cotangent,
    gain_attn,
    w_qkv,
    w_out,
    gain_ffn,
    w_router,
    shared_gate_up,
    shared_down,
    expert_gate_up,
    expert_down,
):
    stretch = x_in.shape[1]
    group = TEAM_SIZE * stretch
    deep = lax.axis_size("z")
    parts = max(1, deep // TEAM_SIZE)
    at = lax.axis_index("z")
    member = lax.axis_index("core") * lax.axis_size("ulysses") + lax.axis_index("ulysses")
    half_size = HEAD // 2
    spacing = 10000.0 ** (-jnp.arange(half_size).astype(F32) * 2.0 / HEAD)
    positions = (at * group + jnp.arange(group, dtype=jnp.int32)).astype(F32)
    angles = spacing[:, None] * positions[None, :]
    tables, hits = route_tables(expert_ids[0])
    part = at % parts
    context = dict(
        member=member,
        cosine=jnp.cos(angles),
        sine=jnp.sin(angles),
        tables=tables,
        hits=hits,
        parts=parts,
        part=part,
        pieces=deep * TEAM_SIZE,
        split_count=deep * TEAM_SIZE // EXPERTS,
        spans=query_spans(block_ids[0], group, part, parts),
    )
    stream, upstream, sums, terms = layers(
        x_in[0],
        cotangent[0],
        gain_attn,
        w_qkv,
        w_out,
        gain_ffn,
        w_router,
        shared_gate_up,
        shared_down,
        expert_gate_up,
        expert_down,
        context,
    )
    stacked = [jnp.stack([sums[layer][i] for layer in range(LAYERS)]) for i in range(7)]
    return (
        stream.astype(BF16)[None],
        upstream.astype(BF16)[None],
        *stacked,
        *terms,
    )


def solution(mesh):
    dp, blk, ulysses = mesh.devices.shape
    grid = Mesh(mesh.devices.reshape(dp, blk // 2, 2, ulysses), ALL)
    rows = P("dp", SEQ, None)
    in_specs = (
        rows,
        P("dp", None),
        rows,
        rows,
        P(None, ALL),
        P(None, ALL, None),
        P(None, ALL, None),
        P(None, ALL),
        P(None, ALL, None),
        P(None, ALL, None),
        P(None, ALL, None),
        P(None, SEQ, None, None),
        P(None, SEQ, None, None),
    )
    out_specs = (
        rows,
        rows,
        P(None, ALL),
        P(None, ALL, None),
        P(None, ALL, None),
        P(None, ALL),
        P(None, ALL, None),
        P(None, ALL, None),
        P(None, ALL, None),
        P(None, SEQ, None, None),
        P(None, SEQ, None, None),
    )
    return jax.shard_map(local, mesh=grid, in_specs=in_specs, out_specs=out_specs, check_vma=False)
```

time: 976 us -> 724 us (0.74)
  blocking collectives: 155 us -> 42.8 us
  matrix products: 122 us -> 54.7 us
  waiting for transfers between devices: 288 us -> 235 us
  starting transfers between devices: 145 us -> 127 us
  local copies, waits for them, and re-layouts: 81.5 us -> 71.4 us
    all_gather x4 -> x0, blocking collectives: 145 us -> none  [spread(): return lax.all_gather(rows, REST, axis=0, tiled=True)]
    all_to_all x27 -> x16, waiting for transfers between devices: 167 us -> 109 us  [exchange(): return lax.all_to_all(rows, axes, split_axis=0, concat_axis=0, tiled=True)]
    dot_general x28 -> x24, matrix products: 67.5 us -> 28.2 us  [contract(): lax.dot_general(left, right, (((left_dim,), (right_dim,)), ((), ())), pre...]
    all_to_all x1 -> x2, blocking collectives: 9.48 us -> 42.8 us  [exchange(): return lax.all_to_all(rows, axes, split_axis=0, concat_axis=0, tiled=True)]
    all_to_all x27 -> x16, starting transfers between devices: 114 us -> 81.6 us  [exchange(): return lax.all_to_all(rows, axes, split_axis=0, concat_axis=0, tiled=True)]
    dot_general x22 -> x18, matrix products: 54.4 us -> 26.4 us  [the longest x4 6.45 us: feed_output(): jnp.dot(table, returned, preferred_element_type=F32)]
    reshape x22 -> x6, local copies, waits for them, and re-layouts: 29.1 us -> 3.65 us  [the longest x2 3.22 us: qkv_order(): columns.reshape(TEAM_SIZE, width, TEAM_HEADS, 3, HEAD)]
    all_gather x4 -> x3, waiting for transfers between devices: 20.6 us -> 0.04 us  [the longest x2 0.02 us: rest_gather(): return lax.all_gather(rows, REST, axis=0, tiled=True)]
  transfers between devices with their start and end apart: 71 -> 78, of which waited for: 37 -> 35; matrix products, arithmetic and copies ran while one was open for 22% -> 18% of each run, Pallas kernels for 11% -> 15%
where the time goes in v2:
time: 724 us; the launch traced here: 714 us
  waiting for transfers between devices  235 us (32%)
  starting transfers between devices  127 us (18%)
  Pallas kernels  119 us (16%)
  local copies, waits for them, and re-layouts  71.4 us (10%)
  matrix products  54.7 us (8%)
  other arithmetic  47 us (6%)
  blocking collectives  42.8 us (6%)
  between operations  16.7 us (2%)
    all_to_all x16, waiting for transfers between devices, exchange(): return lax.all_to_all(rows, axes, split_axis=0, concat_axis=0, tiled=True)  109 us
    all_to_all x16, starting transfers between devices, exchange(): return lax.all_to_all(rows, axes, split_axis=0, concat_axis=0, tiled=True)  81.6 us
    pallas_call x2, Pallas kernels, expert_grads(): pl.pallas_call(expert_grad_kernel, grid=(chunks, 2), in_specs=in_specs, o...  55.7 us
    ppermute x16, waiting for transfers between devices, from_member(): return lax.ppermute(rows, 'ulysses', SWAP)  47.9 us
    all_to_all x2, blocking collectives, exchange(): return lax.all_to_all(rows, axes, split_axis=0, concat_axis=0, tiled=True)  42.8 us
    pallas_call x3, Pallas kernels, run_expert(): pl.pallas_call(functools.partial(expert_kernel, forward, grads is not Non...  33.2 us
    ppermute x2, waiting for transfers between devices, dp_rows(): other = lax.ppermute(rows, 'dp', SWAP)  31.7 us
    ppermute x16, waiting for transfers between devices, from_member(): return lax.ppermute(rows, TEAM, [(i, 3 - i) for i in range(4)])  29.3 us
  transfers between devices with their start and end apart: 78, of which 35 were waited for; matrix products, arithmetic and copies ran while one was open for 18% of the time, Pallas kernels for 15%

profile of v2, /device:TPU:0, one launch (start us, length us, event | category | flops | bytes accessed | tf_op | source)
XLA Modules:
  0.0 714.5 jit_solution(9021443254466628619)
XLA Ops:
  26.2 5.3 all-to-all-start.1
  33.9 10.7 %all-to-all-done.1 = bf16[4,96,612]{2,1,0:T(8,128)(2,1)S(1)} async-done(((bf16[4,96,612]{2,1,0:T(8,128)(2,1)}), bf16[4,96,612]{2,1,0:T(8,128)(2,1)S(1)}, u32[]{:S(2)}, u32[]{:S(2)}) %all-to-all-start.1) | async-done | bytes 470048 | tf_op jit(solution)/shard_map/all_to_all | solution.py:47
  53.3 8.2 %all-to-all-done.2 = bf16[2,384,612]{1,2,0:T(8,128)(2,1)S(1)} async-done(((bf16[2,384,612]{1,2,0:T(8,128)(2,1)}), bf16[2,384,612]{1,2,0:T(8,128)(2,1)S(1)}, u32[]{:S(2)}, u32[]{:S(2)}) %all-to-all-start.2) | async-done | bytes 940064 | tf_op jit(solution)/shard_map/all_to_all | solution.py:47
  75.2 27.9 %all-to-all-done.3.rows_ref.refs_1_ = bf16[4,192,512]{2,1,0:T(8,128)(2,1)S(1)} async-done(((bf16[4,192,512]{2,1,0:T(8,128)(2,1)}), bf16[4,192,512]{2,1,0:T(8,128)(2,1)S(1)}, u32[]{:S(2)}, u32[]{:S(2)}) %all-to-all-start.3) | async-done | bytes 786464 | tf_op jit(solution)/shard_map/all_to_all | solution.py:47
  108.4 6.8 attend.2
  130.4 10.8 %collective-permute-done.3 = bf16[384,768]{1,0:T(8,128)(2,1)} collective-permute-done((bf16[384,768]{1,0:T(8,128)(2,1)}, bf16[384,768]{1,0:T(8,128)(2,1)}, u32[]{:S(2)}, u32[]{:S(2)}) %collective-permute-start.3) | collective-permute-done | bytes 589856 | tf_op jit(solution)/shard_map/ppermute | solution.py:888
  147.8 6.0 all-to-all-start.5
  158.1 20.9 %collective-permute-done.7 = bf16[384,1024]{1,0:T(8,128)(2,1)} collective-permute-done((bf16[384,1024]{1,0:T(8,128)(2,1)}, bf16[384,1024]{1,0:T(8,128)(2,1)}, u32[]{:S(2)}, u32[]{:S(2)}) %collective-permute-start.7) | collective-permute-done | bytes 786464 | tf_op jit(solution)/shard_map/ppermute | solution.py:888
  180.2 8.7 %expert_forward.1.refs_1_ = bf16[384,768]{1,0:T(8,128)(2,1)} custom-call(bf16[384,768]{1,0:T(8,128)(2,1)S(1)} %bitcast.432, bf16[2,1,768,4096]{3,2,1,0:T(8,128)(2,1)} %up_ref.3, bf16[2,1,768,4096]{3,2,1,0:T(8,128)(2,1)} %up_ref.3, bf16[2,1,2048,768]{3,2,1,0:T(8,128)(2,1)} %down_ref.3), custom_call_target="tpu_custom_call" | custom-call | flops 3623878656 | bytes 10616832 | tf_op jit(solution)/shard_map/expert_forward/pallas_call | solution.py:453
  188.9 6.1 all-to-all-start.6
  205.2 14.3 %all-to-all-done.6 = bf16[16,24,768]{2,1,0:T(8,128)(2,1)S(1)} async-done(((bf16[16,24,768]{2,1,0:T(8,128)(2,1)}), bf16[16,24,768]{2,1,0:T(8,128)(2,1)S(1)}, u32[]{:S(2)}, u32[]{:S(2)}) %all-to-all-start.6) | async-done | bytes 589856 | tf_op jit(solution)/shard_map/all_to_all | solution.py:47
  227.1 5.6 collective-permute-done.15
  237.8 30.2 %all_to_all.90.rows_ref = bf16[4,192,512]{2,1,0:T(8,128)(2,1)S(1)} all-to-all(bf16[4,192,512]{2,1,0:T(8,128)(2,1)S(1)} %concatenate.99), channel_id=1, replica_groups=mesh['dp'=2,'z'=4,'core'=2,'ulysses'=2] {'z'}, dimensions={0} | all-to-all | bytes 1572864 | tf_op jit(solution)/shard_map/all_to_all | solution.py:47
  268.0 6.1 attend.3
  274.2 12.6 %all_to_all.91 = bf16[16,64,128]{2,1,0:T(8,128)(2,1)S(1)} all-to-all(bf16[16,64,128]{2,1,0:T(8,128)(2,1)S(1)} %get-tuple-element.22), channel_id=1, replica_groups=mesh['dp'=2,'z'=4,'core'=2,'ulysses'=2] {'z','core','ulysses'}, dimensions={0} | all-to-all | bytes 524288 | tf_op jit(solution)/shard_map/all_to_all | solution.py:47
  299.8 7.9 %collective-permute-done.25 = bf16[128,768]{1,0:T(8,128)(2,1)} collective-permute-done((bf16[128,768]{1,0:T(8,128)(2,1)}, bf16[128,768]{1,0:T(8,128)(2,1)}, u32[]{:S(2)}, u32[]{:S(2)}) %collective-permute-start.25) | collective-permute-done | bytes 196640 | tf_op jit(solution)/shard_map/ppermute | solution.py:58
  307.7 10.9 %collective-permute-done.23 = bf16[128,768]{1,0:T(8,128)(2,1)} collective-permute-done((bf16[128,768]{1,0:T(8,128)(2,1)}, bf16[128,768]{1,0:T(8,128)(2,1)}, u32[]{:S(2)}, u32[]{:S(2)}) %collective-permute-start.23) | collective-permute-done | bytes 196640 | tf_op jit(solution)/shard_map/ppermute | solution.py:55
  333.9 13.2 %expert_both.1.refs_1_ = bf16[384,1536]{1,0:T(8,128)(2,1)} custom-call(bf16[384,1536]{1,0:T(8,128)(2,1)S(1)} %bitcast.423, bf16[384,1536]{1,0:T(8,128)(2,1)S(1)} %bitcast.424, bf16[2,1,768,4096]{3,2,1,0:T(8,128)(2,1)} %up_ref.3, bf16[2,1,768,4096]{3,2,1,0:T(8,128)(2,1)} %up_ref.3, bf16[2,1,2048,768]{3,2,1,0:T(8,128)(2,1)} %down_ref.3), custom_call_target="tpu_custom_call" | custom-call | flops 7247757312 | bytes 11796480 | tf_op jit(solution)/shard_map/expert_both/pallas_call | solution.py:453
  371.0 9.5 %all-to-all-done.10 = bf16[16,24,1536]{2,1,0:T(8,128)(2,1)} async-done(((bf16[16,24,1536]{2,1,0:T(8,128)(2,1)}), bf16[16,24,1536]{2,1,0:T(8,128)(2,1)}, u32[]{:S(2)}, u32[]{:S(2)}) %all-to-all-start.10) | async-done | bytes 1179680 | tf_op jit(solution)/shard_map/all_to_all | solution.py:47
  401.1 6.0 all-to-all-start.11
  407.2 9.9 %all-to-all-done.11.grad_ref = bf16[16,64,128]{2,1,0:T(8,128)(2,1)S(1)} async-done(((bf16[16,64,128]{2,1,0:T(8,128)(2,1)}), bf16[16,64,128]{2,1,0:T(8,128)(2,1)S(1)}, u32[]{:S(2)}, u32[]{:S(2)}) %all-to-all-start.11) | async-done | bytes 262176 | tf_op jit(solution)/shard_map/all_to_all | solution.py:47
  417.2 8.7 %attend_back.2.refs_0_ = bf16[4,192,512]{2,1,0:T(8,128)(2,1)} custom-call(bf16[4,192,512]{2,1,0:T(8,128)(2,1)S(1)} %all_to_all.90.rows_ref, s32[1,2048]{1,0:T(1,128)S(1)} %bitcast.438, bf16[16,64,128]{2,1,0:T(8,128)(2,1)S(1)} %all-to-all-done.11.grad_ref, f32[64,2048]{1,0:T(8,128)S(1)} %get-tuple-element.24.wide_ref, ...), custom_call_target="tpu_custom_call" | custom-call | flops 50331648 | bytes 1572864 | tf_op jit(solution)/shard_map/attend_back/pallas_call | solution.py:297
  430.3 28.0 %expert_grads.2 = (f32[2,1,768,4096]{3,2,1,0:T(8,128)}, f32[2,1,2048,768]{3,2,1,0:T(8,128)}) custom-call(s32[1]{0:T(128)} %bitcast.100.slot_ref, bf16[384,1536]{1,0:T(8,128)(2,1)S(1)} %bitcast.426, bf16[384,1536]{1,0:T(8,128)(2,1)S(1)} %bitcast.427, bf16[384,1536]{1,0:T(8,128)(2,1)} %collective-permute-done.30.other_rows.other_grads, ...), custom_call_target="tpu_custom_call" | custom-call | flops 14495514624 | bytes 9437184 | tf_op jit(solution)/shard_map/expert_grads/pallas_call | solution.py:527
  479.7 5.1 all-to-all-start.13
  487.2 12.8 %collective-permute-done.44.refs_0_ = bf16[384,640]{1,0:T(8,128)(2,1)S(1)} collective-permute-done((bf16[384,640]{1,0:T(8,128)(2,1)S(1)}, bf16[384,640]{1,0:T(8,128)(2,1)S(1)}, u32[]{:S(2)}, u32[]{:S(2)}) %collective-permute-start.44) | collective-permute-done | bytes 491552 | tf_op jit(solution)/shard_map/ppermute | solution.py:824
  516.8 11.3 %expert_back.1 = bf16[384,768]{1,0:T(8,128)(2,1)} custom-call(bf16[384,768]{1,0:T(8,128)(2,1)S(1)} %bitcast.433, bf16[384,768]{1,0:T(8,128)(2,1)S(1)} %bitcast.429, bf16[2,1,768,4096]{3,2,1,0:T(8,128)(2,1)} %up_ref.3, bf16[2,1,768,4096]{3,2,1,0:T(8,128)(2,1)} %up_ref.3, bf16[2,1,2048,768]{3,2,1,0:T(8,128)(2,1)} %down_ref.3), custom_call_target="tpu_custom_call" | custom-call | flops 6039797760 | bytes 10616832 | tf_op jit(solution)/shard_map/expert_back/pallas_call | solution.py:453
  546.7 5.9 collective-permute-done.37
  552.6 5.4 all-to-all-done.14
  566.3 11.8 %all-to-all-start.15 = ((bf16[16,64,128]{2,1,0:T(8,128)(2,1)}), bf16[16,64,128]{2,1,0:T(8,128)(2,1)S(1)}, u32[]{:S(2)}, u32[]{:S(2)}) async-start(bf16[16,64,128]{2,1,0:T(8,128)(2,1)} %bitcast.117), calls=%async_computation.15 | async-start | bytes 524288 | tf_op jit(solution)/shard_map/all_to_all | solution.py:47
  588.1 8.7 %attend_back.3.refs_2_ = bf16[4,192,512]{2,1,0:T(8,128)(2,1)} custom-call(bf16[4,192,512]{2,1,0:T(8,128)(2,1)S(1)} %copy-done.4, s32[1,2048]{1,0:T(1,128)S(1)} %bitcast.439, bf16[16,64,128]{2,1,0:T(8,128)(2,1)S(1)} %all-to-all-done.15.grad_ref, f32[64,2048]{1,0:T(8,128)S(1)} %copy-done.6, f32[1,2048]{1,0:T(1,128)S(1)} %get-tuple-element.27.log_ref, ...), custom_call_target="tpu_custom_call" | custom-call | flops 50331648 | bytes 1572864 | tf_op jit(solution)/shard_map/attend_back/pallas_call | solution.py:297
  613.1 8.0 %all-to-all-done.16.refs_0_ = bf16[4,192,512]{2,1,0:T(8,128)(2,1)S(1)} async-done(((bf16[4,192,512]{2,1,0:T(8,128)(2,1)}), bf16[4,192,512]{2,1,0:T(8,128)(2,1)S(1)}, u32[]{:S(2)}, u32[]{:S(2)}) %all-to-all-start.16) | async-done | bytes 786464 | tf_op jit(solution)/shard_map/all_to_all | solution.py:47
  650.0 27.6 %expert_grads.3 = (f32[2,1,768,4096]{3,2,1,0:T(8,128)}, f32[2,1,2048,768]{3,2,1,0:T(8,128)}) custom-call(s32[1]{0:T(128)} %bitcast.100.slot_ref, bf16[384,768]{1,0:T(8,128)(2,1)S(1)} %bitcast.435, bf16[384,768]{1,0:T(8,128)(2,1)S(1)} %bitcast.431, ...), custom_call_target="tpu_custom_call", output_to_operand_aliasing={{0}: (8, {}), {1}: (9, {})} | custom-call | flops 3623878656 | bytes 9437184 | tf_op jit(solution)/shard_map/expert_grads/pallas_call | solution.py:527
  (663 shorter events, 326.5 us)
Async XLA Ops:
  16.5 33.1 %collective-permute-start = (bf16[128,768]{1,0:T(8,128)(2,1)S(1)}, bf16[128,768]{1,0:T(8,128)(2,1)S(1)}, u32[]{:S(2)}, u32[]{:S(2)}) collective-permute-start(bf16[128,768]{1,0:T(8,128)(2,1)S(1)} %bitcast.478), channel_id=1, source_target_pairs={{0,2},{2,0},{1,3},{3,1},{4,6},{6,4},{5,7},{7,5},{8,10},{10,8},{9,1... | collective-permute-start | bytes 589832 | tf_op jit(solution)/shard_map/ppermute | solution.py:57
  17.0 32.7 %collective-permute-start.1 = (bf16[128,768]{1,0:T(8,128)(2,1)S(1)}, bf16[128,768]{1,0:T(8,128)(2,1)S(1)}, u32[]{:S(2)}, u32[]{:S(2)}) collective-permute-start(bf16[128,768]{1,0:T(8,128)(2,1)S(1)} %bitcast.479), channel_id=1, source_target_pairs={{0,1},{1,0},{2,3},{3,2},{4,5},{5,4},{6,7},{7,6},{8,9},{9,8},{10,11... | collective-permute-start | bytes 589832 | tf_op jit(solution)/shard_map/ppermute | solution.py:55
  18.9 32.1 %collective-permute-start.2 = (bf16[128,768]{1,0:T(8,128)(2,1)S(1)}, bf16[128,768]{1,0:T(8,128)(2,1)}, u32[]{:S(2)}, u32[]{:S(2)}) collective-permute-start(bf16[128,768]{1,0:T(8,128)(2,1)S(1)} %bitcast.480), channel_id=1, source_target_pairs={{0,3},{1,2},{2,1},{3,0},{4,7},{5,6},{6,5},{7,4},{8,11},{9,10},{10,... | collective-permute-start | bytes 589832 | tf_op jit(solution)/shard_map/ppermute | solution.py:58
  32.3 40.8 %collective-permute-start.8 = (bf16[24,2368]{1,0:T(8,128)(2,1)}, bf16[24,2368]{1,0:T(8,128)(2,1)}, u32[]{:S(2)}, u32[]{:S(2)}) collective-permute-start(bf16[24,2368]{1,0:T(8,128)(2,1)} %get-tuple-element.159), channel_id=1, source_target_pairs={{0,2},{2,0},{1,3},{3,1},{4,6},{6,4},{5,7},{7,5},{8,10},{10,8},{9,1... | collective-permute-start | bytes 341000 | tf_op jit(solution)/shard_map/ppermute | solution.py:57
  32.3 40.8 %collective-permute-start.9 = (bf16[24,2368]{1,0:T(8,128)(2,1)}, bf16[24,2368]{1,0:T(8,128)(2,1)}, u32[]{:S(2)}, u32[]{:S(2)}) collective-permute-start(bf16[24,2368]{1,0:T(8,128)(2,1)} %get-tuple-element.158), channel_id=1, source_target_pairs={{0,1},{1,0},{2,3},{3,2},{4,5},{5,4},{6,7},{7,6},{8,9},{9,8},{10,11... | collective-permute-start | bytes 341000 | tf_op jit(solution)/shard_map/ppermute | solution.py:55
  49.5 70.1 %all-gather.4.cloned.1.call-start = ((), (), s32[]{:S(2)}) async-start(), calls=%async_computation.21 | async-start | bytes 1720320 | tf_op jit(solution)/shard_map/all_gather | solution.py:943
  49.6 23.5 %collective-permute-start.10 = (bf16[24,2368]{1,0:T(8,128)(2,1)}, bf16[24,2368]{1,0:T(8,128)(2,1)}, u32[]{:S(2)}, u32[]{:S(2)}) collective-permute-start(bf16[24,2368]{1,0:T(8,128)(2,1)} %get-tuple-element.157), channel_id=1, source_target_pairs={{0,3},{1,2},{2,1},{3,0},{4,7},{5,6},{6,5},{7,4},{8,11},{9,10},{10,... | collective-permute-start | bytes 341000 | tf_op jit(solution)/shard_map/ppermute | solution.py:58
  68.9 34.1 %all-to-all-start.3 = ((bf16[4,192,512]{2,1,0:T(8,128)(2,1)}), bf16[4,192,512]{2,1,0:T(8,128)(2,1)S(1)}, u32[]{:S(2)}, u32[]{:S(2)}) async-start(bf16[4,192,512]{2,1,0:T(8,128)(2,1)} %concatenate.93), calls=%async_computation.3 | async-start | bytes 1572864 | tf_op jit(solution)/shard_map/all_to_all | solution.py:47
  72.6 127.2 %all-gather.6.cloned.1.call-start = ((), (), s32[]{:S(2)}) async-start(), calls=%async_computation.22 | async-start | bytes 2433024 | tf_op jit(solution)/shard_map/all_gather | solution.py:947
  119.6 167.3 %all-gather.8.cloned.1.call-start = ((), (), s32[]{:S(2)}) async-start(), calls=%async_computation.23 | async-start | bytes 4423680 | tf_op jit(solution)/shard_map/all_gather | solution.py:947
  147.8 32.4 %all-to-all-start.5 = ((bf16[16,24,768]{2,1,0:T(8,128)(2,1)}), bf16[16,24,768]{2,1,0:T(8,128)(2,1)S(1)}, u32[]{:S(2)}, u32[]{:S(2)}) async-start(bf16[16,24,768]{2,1,0:T(8,128)(2,1)} %bitcast.33), calls=%async_computation.5 | async-start | bytes 1179648 | tf_op jit(solution)/shard_map/all_to_all | solution.py:47
  153.8 25.1 %collective-permute-start.7 = (bf16[384,1024]{1,0:T(8,128)(2,1)}, bf16[384,1024]{1,0:T(8,128)(2,1)}, u32[]{:S(2)}, u32[]{:S(2)}) collective-permute-start(bf16[384,1024]{1,0:T(8,128)(2,1)} %later.13), channel_id=1, source_target_pairs={{0,16},{16,0},{1,17},{17,1},{2,18},{18,2},{3,19},{19,3},{4,20},{20... | collective-permute-start | bytes 2359304 | tf_op jit(solution)/shard_map/ppermute | solution.py:888
  188.9 30.5 %all-to-all-start.6 = ((bf16[16,24,768]{2,1,0:T(8,128)(2,1)}), bf16[16,24,768]{2,1,0:T(8,128)(2,1)S(1)}, u32[]{:S(2)}, u32[]{:S(2)}) async-start(bf16[16,24,768]{2,1,0:T(8,128)(2,1)} %bitcast.51), calls=%async_computation.6 | async-start | bytes 1179648 | tf_op jit(solution)/shard_map/all_to_all | solution.py:47
  293.6 40.3 %all-to-all-start.9 = ((bf16[16,24,1536]{2,1,0:T(8,128)(2,1)}), bf16[16,24,1536]{2,1,0:T(8,128)(2,1)S(1)}, u32[]{:S(2)}, u32[]{:S(2)}) async-start(bf16[16,24,1536]{2,1,0:T(8,128)(2,1)} %bitcast.453), calls=%async_computation.9 | async-start | bytes 2359296 | tf_op jit(solution)/shard_map/all_to_all | solution.py:47
  347.1 83.1 %collective-permute-start.30 = (bf16[384,1536]{1,0:T(8,128)(2,1)S(1)}, bf16[384,1536]{1,0:T(8,128)(2,1)}, u32[]{:S(2)}, u32[]{:S(2)}) collective-permute-start(bf16[384,1536]{1,0:T(8,128)(2,1)S(1)} %bitcast.425), channel_id=1, source_target_pairs={{0,16},{16,0},{1,17},{17,1},{2,18},{18,2},{3,19},{19,3},{4,20},{20... | collective-permute-start | bytes 3538952 | tf_op jit(solution)/shard_map/ppermute | solution.py:1065
  349.3 31.1 %all-to-all-start.10 = ((bf16[16,24,1536]{2,1,0:T(8,128)(2,1)}), bf16[16,24,1536]{2,1,0:T(8,128)(2,1)}, u32[]{:S(2)}, u32[]{:S(2)}) async-start(bf16[16,24,1536]{2,1,0:T(8,128)(2,1)} %bitcast.80), calls=%async_computation.10 | async-start | bytes 2359296 | tf_op jit(solution)/shard_map/all_to_all | solution.py:47
  360.6 22.7 %collective-permute-start.22 = (bf16[128,768]{1,0:T(8,128)(2,1)}, bf16[128,768]{1,0:T(8,128)(2,1)}, u32[]{:S(2)}, u32[]{:S(2)}) collective-permute-start(bf16[128,768]{1,0:T(8,128)(2,1)} %get-tuple-element.136), channel_id=1, source_target_pairs={{0,3},{1,2},{2,1},{3,0},{4,7},{5,6},{6,5},{7,4},{8,11},{9,10},{10,... | collective-permute-start | bytes 589832 | tf_op jit(solution)/shard_map/ppermute | solution.py:58
  362.2 22.5 %collective-permute-start.21 = (bf16[128,768]{1,0:T(8,128)(2,1)}, bf16[128,768]{1,0:T(8,128)(2,1)}, u32[]{:S(2)}, u32[]{:S(2)}) collective-permute-start(bf16[128,768]{1,0:T(8,128)(2,1)} %get-tuple-element.137), channel_id=1, source_target_pairs={{0,2},{2,0},{1,3},{3,1},{4,6},{6,4},{5,7},{7,5},{8,10},{10,8},{9,1... | collective-permute-start | bytes 589832 | tf_op jit(solution)/shard_map/ppermute | solution.py:57
  362.6 22.7 %collective-permute-start.20 = (bf16[128,768]{1,0:T(8,128)(2,1)}, bf16[128,768]{1,0:T(8,128)(2,1)}, u32[]{:S(2)}, u32[]{:S(2)}) collective-permute-start(bf16[128,768]{1,0:T(8,128)(2,1)} %get-tuple-element.135), channel_id=1, source_target_pairs={{0,1},{1,0},{2,3},{3,2},{4,5},{5,4},{6,7},{7,6},{8,9},{9,8},{10,11... | collective-permute-start | bytes 589832 | tf_op jit(solution)/shard_map/ppermute | solution.py:55
  365.7 22.0 %collective-permute-start.28 = (bf16[128,768]{1,0:T(8,128)(2,1)}, bf16[128,768]{1,0:T(8,128)(2,1)}, u32[]{:S(2)}, u32[]{:S(2)}) collective-permute-start(bf16[128,768]{1,0:T(8,128)(2,1)} %get-tuple-element.133), channel_id=1, source_target_pairs={{0,3},{1,2},{2,1},{3,0},{4,7},{5,6},{6,5},{7,4},{8,11},{9,10},{10,... | collective-permute-start | bytes 589832 | tf_op jit(solution)/shard_map/ppermute | solution.py:58
  398.7 59.7 %collective-permute-start.29 = (bf16[384,2560]{1,0:T(8,128)(2,1)}, bf16[384,2560]{1,0:T(8,128)(2,1)}, u32[]{:S(2)}, u32[]{:S(2)}) collective-permute-start(bf16[384,2560]{1,0:T(8,128)(2,1)} %dynamic-slice_bitcast_fusion.1.refs_0_), channel_id=1, source_target_pairs={{0,16},{16,0},{1,17},{17,1},{2,18},{18,2},{3,19},{19,3},{4,20},{20... | collective-permute-start | bytes 5898248 | tf_op jit(solution)/shard_map/ppermute | solution.py:824
  425.9 35.8 %all-to-all-start.12 = ((bf16[4,192,512]{2,1,0:T(8,128)(2,1)}), bf16[4,192,512]{2,1,0:T(8,128)(2,1)}, u32[]{:S(2)}, u32[]{:S(2)}) async-start(bf16[4,192,512]{2,1,0:T(8,128)(2,1)} %attend_back.2.refs_0_), calls=%async_computation.12 | async-start | bytes 1572864 | tf_op jit(solution)/shard_map/all_to_all | solution.py:47
  484.9 94.9 %reduce-scatter.4.cloned.1.call-start = ((), (), s32[]{:S(2)}) async-start(), calls=%async_computation.24 | async-start | bytes 614400 | tf_op jit(solution)/shard_map/reduce_scatter | solution.py:831
  503.4 174.2 %reduce-scatter.8.cloned.1.call-start = ((), (), s32[]{:S(2)}) async-start(), calls=%async_computation.26 | async-start | bytes 2457600 | tf_op jit(solution)/shard_map/reduce_scatter | solution.py:831
  528.1 30.0 %all-to-all-start.14 = ((bf16[16,24,768]{2,1,0:T(8,128)(2,1)}), bf16[16,24,768]{2,1,0:T(8,128)(2,1)}, u32[]{:S(2)}, u32[]{:S(2)}) async-start(bf16[16,24,768]{2,1,0:T(8,128)(2,1)} %bitcast.113), calls=%async_computation.14 | async-start | bytes 1179648 | tf_op jit(solution)/shard_map/all_to_all | solution.py:47
  565.0 44.2 %collective-permute-start.40 = (bf16[384,2560]{1,0:T(8,128)(2,1)}, bf16[384,2560]{1,0:T(8,128)(2,1)}, u32[]{:S(2)}, u32[]{:S(2)}) collective-permute-start(bf16[384,2560]{1,0:T(8,128)(2,1)} %dynamic-slice_bitcast_fusion.refs_0_), channel_id=1, source_target_pairs={{0,16},{16,0},{1,17},{17,1},{2,18},{18,2},{3,19},{19,3},{4,20},{20... | collective-permute-start | bytes 5898248 | tf_op jit(solution)/shard_map/ppermute | solution.py:824
  578.8 71.1 %collective-permute-start.54 = (bf16[384,768]{1,0:T(8,128)(2,1)S(1)}, bf16[384,768]{1,0:T(8,128)(2,1)S(1)}, u32[]{:S(2)}, u32[]{:S(2)}) collective-permute-start(bf16[384,768]{1,0:T(8,128)(2,1)S(1)} %bitcast.434), channel_id=1, source_target_pairs={{0,16},{16,0},{1,17},{17,1},{2,18},{18,2},{3,19},{19,3},{4,20},{20... | collective-permute-start | bytes 1769480 | tf_op jit(solution)/shard_map/ppermute | solution.py:1065
  581.3 21.9 %collective-permute-start.46 = (bf16[24,640]{1,0:T(8,128)(2,1)}, bf16[24,640]{1,0:T(8,128)(2,1)}, u32[]{:S(2)}, u32[]{:S(2)}) collective-permute-start(bf16[24,640]{1,0:T(8,128)(2,1)} %get-tuple-element.177), channel_id=1, source_target_pairs={{0,1},{1,0},{2,3},{3,2},{4,5},{5,4},{6,7},{7,6},{8,9},{9,8},{10,11... | collective-permute-start | bytes 92168 | tf_op jit(solution)/shard_map/ppermute | solution.py:55
  596.8 24.3 %all-to-all-start.16 = ((bf16[4,192,512]{2,1,0:T(8,128)(2,1)}), bf16[4,192,512]{2,1,0:T(8,128)(2,1)S(1)}, u32[]{:S(2)}, u32[]{:S(2)}) async-start(bf16[4,192,512]{2,1,0:T(8,128)(2,1)} %attend_back.3.refs_2_), calls=%async_computation.16 | async-start | bytes 1572864 | tf_op jit(solution)/shard_map/all_to_all | solution.py:47
  600.5 96.4 %reduce-scatter.6.cloned.1.call-start = ((), (), s32[]{:S(2)}) async-start(), calls=%async_computation.25 | async-start | bytes 2457600 | tf_op jit(solution)/shard_map/reduce_scatter | solution.py:831
  602.3 47.7 %collective-permute-start.55 = (bf16[384,768]{1,0:T(8,128)(2,1)S(1)}, bf16[384,768]{1,0:T(8,128)(2,1)S(1)}, u32[]{:S(2)}, u32[]{:S(2)}) collective-permute-start(bf16[384,768]{1,0:T(8,128)(2,1)S(1)} %bitcast.430), channel_id=1, source_target_pairs={{0,16},{16,0},{1,17},{17,1},{2,18},{18,2},{3,19},{19,3},{4,20},{20... | collective-permute-start | bytes 1769480 | tf_op jit(solution)/shard_map/ppermute | solution.py:1097
  638.7 52.8 %all-to-all-start.17 = ((bf16[32,24,640]{2,1,0:T(8,128)(2,1)}), bf16[32,24,640]{2,1,0:T(8,128)(2,1)S(1)}, u32[]{:S(2)}, u32[]{:S(2)}) async-start(bf16[32,24,640]{2,1,0:T(8,128)(2,1)} %bitcast.460), calls=%async_computation.17 | async-start | bytes 1966080 | tf_op jit(solution)/shard_map/all_to_all | solution.py:47
  (177 other events, 1885.1 us)
Sparse Core Ops, SparseCore 0:
  53.5 47.0 all-gather.3
  104.1 55.1 all-gather.5
  161.5 81.6 all-gather.7
  503.6 21.2 reduce-scatter.3
  527.1 49.2 reduce-scatter.7
  625.4 56.5 reduce-scatter.5

commit v3 on v2

v3 whole, which is shorter than its diff:
```python
import functools
import math

import jax
import jax.numpy as jnp
from jax import lax
from jax.experimental import pallas as pl
from jax.experimental.pallas import tpu as pltpu
from jax.sharding import Mesh
from jax.sharding import PartitionSpec as P

D = 768
HEADS = 12
HEAD = 64
FF = 2048
EXPERTS = 16
LAYERS = 2
MOST = 21
SLOTS = -(-MOST // 8) * 8
TEAM_SIZE = 4
TEAM_HEADS = HEADS // TEAM_SIZE

ALL = ("dp", "z", "core", "ulysses")
SEQ = ("z", "core", "ulysses")
TEAM = ("core", "ulysses")
REST = ("dp", "z")

NORM_EPS = 1e-06
NEG_BIG = -1e30
PRECISE = lax.Precision.HIGHEST
F32 = jnp.float32
BF16 = jnp.bfloat16
QUERY_TILE = 256
MIB = 1024 * 1024


def vmem(size):
    return pltpu.CompilerParams(vmem_limit_bytes=61 * MIB)


def cost(flops, moved, steps=0):
    return pl.CostEstimate(flops=flops, bytes_accessed=moved, transcendentals=steps)


def contract(left, right, left_dim, right_dim):
    return lax.dot_general(
        left, right, (((left_dim,), (right_dim,)), ((), ())), preferred_element_type=F32
    )


def exchange(rows, axes):
    return lax.all_to_all(rows, axes, split_axis=0, concat_axis=0, tiled=True)


SWAP = [(0, 1), (1, 0)]


def from_member(rows, turn):
    if turn == 1:
        return lax.ppermute(rows, "ulysses", SWAP)
    if turn == 2:
        return lax.ppermute(rows, "core", SWAP)
    return lax.ppermute(rows, TEAM, [(i, 3 - i) for i in range(4)])


def team_gather(rows):
    return jnp.stack([rows] + [from_member(rows, turn) for turn in (1, 2, 3)])


def in_order(stacked, member):
    turns = [jnp.equal(member, i) for i in range(4)]
    pieces = []
    for k in range(4):
        piece = stacked[k ^ 3]
        for i in range(3):
            piece = jnp.where(turns[i], stacked[k ^ i], piece)
        pieces.append(piece)
    return jnp.stack(pieces)


def team_sum(parts):
    total = parts[0].astype(F32)
    for turn in (1, 2, 3):
        total = total + from_member(parts[turn].astype(BF16), turn).astype(F32)
    return total


def rms_factor(stream):
    return lax.rsqrt(jnp.mean(stream * stream, axis=-1, keepdims=True) + NORM_EPS)


def norm_back(stream, gain, factor, upstream):
    weighted = upstream * gain
    inner_mean = jnp.mean(weighted * stream, axis=-1, keepdims=True)
    grad_stream = factor * weighted - stream * factor * factor * factor * inner_mean
    grad_gain = jnp.sum(upstream * stream * factor, axis=0)
    return (grad_stream, grad_gain)


def attention_kernel(full_ref, some_ref, base_ref, rows_ref, limit_ref, out_ref, wide_ref, log_ref, keys):
    span = rows_ref.shape[2]
    step = pl.program_id(0)
    per_block = span // QUERY_TILE

    @pl.when(step == 0)
    def _():
        for s in range(rows_ref.shape[0]):
            keys[s] = rows_ref[s, HEAD : 2 * HEAD, :].T

    tile = base_ref[0] + step
    lanes = pl.ds(pl.multiple_of((tile % per_block) * QUERY_TILE, QUERY_TILE), QUERY_TILE)
    queries = rows_ref[tile // per_block, 0:HEAD, lanes] * BF16(HEAD**-0.5)
    limit = limit_ref[...]
    key_index = lax.broadcasted_iota(jnp.int32, (span, QUERY_TILE), 0)

    def sweep(s, state, masked):
        highest, total, running = state
        scores = jnp.dot(keys[s], queries, preferred_element_type=F32)
        if masked:
            scores = jnp.where(key_index < limit - s * span, scores, NEG_BIG)
        raised = jnp.maximum(highest, jnp.max(scores, axis=0, keepdims=True))
        terms = jnp.exp(scores - raised)
        shrink = jnp.exp(highest - raised)
        total = total * shrink + jnp.sum(terms, axis=0, keepdims=True)
        running = running * shrink + jnp.dot(
            rows_ref[s, 2 * HEAD :, :], terms.astype(BF16), preferred_element_type=F32
        )
        return (raised, total, running)

    state = (
        jnp.full((1, QUERY_TILE), NEG_BIG, F32),
        jnp.zeros((1, QUERY_TILE), F32),
        jnp.zeros((HEAD, QUERY_TILE), F32),
    )
    state = lax.fori_loop(0, full_ref[step], lambda s, c: sweep(s, c, False), state)
    state = lax.fori_loop(full_ref[step], some_ref[step], lambda s, c: sweep(s, c, True), state)
    highest, total, running = state
    result = running / total
    log_ref[...] = highest + jnp.log(total)
    wide_ref[...] = result
    stretch = out_ref.shape[2]
    for i in range(QUERY_TILE // stretch):
        out_ref[i] = result[:, i * stretch : (i + 1) * stretch].astype(BF16)


def attention_back_kernel(
    full_ref, some_ref, base_ref, rows_ref, limit_ref, grad_ref, wide_ref, log_ref, *refs
):
    out_ref, keys, values, key_sum, value_sum = refs[-5:]
    span = rows_ref.shape[2]
    blocks = rows_ref.shape[0]
    step = pl.program_id(0)
    per_block = span // QUERY_TILE

    @pl.when(step == 0)
    def _():
        for s in range(blocks):
            keys[s] = rows_ref[s, HEAD : 2 * HEAD, :].T
            values[s] = rows_ref[s, 2 * HEAD :, :].T
        key_sum[...] = jnp.zeros_like(key_sum)
        value_sum[...] = jnp.zeros_like(value_sum)
        out_ref[...] = jnp.zeros_like(out_ref)

    tile = base_ref[0] + step
    lanes = pl.ds(pl.multiple_of((tile % per_block) * QUERY_TILE, QUERY_TILE), QUERY_TILE)
    queries = rows_ref[tile // per_block, 0:HEAD, lanes] * BF16(HEAD**-0.5)
    limit = limit_ref[...]
    key_index = lax.broadcasted_iota(jnp.int32, (span, QUERY_TILE), 0)
    grads = jnp.concatenate([grad_ref[i] for i in range(grad_ref.shape[0])], axis=1)
    delta = jnp.sum(grads.astype(F32) * wide_ref[...], axis=0, keepdims=True)
    logs = log_ref[...]

    def sweep(s, query_grad, masked):
        scores = jnp.dot(keys[s], queries, preferred_element_type=F32)
        probs = jnp.exp(scores - logs)
        if masked:
            probs = jnp.where(key_index < limit - s * span, probs, 0.0)
        prob_grad = jnp.dot(values[s], grads, preferred_element_type=F32)
        score_grad = (probs * (prob_grad - delta)).astype(BF16)
        value_sum[s] += contract(grads, probs.astype(BF16), 1, 1)
        key_sum[s] += contract(queries, score_grad, 1, 1)
        return query_grad + jnp.dot(
            rows_ref[s, HEAD : 2 * HEAD, :], score_grad, preferred_element_type=F32
        )

    query_grad = jnp.zeros((HEAD, QUERY_TILE), F32)
    query_grad = lax.fori_loop(0, full_ref[step], lambda s, c: sweep(s, c, False), query_grad)
    query_grad = lax.fori_loop(
        full_ref[step], some_ref[step], lambda s, c: sweep(s, c, True), query_grad
    )
    out_ref[tile // per_block, 0:HEAD, lanes] = (query_grad * HEAD**-0.5).astype(BF16)

    @pl.when(step == pl.num_programs(0) - 1)
    def _():
        out_ref[:, HEAD : 2 * HEAD, :] = key_sum[...].astype(BF16)
        out_ref[:, 2 * HEAD :, :] = value_sum[...].astype(BF16)


def fixed_attention_kernel(place_ref, *refs):
    rows_ref, out_ref, wide_ref, log_ref, keys, values = refs[-6:]
    blocks, _, span = rows_ref.shape
    pieces, limit_ref = refs[:blocks], refs[blocks]
    for turn in range(blocks):
        rows_ref[lax.rem(place_ref[1] + blocks - turn, blocks)] = pieces[turn][...]
    length = blocks * span
    stretch = out_ref.shape[2]
    for s in range(blocks):
        keys[s * span : (s + 1) * span, :] = rows_ref[s, HEAD : 2 * HEAD, :].T
        values[:, s * span : (s + 1) * span] = rows_ref[s, 2 * HEAD :, :]
    key_index = lax.broadcasted_iota(jnp.int32, (2 * QUERY_TILE, QUERY_TILE), 0)
    for tile in range(length // QUERY_TILE):
        start = tile * QUERY_TILE
        end = min(start + 2 * QUERY_TILE, length)
        lanes = slice(start % span, start % span + QUERY_TILE)
        queries = rows_ref[start // span, 0:HEAD, lanes] * BF16(HEAD**-0.5)
        scores = jnp.dot(keys[start:end, :], queries, preferred_element_type=F32)
        limit = limit_ref[:, start : start + QUERY_TILE] - start
        scores = jnp.where(key_index[: end - start] < limit, scores, NEG_BIG)
        highest = jnp.max(scores, axis=0, keepdims=True)
        if start > 0:
            before = jnp.dot(keys[:start, :], queries, preferred_element_type=F32)
            highest = jnp.maximum(highest, jnp.max(before, axis=0, keepdims=True))
        terms = jnp.exp(scores - highest)
        total = jnp.sum(terms, axis=0, keepdims=True)
        result = jnp.dot(values[:, start:end], terms.astype(BF16), preferred_element_type=F32)
        if start > 0:
            terms = jnp.exp(before - highest)
            total = total + jnp.sum(terms, axis=0, keepdims=True)
            result = result + jnp.dot(
                values[:, :start], terms.astype(BF16), preferred_element_type=F32
            )
        result = result / total
        log_ref[:, start : start + QUERY_TILE] = highest + jnp.log(total)
        wide_ref[:, start : start + QUERY_TILE] = result
        for i in range(QUERY_TILE // stretch):
            out_ref[start // stretch + i] = result[:, i * stretch : (i + 1) * stretch].astype(BF16)


def fixed_attention_back_kernel(place_ref, rows_ref, limit_ref, grad_ref, wide_ref, log_ref, *refs):
    blocks, _, span = rows_ref.shape
    out_ref, keys, values, key_sum, value_sum = refs[-5:]
    outs = refs[-5 - blocks : -5]
    length = blocks * span
    stretch = grad_ref.shape[2]
    for s in range(blocks):
        keys[s * span : (s + 1) * span, :] = rows_ref[s, HEAD : 2 * HEAD, :].T
        values[s * span : (s + 1) * span, :] = rows_ref[s, 2 * HEAD :, :].T
    key_sum[...] = jnp.zeros_like(key_sum)
    value_sum[...] = jnp.zeros_like(value_sum)
    key_index = lax.broadcasted_iota(jnp.int32, (2 * QUERY_TILE, QUERY_TILE), 0)
    for tile in range(length // QUERY_TILE):
        start = tile * QUERY_TILE
        end = min(start + 2 * QUERY_TILE, length)
        lanes = slice(start % span, start % span + QUERY_TILE)
        queries = rows_ref[start // span, 0:HEAD, lanes] * BF16(HEAD**-0.5)
        pieces = QUERY_TILE // stretch
        grads = jnp.concatenate([grad_ref[tile * pieces + i] for i in range(pieces)], axis=1)
        wide = wide_ref[:, start : start + QUERY_TILE]
        delta = jnp.sum(grads.astype(F32) * wide, axis=0, keepdims=True)
        logs = log_ref[:, start : start + QUERY_TILE]
        limit = limit_ref[:, start : start + QUERY_TILE] - start
        query_grad = jnp.zeros((HEAD, QUERY_TILE), F32)
        for low, high in ((0, start), (start, end)):
            if low == high:
                continue
            scores = jnp.dot(keys[low:high, :], queries, preferred_element_type=F32)
            probs = jnp.exp(scores - logs)
            if low == start:
                probs = jnp.where(key_index[: high - low] < limit, probs, 0.0)
            prob_grad = jnp.dot(values[low:high, :], grads, preferred_element_type=F32)
            score_grad = (probs * (prob_grad - delta)).astype(BF16)
            value_sum[:, low:high] += contract(grads, probs.astype(BF16), 1, 1)
            key_sum[:, low:high] += contract(queries, score_grad, 1, 1)
            query_grad = query_grad + contract(keys[low:high, :], score_grad, 0, 0)
        out_ref[start // span, 0:HEAD, lanes] = (query_grad * HEAD**-0.5).astype(BF16)
    for s in range(blocks):
        out_ref[s, HEAD : 2 * HEAD, :] = key_sum[:, s * span : (s + 1) * span].astype(BF16)
        out_ref[s, 2 * HEAD :, :] = value_sum[:, s * span : (s + 1) * span].astype(BF16)
    for turn in range(blocks):
        outs[turn][...] = out_ref[lax.rem(place_ref[1] + turn, blocks)]


def at_once(shape):
    return pl.BlockSpec(shape, lambda step: (0,) * len(shape))


ANYWHERE = pl.BlockSpec(memory_space=pl.ANY)
IN_SMEM = pl.BlockSpec(memory_space=pltpu.SMEM)


def fixed_attention(pieces, limit, place, stretch, after):
    blocks = len(pieces)
    features, span = pieces[0].shape
    length = blocks * span
    return pl.pallas_call(
        fixed_attention_kernel,
        grid=(1,),
        in_specs=[IN_SMEM, *[at_once(array.shape) for array in (*pieces, limit)]]
        + [ANYWHERE] * len(after),
        out_specs=[
            at_once((blocks, features, span)),
            at_once((length // stretch, HEAD, stretch)),
            at_once((HEAD, length)),
            at_once((1, length)),
        ],
        out_shape=[
            jax.ShapeDtypeStruct((blocks, features, span), BF16),
            jax.ShapeDtypeStruct((length // stretch, HEAD, stretch), BF16),
            jax.ShapeDtypeStruct((HEAD, length), F32),
            jax.ShapeDtypeStruct((1, length), F32),
        ],
        scratch_shapes=[pltpu.VMEM((length, HEAD), BF16), pltpu.VMEM((HEAD, length), BF16)],
        compiler_params=vmem(16 * MIB),
        cost_estimate=cost(features * length * length // 48, features * length * 4, length * length),
        name="attend",
    )(place, *pieces, limit, *after)


def fixed_attention_back(rows, limit, grads, wide, logs, place, later_than):
    blocks, features, span = rows.shape
    length = blocks * span
    return pl.pallas_call(
        fixed_attention_back_kernel,
        grid=(1,),
        in_specs=[
            IN_SMEM,
            *[at_once(array.shape) for array in (rows, limit, grads, wide, logs)],
        ]
        + [ANYWHERE] * len(later_than),
        out_specs=[at_once((features, span))] * blocks,
        out_shape=[jax.ShapeDtypeStruct((features, span), BF16)] * blocks,
        scratch_shapes=[
            pltpu.VMEM(rows.shape, BF16),
            pltpu.VMEM((length, HEAD), BF16),
            pltpu.VMEM((length, HEAD), BF16),
            pltpu.VMEM((HEAD, length), F32),
            pltpu.VMEM((HEAD, length), F32),
        ],
        compiler_params=vmem(20 * MIB),
        cost_estimate=cost(rows.size * length // 16, rows.size * 4, length * length),
        name="attend_back",
    )(place, rows, limit, grads, wide, logs, *later_than)


def whole(shape):
    return pl.BlockSpec(shape, lambda step, *_: (0,) * len(shape))


def tile_at(step, full, some, base):
    return (0, base[0] + step)


def attention(rows, spans, stretch):
    full, some, base, limit, tiles, parts = spans
    blocks, _, span = rows.shape
    length = tiles * QUERY_TILE
    return pl.pallas_call(
        attention_kernel,
        grid_spec=pltpu.PrefetchScalarGridSpec(
            num_scalar_prefetch=3,
            grid=(tiles,),
            in_specs=[whole(rows.shape), pl.BlockSpec((1, QUERY_TILE), tile_at)],
            out_specs=[
                pl.BlockSpec((QUERY_TILE // stretch, HEAD, stretch), lambda step, *_: (step, 0, 0)),
                pl.BlockSpec((HEAD, QUERY_TILE), lambda step, *_: (0, step)),
                pl.BlockSpec((1, QUERY_TILE), lambda step, *_: (0, step)),
            ],
            scratch_shapes=[pltpu.VMEM((blocks, span, HEAD), BF16)],
        ),
        out_shape=[
            jax.ShapeDtypeStruct((length // stretch, HEAD, stretch), BF16),
            jax.ShapeDtypeStruct((HEAD, length), F32),
            jax.ShapeDtypeStruct((1, length), F32),
        ],
        compiler_params=vmem(52 * MIB),
        cost_estimate=cost(rows.size * length // 48, rows.size * 4, length * length),
        name="attend",
    )(full, some, base, rows, limit)


def attention_back(rows, spans, grads, wide, logs, later_than):
    full, some, base, limit, tiles, parts = spans
    blocks, _, span = rows.shape
    stretch = grads.shape[2]
    return pl.pallas_call(
        attention_back_kernel,
        grid_spec=pltpu.PrefetchScalarGridSpec(
            num_scalar_prefetch=3,
            grid=(tiles,),
            in_specs=[
                whole(rows.shape),
                pl.BlockSpec((1, QUERY_TILE), tile_at),
                pl.BlockSpec((QUERY_TILE // stretch, HEAD, stretch), lambda step, *_: (step, 0, 0)),
                pl.BlockSpec((HEAD, QUERY_TILE), lambda step, *_: (0, step)),
                pl.BlockSpec((1, QUERY_TILE), lambda step, *_: (0, step)),
                *[pl.BlockSpec(memory_space=pl.ANY)] * len(later_than),
            ],
            out_specs=whole(rows.shape),
            scratch_shapes=[
                pltpu.VMEM((blocks, span, HEAD), BF16),
                pltpu.VMEM((blocks, span, HEAD), BF16),
                pltpu.VMEM((blocks, HEAD, span), F32),
                pltpu.VMEM((blocks, HEAD, span), F32),
            ],
        ),
        out_shape=jax.ShapeDtypeStruct(rows.shape, BF16),
        compiler_params=vmem(52 * MIB),
        cost_estimate=cost(rows.size * tiles * QUERY_TILE // 16, rows.size * 4, rows.size),
        name="attend_back",
    )(full, some, base, rows, limit, grads, wide, logs, *later_than)


def run_kernel(kernel, operands, outputs, scratch=(), after=(), flops=0, name=None, room=6):
    moved = sum(array.size * array.dtype.itemsize for array in operands)
    size = 2 * moved
    for times, arrays in ((2, outputs), (1, scratch)):
        for shape, dtype in arrays:
            size += times * math.prod(shape) * jnp.dtype(dtype).itemsize
    given, kept = len(operands), len(operands) + len(after)
    return pl.pallas_call(
        lambda *refs: kernel(*refs[:given], *refs[kept:]),
        grid=(1,),
        in_specs=[IN_SMEM, *[at_once(array.shape) for array in operands[1:]]]
        + [ANYWHERE] * len(after),
        out_specs=[at_once(shape) for shape, _ in outputs],
        out_shape=[jax.ShapeDtypeStruct(shape, dtype) for shape, dtype in outputs],
        scratch_shapes=[pltpu.VMEM(shape, dtype) for shape, dtype in scratch],
        compiler_params=vmem(room * MIB + size),
        cost_estimate=cost(flops, moved),
        name=name,
    )(*operands, *after)


def rows_at(index, size):
    return pl.ds(pl.multiple_of(index * size, size), size)


def qkv_kernel(fixed, normed, place_ref, *refs):
    rows_refs, (gain_ref, weight_ref, cosine_ref, sine_ref) = refs[:4], refs[4:8]
    pieces, team, heads = refs[8:-2], refs[-2], refs[-1]
    member = place_ref[0]
    stretch = rows_refs[0].shape[0]
    half = HEAD // 2
    for turn in range(4):
        rows = rows_refs[turn][...]
        if not normed:
            wide = rows.astype(F32)
            rows = (wide * rms_factor(wide) * gain_ref[...]).astype(BF16)
        team[rows_at(member ^ turn, stretch), :] = rows
    projected = contract(weight_ref[...], team[...], 0, 1)
    cosine, sine = cosine_ref[...], sine_ref[...]
    for head in range(TEAM_HEADS):
        for part in range(3):
            at = (head * 3 + part) * HEAD
            first, second = projected[at : at + half], projected[at + half : at + HEAD]
            if part < 2:
                first, second = (
                    first * cosine - second * sine,
                    second * cosine + first * sine,
                )
            heads[head, part * HEAD : part * HEAD + half] = first.astype(BF16)
            heads[head, part * HEAD + half : (part + 1) * HEAD] = second.astype(BF16)
    for turn, piece in enumerate(pieces):
        head = turn
        if fixed:
            head = lax.rem(place_ref[1] + turn, len(pieces)) - place_ref[2]
            head = jnp.clip(head, 0, TEAM_HEADS - 1)
        piece[...] = heads[head]


def qkv_step(rows, normed, gain, weight, after, context):
    group = TEAM_SIZE * rows[0].shape[0]
    fixed = context["parts"] == 1
    return run_kernel(
        functools.partial(qkv_kernel, fixed, normed),
        [context["place"], *rows, gain, weight, context["cosine"], context["sine"]],
        [((3 * HEAD, group), BF16)] * (context["deep"] if fixed else TEAM_HEADS)
        + [((group, D), BF16)],
        [((TEAM_HEADS, 3 * HEAD, group), BF16)],
        after,
        flops=2 * group * D * weight.shape[1],
        name="qkv",
    )


def qkv_back_kernel(fixed, halves, place_ref, *refs):
    count = len(refs) - (16 if halves else 15)
    grads, refs = refs[:count], refs[count:]
    weight_ref, cosine_ref, sine_ref, team_ref, gain_ref, small_ref = refs[:6]
    outs, (stacked, turned, parts, packed) = refs[6:-4], refs[-4:]
    half = HEAD // 2
    stretch = outs[0].shape[0]
    for turn in range(count):
        stacked[turn] = grads[turn][...]
    cosine, sine = cosine_ref[...], sine_ref[...]
    for head in range(TEAM_HEADS):
        at = head
        if fixed:
            at = lax.rem(place_ref[1] - head - place_ref[2] + 2 * count, count)
        rows = stacked[at].astype(F32)
        for part in range(3):
            low = part * HEAD
            first, second = rows[low : low + half], rows[low + half : low + HEAD]
            if part < 2:
                first, second = (
                    first * cosine + second * sine,
                    second * cosine - first * sine,
                )
            low += head * 3 * HEAD
            turned[low : low + half] = first.astype(BF16)
            turned[low + half : low + HEAD] = second.astype(BF16)
    projected_grad = turned[...].T
    normed_grad = contract(projected_grad, weight_ref[...], 1, 1)
    parts[...] = normed_grad.astype(BF16)
    for turn in range(4):
        outs[turn][...] = parts[rows_at(place_ref[0] ^ turn, stretch), :]
    team = team_ref[...]
    edge = projected_grad.shape[1]
    packed[:, :edge] = contract(team, projected_grad, 0, 0).astype(BF16)
    gain_grad = jnp.sum(normed_grad * team.astype(F32), axis=0, keepdims=True) / gain_ref[...]
    small = small_ref[...]
    lane = lax.broadcasted_iota(jnp.int32, small.shape, 1)
    small = jnp.where(lane == 0, jnp.broadcast_to(gain_grad, (128, D)).T, small)
    packed[:, edge:] = small[:, : packed.shape[1] - edge].astype(BF16)
    if halves:
        outs[4][...] = packed[rows_at(place_ref[3], D // 2), :]
        outs[5][...] = packed[rows_at(1 - place_ref[3], D // 2), :]
    else:
        outs[4][...] = packed[...]


def qkv_back_step(grads, weight, team, gain, small, halves, after, context):
    group = team.shape[0]
    width = weight.shape[1] + 64
    packed = [((D // 2, width), BF16)] * 2 if halves else [((D, width), BF16)]
    return run_kernel(
        functools.partial(qkv_back_kernel, context["parts"] == 1, halves),
        [
            context["place"],
            *grads,
            weight,
            context["cosine"],
            context["sine"],
            team,
            gain,
            small,
        ],
        [((group // TEAM_SIZE, D), BF16)] * TEAM_SIZE + packed,
        [
            ((len(grads), 3 * HEAD, group), BF16),
            ((weight.shape[1], group), BF16),
            ((group, D), BF16),
            ((D, width), BF16),
        ],
        after,
        flops=4 * group * D * weight.shape[1],
        name="qkv_back",
    )


def head_slot(head, fixed):
    member = head // TEAM_HEADS
    return (head % TEAM_HEADS + (member // 2 if fixed else 0)) * TEAM_SIZE + member


def chosen(ids_ref, choice):
    ids = ids_ref[:, choice : choice + 1]
    return lax.broadcasted_iota(jnp.int32, (ids.shape[0], 128), 1) == ids + 2


def row_table(slots_ref, choice):
    slots = slots_ref[:, choice : choice + 1]
    index = lax.broadcasted_iota(jnp.int32, (slots.shape[0], EXPERTS * SLOTS), 1)
    return jnp.where(index == slots, 1.0, 0.0).astype(BF16)


def slot_table(turned_ref, choice):
    slots = turned_ref[choice : choice + 1, :]
    index = lax.broadcasted_iota(jnp.int32, (EXPERTS * SLOTS, slots.shape[1]), 0)
    return jnp.where(index == slots, 1.0, 0.0).astype(BF16)


def slots_of_grads(turned_ref, gates, upstream):
    terms = [
        jnp.dot(
            slot_table(turned_ref, c),
            (gates[:, c : c + 1] * upstream).astype(BF16),
            preferred_element_type=F32,
        )
        for c in range(2)
    ]
    return (terms[0] + terms[1]).astype(BF16)


def feed_kernel(fixed, last, place_ref, *refs):
    back_ref, stream_ref, weight_ref, gain_ref, router_ref, ids_ref, turned_ref = refs[:7]
    middle_ref, normed_ref, gates_ref, out_ref, mixed_ref = refs[-5:]
    for head in range(HEADS):
        mixed_ref[head * HEAD : (head + 1) * HEAD, :] = back_ref[head_slot(head, fixed)]
    middle = stream_ref[...].astype(F32) + contract(mixed_ref[...], weight_ref[...], 0, 0)
    normed = (middle * rms_factor(middle) * gain_ref[...]).astype(BF16)
    middle_ref[...] = middle
    normed_ref[...] = normed
    table = slot_table(turned_ref, 0) + slot_table(turned_ref, 1)
    out_ref[:, :D] = jnp.dot(table, normed, preferred_element_type=F32).astype(BF16)
    logits = jnp.dot(normed, router_ref[...], preferred_element_type=F32)
    picked = [
        jnp.sum(jnp.where(chosen(ids_ref, c), logits, 0.0), axis=1, keepdims=True)
        for c in range(2)
    ]
    highest = jnp.maximum(picked[0], picked[1])
    powers = [jnp.exp(pick - highest) for pick in picked]
    total = powers[0] + powers[1]
    gates = jnp.concatenate([powers[0] / total, powers[1] / total], axis=1)
    gates_ref[...] = gates
    if last:
        out_ref[:, D:] = slots_of_grads(turned_ref, gates, refs[7][...].astype(F32))


def feed_step(back, stream, out_weight, gain, router, upstream, after, context):
    stretch = stream.shape[0]
    last = upstream is not None
    operands = [
        context["place"],
        back,
        stream,
        out_weight,
        gain,
        router,
        context["ids"],
        context["turned_slots"],
    ]
    return run_kernel(
        functools.partial(feed_kernel, context["parts"] == 1, last),
        operands + ([upstream] if last else []),
        [
            ((stretch, D), F32),
            ((stretch, D), BF16),
            ((stretch, 2), F32),
            ((EXPERTS * SLOTS, 2 * D if last else D), BF16),
            ((D, stretch), BF16),
        ],
        (),
        after,
        flops=4 * stretch * D * D,
        name="feed",
    )


def add_up(parts):
    total = parts[0][...].astype(F32)
    for part in parts[1:]:
        total = total + part[...].astype(F32)
    return total


def layer_end_kernel(place_ref, *refs):
    returned_ref, middle_ref, gates_ref, slots_ref, gain_ref = refs[:5]
    parts = refs[5:9]
    stream_ref, gap_ref, normed_ref = refs[-3:]
    choices = [
        jnp.dot(row_table(slots_ref, c), returned_ref[...], preferred_element_type=F32)
        for c in range(2)
    ]
    gates = gates_ref[...]
    stream = middle_ref[...] + add_up(parts) + gates[:, 0:1] * choices[0]
    stream = stream + gates[:, 1:2] * choices[1]
    stream_ref[...] = stream
    gap_ref[...] = choices[0] - choices[1]
    normed_ref[...] = (stream * rms_factor(stream) * gain_ref[...]).astype(BF16)


def layer_end_step(returned, feed, parts, next_gain, after, context):
    shape = feed["middle"].shape
    return run_kernel(
        layer_end_kernel,
        [
            context["place"],
            returned,
            feed["middle"],
            feed["gates"],
            context["slots"],
            next_gain,
            *parts,
        ],
        [(shape, F32), (shape, F32), (shape, BF16)],
        (),
        after,
        flops=4 * shape[0] * D * returned.shape[0],
        name="layer_end",
    )


def feed_back_kernel(fixed, last, place_ref, *refs):
    (
        returned_ref,
        middle_ref,
        normed_ref,
        gates_ref,
        slots_ref,
        ids_ref,
        upstream_ref,
        gain_ref,
        router_ref,
        weight_ref,
    ) = refs[:10]
    parts = refs[10:14]
    outs = refs[-4:]
    tables = [row_table(slots_ref, c) for c in range(2)]
    gates = gates_ref[...]
    middle = middle_ref[...]
    upstream = upstream_ref[...].astype(F32)
    if last:
        choices = [
            jnp.dot(table, returned_ref[:, :D], preferred_element_type=F32) for table in tables
        ]
        gap = choices[0] - choices[1]
        output = middle + add_up(refs[14:18]) + gates[:, 0:1] * choices[0]
        refs[-5][...] = (output + gates[:, 1:2] * choices[1]).astype(BF16)
        grad_rows = returned_ref[:, D:]
    else:
        gap = refs[14][...]
        grad_rows = returned_ref[...]
    lead = gates[:, 0:1] * gates[:, 1:2] * jnp.sum(gap * upstream, axis=1, keepdims=True)
    logit_grad = jnp.where(chosen(ids_ref, 0), lead, 0.0) - jnp.where(
        chosen(ids_ref, 1), lead, 0.0
    )
    high = logit_grad.astype(BF16)
    low = (logit_grad - high.astype(F32)).astype(BF16)
    router = router_ref[...]
    normed_grad = (
        add_up(parts)
        + contract(high, router, 1, 1)
        + contract(low, router, 1, 1)
        + jnp.dot(tables[0] + tables[1], grad_rows, preferred_element_type=F32)
    )
    factor = rms_factor(middle)
    norm_grad, _ = norm_back(middle, gain_ref[...], factor, normed_grad)
    middle_grad = upstream + norm_grad
    attn_grad = middle_grad.astype(BF16)
    middle_grad_ref, attn_ref, heads_ref, small_ref = outs
    middle_grad_ref[...] = middle_grad
    attn_ref[...] = attn_grad
    mixed_grad = contract(weight_ref[...], attn_grad, 1, 1).astype(BF16)
    used = set()
    for head in range(HEADS):
        slot = head_slot(head, fixed)
        used.add(slot)
        heads_ref[slot] = mixed_grad[head * HEAD : (head + 1) * HEAD]
    for slot in range(heads_ref.shape[0]):
        if slot not in used:
            heads_ref[slot] = jnp.zeros_like(heads_ref[slot])
    gain_grad = jnp.sum(normed_grad * middle * factor, axis=0, keepdims=True)
    normed = normed_ref[...]
    small = contract(normed, high, 0, 0) + contract(normed, low, 0, 0)
    lane = lax.broadcasted_iota(jnp.int32, small.shape, 1)
    small_ref[...] = jnp.where(lane == 1, jnp.broadcast_to(gain_grad, (128, D)).T, small)


def feed_back_step(returned, feed, upstream, parts, others, weights, last, after, context):
    stretch = feed["middle"].shape[0]
    shape = (stretch, D)
    return run_kernel(
        functools.partial(feed_back_kernel, context["parts"] == 1, last),
        [
            context["place"],
            returned,
            feed["middle"],
            feed["normed_ffn"],
            feed["gates"],
            context["slots"],
            context["ids"],
            upstream,
            weights["gain_two"],
            weights["router"],
            weights["out"],
            *parts,
            *others,
        ],
        ([(shape, BF16)] if last else [])
        + [
            (shape, F32),
            (shape, BF16),
            ((TEAM_SIZE * TEAM_SIZE, HEAD, stretch), BF16),
            ((D, 128), F32),
        ],
        (),
        after,
        flops=4 * stretch * D * D,
        name="feed_back",
    )


def layer_start_kernel(more, place_ref, *refs):
    stream_ref, middle_grad_ref, gain_ref = refs[:3]
    parts = refs[3:7]
    stream = stream_ref[...].astype(F32)
    norm_grad, _ = norm_back(stream, gain_ref[...], rms_factor(stream), add_up(parts))
    upstream = middle_grad_ref[...] + norm_grad
    if more:
        gates_ref, turned_ref, wide_ref, out_ref = refs[7:9] + refs[-3:-2] + refs[-1:]
        wide_ref[...] = upstream
        refs[-2][...] = upstream.astype(BF16)
        out_ref[...] = slots_of_grads(turned_ref, gates_ref[...], upstream)
    else:
        refs[-1][...] = upstream.astype(BF16)


def layer_start_step(stream, middle_grad, gain, parts, feed, context):
    shape = stream.shape
    more = feed is not None
    return run_kernel(
        functools.partial(layer_start_kernel, more),
        [
            context["place"],
            stream,
            middle_grad,
            gain,
            *parts,
            *([feed["gates"], context["turned_slots"]] if more else []),
        ],
        [(shape, F32), (shape, BF16), ((EXPERTS * SLOTS, D), BF16)] if more else [(shape, BF16)],
        flops=4 * shape[0] * D * EXPERTS * SLOTS if more else 0,
        name="layer_start",
    )


def shared_grads_kernel(unit, place_ref, *refs):
    team_ref, joint_ref, hidden_ref, grads_ref = refs[:4]
    joint_outs, down_outs = refs[4:6], refs[6:8]
    half = D // 2
    units = hidden_ref.shape[1] // 2
    for place, dp in enumerate((place_ref[3], 1 - place_ref[3])):
        joint_outs[place][...] = contract(
            team_ref[:, rows_at(dp, half)], joint_ref[...], 0, 0
        ).astype(BF16)
        down = contract(hidden_ref[:, rows_at(dp, units)], grads_ref[...], 0, 0).astype(BF16)
        out = down_outs[place]
        for block in range(units // unit):
            low, high = block * unit, (block + 1) * unit
            at, end = block * half * unit // units, (block + 1) * half * unit // units
            out[at : at + unit] = down[low:high]
            out[at + unit : end] = jnp.zeros((end - at - unit, D), BF16)


def shared_grads_step(team, joint_grad, hidden, grad_team, context):
    return run_kernel(
        functools.partial(shared_grads_kernel, FF // lax.axis_size(ALL)),
        [context["place"], team, joint_grad, hidden, grad_team],
        [((D // 2, joint_grad.shape[1]), BF16)] * 2 + [((D // 2, D), BF16)] * 2,
        flops=2 * team.shape[0] * D * (joint_grad.shape[1] + D),
        name="shared_grads",
    )


def shared_grads(shared, context):
    team, grads, hidden, joint_grad = shared[-4:]
    return shared_grads_step(team, joint_grad, hidden, grads, context)


def out_grads_kernel(place_ref, mixed_ref, attn_ref, own_ref, other_ref):
    for out, dp in zip((own_ref, other_ref), (place_ref[3], 1 - place_ref[3])):
        out[...] = jnp.dot(
            mixed_ref[rows_at(dp, D // 2), :], attn_ref[...], preferred_element_type=F32
        ).astype(BF16)


def out_grads_step(mixed, attn_grad, context):
    return run_kernel(
        out_grads_kernel,
        [context["place"], mixed, attn_grad],
        [((D // 2, D), BF16)] * 2,
        flops=2 * mixed.shape[1] * D * D,
        name="out_grads",
    )


def feed_end_kernel(place_ref, *refs):
    layers_count = (len(refs) - 4) // 9
    pieces = refs[: 4 * layers_count]
    out_pieces = refs[4 * layers_count : 8 * layers_count]
    downs = refs[8 * layers_count : 9 * layers_count]
    joint_out, out_out, down_out, columns = refs[-4:]
    width = joint_out.shape[1]
    joint_width = pieces[0].shape[1]
    unit = down_out.shape[1]
    rest = joint_width // (2 * unit)
    for layer in range(layers_count):
        total = None
        for turn in range(4):
            columns[place_ref[0] ^ turn] = pieces[4 * layer + turn][...].astype(F32)
            part = out_pieces[4 * layer + turn][...].astype(F32)
            total = part if total is None else total + part
        out_out[layer] = total
        for member in range(4):
            rows = columns[member]
            for part in range(2):
                for block in range(rest):
                    low = (part * rest + block) * unit
                    at = part * (joint_out.shape[2] // 2) + (block * 4 + member) * unit
                    joint_out[layer, :, at : at + unit] = rows[:, low : low + unit]
        down_out[layer] = downs[layer][...].astype(F32)


def qkv_end_kernel(place_ref, *refs):
    first_ref, pieces = refs[0], refs[1:-3]
    qkv_out, small_out, columns = refs[-3:]
    edge = TEAM_HEADS * 3 * HEAD
    layers_count = qkv_out.shape[0]
    for layer in range(layers_count):
        small = None
        for turn in range(4):
            if layer == 0:
                total = None
                for block in range(first_ref.shape[0] // 4):
                    part = first_ref[block * 4 + turn].astype(F32)
                    total = part if total is None else total + part
                columns[turn] = total
            else:
                total = pieces[4 * (layer - 1) + turn][...].astype(F32)
                columns[place_ref[0] ^ turn] = total
            part = total[:, edge:]
            small = part if small is None else small + part
        small_out[layer] = small
        for member in range(4):
            rows = columns[member]
            for head in range(TEAM_HEADS):
                for part in range(3):
                    low = (head * 3 + part) * HEAD
                    at = part * D + (member * TEAM_HEADS + head) * HEAD
                    qkv_out[layer, :, at : at + HEAD] = rows[:, low : low + HEAD]


def logistic(values):
    return 0.5 * jnp.tanh(0.5 * values) + 0.5


def swiglu_back(gate_pre, up_pre, hidden_grad):
    sigmoid_gate = logistic(gate_pre)
    silu_gate = gate_pre * sigmoid_gate
    gate_grad = hidden_grad * up_pre * (sigmoid_gate + silu_gate * (1.0 - sigmoid_gate))
    up_grad = hidden_grad * silu_gate
    return (gate_grad.astype(BF16), up_grad.astype(BF16))


def swiglu(gate_pre, up_pre):
    return (gate_pre * logistic(gate_pre) * up_pre).astype(BF16)


def expert_kernel(forward, backward, *refs):
    inputs = 1 + backward
    rows_ref, grads_ref = refs[0], refs[inputs - 1]
    gate_ref, up_ref, down_ref, out_ref, total = refs[inputs:]
    step = pl.program_id(0)
    rows = rows_ref[...]
    gate, up, down = gate_ref[0, 0], up_ref[0, 0], down_ref[0, 0]
    gate_pre = jnp.dot(rows, gate, preferred_element_type=F32)
    up_pre = jnp.dot(rows, up, preferred_element_type=F32)
    terms = []
    if forward:
        terms.append(jnp.dot(swiglu(gate_pre, up_pre), down, preferred_element_type=F32))
    if backward:
        hidden_grad = contract(grads_ref[...], down, 1, 1).astype(BF16).astype(F32)
        gate_grad, up_grad = swiglu_back(gate_pre, up_pre, hidden_grad)
        terms.append(contract(gate_grad, gate, 1, 1) + contract(up_grad, up, 1, 1))

    @pl.when(step == 0)
    def _():
        for i, term in enumerate(terms):
            total[:, i * D : (i + 1) * D] = term

    @pl.when(step > 0)
    def _():
        for i, term in enumerate(terms):
            total[:, i * D : (i + 1) * D] += term

    @pl.when(step == pl.num_programs(0) - 1)
    def _():
        out_ref[...] = total[...].astype(BF16)


def run_expert(layer, joint, down, rows, grads, forward, after=()):
    half = joint.shape[3] // 2
    chunk = min(512, half)
    chunks = half // chunk
    given = [rows] + ([grads] if grads is not None else [])
    count = rows[0].shape[0]
    width = D * (int(forward) + int(grads is not None))
    drop = len(given) + 3
    body = functools.partial(expert_kernel, forward, grads is not None)
    return pl.pallas_call(
        lambda *refs: body(*refs[:drop], *refs[drop + len(after) :]),
        grid=(chunks,),
        in_specs=[
            *[pl.BlockSpec((count, D), lambda i, at=at: (0, at)) for _, at in given],
            pl.BlockSpec((1, 1, D, chunk), lambda i: (layer, 0, 0, i)),
            pl.BlockSpec((1, 1, D, chunk), lambda i: (layer, 0, 0, chunks + i)),
            pl.BlockSpec((1, 1, chunk, D), lambda i: (layer, 0, i, 0)),
            *[ANYWHERE] * len(after),
        ],
        out_specs=pl.BlockSpec((count, width), lambda i: (0, 0)),
        out_shape=jax.ShapeDtypeStruct((count, width), BF16),
        scratch_shapes=[pltpu.VMEM((count, width), F32)],
        compiler_params=vmem(
            4 * len(given) * count * D + 12 * D * chunk + 8 * count * width + 32 * count * chunk
        ),
        cost_estimate=cost(
            2 * count * D * half * (2 + int(forward) + 3 * int(grads is not None)),
            6 * D * half + 4 * count * width,
            count * half,
        ),
        name="expert_forward" if grads is None else "expert_both" if forward else "expert_back",
    )(*[array for array, _ in given], joint, joint, down, *after)


def expert_grad_kernel(place_ref, own_rows, own_grads, other_rows, other_grads, gate_ref, up_ref, down_ref, *refs):
    joint_out, down_out, rows_all, grads_all, turned, hold = refs[-6:]
    count = own_rows.shape[0]

    @pl.when((pl.program_id(0) == 0) & (pl.program_id(1) == 0))
    def _():
        own = rows_at(place_ref[3], count)
        other = rows_at(1 - place_ref[3], count)
        rows_all[own, :] = own_rows[...]
        rows_all[other, :] = other_rows[...]
        grads_all[own, :] = own_grads[...]
        grads_all[other, :] = other_grads[...]
        turned[...] = rows_all[...].T

    @pl.when(pl.program_id(1) == 0)
    def _():
        rows = rows_all[...]
        grads = grads_all[...]
        gate_pre = jnp.dot(rows, gate_ref[0, 0], preferred_element_type=F32)
        up_pre = jnp.dot(rows, up_ref[0, 0], preferred_element_type=F32)
        hidden_grad = contract(grads, down_ref[0, 0], 1, 1).astype(BF16).astype(F32)
        gate_grad, up_grad = swiglu_back(gate_pre, up_pre, hidden_grad)
        hold[...] = up_grad
        down_out[0, 0] = contract(swiglu(gate_pre, up_pre), grads, 0, 0)
        joint_out[0, 0] = jnp.dot(turned[...], gate_grad, preferred_element_type=F32)

    @pl.when(pl.program_id(1) == 1)
    def _():
        joint_out[0, 0] = jnp.dot(turned[...], hold[...], preferred_element_type=F32)


def expert_grads(layer, part, own, other, joint, down, before, later_than, context):
    half = joint.shape[3] // 2
    given = [*own, *other]
    count = given[0][0].shape[0]
    chunk = min(512 if count <= 512 else 128, half // 2)
    chunks = half // chunk
    steps = chunks // 2
    first = part * steps
    in_specs = [
        IN_SMEM,
        *[pl.BlockSpec((count, D), lambda i, h, at=at: (0, at)) for _, at in given],
        pl.BlockSpec((1, 1, D, chunk), lambda i, h: (layer, 0, 0, first + i)),
        pl.BlockSpec((1, 1, D, chunk), lambda i, h: (layer, 0, 0, chunks + first + i)),
        pl.BlockSpec((1, 1, chunk, D), lambda i, h: (layer, 0, first + i, 0)),
    ]
    operands = [context["place"]] + [array for array, _ in given] + [joint, joint, down]
    aliases = {}
    if before is not None:
        aliases = {len(operands): 0, len(operands) + 1: 1}
        operands += list(before)
    operands.append(later_than)
    in_specs += [ANYWHERE] * (len(operands) - len(in_specs))
    return pl.pallas_call(
        expert_grad_kernel,
        grid=(steps, 2),
        in_specs=in_specs,
        out_specs=[
            pl.BlockSpec((1, 1, D, chunk), lambda i, h: (layer, 0, 0, h * chunks + first + i)),
            pl.BlockSpec((1, 1, chunk, D), lambda i, h: (layer, 0, first + i, 0)),
        ],
        out_shape=[
            jax.ShapeDtypeStruct(joint.shape, F32),
            jax.ShapeDtypeStruct(down.shape, F32),
        ],
        scratch_shapes=[
            pltpu.VMEM((2 * count, D), BF16),
            pltpu.VMEM((2 * count, D), BF16),
            pltpu.VMEM((D, 2 * count), BF16),
            pltpu.VMEM((2 * count, chunk), BF16),
        ],
        input_output_aliases=aliases,
        compiler_params=vmem(30 * count * D + 28 * D * chunk + 56 * count * chunk),
        cost_estimate=cost(12 * count * D * half, 9 * D * half, count * half),
        name="expert_grads",
    )(*operands)


def nothing(*refs):
    pass


def later(rows, *others):
    return pl.pallas_call(
        nothing,
        in_specs=[pl.BlockSpec(memory_space=pl.ANY)] * (1 + len(others)),
        out_specs=pl.BlockSpec(memory_space=pl.ANY),
        out_shape=jax.ShapeDtypeStruct(rows.shape, rows.dtype),
        input_output_aliases={0: 0},
        name="later",
    )(rows, *others)


def route_slots(route_ids):
    stretch_rows = route_ids.shape[0]
    experts_row = jnp.arange(EXPERTS, dtype=jnp.int32)
    route_hits = (route_ids[:, :, None] == experts_row[None, None, :]).astype(jnp.int32)
    running = jnp.cumsum(route_hits.reshape(2 * stretch_rows, EXPERTS), axis=0) - 1
    running = running.reshape(stretch_rows, 2, EXPERTS)
    return route_ids * SLOTS + jnp.sum(route_hits * running, axis=2)


def send_rows(outgoing, split_count):
    width = outgoing.shape[1]
    outgoing = outgoing.reshape(EXPERTS, SLOTS, width)
    if split_count > 1:
        outgoing = jnp.repeat(outgoing, split_count, axis=0)
    return exchange(outgoing, SEQ).reshape(-1, width)


def return_rows(rows, split_count):
    width = rows.shape[1]
    returned = exchange(rows.reshape(-1, SLOTS, width), SEQ)
    if split_count > 1:
        returned = (
            returned.reshape(EXPERTS, split_count, SLOTS, width).astype(F32).sum(axis=1)
        ).astype(BF16)
    return returned.reshape(EXPERTS * SLOTS, width)


def shared_kernel(forward, backward, place_ref, *refs):
    rows_refs, refs = refs[:4], refs[4:]
    if backward:
        grads_refs, refs = refs[:4], refs[4:]
    joint_ref, down_ref = refs[:2]
    outs = refs[2:]
    stretch = rows_refs[0].shape[0]
    team = jnp.concatenate([ref[...] for ref in rows_refs], axis=0)
    joint, down = joint_ref[...], down_ref[...]
    half = joint.shape[1] // 2
    pre = jnp.dot(team, joint, preferred_element_type=F32)
    gate_pre, up_pre = pre[:, :half], pre[:, half:]
    hidden = swiglu(gate_pre, up_pre)
    if forward:
        result = jnp.dot(hidden, down, preferred_element_type=F32)
        for turn in range(4):
            outs[turn][...] = result[turn * stretch : (turn + 1) * stretch].astype(BF16)
        outs = outs[4:]
    if backward:
        grads = jnp.concatenate([ref[...] for ref in grads_refs], axis=0)
        hidden_grad = contract(grads, down, 1, 1).astype(BF16).astype(F32)
        gate_grad, up_grad = swiglu_back(gate_pre, up_pre, hidden_grad)
        joint_grad = jnp.concatenate([gate_grad, up_grad], axis=1)
        result = contract(joint_grad, joint, 1, 1)
        for turn in range(4):
            outs[turn][...] = result[turn * stretch : (turn + 1) * stretch].astype(BF16)
        team_out, grads_out, hidden_out, joint_out = outs[4:]
        team_out[...] = team
        grads_out[...] = grads
        hidden_out[...] = hidden
        joint_out[...] = joint_grad


def shared_step(rows, grads, joint, down, forward, after, context):
    stretch = rows[0].shape[0]
    group = TEAM_SIZE * stretch
    backward = grads is not None
    parts = [((stretch, D), BF16)] * 4
    outputs = list(parts) if forward else []
    if backward:
        outputs += parts + [
            ((group, D), BF16),
            ((group, D), BF16),
            ((group, down.shape[0]), BF16),
            ((group, joint.shape[1]), BF16),
        ]
    return run_kernel(
        functools.partial(shared_kernel, forward, backward),
        [context["place"], *rows, *(grads if backward else []), joint, down],
        outputs,
        (),
        after,
        flops=2 * group * joint.size * (3 if backward else 1),
        name="shared",
        room=16,
    )


def z_turn(pieces, out):
    count = len(pieces)
    arrived = [pieces[0]]
    for turn in range(1, count):
        pairs = []
        for z in range(count):
            for core in range(2):
                to = (z + turn) % count
                if 0 <= (to if out else z) - core < TEAM_HEADS:
                    pairs.append((z * 2 + core, to * 2 + core))
        arrived.append(lax.ppermute(pieces[turn], ("z", "core"), pairs))
    return arrived


def to_heads(pieces, context):
    parts = context["parts"]
    if parts == 1:
        return z_turn(pieces, True)
    heads = jnp.stack([*pieces, jnp.zeros_like(pieces[0])])
    return [exchange(jnp.repeat(heads, parts, axis=0), "z")]


def attention_forward(arrived, after, context, stretch):
    parts = context["parts"]
    if parts == 1:
        rows, attended, wide, logs = fixed_attention(
            arrived, context["spans"][3], context["place"], stretch, after
        )
        return (exchange(attended, SEQ), (rows, wide, logs))
    (rows,) = arrived
    attended, wide, logs = attention(rows, context["spans"], stretch)
    count = context["deep"] * TEAM_SIZE
    attended = lax.dynamic_update_slice_in_dim(
        jnp.zeros((count, HEAD, stretch), BF16), attended, context["part"] * (count // parts), 0
    )
    back = exchange(attended, SEQ).reshape(TEAM_SIZE, parts, TEAM_SIZE, HEAD, stretch)
    back = back.astype(F32).sum(axis=1).astype(BF16)
    return (back.reshape(-1, HEAD, stretch), (rows, wide, logs))


def attention_backward(head_grads, saved, after, context):
    parts = context["parts"]
    rows, wide, logs = saved
    if parts == 1:
        grads = exchange(head_grads, SEQ)
        pieces = fixed_attention_back(
            rows, context["spans"][3], grads, wide, logs, context["place"], after
        )
        return (z_turn(pieces, False), pieces[0])
    stretch = head_grads.shape[2]
    head_grads = head_grads.reshape(TEAM_SIZE, TEAM_SIZE, HEAD, stretch)
    grads = exchange(jnp.repeat(head_grads, parts, axis=0).reshape(-1, HEAD, stretch), SEQ)
    count = grads.shape[0] // parts
    grads = lax.dynamic_slice_in_dim(grads, context["part"] * count, count, 0)
    rows_grad = attention_back(rows, context["spans"], grads, wide, logs, after)
    back = exchange(rows_grad, "z")
    back = back.reshape((TEAM_SIZE, parts) + back.shape[1:]).astype(F32).sum(axis=1).astype(BF16)
    return ([back[i] for i in range(TEAM_HEADS)], rows_grad)


def team_pieces(rows, member):
    pieces = rows.reshape(TEAM_SIZE, -1, rows.shape[1])
    parts = [lax.dynamic_index_in_dim(pieces, member ^ k, 0, keepdims=False) for k in range(4)]
    return [parts[0]] + [from_member(parts[k], k) for k in (1, 2, 3)]


def team_turn(rows, member):
    return in_order(jnp.stack(team_pieces(rows, member)), member)


def swap(rows):
    return lax.ppermute(rows, "dp", SWAP)


def beside(pairs):
    return jnp.concatenate(
        [(own.astype(F32) + other.astype(F32)).astype(BF16) for own, other in pairs], axis=1
    )


def z_sum(rows):
    return lax.psum_scatter(rows, "z", scatter_dimension=0, tiled=True)


def z_sum_direct(rows):
    count = lax.axis_size("z")
    if count > 4:
        return z_sum(rows)
    at = lax.axis_index("z")
    blocks = rows.reshape(count, -1, rows.shape[1])
    total = lax.dynamic_index_in_dim(blocks, at, 0, keepdims=False).astype(F32)
    for turn in range(1, count):
        block = lax.dynamic_index_in_dim(blocks, (at + turn) % count, 0, keepdims=False)
        block = lax.ppermute(block, "z", [(i, (i + turn) % count) for i in range(count)])
        total = total + block.astype(F32)
    return total.astype(BF16)


def to_team(parts):
    return [parts[0]] + [from_member(parts[k], k) for k in (1, 2, 3)]


def from_team(rows):
    return [rows] + [from_member(rows, k) for k in (1, 2, 3)]


def spread(rows, axes):
    count = lax.axis_size(axes)
    copies = jnp.broadcast_to(rows[None], (count,) + rows.shape)
    return exchange(copies, axes).reshape((-1,) + rows.shape[1:])


def dp_rows(rows):
    other = lax.ppermute(rows, "dp", SWAP)
    first = lax.axis_index("dp") == 0
    return jnp.concatenate([jnp.where(first, rows, other), jnp.where(first, other, rows)], axis=0)


def small_weights(gain_attn, gain_ffn, w_router):
    small = jnp.concatenate([gain_attn[:, :, None], gain_ffn[:, :, None], w_router], axis=2)
    small = small.transpose(1, 0, 2).reshape(gain_attn.shape[1], -1)
    return jnp.broadcast_to(small[None], (TEAM_SIZE,) + small.shape)


def split_small(smalls):
    weights = []
    for layer in range(LAYERS):
        part = smalls[:, layer * (2 + EXPERTS) : (layer + 1) * (2 + EXPERTS)]
        gains = part[:, :2].astype(F32).T
        weights.append(
            dict(
                gain_one=gains[0:1],
                gain_two=gains[1:2],
                router=jnp.pad(part, ((0, 0), (0, 128 - part.shape[1]))),
            )
        )
    return weights


def qkv_columns(w_qkv):
    width = w_qkv.shape[0]
    blocks = w_qkv.reshape(width, 3, TEAM_SIZE, TEAM_HEADS, HEAD)
    return blocks.transpose(2, 0, 3, 1, 4).reshape(TEAM_SIZE, width, -1)


def joint_columns(shared_gate_up):
    total = lax.axis_size(ALL)
    width = shared_gate_up.shape[0]
    blocks = shared_gate_up.reshape(width, 2, total // TEAM_SIZE, TEAM_SIZE, FF // total)
    return blocks.transpose(3, 0, 1, 2, 4).reshape(TEAM_SIZE, width, -1)


def padded_rows(shared_down):
    total = lax.axis_size(ALL)
    return jnp.pad(shared_down, ((0, TEAM_SIZE * D // total - shared_down.shape[0]), (0, 0)))


def down_rows(padded):
    total = lax.axis_size(ALL)
    return padded.reshape(total // TEAM_SIZE, -1, D)[:, : FF // total].reshape(-1, D)


def side_by_side(*arrays):
    return jnp.concatenate(arrays, axis=2)


def copies(rows):
    return jnp.broadcast_to(rows[None], (TEAM_SIZE,) + rows.shape)


def z_gather(rows):
    return lax.all_gather(rows, "z", axis=0, tiled=True)


def rest_gather(rows):
    return lax.all_gather(rows, REST, axis=0, tiled=True)


def dp_gather(rows, edges, token):
    parts = []
    for low, high in zip(edges, edges[1:]):
        token = dp_rows(later(rows[:, low:high], token))
        parts.append(token)
    return parts


def layers(
    x_in,
    cotangent,
    gain_attn,
    w_qkv,
    w_out,
    gain_ffn,
    w_router,
    shared_gate_up,
    shared_down,
    joint,
    down,
    context,
):
    split_count = context["split_count"]
    member = context["member"]
    stretch = x_in.shape[0]
    last = LAYERS - 1

    width = w_qkv.shape[1]
    qkv_width, joint_width = 3 * D // TEAM_SIZE, 2 * FF // TEAM_SIZE
    small = small_weights(gain_attn, gain_ffn, w_router)
    rows = side_by_side(qkv_columns(w_qkv[0]), small).reshape(TEAM_SIZE * width, -1)
    rows = team_turn(rows, member).reshape(TEAM_SIZE * width, -1)
    first_rows = spread(rows, "z")
    rows = side_by_side(copies(w_out[0]), joint_columns(shared_gate_up[0]))
    rows = exchange(rows, TEAM).reshape(TEAM_SIZE * width, -1)
    main_rows = jnp.concatenate([rows, padded_rows(shared_down[0])], axis=1)
    main_rows = z_gather(later(main_rows, first_rows))
    if LAYERS > 1:
        rows = side_by_side(
            *[qkv_columns(w_qkv[layer]) for layer in range(1, LAYERS)],
            *[copies(w_out[layer]) for layer in range(1, LAYERS)],
            *[joint_columns(shared_gate_up[layer]) for layer in range(1, LAYERS)],
        )
        rows = team_turn(rows.reshape(TEAM_SIZE * width, -1), member)
        rows = rows.reshape(TEAM_SIZE * width, -1)
        more_edges = [(LAYERS - 1) * qkv_width]
        for size in (D, joint_width):
            more_edges.append(more_edges[-1] + (LAYERS - 1) * size)
        more_rows = jnp.concatenate(
            [rows, *[padded_rows(shared_down[layer]) for layer in range(1, LAYERS)]], axis=1
        )
    first_rows = dp_rows(first_rows)
    weights = split_small(first_rows[:, qkv_width:])
    weights[0]["qkv"] = first_rows[:, :qkv_width]

    stream = x_in
    rows = from_team(x_in)
    grad_rows = from_team(cotangent)
    feeds = []
    for layer in range(LAYERS):
        mine = weights[layer]
        *pieces, team = qkv_step(
            rows,
            layer > 0,
            mine["gain_one"],
            mine["qkv"],
            [mine["out"]] if layer > 0 else [],
            context,
        )
        if layer == 0:
            at, held_rows, edges = 0, main_rows, [0, D, D + joint_width]
        else:
            at, held_rows, edges = layer - 1, more_rows, more_edges
        columns = [
            held_rows[:, low + at * size : low + (at + 1) * size]
            for low, size in zip(edges, (D, joint_width, D))
        ]
        after = grad_rows[1:] if layer == last else []
        back, attended = attention_forward(to_heads(pieces, context), after, context, stretch)
        if layer == 0:
            mine["out"] = dp_rows(later(columns[0], attended[1]))
        if layer == 0 and LAYERS > 1:
            more_rows = z_gather(later(more_rows, attended[1]))
        middle, normed_ffn, gates, outgoing, mixed = feed_step(
            back,
            stream,
            mine["out"],
            mine["gain_two"],
            mine["router"],
            cotangent if layer == last else None,
            [feeds[0]["other"]] if layer > 0 else [],
            context,
        )
        mine["joint"] = dp_rows(later(columns[1], attended[1] if layer > 0 else normed_ffn))
        down_padded = dp_rows(later(columns[2], attended[1] if layer > 0 else normed_ffn))
        mine["down"] = down_rows(down_padded)
        arrived = send_rows(outgoing, split_count)
        other = swap(arrived)
        ffn_rows = from_team(normed_ffn)
        returned = run_expert(
            layer,
            joint,
            down,
            (arrived, 0),
            (arrived, 1) if layer == last else None,
            True,
            [*ffn_rows[1:], mine["joint"], *([down_padded] if layer > 0 else [])],
        )
        shared = shared_step(
            ffn_rows,
            grad_rows if layer == last else None,
            mine["joint"],
            mine["down"],
            True,
            [returned],
            context,
        )
        if layer == 0:
            for i in range(1, LAYERS):
                columns = more_rows[:, (i - 1) * qkv_width : i * qkv_width]
                weights[i]["qkv"] = dp_rows(later(columns, returned))
        returned = return_rows(returned, split_count)
        feed = dict(
            stream=stream,
            team=team,
            attended=attended,
            middle=middle,
            normed_ffn=normed_ffn,
            gates=gates,
            mixed=mixed,
            arrived=arrived,
            other=other,
            ffn_rows=ffn_rows,
        )
        feeds.append(feed)
        parts = to_team(shared[:4])
        if layer < last:
            stream, feed["gap"], normed = layer_end_step(
                returned, feed, parts, weights[layer + 1]["gain_one"], [weights[layer + 1]["qkv"]], context
            )
            rows = from_team(normed)
            low = more_edges[0] + layer * D
            weights[layer + 1]["out"] = dp_rows(later(more_rows[:, low : low + D], normed))

    upstream = cotangent
    terms = None
    unit = FF // lax.axis_size(ALL)
    feed_parts, head_parts = [None] * LAYERS, [None] * LAYERS
    for layer in reversed(range(LAYERS)):
        feed, mine = feeds[layer], weights[layer]
        arrived, other = feed["arrived"], feed["other"]
        if layer == last:
            grads, other_grads = (arrived, 1), (other, 1)
            shared_parts = shared_grads(shared, context)
            output, middle_grad, attn_grad, head_grads, small = feed_back_step(
                returned,
                feed,
                upstream,
                to_team(shared[4:8]),
                parts,
                mine,
                True,
                [shared_parts[1], shared_parts[3]],
                context,
            )
        else:
            arrived_grad = send_rows(outgoing_grads, split_count)
            grads, other_grads = (arrived_grad, 0), (swap(arrived_grad), 0)
            grad_rows = from_team(upstream_rows)
            waiting = [(own, swap(rows)) for own, rows in waiting[:2]]
            returned = run_expert(
                layer,
                joint,
                down,
                (arrived, 0),
                (arrived_grad, 0),
                False,
                [*grad_rows[1:], *[rows for _, rows in waiting], terms[1]],
            )
            shared = shared_step(
                feed["ffn_rows"],
                grad_rows,
                mine["joint"],
                mine["down"],
                False,
                [returned],
                context,
            )
            waiting = [(own, later(rows, shared[0])) for own, rows in waiting]
            waiting_sum = z_sum(beside([*waiting, waited]))
            returned = return_rows(returned, split_count)
            shared_parts = shared_grads(shared, context)
            middle_grad, attn_grad, head_grads, small = feed_back_step(
                returned,
                feed,
                upstream,
                to_team(shared[:4]),
                [feed["gap"]],
                mine,
                False,
                [shared_parts[1], shared_parts[3]],
                context,
            )
        out_own, out_other = out_grads_step(feed["mixed"], attn_grad, context)
        joint_arrived, down_arrived = swap(shared_parts[1]), swap(shared_parts[3])
        out_arrived = swap(out_other)
        joint_sum = z_sum(beside([(shared_parts[0], later(joint_arrived, head_grads))]))
        pieces, token = attention_backward(
            head_grads,
            feed["attended"],
            [out_other, other_grads[0]] + ([waiting_sum] if layer < last else []),
            context,
        )
        held = ((arrived, 0), grads), ((other, 0), other_grads)
        terms = expert_grads(layer, 0, *held, joint, down, terms, token, context)
        results = qkv_back_step(
            pieces,
            mine["qkv"],
            feed["team"],
            mine["gain_one"],
            small,
            layer > 0,
            [down_arrived, terms[1], joint_sum] + ([] if layer > 0 else [out_arrived]),
            context,
        )
        normed_parts, packed = to_team(results[:4]), results[4:]
        if layer > 0:
            waiting = [packed, (out_own, out_other)]
            waited = (shared_parts[2], down_arrived)
            upstream, upstream_rows, outgoing_grads = layer_start_step(
                feed["stream"], middle_grad, mine["gain_one"], normed_parts, feeds[layer - 1], context
            )
            terms = expert_grads(layer, 1, *held, joint, down, terms, outgoing_grads, context)
        else:
            (upstream_rows,) = layer_start_step(
                feed["stream"], middle_grad, mine["gain_one"], normed_parts, None, context
            )
            total = lax.axis_size(ALL)
            first_sum = exchange(packed[0].reshape(total, D // total, -1), ALL)
            tail_sum = z_sum(
                beside(
                    [
                        (out_own, later(out_arrived, packed[0])),
                        (shared_parts[2], down_arrived),
                    ]
                )
            )
            terms = expert_grads(layer, 1, *held, joint, down, terms, packed[0], context)
        feed_parts[layer] = [
            team_pieces(joint_sum, member),
            team_pieces(tail_sum[:, :D], member) if layer == 0 else None,
            tail_sum[:unit, D:] if layer == 0 else None,
        ]
        if layer < last:
            edge = waiting_sum.shape[1] - 2 * D
            head_parts[layer + 1] = team_pieces(waiting_sum[:, :edge], member)
            feed_parts[layer + 1][1] = team_pieces(waiting_sum[:, edge : edge + D], member)
            feed_parts[layer + 1][2] = waiting_sum[:unit, edge + D :]
    joint_sum, out_sum, down_sum = run_kernel(
        feed_end_kernel,
        [
            context["place"],
            *[piece for pieces, _, _ in feed_parts for piece in pieces],
            *[piece for _, pieces, _ in feed_parts for piece in pieces],
            *[rows for _, _, rows in feed_parts],
        ],
        [
            ((LAYERS, width, 2 * FF), F32),
            ((LAYERS, width, D), F32),
            ((LAYERS, unit, D), F32),
        ],
        [((TEAM_SIZE, width, joint_width), F32)],
        name="feed_end",
    )
    qkv_sum, small_sum = run_kernel(
        qkv_end_kernel,
        [context["place"], first_sum, *[piece for pieces in head_parts[1:] for piece in pieces]],
        [((LAYERS, width, 3 * D), F32), ((LAYERS, width, 64), F32)],
        [((TEAM_SIZE, width, first_sum.shape[2]), F32)],
        name="qkv_end",
    )
    dense = (
        small_sum[:, :, 0],
        qkv_sum,
        out_sum,
        small_sum[:, :, 1],
        small_sum[:, :, 2 : 2 + EXPERTS],
        joint_sum,
        down_sum,
    )
    return (output, upstream_rows, dense, terms)


def query_spans(block_row, group, part, parts):
    length = block_row.shape[0]
    limit = jnp.sum((block_row[None, :] <= block_row[:, None]).astype(jnp.int32), axis=1)
    tiles = length // QUERY_TILE // parts
    base = part * tiles
    ends = lax.dynamic_slice_in_dim(limit.reshape(-1, QUERY_TILE), base, tiles, 0)
    full = ends[:, 0] // group
    some = (ends[:, -1] + group - 1) // group
    base = jnp.full((1,), base, jnp.int32)
    return (full, some, base, limit[None, :], tiles, parts)


def local(
    x_in,
    block_ids,
    expert_ids,
    cotangent,
    gain_attn,
    w_qkv,
    w_out,
    gain_ffn,
    w_router,
    shared_gate_up,
    shared_down,
    expert_gate_up,
    expert_down,
):
    stretch = x_in.shape[1]
    group = TEAM_SIZE * stretch
    deep = lax.axis_size("z")
    parts = max(1, deep // TEAM_SIZE)
    at = lax.axis_index("z")
    member = lax.axis_index("core") * lax.axis_size("ulysses") + lax.axis_index("ulysses")
    half_size = HEAD // 2
    spacing = 10000.0 ** (-jnp.arange(half_size).astype(F32) * 2.0 / HEAD)
    positions = (at * group + jnp.arange(group, dtype=jnp.int32)).astype(F32)
    angles = spacing[:, None] * positions[None, :]
    part = at % parts
    slots = route_slots(expert_ids[0])
    place = [member, at, lax.axis_index("core"), lax.axis_index("dp")]
    context = dict(
        member=member,
        place=jnp.stack(place).astype(jnp.int32),
        cosine=jnp.cos(angles),
        sine=jnp.sin(angles),
        ids=expert_ids[0],
        slots=slots,
        turned_slots=slots.T,
        parts=parts,
        part=part,
        deep=deep,
        split_count=deep * TEAM_SIZE // EXPERTS,
        spans=query_spans(block_ids[0], group, part, parts),
    )
    output, grad_x, dense, terms = layers(
        x_in[0],
        cotangent[0],
        gain_attn,
        w_qkv,
        w_out,
        gain_ffn,
        w_router,
        shared_gate_up,
        shared_down,
        expert_gate_up,
        expert_down,
        context,
    )
    return (output[None], grad_x[None], *dense, *terms)


def solution(mesh):
    dp, blk, ulysses = mesh.devices.shape
    grid = Mesh(mesh.devices.reshape(dp, blk // 2, 2, ulysses), ALL)
    rows = P("dp", SEQ, None)
    in_specs = (
        rows,
        P("dp", None),
        rows,
        rows,
        P(None, ALL),
        P(None, ALL, None),
        P(None, ALL, None),
        P(None, ALL),
        P(None, ALL, None),
        P(None, ALL, None),
        P(None, ALL, None),
        P(None, SEQ, None, None),
        P(None, SEQ, None, None),
    )
    out_specs = (
        rows,
        rows,
        P(None, ALL),
        P(None, ALL, None),
        P(None, ALL, None),
        P(None, ALL),
        P(None, ALL, None),
        P(None, ALL, None),
        P(None, ALL, None),
        P(None, SEQ, None, None),
        P(None, SEQ, None, None),
    )
    return jax.shard_map(local, mesh=grid, in_specs=in_specs, out_specs=out_specs, check_vma=False)
```

time: 724 us -> 727 us (level)
  Pallas kernels: 119 us -> 208 us
  matrix products: 54.7 us -> 0 us
  starting transfers between devices: 127 us -> 180 us
  blocking collectives: 42.8 us -> 0 us
  local copies, waits for them, and re-layouts: 71.4 us -> 54.7 us
  other arithmetic: 47 us -> 33.4 us
  waiting for transfers between devices: 235 us -> 225 us
    pallas_call x9 -> x31, Pallas kernels: 119 us -> 208 us  [the longest x20 77.2 us: run_kernel(): pl.pallas_call(lambda *refs: kernel(*refs[:given], *refs[kept:]), grid=(1...]
    dot_general x42 -> x0, matrix products: 54.7 us -> none  [the longest x24 28.2 us: contract(): lax.dot_general(left, right, (((left_dim,), (right_dim,)), ((), ())), pre...]
    all_to_all x16 -> x13, waiting for transfers between devices: 109 us -> 58.6 us  [exchange(): return lax.all_to_all(rows, axes, split_axis=0, concat_axis=0, tiled=True)]
    ppermute x6 -> x22, starting transfers between devices: 4.94 us -> 51.2 us  [the longest x12 40.1 us: z_turn(): arrived.append(lax.ppermute(pieces[turn], ('z', 'core'), pairs))]
    all_to_all x2 -> x0, blocking collectives: 42.8 us -> none  [exchange(): return lax.all_to_all(rows, axes, split_axis=0, concat_axis=0, tiled=True)]
    ppermute x6 -> x22, waiting for transfers between devices: 16.6 us -> 48.4 us  [the longest x12 29 us: z_turn(): arrived.append(lax.ppermute(pieces[turn], ('z', 'core'), pairs))]
    ppermute x2 -> x8, waiting for transfers between devices: 31.7 us -> 59.7 us  [dp_rows(): other = lax.ppermute(rows, 'dp', SWAP)]
    ppermute x16 -> x19, waiting for transfers between devices: 47.9 us -> 36.2 us  [from_member(): return lax.ppermute(rows, 'ulysses', SWAP)]
  transfers between devices with their start and end apart: 78 -> 106, of which waited for: 35 -> 36; matrix products, arithmetic and copies ran while one was open for 18% -> 9% of each run, Pallas kernels for 15% -> 22%
where the time goes in v3:
time: 727 us; the launch traced here: 718 us
  waiting for transfers between devices  225 us (31%)
  Pallas kernels  208 us (29%)
  starting transfers between devices  180 us (25%)
  local copies, waits for them, and re-layouts  54.7 us (8%)
  other arithmetic  33.4 us (5%)
  between operations  16.3 us (2%)
    pallas_call x20, Pallas kernels, run_kernel(): pl.pallas_call(lambda *refs: kernel(*refs[:given], *refs[kept:]), grid=(1...  77.2 us
    all_to_all x13, starting transfers between devices, exchange(): return lax.all_to_all(rows, axes, split_axis=0, concat_axis=0, tiled=True)  76.2 us
    pallas_call x4, Pallas kernels, expert_grads(): pl.pallas_call(expert_grad_kernel, grid=(steps, 2), in_specs=in_specs, ou...  60.8 us
    ppermute x8, waiting for transfers between devices, dp_rows(): other = lax.ppermute(rows, 'dp', SWAP)  59.7 us
    all_to_all x13, waiting for transfers between devices, exchange(): return lax.all_to_all(rows, axes, split_axis=0, concat_axis=0, tiled=True)  58.6 us
    ppermute x12, starting transfers between devices, z_turn(): arrived.append(lax.ppermute(pieces[turn], ('z', 'core'), pairs))  40.1 us
    ppermute x19, waiting for transfers between devices, from_member(): return lax.ppermute(rows, 'ulysses', SWAP)  36.2 us
    pallas_call x3, Pallas kernels, run_expert(): pl.pallas_call(lambda *refs: body(*refs[:drop], *refs[drop + len(after):]...  34.2 us
  transfers between devices with their start and end apart: 106, of which 36 were waited for; matrix products, arithmetic and copies ran while one was open for 9% of the time, Pallas kernels for 22%

profile of v3, /device:TPU:0, one launch (start us, length us, event | category | flops | bytes accessed | tf_op | source)
XLA Modules:
  0.0 717.8 jit_solution(12650342705942604537)
XLA Ops:
  35.2 12.2 %all-to-all-done = bf16[4,96,612]{2,1,0:T(8,128)(2,1)S(1)} async-done(((bf16[4,96,612]{2,1,0:T(8,128)(2,1)}), bf16[4,96,612]{2,1,0:T(8,128)(2,1)S(1)}, u32[]{:S(2)}, u32[]{:S(2)}) %all-to-all-start) | async-done | bytes 470048 | tf_op jit(solution)/shard_map/all_to_all | solution.py:52
  56.6 10.2 %collective-permute-done.6 = bf16[384,612]{0,1:T(8,128)(2,1)S(1)} collective-permute-done((bf16[384,612]{0,1:T(8,128)(2,1)S(1)}, bf16[384,612]{0,1:T(8,128)(2,1)S(1)}, u32[]{:S(2)}, u32[]{:S(2)}) %collective-permute-start.6) | collective-permute-done | bytes 470048 | tf_op jit(solution)/shard_map/ppermute | solution.py:1307
  79.8 9.3 %collective-permute-done.7.refs_1_ = bf16[192,512]{1,0:T(8,128)(2,1)S(1)} collective-permute-done((bf16[192,512]{1,0:T(8,128)(2,1)}, bf16[192,512]{1,0:T(8,128)(2,1)S(1)}, u32[]{:S(2)}, u32[]{:S(2)}) %collective-permute-start.7) | collective-permute-done | bytes 196640 | tf_op jit(solution)/shard_map/ppermute | solution.py:1204
  89.1 11.1 %collective-permute-done.8.refs_2_ = bf16[192,512]{1,0:T(8,128)(2,1)S(1)} collective-permute-done((bf16[192,512]{1,0:T(8,128)(2,1)}, bf16[192,512]{1,0:T(8,128)(2,1)S(1)}, u32[]{:S(2)}, u32[]{:S(2)}) %collective-permute-start.8) | collective-permute-done | bytes 196640 | tf_op jit(solution)/shard_map/ppermute | solution.py:1204
  101.0 7.8 %attend.2 = (bf16[4,192,512]{2,1,0:T(8,128)(2,1)}, bf16[16,64,128]{2,1,0:T(8,128)(2,1)}, f32[64,2048]{1,0:T(8,128)}, f32[1,2048]{1,0:T(1,128)}) custom-call(s32[4]{0:T(128)} %pad_add_fusion.refs_0_.place_ref, bf16[192,512]{1,0:T(8,128)(2,1)} %get-tuple-element.122.refs_0_, bf16[192,512]{1,0:T(8,128)(2,1)} %copy-done.112, bf16[192,512]{1,0:T(8,128)(2,1)} %copy-done.114, ...), custom_call_target="tpu_custom_call" | custom-call | flops 16777216 | bytes 1572864 | tf_op jit(solution)/shard_map/attend/pallas_call | solution.py:295
  126.5 9.5 %all-to-all-done.1.refs_1_ = bf16[16,64,128]{2,1,0:T(8,128)(2,1)S(1)} async-done(((bf16[16,64,128]{2,1,0:T(8,128)(2,1)}), bf16[16,64,128]{2,1,0:T(8,128)(2,1)S(1)}, u32[]{:S(2)}, u32[]{:S(2)}) %all-to-all-start.1) | async-done | bytes 262176 | tf_op jit(solution)/shard_map/all_to_all | solution.py:52
  150.3 10.4 %collective-permute-done.14 = bf16[384,1024]{1,0:T(8,128)(2,1)} collective-permute-done((bf16[384,1024]{1,0:T(8,128)(2,1)}, bf16[384,1024]{1,0:T(8,128)(2,1)}, u32[]{:S(2)}, u32[]{:S(2)}) %collective-permute-start.14) | collective-permute-done | bytes 786464 | tf_op jit(solution)/shard_map/ppermute | solution.py:1307
  163.3 7.7 %all-to-all-done.3 = bf16[16,24,768]{2,1,0:T(8,128)(2,1)S(1)} async-done(((bf16[16,24,768]{2,1,0:T(8,128)(2,1)}), bf16[16,24,768]{2,1,0:T(8,128)(2,1)S(1)}, u32[]{:S(2)}, u32[]{:S(2)}) %all-to-all-start.3) | async-done | bytes 589856 | tf_op jit(solution)/shard_map/all_to_all | solution.py:52
  171.8 8.5 %expert_forward.1.refs_7_.refs_1_ = bf16[384,768]{1,0:T(8,128)(2,1)} custom-call(bf16[384,768]{1,0:T(8,128)(2,1)} %bitcast.190, bf16[2,1,768,4096]{3,2,1,0:T(8,128)(2,1)} %up_ref.7, bf16[2,1,768,4096]{3,2,1,0:T(8,128)(2,1)} %up_ref.7, bf16[2,1,2048,768]{3,2,1,0:T(8,128)(2,1)} %down_ref.7, bf16[128,768]{1,0:T(8,128)(2,1)} %copy-done.35, ...), custom_call_target="tpu_custom_call" | custom-call | flops 3623878656 | bytes 10616832 | tf_op jit(solution)/shard_map/expert_forward/pallas_call | solution.py:991
  180.3 9.0 %all-to-all-start.4 = ((bf16[16,24,768]{2,1,0:T(8,128)(2,1)}), bf16[16,24,768]{2,1,0:T(8,128)(2,1)S(1)}, u32[]{:S(2)}, u32[]{:S(2)}) async-start(bf16[16,24,768]{2,1,0:T(8,128)(2,1)} %bitcast.199), calls=%async_computation.4 | async-start | bytes 1179648 | tf_op jit(solution)/shard_map/all_to_all | solution.py:52
  221.0 11.9 %collective-permute-done.26 = bf16[384,768]{1,0:T(8,128)(2,1)S(1)} collective-permute-done((bf16[384,768]{1,0:T(8,128)(2,1)}, bf16[384,768]{1,0:T(8,128)(2,1)S(1)}, u32[]{:S(2)}, u32[]{:S(2)}) %collective-permute-start.26) | collective-permute-done | bytes 589856 | tf_op jit(solution)/shard_map/ppermute | solution.py:1307
  255.4 6.7 collective-permute-done.28.refs_2_
  262.9 7.8 %attend.3 = (bf16[4,192,512]{2,1,0:T(8,128)(2,1)}, bf16[16,64,128]{2,1,0:T(8,128)(2,1)}, f32[64,2048]{1,0:T(8,128)}, f32[1,2048]{1,0:T(1,128)}) custom-call(s32[4]{0:T(128)} %pad_add_fusion.refs_0_.place_ref, bf16[192,512]{1,0:T(8,128)(2,1)} %get-tuple-element.137.refs_0_, bf16[192,512]{1,0:T(8,128)(2,1)} %copy-done.110, bf16[192,512]{1,0:T(8,128)(2,1)} %copy-done.111, ...), custom_call_target="tpu_custom_call" | custom-call | flops 16777216 | bytes 1572864 | tf_op jit(solution)/shard_map/attend/pallas_call | solution.py:295
  276.9 9.1 %all-to-all-done.5.refs_1_ = bf16[16,64,128]{2,1,0:T(8,128)(2,1)S(1)} async-done(((bf16[16,64,128]{2,1,0:T(8,128)(2,1)}), bf16[16,64,128]{2,1,0:T(8,128)(2,1)S(1)}, u32[]{:S(2)}, u32[]{:S(2)}) %all-to-all-start.5) | async-done | bytes 262176 | tf_op jit(solution)/shard_map/all_to_all | solution.py:52
  301.6 9.8 %collective-permute-done.38 = bf16[384,768]{1,0:T(8,128)(2,1)S(1)} collective-permute-done((bf16[384,768]{1,0:T(8,128)(2,1)}, bf16[384,768]{1,0:T(8,128)(2,1)S(1)}, u32[]{:S(2)}, u32[]{:S(2)}) %collective-permute-start.38) | collective-permute-done | bytes 589856 | tf_op jit(solution)/shard_map/ppermute | solution.py:1307
  312.6 15.1 %collective-permute-done.37 = bf16[384,1024]{1,0:T(8,128)(2,1)S(1)} collective-permute-done((bf16[384,1024]{1,0:T(8,128)(2,1)}, bf16[384,1024]{1,0:T(8,128)(2,1)S(1)}, u32[]{:S(2)}, u32[]{:S(2)}) %collective-permute-start.37) | collective-permute-done | bytes 786464 | tf_op jit(solution)/shard_map/ppermute | solution.py:1307
  330.3 13.8 %expert_both.1.refs_11_ = bf16[384,1536]{1,0:T(8,128)(2,1)} custom-call(bf16[384,1536]{1,0:T(8,128)(2,1)} %bitcast.183, bf16[384,1536]{1,0:T(8,128)(2,1)} %bitcast.184, bf16[2,1,768,4096]{3,2,1,0:T(8,128)(2,1)} %up_ref.7, bf16[2,1,768,4096]{3,2,1,0:T(8,128)(2,1)} %up_ref.7, bf16[2,1,2048,768]{3,2,1,0:T(8,128)(2,1)} %down_ref.7, bf16[128,768]{1,0:T(8,128)(2,1)} %copy-done.49, ...), custom_call_target="tpu_custom_call" | custom-call | flops 7247757312 | bytes 11796480 | tf_op jit(solution)/shard_map/expert_both/pallas_call | solution.py:991
  351.2 6.5 shared.4
  367.3 6.5 collective-permute-done.39.refs_12_
  415.9 10.2 %attend_back.2 = (bf16[192,512]{1,0:T(8,128)(2,1)}, bf16[192,512]{1,0:T(8,128)(2,1)}, bf16[192,512]{1,0:T(8,128)(2,1)}, bf16[192,512]{1,0:T(8,128)(2,1)}) custom-call(s32[4]{0:T(128)} %pad_add_fusion.refs_0_.place_ref, bf16[4,192,512]{2,1,0:T(8,128)(2,1)} %get-tuple-element.164.rows_ref, s32[1,2048]{1,0:T(1,128)} %bitcast.248, ...), custom_call_target="tpu_custom_call" | custom-call | flops 50331648 | bytes 1572864 | tf_op jit(solution)/shard_map/attend_back/pallas_call | solution.py:322
  436.9 15.2 %expert_grads.4 = (f32[2,1,768,4096]{3,2,1,0:T(8,128)}, f32[2,1,2048,768]{3,2,1,0:T(8,128)}) custom-call(s32[4]{0:T(128)} %pad_add_fusion.refs_0_.place_ref, bf16[384,1536]{1,0:T(8,128)(2,1)} %bitcast.185, bf16[384,1536]{1,0:T(8,128)(2,1)} %bitcast.186, bf16[384,1536]{1,0:T(8,128)(2,1)} %copy-done.2, bf16[384,1536]{1,0:T(8,128)(2,1)} %copy-done.2, ...), custom_call_target="tpu_custom_call" | custom-call | flops 7247757312 | bytes 14155776 | tf_op jit(solution)/shard_map/expert_grads/pallas_call | solution.py:1069
  480.7 15.2 %expert_grads.5 = (f32[2,1,768,4096]{3,2,1,0:T(8,128)}, f32[2,1,2048,768]{3,2,1,0:T(8,128)}) custom-call(s32[4]{0:T(128)} %pad_add_fusion.refs_0_.place_ref, bf16[384,1536]{1,0:T(8,128)(2,1)} %bitcast.187, bf16[384,1536]{1,0:T(8,128)(2,1)} %bitcast.188, bf16[384,1536]{1,0:T(8,128)(2,1)} %copy-done.2, ...), custom_call_target="tpu_custom_call", output_to_operand_aliasing={{0}: (8, {}), {1}: (9, {})} | custom-call | flops 7247757312 | bytes 14155776 | tf_op jit(solution)/shard_map/expert_grads/pallas_call | solution.py:1069
  496.0 7.0 collective-permute-done.57.refs_8_.refs_0_
  504.0 11.8 %expert_back.1.refs_11_ = bf16[384,768]{1,0:T(8,128)(2,1)} custom-call(bf16[384,768]{1,0:T(8,128)(2,1)} %bitcast.191, bf16[384,768]{1,0:T(8,128)(2,1)} %bitcast.195, bf16[2,1,768,4096]{3,2,1,0:T(8,128)(2,1)} %up_ref.7, bf16[2,1,768,4096]{3,2,1,0:T(8,128)(2,1)} %up_ref.7, bf16[2,1,2048,768]{3,2,1,0:T(8,128)(2,1)} %down_ref.7, bf16[128,768]{1,0:T(8,128)(2,1)} %copy-done.53, ...), custom_call_target="tpu_custom_call" | custom-call | flops 6039797760 | bytes 10616832 | tf_op jit(solution)/shard_map/expert_back/pallas_call | solution.py:991
  540.6 7.9 %collective-permute-done.59.refs_12_ = bf16[128,768]{1,0:T(8,128)(2,1)S(1)} collective-permute-done((bf16[128,768]{1,0:T(8,128)(2,1)S(1)}, bf16[128,768]{1,0:T(8,128)(2,1)S(1)}, u32[]{:S(2)}, u32[]{:S(2)}) %collective-permute-start.59) | collective-permute-done | bytes 196640 | tf_op jit(solution)/shard_map/ppermute | solution.py:60
  567.4 11.1 %all-to-all-start.11 = ((bf16[16,64,128]{2,1,0:T(8,128)(2,1)}), bf16[16,64,128]{2,1,0:T(8,128)(2,1)}, u32[]{:S(2)}, u32[]{:S(2)}) async-start(bf16[16,64,128]{2,1,0:T(8,128)(2,1)} %get-tuple-element.201.refs_1_), calls=%async_computation.12 | async-start | bytes 524288 | tf_op jit(solution)/shard_map/all_to_all | solution.py:52
  584.5 7.9 %collective-permute-done.62.refs_1_.other_grads = bf16[384,768]{1,0:T(8,128)(2,1)S(1)} collective-permute-done((bf16[384,768]{1,0:T(8,128)(2,1)S(1)}, bf16[384,768]{1,0:T(8,128)(2,1)S(1)}, u32[]{:S(2)}, u32[]{:S(2)}) %collective-permute-start.62) | collective-permute-done | bytes 589856 | tf_op jit(solution)/shard_map/ppermute | solution.py:1265
  593.2 10.1 %attend_back.3 = (bf16[192,512]{1,0:T(8,128)(2,1)}, bf16[192,512]{1,0:T(8,128)(2,1)}, bf16[192,512]{1,0:T(8,128)(2,1)}, bf16[192,512]{1,0:T(8,128)(2,1)}) custom-call(s32[4]{0:T(128)} %pad_add_fusion.refs_0_.place_ref, bf16[4,192,512]{2,1,0:T(8,128)(2,1)} %get-tuple-element.200.rows_ref, s32[1,2048]{1,0:T(1,128)} %bitcast.249, ...), custom_call_target="tpu_custom_call" | custom-call | flops 50331648 | bytes 1572864 | tf_op jit(solution)/shard_map/attend_back/pallas_call | solution.py:322
  603.4 8.9 %collective-permute-start.63 = (bf16[192,512]{1,0:T(8,128)(2,1)}, bf16[192,512]{1,0:T(8,128)(2,1)S(1)}, u32[]{:S(2)}, u32[]{:S(2)}) collective-permute-start(bf16[192,512]{1,0:T(8,128)(2,1)} %get-tuple-element.210), channel_id=1, source_target_pairs={{0,4},{4,8},{6,10},{8,12},{10,14},{14,2},{1,5},{5,9},{7,11},{9,13}... | collective-permute-start | bytes 589832 | tf_op jit(solution)/shard_map/ppermute | solution.py:1204
  619.7 15.2 %expert_grads.6 = (f32[2,1,768,4096]{3,2,1,0:T(8,128)}, f32[2,1,2048,768]{3,2,1,0:T(8,128)}) custom-call(s32[4]{0:T(128)} %pad_add_fusion.refs_0_.place_ref, bf16[384,768]{1,0:T(8,128)(2,1)} %bitcast.192, bf16[384,768]{1,0:T(8,128)(2,1)} %bitcast.196, bf16[384,768]{1,0:T(8,128)(2,1)} %copy-done.10, ...), custom_call_target="tpu_custom_call", output_to_operand_aliasing={{0}: (8, {}), {1}: (9, {})} | custom-call | flops 7247757312 | bytes 14155776 | tf_op jit(solution)/shard_map/expert_grads/pallas_call | solution.py:1069
  654.4 7.3 %collective-permute-done.69.refs_5_ = bf16[128,768]{1,0:T(8,128)(2,1)S(1)} collective-permute-done((bf16[128,768]{1,0:T(8,128)(2,1)S(1)}, bf16[128,768]{1,0:T(8,128)(2,1)S(1)}, u32[]{:S(2)}, u32[]{:S(2)}) %collective-permute-start.69) | collective-permute-done | bytes 196640 | tf_op jit(solution)/shard_map/ppermute | solution.py:60
  665.7 15.2 %expert_grads.7 = (f32[2,1,768,4096]{3,2,1,0:T(8,128)}, f32[2,1,2048,768]{3,2,1,0:T(8,128)}) custom-call(s32[4]{0:T(128)} %pad_add_fusion.refs_0_.place_ref, bf16[384,768]{1,0:T(8,128)(2,1)} %bitcast.193, bf16[384,768]{1,0:T(8,128)(2,1)} %bitcast.197, bf16[384,768]{1,0:T(8,128)(2,1)} %copy-done.10, ...), custom_call_target="tpu_custom_call", output_to_operand_aliasing={{0}: (8, {}), {1}: (9, {})} | custom-call | flops 7247757312 | bytes 14155776 | tf_op jit(solution)/shard_map/expert_grads/pallas_call | solution.py:1069
  (574 shorter events, 375.7 us)
Async XLA Ops:
  7.2 61.7 %collective-permute-start.2 = (bf16[128,768]{1,0:T(8,128)(2,1)}, bf16[128,768]{1,0:T(8,128)(2,1)S(1)}, u32[]{:S(2)}, u32[]{:S(2)}) collective-permute-start(bf16[128,768]{1,0:T(8,128)(2,1)} %bitcast.215), channel_id=1, source_target_pairs={{0,3},{1,2},{2,1},{3,0},{4,7},{5,6},{6,5},{7,4},{8,11},{9,10},{10,... | collective-permute-start | bytes 589832 | tf_op jit(solution)/shard_map/ppermute | solution.py:63
  9.7 59.3 %collective-permute-start.1 = (bf16[128,768]{1,0:T(8,128)(2,1)}, bf16[128,768]{1,0:T(8,128)(2,1)}, u32[]{:S(2)}, u32[]{:S(2)}) collective-permute-start(bf16[128,768]{1,0:T(8,128)(2,1)} %bitcast.216), channel_id=1, source_target_pairs={{0,2},{2,0},{1,3},{3,1},{4,6},{6,4},{5,7},{7,5},{8,10},{10,8},{9,1... | collective-permute-start | bytes 589832 | tf_op jit(solution)/shard_map/ppermute | solution.py:62
  23.0 30.8 %collective-permute-start.21 = (bf16[24,2368]{1,0:T(8,128)(2,1)S(1)}, bf16[24,2368]{1,0:T(8,128)(2,1)S(1)}, u32[]{:S(2)}, u32[]{:S(2)}) collective-permute-start(bf16[24,2368]{1,0:T(8,128)(2,1)S(1)} %get-tuple-element.296), channel_id=1, source_target_pairs={{0,3},{1,2},{2,1},{3,0},{4,7},{5,6},{6,5},{7,4},{8,11},{9,10},{10,... | collective-permute-start | bytes 341000 | tf_op jit(solution)/shard_map/ppermute | solution.py:63
  24.8 30.1 %collective-permute-start.20 = (bf16[24,2368]{1,0:T(8,128)(2,1)S(1)}, bf16[24,2368]{1,0:T(8,128)(2,1)S(1)}, u32[]{:S(2)}, u32[]{:S(2)}) collective-permute-start(bf16[24,2368]{1,0:T(8,128)(2,1)S(1)} %get-tuple-element.297), channel_id=1, source_target_pairs={{0,1},{1,0},{2,3},{3,2},{4,5},{5,4},{6,7},{7,6},{8,9},{9,8},{10,11... | collective-permute-start | bytes 341000 | tf_op jit(solution)/shard_map/ppermute | solution.py:60
  25.2 31.2 %collective-permute-start.19 = (bf16[24,2368]{1,0:T(8,128)(2,1)S(1)}, bf16[24,2368]{1,0:T(8,128)(2,1)S(1)}, u32[]{:S(2)}, u32[]{:S(2)}) collective-permute-start(bf16[24,2368]{1,0:T(8,128)(2,1)S(1)} %get-tuple-element.298), channel_id=1, source_target_pairs={{0,2},{2,0},{1,3},{3,1},{4,6},{6,4},{5,7},{7,5},{8,10},{10,8},{9,1... | collective-permute-start | bytes 341000 | tf_op jit(solution)/shard_map/ppermute | solution.py:62
  34.4 75.3 %all-gather.3.cloned.1.call-start = ((), (), s32[]{:S(2)}) async-start(), calls=%async_computation.17 | async-start | bytes 2457600 | tf_op jit(solution)/shard_map/all_gather | solution.py:1365
  48.3 142.2 %all-gather.5.cloned.1.call-start = ((), (), s32[]{:S(2)}) async-start(), calls=%async_computation.18 | async-start | bytes 3072000 | tf_op jit(solution)/shard_map/all_gather | solution.py:1365
  140.1 30.9 %all-to-all-start.3 = ((bf16[16,24,768]{2,1,0:T(8,128)(2,1)}), bf16[16,24,768]{2,1,0:T(8,128)(2,1)S(1)}, u32[]{:S(2)}, u32[]{:S(2)}) async-start(bf16[16,24,768]{2,1,0:T(8,128)(2,1)} %bitcast.29), calls=%async_computation.3 | async-start | bytes 1179648 | tf_op jit(solution)/shard_map/all_to_all | solution.py:52
  149.1 40.2 %collective-permute-start.15 = (bf16[384,768]{1,0:T(8,128)(2,1)}, bf16[384,768]{1,0:T(8,128)(2,1)}, u32[]{:S(2)}, u32[]{:S(2)}) collective-permute-start(bf16[384,768]{1,0:T(8,128)(2,1)} %later.17), channel_id=1, source_target_pairs={{0,16},{16,0},{1,17},{17,1},{2,18},{18,2},{3,19},{19,3},{4,20},{20... | collective-permute-start | bytes 1769480 | tf_op jit(solution)/shard_map/ppermute | solution.py:1307
  180.3 33.1 %all-to-all-start.4 = ((bf16[16,24,768]{2,1,0:T(8,128)(2,1)}), bf16[16,24,768]{2,1,0:T(8,128)(2,1)S(1)}, u32[]{:S(2)}, u32[]{:S(2)}) async-start(bf16[16,24,768]{2,1,0:T(8,128)(2,1)} %bitcast.199), calls=%async_computation.4 | async-start | bytes 1179648 | tf_op jit(solution)/shard_map/all_to_all | solution.py:52
  218.7 31.6 %collective-permute-start.32 = (bf16[128,768]{1,0:T(8,128)(2,1)S(1)}, bf16[128,768]{1,0:T(8,128)(2,1)S(1)}, u32[]{:S(2)}, u32[]{:S(2)}) collective-permute-start(bf16[128,768]{1,0:T(8,128)(2,1)S(1)} %bitcast.234), channel_id=1, source_target_pairs={{0,3},{1,2},{2,1},{3,0},{4,7},{5,6},{6,5},{7,4},{8,11},{9,10},{10,... | collective-permute-start | bytes 589832 | tf_op jit(solution)/shard_map/ppermute | solution.py:63
  218.9 32.8 %collective-permute-start.31 = (bf16[128,768]{1,0:T(8,128)(2,1)S(1)}, bf16[128,768]{1,0:T(8,128)(2,1)S(1)}, u32[]{:S(2)}, u32[]{:S(2)}) collective-permute-start(bf16[128,768]{1,0:T(8,128)(2,1)S(1)} %bitcast.235), channel_id=1, source_target_pairs={{0,2},{2,0},{1,3},{3,1},{4,6},{6,4},{5,7},{7,5},{8,10},{10,8},{9,1... | collective-permute-start | bytes 589832 | tf_op jit(solution)/shard_map/ppermute | solution.py:62
  291.0 38.1 %all-to-all-start.6 = ((bf16[16,24,1536]{2,1,0:T(8,128)(2,1)}), bf16[16,24,1536]{2,1,0:T(8,128)(2,1)S(1)}, u32[]{:S(2)}, u32[]{:S(2)}) async-start(bf16[16,24,1536]{2,1,0:T(8,128)(2,1)} %bitcast.225), calls=%async_computation.6 | async-start | bytes 2359296 | tf_op jit(solution)/shard_map/all_to_all | solution.py:52
  298.4 29.3 %collective-permute-start.37 = (bf16[384,1024]{1,0:T(8,128)(2,1)}, bf16[384,1024]{1,0:T(8,128)(2,1)S(1)}, u32[]{:S(2)}, u32[]{:S(2)}) collective-permute-start(bf16[384,1024]{1,0:T(8,128)(2,1)} %later.21), channel_id=1, source_target_pairs={{0,16},{16,0},{1,17},{17,1},{2,18},{18,2},{3,19},{19,3},{4,20},{20... | collective-permute-start | bytes 2359304 | tf_op jit(solution)/shard_map/ppermute | solution.py:1307
  299.5 29.6 %collective-permute-start.36 = (bf16[128,768]{1,0:T(8,128)(2,1)S(1)}, bf16[128,768]{1,0:T(8,128)(2,1)S(1)}, u32[]{:S(2)}, u32[]{:S(2)}) collective-permute-start(bf16[128,768]{1,0:T(8,128)(2,1)S(1)} %copy-done.73), channel_id=1, source_target_pairs={{0,3},{1,2},{2,1},{3,0},{4,7},{5,6},{6,5},{7,4},{8,11},{9,10},{10,... | collective-permute-start | bytes 589832 | tf_op jit(solution)/shard_map/ppermute | solution.py:63
  300.6 28.6 %collective-permute-start.35 = (bf16[128,768]{1,0:T(8,128)(2,1)S(1)}, bf16[128,768]{1,0:T(8,128)(2,1)S(1)}, u32[]{:S(2)}, u32[]{:S(2)}) collective-permute-start(bf16[128,768]{1,0:T(8,128)(2,1)S(1)} %copy-done.73), channel_id=1, source_target_pairs={{0,2},{2,0},{1,3},{3,1},{4,6},{6,4},{5,7},{7,5},{8,10},{10,8},{9,1... | collective-permute-start | bytes 589832 | tf_op jit(solution)/shard_map/ppermute | solution.py:62
  301.5 27.6 %collective-permute-start.34 = (bf16[128,768]{1,0:T(8,128)(2,1)S(1)}, bf16[128,768]{1,0:T(8,128)(2,1)S(1)}, u32[]{:S(2)}, u32[]{:S(2)}) collective-permute-start(bf16[128,768]{1,0:T(8,128)(2,1)S(1)} %copy-done.73), channel_id=1, source_target_pairs={{0,1},{1,0},{2,3},{3,2},{4,5},{5,4},{6,7},{7,6},{8,9},{9,8},{10,11... | collective-permute-start | bytes 589832 | tf_op jit(solution)/shard_map/ppermute | solution.py:60
  344.2 45.0 %all-to-all-start.7 = ((bf16[16,24,1536]{2,1,0:T(8,128)(2,1)}), bf16[16,24,1536]{2,1,0:T(8,128)(2,1)}, u32[]{:S(2)}, u32[]{:S(2)}) async-start(bf16[16,24,1536]{2,1,0:T(8,128)(2,1)} %bitcast.201), calls=%async_computation.7 | async-start | bytes 2359296 | tf_op jit(solution)/shard_map/all_to_all | solution.py:52
  350.2 102.1 %reduce-scatter.5.cloned.1.call-start = ((), (), s32[]{:S(2)}) async-start(), calls=%async_computation.19 | async-start | bytes 983040 | tf_op jit(solution)/shard_map/reduce_scatter | solution.py:1275
  362.3 32.1 %collective-permute-start.50 = (bf16[384,1024]{1,0:T(8,128)(2,1)}, bf16[384,1024]{1,0:T(8,128)(2,1)}, u32[]{:S(2)}, u32[]{:S(2)}) collective-permute-start(bf16[384,1024]{1,0:T(8,128)(2,1)} %get-tuple-element.160.refs_19_), channel_id=1, source_target_pairs={{0,16},{16,0},{1,17},{17,1},{2,18},{18,2},{3,19},{19,3},{4,20},{20... | collective-permute-start | bytes 2359304 | tf_op jit(solution)/shard_map/ppermute | solution.py:1265
  380.7 28.8 %collective-permute-start.45 = (bf16[384,1536]{1,0:T(8,128)(2,1)S(1)}, bf16[384,1536]{1,0:T(8,128)(2,1)S(1)}, u32[]{:S(2)}, u32[]{:S(2)}) collective-permute-start(bf16[384,1536]{1,0:T(8,128)(2,1)S(1)} %bitcast.189), channel_id=1, source_target_pairs={{0,16},{16,0},{1,17},{17,1},{2,18},{18,2},{3,19},{19,3},{4,20},{20... | collective-permute-start | bytes 3538952 | tf_op jit(solution)/shard_map/ppermute | solution.py:1265
  402.7 49.5 %collective-permute-start.49 = (bf16[384,768]{1,0:T(8,128)(2,1)}, bf16[384,768]{1,0:T(8,128)(2,1)S(1)}, u32[]{:S(2)}, u32[]{:S(2)}) collective-permute-start(bf16[384,768]{1,0:T(8,128)(2,1)} %get-tuple-element.161.refs_20_), channel_id=1, source_target_pairs={{0,16},{16,0},{1,17},{17,1},{2,18},{18,2},{3,19},{19,3},{4,20},{20... | collective-permute-start | bytes 1769480 | tf_op jit(solution)/shard_map/ppermute | solution.py:1265
  470.1 32.9 %all-to-all-start.9 = ((bf16[16,24,768]{2,1,0:T(8,128)(2,1)}), bf16[16,24,768]{2,1,0:T(8,128)(2,1)S(1)}, u32[]{:S(2)}, u32[]{:S(2)}) async-start(bf16[16,24,768]{2,1,0:T(8,128)(2,1)} %bitcast.211), calls=%async_computation.10 | async-start | bytes 1179648 | tf_op jit(solution)/shard_map/all_to_all | solution.py:52
  476.1 116.3 %reduce-scatter.7.cloned.1.call-start = ((), (), s32[]{:S(2)}) async-start(), calls=%async_computation.20 | async-start | bytes 2088960 | tf_op jit(solution)/shard_map/reduce_scatter | solution.py:1275
  526.6 29.6 %all-to-all-start.10 = ((bf16[16,24,768]{2,1,0:T(8,128)(2,1)}), bf16[16,24,768]{2,1,0:T(8,128)(2,1)S(1)}, u32[]{:S(2)}, u32[]{:S(2)}) async-start(bf16[16,24,768]{2,1,0:T(8,128)(2,1)} %bitcast.59), calls=%async_computation.11 | async-start | bytes 1179648 | tf_op jit(solution)/shard_map/all_to_all | solution.py:52
  532.3 102.7 %reduce-scatter.9.cloned.1.call-start = ((), (), s32[]{:S(2)}) async-start(), calls=%async_computation.21 | async-start | bytes 983040 | tf_op jit(solution)/shard_map/reduce_scatter | solution.py:1275
  578.5 116.7 %reduce-scatter.11.cloned.1.call-start = ((), (), s32[]{:S(2)}) async-start(), calls=%async_computation.22 | async-start | bytes 1474560 | tf_op jit(solution)/shard_map/reduce_scatter | solution.py:1275
  583.6 51.3 %collective-permute-start.68 = (bf16[384,768]{1,0:T(8,128)(2,1)}, bf16[384,768]{1,0:T(8,128)(2,1)S(1)}, u32[]{:S(2)}, u32[]{:S(2)}) collective-permute-start(bf16[384,768]{1,0:T(8,128)(2,1)} %get-tuple-element.205.refs_0_), channel_id=1, source_target_pairs={{0,16},{16,0},{1,17},{17,1},{2,18},{18,2},{3,19},{19,3},{4,20},{20... | collective-permute-start | bytes 1769480 | tf_op jit(solution)/shard_map/ppermute | solution.py:1265
  603.4 31.6 %collective-permute-start.63 = (bf16[192,512]{1,0:T(8,128)(2,1)}, bf16[192,512]{1,0:T(8,128)(2,1)S(1)}, u32[]{:S(2)}, u32[]{:S(2)}) collective-permute-start(bf16[192,512]{1,0:T(8,128)(2,1)} %get-tuple-element.210), channel_id=1, source_target_pairs={{0,4},{4,8},{6,10},{8,12},{10,14},{14,2},{1,5},{5,9},{7,11},{9,13}... | collective-permute-start | bytes 589832 | tf_op jit(solution)/shard_map/ppermute | solution.py:1204
  643.9 48.0 %all-to-all-start.12 = ((bf16[32,24,640]{2,1,0:T(8,128)(2,1)}), bf16[32,24,640]{2,1,0:T(8,128)(2,1)S(1)}, u32[]{:S(2)}, u32[]{:S(2)}) async-start(bf16[32,24,640]{2,1,0:T(8,128)(2,1)} %bitcast.62), calls=%async_computation.15 | async-start | bytes 1966080 | tf_op jit(solution)/shard_map/all_to_all | solution.py:52
  647.9 48.2 %collective-permute-start.80 = (bf16[24,1024]{1,0:T(8,128)(2,1)S(1)}, bf16[24,1024]{1,0:T(8,128)(2,1)S(1)}, u32[]{:S(2)}, u32[]{:S(2)}) collective-permute-start(bf16[24,1024]{1,0:T(8,128)(2,1)S(1)} %get-tuple-element.307), channel_id=1, source_target_pairs={{0,3},{1,2},{2,1},{3,0},{4,7},{5,6},{6,5},{7,4},{8,11},{9,10},{10,... | collective-permute-start | bytes 147464 | tf_op jit(solution)/shard_map/ppermute | solution.py:63
  649.4 48.3 %collective-permute-start.79 = (bf16[24,1024]{1,0:T(8,128)(2,1)S(1)}, bf16[24,1024]{1,0:T(8,128)(2,1)S(1)}, u32[]{:S(2)}, u32[]{:S(2)}) collective-permute-start(bf16[24,1024]{1,0:T(8,128)(2,1)S(1)} %get-tuple-element.308), channel_id=1, source_target_pairs={{0,2},{2,0},{1,3},{3,1},{4,6},{6,4},{5,7},{7,5},{8,10},{10,8},{9,1... | collective-permute-start | bytes 147464 | tf_op jit(solution)/shard_map/ppermute | solution.py:62
  (193 other events, 1827.0 us)
Sparse Core Ops, SparseCore 0:
  48.4 53.0 all-gather.2
  108.9 71.2 all-gather.4
  397.1 27.7 reduce-scatter.4
  526.7 47.3 reduce-scatter.6
  576.2 24.7 reduce-scatter.8
  644.0 42.9 reduce-scatter.10

commit v4 on v3

--- a/solution.py
+++ b/solution.py
@@ -715,12 +715,13 @@
             jnp.dot(table, returned_ref[:, :D], preferred_element_type=F32) for table in tables
         ]
         gap = choices[0] - choices[1]
-        output = middle + add_up(refs[14:18]) + gates[:, 0:1] * choices[0]
+        sums = add_up(parts)
+        output = middle + sums[:, :D] + gates[:, 0:1] * choices[0]
         refs[-5][...] = (output + gates[:, 1:2] * choices[1]).astype(BF16)
-        grad_rows = returned_ref[:, D:]
+        grad_rows, shared_grad = returned_ref[:, D:], sums[:, D:]
     else:
         gap = refs[14][...]
-        grad_rows = returned_ref[...]
+        grad_rows, shared_grad = returned_ref[...], add_up(parts)
     lead = gates[:, 0:1] * gates[:, 1:2] * jnp.sum(gap * upstream, axis=1, keepdims=True)
     logit_grad = jnp.where(chosen(ids_ref, 0), lead, 0.0) - jnp.where(
         chosen(ids_ref, 1), lead, 0.0
@@ -729,7 +730,7 @@
     low = (logit_grad - high.astype(F32)).astype(BF16)
     router = router_ref[...]
     normed_grad = (
-        add_up(parts)
+        shared_grad
         + contract(high, router, 1, 1)
         + contract(low, router, 1, 1)
         + jnp.dot(tables[0] + tables[1], grad_rows, preferred_element_type=F32)
@@ -843,19 +844,21 @@
             out[at + unit : end] = jnp.zeros((end - at - unit, D), BF16)
 
 
-def shared_grads_step(team, joint_grad, hidden, grad_team, context):
+def shared_grads_step(team, joint_grad, hidden, grad_team, after, context):
     return run_kernel(
         functools.partial(shared_grads_kernel, FF // lax.axis_size(ALL)),
         [context["place"], team, joint_grad, hidden, grad_team],
         [((D // 2, joint_grad.shape[1]), BF16)] * 2 + [((D // 2, D), BF16)] * 2,
+        (),
+        after,
         flops=2 * team.shape[0] * D * (joint_grad.shape[1] + D),
         name="shared_grads",
     )
 
 
-def shared_grads(shared, context):
+def shared_grads(shared, after, context):
     team, grads, hidden, joint_grad = shared[-4:]
-    return shared_grads_step(team, joint_grad, hidden, grads, context)
+    return shared_grads_step(team, joint_grad, hidden, grads, after, context)
 
 
 def out_grads_kernel(place_ref, mixed_ref, attn_ref, own_ref, other_ref):
@@ -1064,7 +1067,7 @@
     if before is not None:
         aliases = {len(operands): 0, len(operands) + 1: 1}
         operands += list(before)
-    operands.append(later_than)
+    operands += later_than
     in_specs += [ANYWHERE] * (len(operands) - len(in_specs))
     return pl.pallas_call(
         expert_grad_kernel,
@@ -1138,7 +1141,7 @@
     if backward:
         grads_refs, refs = refs[:4], refs[4:]
     joint_ref, down_ref = refs[:2]
-    outs = refs[2:]
+    parts, outs = refs[2:6], refs[6:]
     stretch = rows_refs[0].shape[0]
     team = jnp.concatenate([ref[...] for ref in rows_refs], axis=0)
     joint, down = joint_ref[...], down_ref[...]
@@ -1146,34 +1149,34 @@
     pre = jnp.dot(team, joint, preferred_element_type=F32)
     gate_pre, up_pre = pre[:, :half], pre[:, half:]
     hidden = swiglu(gate_pre, up_pre)
+    results = []
     if forward:
-        result = jnp.dot(hidden, down, preferred_element_type=F32)
-        for turn in range(4):
-            outs[turn][...] = result[turn * stretch : (turn + 1) * stretch].astype(BF16)
-        outs = outs[4:]
+        results.append(jnp.dot(hidden, down, preferred_element_type=F32))
     if backward:
         grads = jnp.concatenate([ref[...] for ref in grads_refs], axis=0)
         hidden_grad = contract(grads, down, 1, 1).astype(BF16).astype(F32)
         gate_grad, up_grad = swiglu_back(gate_pre, up_pre, hidden_grad)
         joint_grad = jnp.concatenate([gate_grad, up_grad], axis=1)
-        result = contract(joint_grad, joint, 1, 1)
-        for turn in range(4):
-            outs[turn][...] = result[turn * stretch : (turn + 1) * stretch].astype(BF16)
-        team_out, grads_out, hidden_out, joint_out = outs[4:]
+        results.append(contract(joint_grad, joint, 1, 1))
+        team_out, grads_out, hidden_out, joint_out = outs
         team_out[...] = team
         grads_out[...] = grads
         hidden_out[...] = hidden
         joint_out[...] = joint_grad
+    for place, result in enumerate(results):
+        for turn in range(4):
+            parts[turn][:, place * D : (place + 1) * D] = result[
+                turn * stretch : (turn + 1) * stretch
+            ].astype(BF16)
 
 
 def shared_step(rows, grads, joint, down, forward, after, context):
     stretch = rows[0].shape[0]
     group = TEAM_SIZE * stretch
     backward = grads is not None
-    parts = [((stretch, D), BF16)] * 4
-    outputs = list(parts) if forward else []
+    outputs = [((stretch, D * (int(forward) + int(backward))), BF16)] * 4
     if backward:
-        outputs += parts + [
+        outputs += [
             ((group, D), BF16),
             ((group, D), BF16),
             ((group, down.shape[0]), BF16),
@@ -1231,18 +1234,23 @@
     return (back.reshape(-1, HEAD, stretch), (rows, wide, logs))
 
 
-def attention_backward(head_grads, saved, after, context):
+def grads_to_heads(head_grads, context):
+    parts = context["parts"]
+    if parts > 1:
+        stretch = head_grads.shape[2]
+        head_grads = head_grads.reshape(TEAM_SIZE, TEAM_SIZE, HEAD, stretch)
+        head_grads = jnp.repeat(head_grads, parts, axis=0).reshape(-1, HEAD, stretch)
+    return exchange(head_grads, SEQ)
+
+
+def attention_backward(grads, saved, after, context):
     parts = context["parts"]
     rows, wide, logs = saved
     if parts == 1:
-        grads = exchange(head_grads, SEQ)
         pieces = fixed_attention_back(
             rows, context["spans"][3], grads, wide, logs, context["place"], after
         )
         return (z_turn(pieces, False), pieces[0])
-    stretch = head_grads.shape[2]
-    head_grads = head_grads.reshape(TEAM_SIZE, TEAM_SIZE, HEAD, stretch)
-    grads = exchange(jnp.repeat(head_grads, parts, axis=0).reshape(-1, HEAD, stretch), SEQ)
     count = grads.shape[0] // parts
     grads = lax.dynamic_slice_in_dim(grads, context["part"] * count, count, 0)
     rows_grad = attention_back(rows, context["spans"], grads, wide, logs, after)
@@ -1435,7 +1443,7 @@
             layer > 0,
             mine["gain_one"],
             mine["qkv"],
-            [mine["out"]] if layer > 0 else [],
+            (),
             context,
         )
         if layer == 0:
@@ -1447,9 +1455,14 @@
             for low, size in zip(edges, (D, joint_width, D))
         ]
         after = grad_rows[1:] if layer == last else []
-        back, attended = attention_forward(to_heads(pieces, context), after, context, stretch)
+        if layer > 0:
+            after = [*after, mine["out"], feeds[0]["other"]]
+        at_heads = to_heads(pieces, context)
         if layer == 0:
-            mine["out"] = dp_rows(later(columns[0], attended[1]))
+            mine["out"] = dp_rows(later(columns[0], at_heads[min(2, len(at_heads) - 1)]))
+        back, attended = attention_forward(at_heads, after, context, stretch)
+        if layer > 0:
+            mine["joint"] = dp_rows(later(columns[1], attended[1]))
         if layer == 0 and LAYERS > 1:
             more_rows = z_gather(later(more_rows, attended[1]))
         middle, normed_ffn, gates, outgoing, mixed = feed_step(
@@ -1459,15 +1472,29 @@
             mine["gain_two"],
             mine["router"],
             cotangent if layer == last else None,
-            [feeds[0]["other"]] if layer > 0 else [],
+            [mine["joint"]] if layer > 0 else [],
             context,
         )
-        mine["joint"] = dp_rows(later(columns[1], attended[1] if layer > 0 else normed_ffn))
-        down_padded = dp_rows(later(columns[2], attended[1] if layer > 0 else normed_ffn))
+        if layer == 0:
+            mine["joint"] = dp_rows(later(columns[1], normed_ffn))
+        down_padded = dp_rows(later(columns[2], normed_ffn))
         mine["down"] = down_rows(down_padded)
         arrived = send_rows(outgoing, split_count)
         other = swap(arrived)
         ffn_rows = from_team(normed_ffn)
+        def branch(after):
+            return shared_step(
+                ffn_rows,
+                grad_rows if layer == last else None,
+                mine["joint"],
+                mine["down"],
+                True,
+                after,
+                context,
+            )
+
+        if layer == last:
+            shared = branch([])
         returned = run_expert(
             layer,
             joint,
@@ -1475,17 +1502,10 @@
             (arrived, 0),
             (arrived, 1) if layer == last else None,
             True,
-            [*ffn_rows[1:], mine["joint"], *([down_padded] if layer > 0 else [])],
+            [shared[0]] if layer == last else [*ffn_rows[1:], mine["joint"]],
         )
-        shared = shared_step(
-            ffn_rows,
-            grad_rows if layer == last else None,
-            mine["joint"],
-            mine["down"],
-            True,
-            [returned],
-            context,
-        )
+        if layer < last:
+            shared = branch([returned])
         if layer == 0:
             for i in range(1, LAYERS):
                 columns = more_rows[:, (i - 1) * qkv_width : i * qkv_width]
@@ -1522,13 +1542,13 @@
         arrived, other = feed["arrived"], feed["other"]
         if layer == last:
             grads, other_grads = (arrived, 1), (other, 1)
-            shared_parts = shared_grads(shared, context)
+            shared_parts = shared_grads(shared, [parts[2]], context)
             output, middle_grad, attn_grad, head_grads, small = feed_back_step(
                 returned,
                 feed,
                 upstream,
-                to_team(shared[4:8]),
                 parts,
+                [],
                 mine,
                 True,
                 [shared_parts[1], shared_parts[3]],
@@ -1538,7 +1558,16 @@
             arrived_grad = send_rows(outgoing_grads, split_count)
             grads, other_grads = (arrived_grad, 0), (swap(arrived_grad), 0)
             grad_rows = from_team(upstream_rows)
-            waiting = [(own, swap(rows)) for own, rows in waiting[:2]]
+            waiting = [(own, swap(rows)) for own, rows in waiting]
+            shared = shared_step(
+                feed["ffn_rows"],
+                grad_rows,
+                mine["joint"],
+                mine["down"],
+                False,
+                [],
+                context,
+            )
             returned = run_expert(
                 layer,
                 joint,
@@ -1546,44 +1575,43 @@
                 (arrived, 0),
                 (arrived_grad, 0),
                 False,
-                [*grad_rows[1:], *[rows for _, rows in waiting], terms[1]],
+                [shared[0], *[rows for _, rows in waiting]],
             )
-            shared = shared_step(
-                feed["ffn_rows"],
-                grad_rows,
-                mine["joint"],
-                mine["down"],
-                False,
-                [returned],
-                context,
+            terms = expert_grads(
+                *rest_of_terms, terms, [returned, other_grads[0]], context
             )
-            waiting = [(own, later(rows, shared[0])) for own, rows in waiting]
-            waiting_sum = z_sum(beside([*waiting, waited]))
             returned = return_rows(returned, split_count)
-            shared_parts = shared_grads(shared, context)
+            parts = to_team(shared[:4])
+            shared_parts = shared_grads(shared, [parts[2]], context)
+            waiting = [(own, later(rows, parts[1])) for own, rows in waiting]
+            waiting_sum = z_sum(beside([*waiting, *waited]))
             middle_grad, attn_grad, head_grads, small = feed_back_step(
                 returned,
                 feed,
                 upstream,
-                to_team(shared[:4]),
+                parts,
                 [feed["gap"]],
                 mine,
                 False,
-                [shared_parts[1], shared_parts[3]],
+                [shared_parts[1], shared_parts[3], terms[1]],
                 context,
             )
         out_own, out_other = out_grads_step(feed["mixed"], attn_grad, context)
         joint_arrived, down_arrived = swap(shared_parts[1]), swap(shared_parts[3])
         out_arrived = swap(out_other)
-        joint_sum = z_sum(beside([(shared_parts[0], later(joint_arrived, head_grads))]))
+        at_heads = grads_to_heads(head_grads, context)
+        halves = [(shared_parts[0], later(joint_arrived, at_heads))]
+        if layer == 0:
+            halves.append((shared_parts[2], down_arrived))
+        shared_sum = z_sum(beside(halves))
         pieces, token = attention_backward(
-            head_grads,
+            at_heads,
             feed["attended"],
-            [out_other, other_grads[0]] + ([waiting_sum] if layer < last else []),
+            [],
             context,
         )
         held = ((arrived, 0), grads), ((other, 0), other_grads)
-        terms = expert_grads(layer, 0, *held, joint, down, terms, token, context)
+        terms = expert_grads(layer, 0, *held, joint, down, terms, [token], context)
         results = qkv_back_step(
             pieces,
             mine["qkv"],
@@ -1591,42 +1619,41 @@
             mine["gain_one"],
             small,
             layer > 0,
-            [down_arrived, terms[1], joint_sum] + ([] if layer > 0 else [out_arrived]),
+            [shared_sum, out_arrived, terms[1]] + ([down_arrived] if layer > 0 else [waiting_sum]),
             context,
         )
         normed_parts, packed = to_team(results[:4]), results[4:]
         if layer > 0:
-            waiting = [packed, (out_own, out_other)]
-            waited = (shared_parts[2], down_arrived)
+            waiting = [packed]
+            waited = [(out_own, out_arrived), (shared_parts[2], down_arrived)]
             upstream, upstream_rows, outgoing_grads = layer_start_step(
                 feed["stream"], middle_grad, mine["gain_one"], normed_parts, feeds[layer - 1], context
             )
-            terms = expert_grads(layer, 1, *held, joint, down, terms, outgoing_grads, context)
+            rest_of_terms = (layer, 1, *held, joint, down)
         else:
             (upstream_rows,) = layer_start_step(
                 feed["stream"], middle_grad, mine["gain_one"], normed_parts, None, context
             )
             total = lax.axis_size(ALL)
             first_sum = exchange(packed[0].reshape(total, D // total, -1), ALL)
-            tail_sum = z_sum(
-                beside(
-                    [
-                        (out_own, later(out_arrived, packed[0])),
-                        (shared_parts[2], down_arrived),
-                    ]
-                )
-            )
-            terms = expert_grads(layer, 1, *held, joint, down, terms, packed[0], context)
-        feed_parts[layer] = [
-            team_pieces(joint_sum, member),
-            team_pieces(tail_sum[:, :D], member) if layer == 0 else None,
-            tail_sum[:unit, D:] if layer == 0 else None,
-        ]
+            out_sum = z_sum(beside([(out_own, later(out_arrived, packed[0]))]))
         if layer < last:
             edge = waiting_sum.shape[1] - 2 * D
             head_parts[layer + 1] = team_pieces(waiting_sum[:, :edge], member)
             feed_parts[layer + 1][1] = team_pieces(waiting_sum[:, edge : edge + D], member)
             feed_parts[layer + 1][2] = waiting_sum[:unit, edge + D :]
+        feed_parts[layer] = [
+            team_pieces(shared_sum[:, :joint_width], member),
+            None,
+            shared_sum[:unit, joint_width:] if layer == 0 else None,
+        ]
+        if layer == 0:
+            early = [packed[0], *feed_parts[0][0][1:]]
+            for later_layer in range(1, LAYERS):
+                early += head_parts[later_layer][1:]
+                early += feed_parts[later_layer][0][1:] + feed_parts[later_layer][1][1:]
+            terms = expert_grads(layer, 1, *held, joint, down, terms, early, context)
+            feed_parts[0][1] = team_pieces(later(out_sum, terms[1]), member)
     joint_sum, out_sum, down_sum = run_kernel(
         feed_end_kernel,
         [

time: 727 us -> 681 us (0.937)
  waiting for transfers between devices: 225 us -> 192 us
  starting transfers between devices: 180 us -> 162 us
    ppermute x10, waiting for transfers between devices: 19.4 us -> 4.17 us  [swap(): return lax.ppermute(rows, 'dp', SWAP)]
    ppermute x12, starting transfers between devices: 40.1 us -> 28.5 us  [z_turn(): arrived.append(lax.ppermute(pieces[turn], ('z', 'core'), pairs))]
    ppermute x8, waiting for transfers between devices: 59.7 us -> 49.4 us  [dp_rows(): other = lax.ppermute(rows, 'dp', SWAP)]
    all_to_all x13, waiting for transfers between devices: 58.6 us -> 48.5 us  [exchange(): return lax.all_to_all(rows, axes, split_axis=0, concat_axis=0, tiled=True)]
    unnamed x238 -> x216, local copies, waits for them, and re-layouts: 20 us -> 25.4 us
    ppermute x19 -> x18, starting transfers between devices: 16.2 us -> 11.1 us  [from_member(): return lax.ppermute(rows, TEAM, [(i, 3 - i) for i in range(4)])]
    ppermute x19 -> x18, starting transfers between devices: 21.4 us -> 24.4 us  [from_member(): return lax.ppermute(rows, 'ulysses', SWAP)]
    ppermute x19 -> x18, waiting for transfers between devices: 21.9 us -> 23.2 us  [from_member(): return lax.ppermute(rows, TEAM, [(i, 3 - i) for i in range(4)])]
  transfers between devices with their start and end apart: 106 -> 103, of which waited for: 36 -> 35; matrix products, arithmetic and copies ran while one was open for 9% -> 9% of each run, Pallas kernels for 22% -> 25%
where the time goes in v4:
time: 681 us; the launch traced here: 670 us
  Pallas kernels  208 us (31%)
  waiting for transfers between devices  192 us (28%)
  starting transfers between devices  162 us (24%)
  local copies, waits for them, and re-layouts  57.8 us (8%)
  other arithmetic  33.7 us (5%)
  between operations  15.8 us (2%)
    pallas_call x20, Pallas kernels, run_kernel(): pl.pallas_call(lambda *refs: kernel(*refs[:given], *refs[kept:]), grid=(1...  77.1 us
    all_to_all x13, starting transfers between devices, exchange(): return lax.all_to_all(rows, axes, split_axis=0, concat_axis=0, tiled=True)  76.6 us
    pallas_call x4, Pallas kernels, expert_grads(): pl.pallas_call(expert_grad_kernel, grid=(steps, 2), in_specs=in_specs, ou...  60.9 us
    ppermute x8, waiting for transfers between devices, dp_rows(): other = lax.ppermute(rows, 'dp', SWAP)  49.4 us
    all_to_all x13, waiting for transfers between devices, exchange(): return lax.all_to_all(rows, axes, split_axis=0, concat_axis=0, tiled=True)  48.5 us
    ppermute x18, waiting for transfers between devices, from_member(): return lax.ppermute(rows, 'ulysses', SWAP)  36.9 us
    pallas_call x3, Pallas kernels, run_expert(): pl.pallas_call(lambda *refs: body(*refs[:drop], *refs[drop + len(after):]...  34.2 us
    ppermute x12, waiting for transfers between devices, z_turn(): arrived.append(lax.ppermute(pieces[turn], ('z', 'core'), pairs))  29.2 us
  transfers between devices with their start and end apart: 103, of which 35 were waited for; matrix products, arithmetic and copies ran while one was open for 9% of the time, Pallas kernels for 25%

profile of v4, /device:TPU:0, one launch (start us, length us, event | category | flops | bytes accessed | tf_op | source)
XLA Modules:
  0.0 669.7 jit_solution(16414601503892489104)
XLA Ops:
  33.0 12.2 %all-to-all-done = bf16[4,96,612]{2,1,0:T(8,128)(2,1)S(1)} async-done(((bf16[4,96,612]{2,1,0:T(8,128)(2,1)}), bf16[4,96,612]{2,1,0:T(8,128)(2,1)S(1)}, u32[]{:S(2)}, u32[]{:S(2)}) %all-to-all-start) | async-done | bytes 470048 | tf_op jit(solution)/shard_map/all_to_all | solution.py:52
  53.4 12.0 %collective-permute-done.6 = bf16[384,612]{0,1:T(8,128)(2,1)S(1)} collective-permute-done((bf16[384,612]{0,1:T(8,128)(2,1)S(1)}, bf16[384,612]{0,1:T(8,128)(2,1)S(1)}, u32[]{:S(2)}, u32[]{:S(2)}) %collective-permute-start.6) | collective-permute-done | bytes 470048 | tf_op jit(solution)/shard_map/ppermute | solution.py:1315
  78.5 9.3 %collective-permute-done.7.refs_1_ = bf16[192,512]{1,0:T(8,128)(2,1)S(1)} collective-permute-done((bf16[192,512]{1,0:T(8,128)(2,1)}, bf16[192,512]{1,0:T(8,128)(2,1)S(1)}, u32[]{:S(2)}, u32[]{:S(2)}) %collective-permute-start.7) | collective-permute-done | bytes 196640 | tf_op jit(solution)/shard_map/ppermute | solution.py:1207
  87.8 10.4 %collective-permute-done.8.refs_2_.refs_1_ = bf16[192,512]{1,0:T(8,128)(2,1)S(1)} collective-permute-done((bf16[192,512]{1,0:T(8,128)(2,1)}, bf16[192,512]{1,0:T(8,128)(2,1)S(1)}, u32[]{:S(2)}, u32[]{:S(2)}) %collective-permute-start.8) | collective-permute-done | bytes 196640 | tf_op jit(solution)/shard_map/ppermute | solution.py:1207
  99.0 7.8 %attend.2 = (bf16[4,192,512]{2,1,0:T(8,128)(2,1)}, bf16[16,64,128]{2,1,0:T(8,128)(2,1)}, f32[64,2048]{1,0:T(8,128)}, f32[1,2048]{1,0:T(1,128)}) custom-call(s32[4]{0:T(128)} %pad_add_fusion.refs_0_.place_ref, bf16[192,512]{1,0:T(8,128)(2,1)} %get-tuple-element.118.refs_0_, bf16[192,512]{1,0:T(8,128)(2,1)} %copy-done.101, bf16[192,512]{1,0:T(8,128)(2,1)} %copy-done.76, ...), custom_call_target="tpu_custom_call" | custom-call | flops 16777216 | bytes 1572864 | tf_op jit(solution)/shard_map/attend/pallas_call | solution.py:295
  125.3 8.2 %all-to-all-done.1.refs_1_ = bf16[16,64,128]{2,1,0:T(8,128)(2,1)S(1)} async-done(((bf16[16,64,128]{2,1,0:T(8,128)(2,1)}), bf16[16,64,128]{2,1,0:T(8,128)(2,1)S(1)}, u32[]{:S(2)}, u32[]{:S(2)}) %all-to-all-start.1) | async-done | bytes 262176 | tf_op jit(solution)/shard_map/all_to_all | solution.py:52
  137.5 6.4 all-to-all-start.3
  147.6 10.6 %collective-permute-done.14 = bf16[384,1024]{1,0:T(8,128)(2,1)} collective-permute-done((bf16[384,1024]{1,0:T(8,128)(2,1)}, bf16[384,1024]{1,0:T(8,128)(2,1)}, u32[]{:S(2)}, u32[]{:S(2)}) %collective-permute-start.14) | collective-permute-done | bytes 786464 | tf_op jit(solution)/shard_map/ppermute | solution.py:1315
  160.7 7.8 %all-to-all-done.3 = bf16[16,24,768]{2,1,0:T(8,128)(2,1)S(1)} async-done(((bf16[16,24,768]{2,1,0:T(8,128)(2,1)}), bf16[16,24,768]{2,1,0:T(8,128)(2,1)S(1)}, u32[]{:S(2)}, u32[]{:S(2)}) %all-to-all-start.3) | async-done | bytes 589856 | tf_op jit(solution)/shard_map/all_to_all | solution.py:52
  169.4 8.5 %expert_forward.1.refs_7_.refs_1_ = bf16[384,768]{1,0:T(8,128)(2,1)} custom-call(bf16[384,768]{1,0:T(8,128)(2,1)} %bitcast.190, bf16[2,1,768,4096]{3,2,1,0:T(8,128)(2,1)} %up_ref.7, bf16[2,1,768,4096]{3,2,1,0:T(8,128)(2,1)} %up_ref.7, bf16[2,1,2048,768]{3,2,1,0:T(8,128)(2,1)} %down_ref.7, bf16[128,768]{1,0:T(8,128)(2,1)} %copy-done.35, ...), custom_call_target="tpu_custom_call" | custom-call | flops 3623878656 | bytes 10616832 | tf_op jit(solution)/shard_map/expert_forward/pallas_call | solution.py:994
  177.9 8.9 %all-to-all-start.4 = ((bf16[16,24,768]{2,1,0:T(8,128)(2,1)}), bf16[16,24,768]{2,1,0:T(8,128)(2,1)S(1)}, u32[]{:S(2)}, u32[]{:S(2)}) async-start(bf16[16,24,768]{2,1,0:T(8,128)(2,1)} %bitcast.199), calls=%async_computation.4 | async-start | bytes 1179648 | tf_op jit(solution)/shard_map/all_to_all | solution.py:52
  243.0 7.5 %collective-permute-done.27.refs_2_ = bf16[192,512]{1,0:T(8,128)(2,1)} collective-permute-done((bf16[192,512]{1,0:T(8,128)(2,1)}, bf16[192,512]{1,0:T(8,128)(2,1)}, u32[]{:S(2)}, u32[]{:S(2)}) %collective-permute-start.27) | collective-permute-done | bytes 196640 | tf_op jit(solution)/shard_map/ppermute | solution.py:1207
  250.5 7.8 %attend.3 = (bf16[4,192,512]{2,1,0:T(8,128)(2,1)}, bf16[16,64,128]{2,1,0:T(8,128)(2,1)}, f32[64,2048]{1,0:T(8,128)}, f32[1,2048]{1,0:T(1,128)}) custom-call(s32[4]{0:T(128)} %pad_add_fusion.refs_0_.place_ref, bf16[192,512]{1,0:T(8,128)(2,1)} %get-tuple-element.133.refs_0_, bf16[192,512]{1,0:T(8,128)(2,1)} %collective-permute-done.26.refs_1_, ...), custom_call_target="tpu_custom_call" | custom-call | flops 16777216 | bytes 1572864 | tf_op jit(solution)/shard_map/attend/pallas_call | solution.py:295
  264.7 10.3 %collective-permute-done.34 = bf16[384,1024]{1,0:T(8,128)(2,1)S(1)} collective-permute-done((bf16[384,1024]{1,0:T(8,128)(2,1)}, bf16[384,1024]{1,0:T(8,128)(2,1)S(1)}, u32[]{:S(2)}, u32[]{:S(2)}) %collective-permute-start.34) | collective-permute-done | bytes 786464 | tf_op jit(solution)/shard_map/ppermute | solution.py:1315
  290.1 12.9 %collective-permute-done.38 = bf16[384,768]{1,0:T(8,128)(2,1)S(1)} collective-permute-done((bf16[384,768]{1,0:T(8,128)(2,1)}, bf16[384,768]{1,0:T(8,128)(2,1)S(1)}, u32[]{:S(2)}, u32[]{:S(2)}) %collective-permute-start.38) | collective-permute-done | bytes 589856 | tf_op jit(solution)/shard_map/ppermute | solution.py:1315
  308.2 6.6 shared.4
  315.9 13.8 %expert_both.1 = bf16[384,1536]{1,0:T(8,128)(2,1)} custom-call(bf16[384,1536]{1,0:T(8,128)(2,1)} %bitcast.183, bf16[384,1536]{1,0:T(8,128)(2,1)} %bitcast.184, bf16[2,1,768,4096]{3,2,1,0:T(8,128)(2,1)} %up_ref.7, bf16[2,1,768,4096]{3,2,1,0:T(8,128)(2,1)} %up_ref.7, bf16[2,1,2048,768]{3,2,1,0:T(8,128)(2,1)} %down_ref.7, ...), custom_call_target="tpu_custom_call" | custom-call | flops 7247757312 | bytes 11796480 | tf_op jit(solution)/shard_map/expert_both/pallas_call | solution.py:994
  342.7 13.3 %collective-permute-done.39.refs_12_ = bf16[128,1536]{1,0:T(8,128)(2,1)S(1)} collective-permute-done((bf16[128,1536]{1,0:T(8,128)(2,1)}, bf16[128,1536]{1,0:T(8,128)(2,1)S(1)}, u32[]{:S(2)}, u32[]{:S(2)}) %collective-permute-start.39) | collective-permute-done | bytes 393248 | tf_op jit(solution)/shard_map/ppermute | solution.py:60
  356.0 10.6 %collective-permute-done.41.refs_14_ = bf16[128,1536]{1,0:T(8,128)(2,1)S(1)} collective-permute-done((bf16[128,1536]{1,0:T(8,128)(2,1)S(1)}, bf16[128,1536]{1,0:T(8,128)(2,1)S(1)}, u32[]{:S(2)}, u32[]{:S(2)}) %collective-permute-start.41) | collective-permute-done | bytes 393248 | tf_op jit(solution)/shard_map/ppermute | solution.py:63
  379.1 8.5 %all-to-all-done.8.grad_ref.refs_1_ = bf16[16,64,128]{2,1,0:T(8,128)(2,1)S(1)} async-done(((bf16[16,64,128]{2,1,0:T(8,128)(2,1)}), bf16[16,64,128]{2,1,0:T(8,128)(2,1)S(1)}, u32[]{:S(2)}, u32[]{:S(2)}) %all-to-all-start.8) | async-done | bytes 262176 | tf_op jit(solution)/shard_map/all_to_all | solution.py:52
  395.4 10.2 %attend_back.2 = (bf16[192,512]{1,0:T(8,128)(2,1)}, bf16[192,512]{1,0:T(8,128)(2,1)}, bf16[192,512]{1,0:T(8,128)(2,1)}, bf16[192,512]{1,0:T(8,128)(2,1)}) custom-call(s32[4]{0:T(128)} %pad_add_fusion.refs_0_.place_ref, bf16[4,192,512]{2,1,0:T(8,128)(2,1)} %get-tuple-element.156.rows_ref, s32[1,2048]{1,0:T(1,128)} %bitcast.244, ...), custom_call_target="tpu_custom_call" | custom-call | flops 50331648 | bytes 1572864 | tf_op jit(solution)/shard_map/attend_back/pallas_call | solution.py:322
  414.0 15.2 %expert_grads.4 = (f32[2,1,768,4096]{3,2,1,0:T(8,128)}, f32[2,1,2048,768]{3,2,1,0:T(8,128)}) custom-call(s32[4]{0:T(128)} %pad_add_fusion.refs_0_.place_ref, bf16[384,1536]{1,0:T(8,128)(2,1)} %bitcast.185, bf16[384,1536]{1,0:T(8,128)(2,1)} %bitcast.186, bf16[384,1536]{1,0:T(8,128)(2,1)} %copy-done.2, bf16[384,1536]{1,0:T(8,128)(2,1)} %copy-done.2, ...), custom_call_target="tpu_custom_call" | custom-call | flops 7247757312 | bytes 14155776 | tf_op jit(solution)/shard_map/expert_grads/pallas_call | solution.py:1072
  450.6 6.0 all-to-all-start.9
  462.2 7.6 %collective-permute-done.52.refs_6_ = bf16[128,768]{1,0:T(8,128)(2,1)S(1)} collective-permute-done((bf16[128,768]{1,0:T(8,128)(2,1)S(1)}, bf16[128,768]{1,0:T(8,128)(2,1)S(1)}, u32[]{:S(2)}, u32[]{:S(2)}) %collective-permute-start.52) | collective-permute-done | bytes 196640 | tf_op jit(solution)/shard_map/ppermute | solution.py:60
  482.6 11.8 %expert_back.1.refs_2_ = bf16[384,768]{1,0:T(8,128)(2,1)} custom-call(bf16[384,768]{1,0:T(8,128)(2,1)} %bitcast.191, bf16[384,768]{1,0:T(8,128)(2,1)} %bitcast.195, bf16[2,1,768,4096]{3,2,1,0:T(8,128)(2,1)} %up_ref.7, bf16[2,1,768,4096]{3,2,1,0:T(8,128)(2,1)} %up_ref.7, bf16[2,1,2048,768]{3,2,1,0:T(8,128)(2,1)} %down_ref.7, ...), custom_call_target="tpu_custom_call" | custom-call | flops 6039797760 | bytes 10616832 | tf_op jit(solution)/shard_map/expert_back/pallas_call | solution.py:994
  515.2 15.2 %expert_grads.5 = (f32[2,1,768,4096]{3,2,1,0:T(8,128)}, f32[2,1,2048,768]{3,2,1,0:T(8,128)}) custom-call(s32[4]{0:T(128)} %pad_add_fusion.refs_0_.place_ref, bf16[384,1536]{1,0:T(8,128)(2,1)} %bitcast.187, bf16[384,1536]{1,0:T(8,128)(2,1)} %bitcast.188, bf16[384,1536]{1,0:T(8,128)(2,1)} %copy-done.2, ...), custom_call_target="tpu_custom_call", output_to_operand_aliasing={{0}: (8, {}), {1}: (9, {})} | custom-call | flops 7247757312 | bytes 14155776 | tf_op jit(solution)/shard_map/expert_grads/pallas_call | solution.py:1072
  535.7 10.7 %all-to-all-start.11 = ((bf16[16,64,128]{2,1,0:T(8,128)(2,1)}), bf16[16,64,128]{2,1,0:T(8,128)(2,1)S(1)}, u32[]{:S(2)}, u32[]{:S(2)}) async-start(bf16[16,64,128]{2,1,0:T(8,128)(2,1)} %get-tuple-element.193), calls=%async_computation.12 | async-start | bytes 524288 | tf_op jit(solution)/shard_map/all_to_all | solution.py:52
  547.9 8.4 %all-to-all-done.11.grad_ref.refs_1_ = bf16[16,64,128]{2,1,0:T(8,128)(2,1)S(1)} async-done(((bf16[16,64,128]{2,1,0:T(8,128)(2,1)}), bf16[16,64,128]{2,1,0:T(8,128)(2,1)S(1)}, u32[]{:S(2)}, u32[]{:S(2)}) %all-to-all-start.11) | async-done | bytes 262176 | tf_op jit(solution)/shard_map/all_to_all | solution.py:52
  562.4 10.3 %attend_back.3 = (bf16[192,512]{1,0:T(8,128)(2,1)}, bf16[192,512]{1,0:T(8,128)(2,1)}, bf16[192,512]{1,0:T(8,128)(2,1)}, bf16[192,512]{1,0:T(8,128)(2,1)}) custom-call(s32[4]{0:T(128)} %pad_add_fusion.refs_0_.place_ref, bf16[4,192,512]{2,1,0:T(8,128)(2,1)} %get-tuple-element.192.rows_ref, s32[1,2048]{1,0:T(1,128)} %bitcast.245, ...), custom_call_target="tpu_custom_call" | custom-call | flops 50331648 | bytes 1572864 | tf_op jit(solution)/shard_map/attend_back/pallas_call | solution.py:322
  580.9 15.3 %expert_grads.6 = (f32[2,1,768,4096]{3,2,1,0:T(8,128)}, f32[2,1,2048,768]{3,2,1,0:T(8,128)}) custom-call(s32[4]{0:T(128)} %pad_add_fusion.refs_0_.place_ref, bf16[384,768]{1,0:T(8,128)(2,1)} %bitcast.192, bf16[384,768]{1,0:T(8,128)(2,1)} %bitcast.196, bf16[384,768]{1,0:T(8,128)(2,1)} %copy-done.22, ...), custom_call_target="tpu_custom_call", output_to_operand_aliasing={{0}: (8, {}), {1}: (9, {})} | custom-call | flops 7247757312 | bytes 14155776 | tf_op jit(solution)/shard_map/expert_grads/pallas_call | solution.py:1072
  603.3 6.7 %all-to-all-start.12 = ((bf16[32,24,640]{2,1,0:T(8,128)(2,1)}), bf16[32,24,640]{2,1,0:T(8,128)(2,1)S(1)}, u32[]{:S(2)}, u32[]{:S(2)}) async-start(bf16[32,24,640]{2,1,0:T(8,128)(2,1)} %bitcast.200), calls=%async_computation.15 | async-start | bytes 1966080 | tf_op jit(solution)/shard_map/all_to_all | solution.py:52
  629.9 15.2 %expert_grads.7 = (f32[2,1,768,4096]{3,2,1,0:T(8,128)}, f32[2,1,2048,768]{3,2,1,0:T(8,128)}) custom-call(s32[4]{0:T(128)} %pad_add_fusion.refs_0_.place_ref, bf16[384,768]{1,0:T(8,128)(2,1)} %bitcast.193, bf16[384,768]{1,0:T(8,128)(2,1)} %bitcast.197, bf16[384,768]{1,0:T(8,128)(2,1)} %copy-done.22, ...), custom_call_target="tpu_custom_call", output_to_operand_aliasing={{0}: (8, {}), {1}: (9, {})} | custom-call | flops 7247757312 | bytes 14155776 | tf_op jit(solution)/shard_map/expert_grads/pallas_call | solution.py:1072
  (547 shorter events, 327.6 us)
Async XLA Ops:
  7.2 60.3 %collective-permute-start = (bf16[128,768]{1,0:T(8,128)(2,1)}, bf16[128,768]{1,0:T(8,128)(2,1)S(1)}, u32[]{:S(2)}, u32[]{:S(2)}) collective-permute-start(bf16[128,768]{1,0:T(8,128)(2,1)} %bitcast.216), channel_id=1, source_target_pairs={{0,1},{1,0},{2,3},{3,2},{4,5},{5,4},{6,7},{7,6},{8,9},{9,8},{10,11... | collective-permute-start | bytes 589832 | tf_op jit(solution)/shard_map/ppermute | solution.py:60
  10.3 57.3 %collective-permute-start.1 = (bf16[128,768]{1,0:T(8,128)(2,1)}, bf16[128,768]{1,0:T(8,128)(2,1)}, u32[]{:S(2)}, u32[]{:S(2)}) collective-permute-start(bf16[128,768]{1,0:T(8,128)(2,1)} %bitcast.217), channel_id=1, source_target_pairs={{0,2},{2,0},{1,3},{3,1},{4,6},{6,4},{5,7},{7,5},{8,10},{10,8},{9,1... | collective-permute-start | bytes 589832 | tf_op jit(solution)/shard_map/ppermute | solution.py:62
  20.8 30.9 %collective-permute-start.19 = (bf16[24,2368]{1,0:T(8,128)(2,1)S(1)}, bf16[24,2368]{1,0:T(8,128)(2,1)S(1)}, u32[]{:S(2)}, u32[]{:S(2)}) collective-permute-start(bf16[24,2368]{1,0:T(8,128)(2,1)S(1)} %get-tuple-element.290), channel_id=1, source_target_pairs={{0,2},{2,0},{1,3},{3,1},{4,6},{6,4},{5,7},{7,5},{8,10},{10,8},{9,1... | collective-permute-start | bytes 341000 | tf_op jit(solution)/shard_map/ppermute | solution.py:62
  21.5 30.2 %collective-permute-start.20 = (bf16[24,2368]{1,0:T(8,128)(2,1)S(1)}, bf16[24,2368]{1,0:T(8,128)(2,1)S(1)}, u32[]{:S(2)}, u32[]{:S(2)}) collective-permute-start(bf16[24,2368]{1,0:T(8,128)(2,1)S(1)} %get-tuple-element.289), channel_id=1, source_target_pairs={{0,1},{1,0},{2,3},{3,2},{4,5},{5,4},{6,7},{7,6},{8,9},{9,8},{10,11... | collective-permute-start | bytes 341000 | tf_op jit(solution)/shard_map/ppermute | solution.py:60
  23.0 30.3 %collective-permute-start.21 = (bf16[24,2368]{1,0:T(8,128)(2,1)S(1)}, bf16[24,2368]{1,0:T(8,128)(2,1)S(1)}, u32[]{:S(2)}, u32[]{:S(2)}) collective-permute-start(bf16[24,2368]{1,0:T(8,128)(2,1)S(1)} %get-tuple-element.288), channel_id=1, source_target_pairs={{0,3},{1,2},{2,1},{3,0},{4,7},{5,6},{6,5},{7,4},{8,11},{9,10},{10,... | collective-permute-start | bytes 341000 | tf_op jit(solution)/shard_map/ppermute | solution.py:63
  32.1 75.6 %all-gather.3.cloned.1.call-start = ((), (), s32[]{:S(2)}) async-start(), calls=%async_computation.17 | async-start | bytes 2457600 | tf_op jit(solution)/shard_map/all_gather | solution.py:1373
  46.0 142.0 %all-gather.5.cloned.1.call-start = ((), (), s32[]{:S(2)}) async-start(), calls=%async_computation.18 | async-start | bytes 3072000 | tf_op jit(solution)/shard_map/all_gather | solution.py:1373
  73.8 24.4 %collective-permute-start.8 = (bf16[192,512]{1,0:T(8,128)(2,1)}, bf16[192,512]{1,0:T(8,128)(2,1)S(1)}, u32[]{:S(2)}, u32[]{:S(2)}) collective-permute-start(bf16[192,512]{1,0:T(8,128)(2,1)} %get-tuple-element.120), channel_id=1, source_target_pairs={{0,8},{2,10},{6,14},{8,0},{12,4},{14,6},{1,9},{3,11},{7,15},{9,1},... | collective-permute-start | bytes 589832 | tf_op jit(solution)/shard_map/ppermute | solution.py:1207
  137.5 31.0 %all-to-all-start.3 = ((bf16[16,24,768]{2,1,0:T(8,128)(2,1)}), bf16[16,24,768]{2,1,0:T(8,128)(2,1)S(1)}, u32[]{:S(2)}, u32[]{:S(2)}) async-start(bf16[16,24,768]{2,1,0:T(8,128)(2,1)} %bitcast.29), calls=%async_computation.3 | async-start | bytes 1179648 | tf_op jit(solution)/shard_map/all_to_all | solution.py:52
  146.7 40.1 %collective-permute-start.15 = (bf16[384,768]{1,0:T(8,128)(2,1)}, bf16[384,768]{1,0:T(8,128)(2,1)}, u32[]{:S(2)}, u32[]{:S(2)}) collective-permute-start(bf16[384,768]{1,0:T(8,128)(2,1)} %later.17), channel_id=1, source_target_pairs={{0,16},{16,0},{1,17},{17,1},{2,18},{18,2},{3,19},{19,3},{4,20},{20... | collective-permute-start | bytes 1769480 | tf_op jit(solution)/shard_map/ppermute | solution.py:1315
  177.9 33.0 %all-to-all-start.4 = ((bf16[16,24,768]{2,1,0:T(8,128)(2,1)}), bf16[16,24,768]{2,1,0:T(8,128)(2,1)S(1)}, u32[]{:S(2)}, u32[]{:S(2)}) async-start(bf16[16,24,768]{2,1,0:T(8,128)(2,1)} %bitcast.199), calls=%async_computation.4 | async-start | bytes 1179648 | tf_op jit(solution)/shard_map/all_to_all | solution.py:52
  281.4 33.4 %all-to-all-start.6 = ((bf16[16,24,1536]{2,1,0:T(8,128)(2,1)}), bf16[16,24,1536]{2,1,0:T(8,128)(2,1)S(1)}, u32[]{:S(2)}, u32[]{:S(2)}) async-start(bf16[16,24,1536]{2,1,0:T(8,128)(2,1)} %bitcast.229), calls=%async_computation.6 | async-start | bytes 2359296 | tf_op jit(solution)/shard_map/all_to_all | solution.py:52
  329.7 36.9 %all-to-all-start.7 = ((bf16[16,24,1536]{2,1,0:T(8,128)(2,1)}), bf16[16,24,1536]{2,1,0:T(8,128)(2,1)S(1)}, u32[]{:S(2)}, u32[]{:S(2)}) async-start(bf16[16,24,1536]{2,1,0:T(8,128)(2,1)} %bitcast.201), calls=%async_computation.7 | async-start | bytes 2359296 | tf_op jit(solution)/shard_map/all_to_all | solution.py:52
  336.6 30.0 %collective-permute-start.41 = (bf16[128,1536]{1,0:T(8,128)(2,1)S(1)}, bf16[128,1536]{1,0:T(8,128)(2,1)S(1)}, u32[]{:S(2)}, u32[]{:S(2)}) collective-permute-start(bf16[128,1536]{1,0:T(8,128)(2,1)S(1)} %copy-done.89), channel_id=1, source_target_pairs={{0,3},{1,2},{2,1},{3,0},{4,7},{5,6},{6,5},{7,4},{8,11},{9,10},{10,... | collective-permute-start | bytes 1179656 | tf_op jit(solution)/shard_map/ppermute | solution.py:63
  341.8 37.3 %collective-permute-start.45 = (bf16[384,1024]{1,0:T(8,128)(2,1)}, bf16[384,1024]{1,0:T(8,128)(2,1)}, u32[]{:S(2)}, u32[]{:S(2)}) collective-permute-start(bf16[384,1024]{1,0:T(8,128)(2,1)} %get-tuple-element.152.refs_15_), channel_id=1, source_target_pairs={{0,16},{16,0},{1,17},{17,1},{2,18},{18,2},{3,19},{19,3},{4,20},{20... | collective-permute-start | bytes 2359304 | tf_op jit(solution)/shard_map/ppermute | solution.py:1273
  377.7 54.2 %reduce-scatter.5.cloned.1.call-start = ((), (), s32[]{:S(2)}) async-start(), calls=%async_computation.19 | async-start | bytes 983040 | tf_op jit(solution)/shard_map/reduce_scatter | solution.py:1283
  378.1 33.7 %collective-permute-start.47 = (bf16[384,1536]{1,0:T(8,128)(2,1)S(1)}, bf16[384,1536]{1,0:T(8,128)(2,1)S(1)}, u32[]{:S(2)}, u32[]{:S(2)}) collective-permute-start(bf16[384,1536]{1,0:T(8,128)(2,1)S(1)} %bitcast.189), channel_id=1, source_target_pairs={{0,16},{16,0},{1,17},{17,1},{2,18},{18,2},{3,19},{19,3},{4,20},{20... | collective-permute-start | bytes 3538952 | tf_op jit(solution)/shard_map/ppermute | solution.py:1273
  390.9 38.3 %collective-permute-start.48 = (bf16[384,768]{1,0:T(8,128)(2,1)}, bf16[384,768]{1,0:T(8,128)(2,1)}, u32[]{:S(2)}, u32[]{:S(2)}) collective-permute-start(bf16[384,768]{1,0:T(8,128)(2,1)} %get-tuple-element.153.refs_16_), channel_id=1, source_target_pairs={{0,16},{16,0},{1,17},{17,1},{2,18},{18,2},{3,19},{19,3},{4,20},{20... | collective-permute-start | bytes 1769480 | tf_op jit(solution)/shard_map/ppermute | solution.py:1273
  394.3 37.5 %collective-permute-start.46 = (bf16[384,768]{1,0:T(8,128)(2,1)}, bf16[384,768]{1,0:T(8,128)(2,1)S(1)}, u32[]{:S(2)}, u32[]{:S(2)}) collective-permute-start(bf16[384,768]{1,0:T(8,128)(2,1)} %get-tuple-element.168), channel_id=1, source_target_pairs={{0,16},{16,0},{1,17},{17,1},{2,18},{18,2},{3,19},{19,3},{4,20},{20... | collective-permute-start | bytes 1769480 | tf_op jit(solution)/shard_map/ppermute | solution.py:1273
  405.6 26.2 %collective-permute-start.42 = (bf16[192,512]{1,0:T(8,128)(2,1)}, bf16[192,512]{1,0:T(8,128)(2,1)}, u32[]{:S(2)}, u32[]{:S(2)}) collective-permute-start(bf16[192,512]{1,0:T(8,128)(2,1)} %get-tuple-element.160), channel_id=1, source_target_pairs={{0,4},{4,8},{6,10},{8,12},{10,14},{14,2},{1,5},{5,9},{7,11},{9,13}... | collective-permute-start | bytes 589832 | tf_op jit(solution)/shard_map/ppermute | solution.py:1207
  450.6 30.9 %all-to-all-start.9 = ((bf16[16,24,768]{2,1,0:T(8,128)(2,1)}), bf16[16,24,768]{2,1,0:T(8,128)(2,1)S(1)}, u32[]{:S(2)}, u32[]{:S(2)}) async-start(bf16[16,24,768]{2,1,0:T(8,128)(2,1)} %bitcast.234), calls=%async_computation.10 | async-start | bytes 1179648 | tf_op jit(solution)/shard_map/all_to_all | solution.py:52
  456.7 141.5 %reduce-scatter.9.cloned.1.call-start = ((), (), s32[]{:S(2)}) async-start(), calls=%async_computation.21 | async-start | bytes 2088960 | tf_op jit(solution)/shard_map/reduce_scatter | solution.py:1283
  457.9 23.7 %collective-permute-start.55 = (bf16[384,640]{1,0:T(8,128)(2,1)}, bf16[384,640]{1,0:T(8,128)(2,1)S(1)}, u32[]{:S(2)}, u32[]{:S(2)}) collective-permute-start(bf16[384,640]{1,0:T(8,128)(2,1)} %get-tuple-element.177), channel_id=1, source_target_pairs={{0,16},{16,0},{1,17},{17,1},{2,18},{18,2},{3,19},{19,3},{4,20},{20... | collective-permute-start | bytes 1474568 | tf_op jit(solution)/shard_map/ppermute | solution.py:1273
  499.8 30.6 %all-to-all-start.10 = ((bf16[16,24,768]{2,1,0:T(8,128)(2,1)}), bf16[16,24,768]{2,1,0:T(8,128)(2,1)S(1)}, u32[]{:S(2)}, u32[]{:S(2)}) async-start(bf16[16,24,768]{2,1,0:T(8,128)(2,1)} %bitcast.59), calls=%async_computation.11 | async-start | bytes 1179648 | tf_op jit(solution)/shard_map/all_to_all | solution.py:52
  504.9 25.6 %collective-permute-start.58 = (bf16[128,768]{1,0:T(8,128)(2,1)}, bf16[128,768]{1,0:T(8,128)(2,1)S(1)}, u32[]{:S(2)}, u32[]{:S(2)}) collective-permute-start(bf16[128,768]{1,0:T(8,128)(2,1)} %get-tuple-element.181), channel_id=1, source_target_pairs={{0,3},{1,2},{2,1},{3,0},{4,7},{5,6},{6,5},{7,4},{8,11},{9,10},{10,... | collective-permute-start | bytes 589832 | tf_op jit(solution)/shard_map/ppermute | solution.py:63
  511.6 36.3 %collective-permute-start.63 = (bf16[384,1024]{1,0:T(8,128)(2,1)}, bf16[384,1024]{1,0:T(8,128)(2,1)S(1)}, u32[]{:S(2)}, u32[]{:S(2)}) collective-permute-start(bf16[384,1024]{1,0:T(8,128)(2,1)} %get-tuple-element.187.refs_16_), channel_id=1, source_target_pairs={{0,16},{16,0},{1,17},{17,1},{2,18},{18,2},{3,19},{19,3},{4,20},{20... | collective-permute-start | bytes 2359304 | tf_op jit(solution)/shard_map/ppermute | solution.py:1273
  512.9 33.5 %collective-permute-start.64 = (bf16[384,768]{1,0:T(8,128)(2,1)}, bf16[384,768]{1,0:T(8,128)(2,1)}, u32[]{:S(2)}, u32[]{:S(2)}) collective-permute-start(bf16[384,768]{1,0:T(8,128)(2,1)} %get-tuple-element.188.refs_17_), channel_id=1, source_target_pairs={{0,16},{16,0},{1,17},{17,1},{2,18},{18,2},{3,19},{19,3},{4,20},{20... | collective-permute-start | bytes 1769480 | tf_op jit(solution)/shard_map/ppermute | solution.py:1273
  546.4 51.8 %reduce-scatter.7.cloned.1.call-start = ((), (), s32[]{:S(2)}) async-start(), calls=%async_computation.20 | async-start | bytes 1720320 | tf_op jit(solution)/shard_map/reduce_scatter | solution.py:1283
  562.2 34.0 %collective-permute-start.65 = (bf16[384,768]{1,0:T(8,128)(2,1)}, bf16[384,768]{1,0:T(8,128)(2,1)S(1)}, u32[]{:S(2)}, u32[]{:S(2)}) collective-permute-start(bf16[384,768]{1,0:T(8,128)(2,1)} %get-tuple-element.205), channel_id=1, source_target_pairs={{0,16},{16,0},{1,17},{17,1},{2,18},{18,2},{3,19},{19,3},{4,20},{20... | collective-permute-start | bytes 1769480 | tf_op jit(solution)/shard_map/ppermute | solution.py:1273
  572.8 23.4 %collective-permute-start.60 = (bf16[192,512]{1,0:T(8,128)(2,1)}, bf16[192,512]{1,0:T(8,128)(2,1)S(1)}, u32[]{:S(2)}, u32[]{:S(2)}) collective-permute-start(bf16[192,512]{1,0:T(8,128)(2,1)} %get-tuple-element.196), channel_id=1, source_target_pairs={{0,4},{4,8},{6,10},{8,12},{10,14},{14,2},{1,5},{5,9},{7,11},{9,13}... | collective-permute-start | bytes 589832 | tf_op jit(solution)/shard_map/ppermute | solution.py:1207
  603.3 53.1 %all-to-all-start.12 = ((bf16[32,24,640]{2,1,0:T(8,128)(2,1)}), bf16[32,24,640]{2,1,0:T(8,128)(2,1)S(1)}, u32[]{:S(2)}, u32[]{:S(2)}) async-start(bf16[32,24,640]{2,1,0:T(8,128)(2,1)} %bitcast.200), calls=%async_computation.15 | async-start | bytes 1966080 | tf_op jit(solution)/shard_map/all_to_all | solution.py:52
  610.0 35.1 %reduce-scatter.11.cloned.1.call-start = ((), (), s32[]{:S(2)}) async-start(), calls=%async_computation.22 | async-start | bytes 737280 | tf_op jit(solution)/shard_map/reduce_scatter | solution.py:1283
  (180 other events, 1417.3 us)
Sparse Core Ops, SparseCore 0:
  46.1 52.8 all-gather.2
  106.9 70.6 all-gather.4
  391.0 21.2 reduce-scatter.4
  497.7 45.9 reduce-scatter.8
  559.9 37.2 reduce-scatter.6
  613.5 28.3 reduce-scatter.10

commit v5 on v4

--- a/solution.py
+++ b/solution.py
@@ -868,11 +868,13 @@
         ).astype(BF16)
 
 
-def out_grads_step(mixed, attn_grad, context):
+def out_grads_step(mixed, attn_grad, after, context):
     return run_kernel(
         out_grads_kernel,
         [context["place"], mixed, attn_grad],
         [((D // 2, D), BF16)] * 2,
+        (),
+        after,
         flops=2 * mixed.shape[1] * D * D,
         name="out_grads",
     )
@@ -906,23 +908,15 @@
 
 
 def qkv_end_kernel(place_ref, *refs):
-    first_ref, pieces = refs[0], refs[1:-3]
+    pieces = refs[:-3]
     qkv_out, small_out, columns = refs[-3:]
     edge = TEAM_HEADS * 3 * HEAD
-    layers_count = qkv_out.shape[0]
-    for layer in range(layers_count):
+    for layer in range(qkv_out.shape[0]):
         small = None
         for turn in range(4):
-            if layer == 0:
-                total = None
-                for block in range(first_ref.shape[0] // 4):
-                    part = first_ref[block * 4 + turn].astype(F32)
-                    total = part if total is None else total + part
-                columns[turn] = total
-            else:
-                total = pieces[4 * (layer - 1) + turn][...].astype(F32)
-                columns[place_ref[0] ^ turn] = total
-            part = total[:, edge:]
+            piece = pieces[4 * layer + turn][...].astype(F32)
+            columns[place_ref[0] ^ turn] = piece
+            part = piece[:, edge:]
             small = part if small is None else small + part
         small_out[layer] = small
         for member in range(4):
@@ -1047,14 +1041,13 @@
         joint_out[0, 0] = jnp.dot(turned[...], hold[...], preferred_element_type=F32)
 
 
-def expert_grads(layer, part, own, other, joint, down, before, later_than, context):
+def expert_grads(layer, quarters, own, other, joint, down, before, later_than, context):
     half = joint.shape[3] // 2
     given = [*own, *other]
     count = given[0][0].shape[0]
-    chunk = min(512 if count <= 512 else 128, half // 2)
+    chunk = min(512 if count <= 512 else 128, half // 4)
     chunks = half // chunk
-    steps = chunks // 2
-    first = part * steps
+    first, steps = [quarter * chunks // 4 for quarter in quarters]
     in_specs = [
         IN_SMEM,
         *[pl.BlockSpec((count, D), lambda i, h, at=at: (0, at)) for _, at in given],
@@ -1089,7 +1082,9 @@
         ],
         input_output_aliases=aliases,
         compiler_params=vmem(30 * count * D + 28 * D * chunk + 56 * count * chunk),
-        cost_estimate=cost(12 * count * D * half, 9 * D * half, count * half),
+        cost_estimate=cost(
+            24 * count * D * chunk * steps, 18 * D * chunk * steps, 2 * count * chunk * steps
+        ),
         name="expert_grads",
     )(*operands)
 
@@ -1361,6 +1356,17 @@
     return padded.reshape(total // TEAM_SIZE, -1, D)[:, : FF // total].reshape(-1, D)
 
 
+def folded(w_out):
+    return w_out.reshape(TEAM_SIZE * w_out.shape[0], -1)
+
+
+def out_rows(rows, member):
+    width = D // lax.axis_size(ALL)
+    rows = dp_rows(rows.reshape(-1, D))
+    rows = in_order(jnp.stack(from_team(rows)), member)
+    return rows.reshape(TEAM_SIZE, -1, width, D).transpose(1, 0, 2, 3).reshape(D, D)
+
+
 def side_by_side(*arrays):
     return jnp.concatenate(arrays, axis=2)
 
@@ -1410,23 +1416,28 @@
     rows = side_by_side(qkv_columns(w_qkv[0]), small).reshape(TEAM_SIZE * width, -1)
     rows = team_turn(rows, member).reshape(TEAM_SIZE * width, -1)
     first_rows = spread(rows, "z")
-    rows = side_by_side(copies(w_out[0]), joint_columns(shared_gate_up[0]))
-    rows = exchange(rows, TEAM).reshape(TEAM_SIZE * width, -1)
-    main_rows = jnp.concatenate([rows, padded_rows(shared_down[0])], axis=1)
+    rows = exchange(joint_columns(shared_gate_up[0]), TEAM).reshape(TEAM_SIZE * width, -1)
+    main_rows = jnp.concatenate([folded(w_out[0]), rows, padded_rows(shared_down[0])], axis=1)
     main_rows = z_gather(later(main_rows, first_rows))
     if LAYERS > 1:
         rows = side_by_side(
             *[qkv_columns(w_qkv[layer]) for layer in range(1, LAYERS)],
-            *[copies(w_out[layer]) for layer in range(1, LAYERS)],
             *[joint_columns(shared_gate_up[layer]) for layer in range(1, LAYERS)],
         )
         rows = team_turn(rows.reshape(TEAM_SIZE * width, -1), member)
         rows = rows.reshape(TEAM_SIZE * width, -1)
-        more_edges = [(LAYERS - 1) * qkv_width]
-        for size in (D, joint_width):
+        edge = (LAYERS - 1) * qkv_width
+        more_edges = [edge]
+        for size in (D // TEAM_SIZE, joint_width):
             more_edges.append(more_edges[-1] + (LAYERS - 1) * size)
         more_rows = jnp.concatenate(
-            [rows, *[padded_rows(shared_down[layer]) for layer in range(1, LAYERS)]], axis=1
+            [
+                rows[:, :edge],
+                *[folded(w_out[layer]) for layer in range(1, LAYERS)],
+                rows[:, edge:],
+                *[padded_rows(shared_down[layer]) for layer in range(1, LAYERS)],
+            ],
+            axis=1,
         )
     first_rows = dp_rows(first_rows)
     weights = split_small(first_rows[:, qkv_width:])
@@ -1447,19 +1458,19 @@
             context,
         )
         if layer == 0:
-            at, held_rows, edges = 0, main_rows, [0, D, D + joint_width]
+            at, held_rows = 0, main_rows
+            edges = [0, D // TEAM_SIZE, D // TEAM_SIZE + joint_width]
         else:
             at, held_rows, edges = layer - 1, more_rows, more_edges
         columns = [
             held_rows[:, low + at * size : low + (at + 1) * size]
-            for low, size in zip(edges, (D, joint_width, D))
+            for low, size in zip(edges, (D // TEAM_SIZE, joint_width, D))
         ]
         after = grad_rows[1:] if layer == last else []
         if layer > 0:
-            after = [*after, mine["out"], feeds[0]["other"]]
+            after = [*after, feeds[0]["other"]]
+        mine["out"] = out_rows(later(columns[0], pieces[0]), member)
         at_heads = to_heads(pieces, context)
-        if layer == 0:
-            mine["out"] = dp_rows(later(columns[0], at_heads[min(2, len(at_heads) - 1)]))
         back, attended = attention_forward(at_heads, after, context, stretch)
         if layer > 0:
             mine["joint"] = dp_rows(later(columns[1], attended[1]))
@@ -1530,8 +1541,6 @@
                 returned, feed, parts, weights[layer + 1]["gain_one"], [weights[layer + 1]["qkv"]], context
             )
             rows = from_team(normed)
-            low = more_edges[0] + layer * D
-            weights[layer + 1]["out"] = dp_rows(later(more_rows[:, low : low + D], normed))
 
     upstream = cotangent
     terms = None
@@ -1558,6 +1567,8 @@
             arrived_grad = send_rows(outgoing_grads, split_count)
             grads, other_grads = (arrived_grad, 0), (swap(arrived_grad), 0)
             grad_rows = from_team(upstream_rows)
+            waited = [(waited[0][0], later(waited[0][1], grad_rows[2])), *waited[1:]]
+            waited_sum = z_sum(beside(waited))
             waiting = [(own, swap(rows)) for own, rows in waiting]
             shared = shared_step(
                 feed["ffn_rows"],
@@ -1565,7 +1576,7 @@
                 mine["joint"],
                 mine["down"],
                 False,
-                [],
+                [terms[1]],
                 context,
             )
             returned = run_expert(
@@ -1577,14 +1588,11 @@
                 False,
                 [shared[0], *[rows for _, rows in waiting]],
             )
-            terms = expert_grads(
-                *rest_of_terms, terms, [returned, other_grads[0]], context
-            )
             returned = return_rows(returned, split_count)
             parts = to_team(shared[:4])
-            shared_parts = shared_grads(shared, [parts[2]], context)
-            waiting = [(own, later(rows, parts[1])) for own, rows in waiting]
-            waiting_sum = z_sum(beside([*waiting, *waited]))
+            shared_parts = shared_grads(shared, [parts[2], other_grads[0]], context)
+            waiting = [(own, later(rows, parts[1], waited_sum)) for own, rows in waiting]
+            waiting_sum = z_sum(beside(waiting))
             middle_grad, attn_grad, head_grads, small = feed_back_step(
                 returned,
                 feed,
@@ -1593,66 +1601,77 @@
                 [feed["gap"]],
                 mine,
                 False,
-                [shared_parts[1], shared_parts[3], terms[1]],
+                [shared_parts[1], shared_parts[3], waited_sum],
                 context,
             )
-        out_own, out_other = out_grads_step(feed["mixed"], attn_grad, context)
+            terms = expert_grads(*rest_of_terms, terms, [attn_grad, other_grads[0]], context)
         joint_arrived, down_arrived = swap(shared_parts[1]), swap(shared_parts[3])
-        out_arrived = swap(out_other)
         at_heads = grads_to_heads(head_grads, context)
-        halves = [(shared_parts[0], later(joint_arrived, at_heads))]
         if layer == 0:
-            halves.append((shared_parts[2], down_arrived))
-        shared_sum = z_sum(beside(halves))
+            out_own, out_other = out_grads_step(feed["mixed"], attn_grad, [], context)
+            out_arrived = swap(out_other)
+            halves = [(shared_parts[0], later(joint_arrived, out_other))]
+            shared_sum = z_sum(beside([*halves, (shared_parts[2], down_arrived)]))
         pieces, token = attention_backward(
             at_heads,
             feed["attended"],
-            [],
+            [waiting_sum, joint_arrived, down_arrived, terms[1]] if layer < last else [],
             context,
         )
+        if layer > 0:
+            out_own, out_other = out_grads_step(
+                feed["mixed"], attn_grad, [pieces[min(1, len(pieces) - 1)]], context
+            )
+            out_arrived = swap(out_other)
         held = ((arrived, 0), grads), ((other, 0), other_grads)
-        terms = expert_grads(layer, 0, *held, joint, down, terms, [token], context)
+        terms = expert_grads(layer, (0, 2), *held, joint, down, terms, [token], context)
         results = qkv_back_step(
             pieces,
             mine["qkv"],
             feed["team"],
             mine["gain_one"],
             small,
-            layer > 0,
-            [shared_sum, out_arrived, terms[1]] + ([down_arrived] if layer > 0 else [waiting_sum]),
+            True,
+            [terms[1]] + ([down_arrived, joint_arrived] if layer > 0 else [out_arrived]),
             context,
         )
         normed_parts, packed = to_team(results[:4]), results[4:]
         if layer > 0:
             waiting = [packed]
-            waited = [(out_own, out_arrived), (shared_parts[2], down_arrived)]
+            waited = [
+                (out_own, out_arrived),
+                (shared_parts[2], down_arrived),
+                (shared_parts[0], joint_arrived),
+            ]
             upstream, upstream_rows, outgoing_grads = layer_start_step(
                 feed["stream"], middle_grad, mine["gain_one"], normed_parts, feeds[layer - 1], context
             )
-            rest_of_terms = (layer, 1, *held, joint, down)
+            terms = expert_grads(
+                layer, (2, 1), *held, joint, down, terms, [outgoing_grads], context
+            )
+            rest_of_terms = (layer, (3, 1), *held, joint, down)
         else:
             (upstream_rows,) = layer_start_step(
                 feed["stream"], middle_grad, mine["gain_one"], normed_parts, None, context
             )
-            total = lax.axis_size(ALL)
-            first_sum = exchange(packed[0].reshape(total, D // total, -1), ALL)
+            qkv_arrived = swap(packed[1])
             out_sum = z_sum(beside([(out_own, later(out_arrived, packed[0]))]))
         if layer < last:
-            edge = waiting_sum.shape[1] - 2 * D
-            head_parts[layer + 1] = team_pieces(waiting_sum[:, :edge], member)
-            feed_parts[layer + 1][1] = team_pieces(waiting_sum[:, edge : edge + D], member)
-            feed_parts[layer + 1][2] = waiting_sum[:unit, edge + D :]
-        feed_parts[layer] = [
-            team_pieces(shared_sum[:, :joint_width], member),
-            None,
-            shared_sum[:unit, joint_width:] if layer == 0 else None,
-        ]
+            head_parts[layer + 1] = team_pieces(waiting_sum, member)
+            feed_parts[layer + 1][1] = team_pieces(waited_sum[:, :D], member)
+            feed_parts[layer + 1][2] = waited_sum[:unit, D : 2 * D]
+            feed_parts[layer + 1][0] = team_pieces(waited_sum[:, 2 * D :], member)
+        feed_parts[layer] = [None] * 3
         if layer == 0:
-            early = [packed[0], *feed_parts[0][0][1:]]
-            for later_layer in range(1, LAYERS):
-                early += head_parts[later_layer][1:]
-                early += feed_parts[later_layer][0][1:] + feed_parts[later_layer][1][1:]
-            terms = expert_grads(layer, 1, *held, joint, down, terms, early, context)
+            feed_parts[0][0] = team_pieces(shared_sum[:, :joint_width], member)
+            feed_parts[0][2] = shared_sum[:unit, joint_width:]
+        if layer == 0:
+            terms = expert_grads(
+                layer, (2, 2), *held, joint, down, terms, [packed[0], shared_sum], context
+            )
+            early = later(qkv_arrived, terms[1], *normed_parts[1:])
+            qkv_sum = z_sum_direct(beside([(packed[0], early)]))
+            head_parts[0] = team_pieces(qkv_sum, member)
             feed_parts[0][1] = team_pieces(later(out_sum, terms[1]), member)
     joint_sum, out_sum, down_sum = run_kernel(
         feed_end_kernel,
@@ -1672,9 +1691,9 @@
     )
     qkv_sum, small_sum = run_kernel(
         qkv_end_kernel,
-        [context["place"], first_sum, *[piece for pieces in head_parts[1:] for piece in pieces]],
+        [context["place"], *[piece for pieces in head_parts for piece in pieces]],
         [((LAYERS, width, 3 * D), F32), ((LAYERS, width, 64), F32)],
-        [((TEAM_SIZE, width, first_sum.shape[2]), F32)],
+        [((TEAM_SIZE, width, qkv_width + 64), F32)],
         name="qkv_end",
     )
     dense = (

time: 681 us -> 675 us (level)
  waiting for transfers between devices: 192 us -> 167 us
  starting transfers between devices: 162 us -> 175 us
    ppermute x18 -> x21, waiting for transfers between devices: 23.2 us -> 37.8 us  [from_member(): return lax.ppermute(rows, TEAM, [(i, 3 - i) for i in range(4)])]
    all_to_all x13 -> x12, waiting for transfers between devices: 48.5 us -> 35.8 us  [exchange(): return lax.all_to_all(rows, axes, split_axis=0, concat_axis=0, tiled=True)]
    ppermute x8, waiting for transfers between devices: 49.4 us -> 36.8 us  [dp_rows(): other = lax.ppermute(rows, 'dp', SWAP)]
    ppermute x12, waiting for transfers between devices: 29.2 us -> 18.6 us  [z_turn(): arrived.append(lax.ppermute(pieces[turn], ('z', 'core'), pairs))]
    all_to_all x13 -> x12, starting transfers between devices: 76.6 us -> 66.1 us  [exchange(): return lax.all_to_all(rows, axes, split_axis=0, concat_axis=0, tiled=True)]
    ppermute x0 -> x3, starting transfers between devices: none -> 9.59 us  [z_sum_direct(): lax.ppermute(block, 'z', [(i, (i + turn) % count) for i in range(count)])]
    ppermute x18 -> x21, waiting for transfers between devices: 36.9 us -> 29.1 us  [from_member(): return lax.ppermute(rows, 'ulysses', SWAP)]
    all_gather x2, waiting for transfers between devices: 0.04 us -> 7.38 us  [z_gather(): return lax.all_gather(rows, 'z', axis=0, tiled=True)]
  transfers between devices with their start and end apart: 103 -> 115, of which waited for: 35 -> 34; matrix products, arithmetic and copies ran while one was open for 9% -> 10% of each run, Pallas kernels for 25% -> 25%
where the time goes in v5:
time: 675 us; the launch traced here: 663 us
  Pallas kernels  209 us (31%)
  starting transfers between devices  175 us (26%)
  waiting for transfers between devices  167 us (25%)
  local copies, waits for them, and re-layouts  61.5 us (9%)
  other arithmetic  33.7 us (5%)
  between operations  16.4 us (2%)
    pallas_call x20, Pallas kernels, run_kernel(): pl.pallas_call(lambda *refs: kernel(*refs[:given], *refs[kept:]), grid=(1...  76.4 us
    all_to_all x12, starting transfers between devices, exchange(): return lax.all_to_all(rows, axes, split_axis=0, concat_axis=0, tiled=True)  66.1 us
    pallas_call x5, Pallas kernels, expert_grads(): pl.pallas_call(expert_grad_kernel, grid=(steps, 2), in_specs=in_specs, ou...  62.9 us
    ppermute x21, waiting for transfers between devices, from_member(): return lax.ppermute(rows, TEAM, [(i, 3 - i) for i in range(4)])  37.8 us
    ppermute x8, waiting for transfers between devices, dp_rows(): other = lax.ppermute(rows, 'dp', SWAP)  36.8 us
    all_to_all x12, waiting for transfers between devices, exchange(): return lax.all_to_all(rows, axes, split_axis=0, concat_axis=0, tiled=True)  35.8 us
    pallas_call x3, Pallas kernels, run_expert(): pl.pallas_call(lambda *refs: body(*refs[:drop], *refs[drop + len(after):]...  34.2 us
    ppermute x21, starting transfers between devices, from_member(): return lax.ppermute(rows, 'ulysses', SWAP)  31.2 us
  transfers between devices with their start and end apart: 115, of which 34 were waited for; matrix products, arithmetic and copies ran while one was open for 10% of the time, Pallas kernels for 25%

profile of v5, /device:TPU:0, one launch (start us, length us, event | category | flops | bytes accessed | tf_op | source)
XLA Modules:
  0.0 663.3 jit_solution(16748596863188259350)
XLA Ops:
  33.0 10.4 %all-to-all-done = bf16[4,96,612]{2,1,0:T(8,128)(2,1)S(1)} async-done(((bf16[4,96,612]{2,1,0:T(8,128)(2,1)}), bf16[4,96,612]{2,1,0:T(8,128)(2,1)S(1)}, u32[]{:S(2)}, u32[]{:S(2)}) %all-to-all-start) | async-done | bytes 470048 | tf_op jit(solution)/shard_map/all_to_all | solution.py:52
  51.6 12.0 %collective-permute-done.6 = bf16[384,612]{0,1:T(8,128)(2,1)S(1)} collective-permute-done((bf16[384,612]{0,1:T(8,128)(2,1)S(1)}, bf16[384,612]{0,1:T(8,128)(2,1)S(1)}, u32[]{:S(2)}, u32[]{:S(2)}) %collective-permute-start.6) | collective-permute-done | bytes 470048 | tf_op jit(solution)/shard_map/ppermute | solution.py:1310
  76.0 7.4 %all-gather.3.cloned.1.call-done = bf16[384,1984]{1,0:T(8,128)(2,1)} async-done(((bf16[96,1984]{1,0:T(8,128)(2,1)}), bf16[384,1984]{1,0:T(8,128)(2,1)}) %all-gather.3.cloned.1.call-update) | async-done | bytes 1523728 | tf_op jit(solution)/shard_map/all_gather | solution.py:1379
  91.0 7.8 %attend.2 = (bf16[4,192,512]{2,1,0:T(8,128)(2,1)}, bf16[16,64,128]{2,1,0:T(8,128)(2,1)}, f32[64,2048]{1,0:T(8,128)}, f32[1,2048]{1,0:T(1,128)}) custom-call(s32[4]{0:T(128)} %pad_add_fusion.refs_0_.place_ref, bf16[192,512]{1,0:T(8,128)(2,1)} %get-tuple-element.121.refs_0_.refs_1_, bf16[192,512]{1,0:T(8,128)(2,1)} %copy-done.104, ...), custom_call_target="tpu_custom_call" | custom-call | flops 16777216 | bytes 1572864 | tf_op jit(solution)/shard_map/attend/pallas_call | solution.py:295
  109.7 6.3 collective-permute-done.13
  126.0 6.2 all-to-all-start.3
  137.2 8.0 %collective-permute-done.17 = bf16[384,1024]{1,0:T(8,128)(2,1)} collective-permute-done((bf16[384,1024]{1,0:T(8,128)(2,1)}, bf16[384,1024]{1,0:T(8,128)(2,1)}, u32[]{:S(2)}, u32[]{:S(2)}) %collective-permute-start.17) | collective-permute-done | bytes 786464 | tf_op jit(solution)/shard_map/ppermute | solution.py:1310
  147.9 9.2 %all-to-all-done.3 = bf16[16,24,768]{2,1,0:T(8,128)(2,1)S(1)} async-done(((bf16[16,24,768]{2,1,0:T(8,128)(2,1)}), bf16[16,24,768]{2,1,0:T(8,128)(2,1)S(1)}, u32[]{:S(2)}, u32[]{:S(2)}) %all-to-all-start.3) | async-done | bytes 589856 | tf_op jit(solution)/shard_map/all_to_all | solution.py:52
  157.9 8.6 %expert_forward.1.refs_7_.refs_1_ = bf16[384,768]{1,0:T(8,128)(2,1)} custom-call(bf16[384,768]{1,0:T(8,128)(2,1)} %bitcast.216, bf16[2,1,768,4096]{3,2,1,0:T(8,128)(2,1)} %up_ref.9, bf16[2,1,768,4096]{3,2,1,0:T(8,128)(2,1)} %up_ref.9, bf16[2,1,2048,768]{3,2,1,0:T(8,128)(2,1)} %down_ref.9, bf16[128,768]{1,0:T(8,128)(2,1)} %copy-done.26, ...), custom_call_target="tpu_custom_call" | custom-call | flops 3623878656 | bytes 10616832 | tf_op jit(solution)/shard_map/expert_forward/pallas_call | solution.py:988
  166.5 6.9 %all-to-all-start.4 = ((bf16[16,24,768]{2,1,0:T(8,128)(2,1)}), bf16[16,24,768]{2,1,0:T(8,128)(2,1)S(1)}, u32[]{:S(2)}, u32[]{:S(2)}) async-start(bf16[16,24,768]{2,1,0:T(8,128)(2,1)} %bitcast.225), calls=%async_computation.4 | async-start | bytes 1179648 | tf_op jit(solution)/shard_map/all_to_all | solution.py:52
  230.9 7.8 %collective-permute-done.30.refs_2_ = bf16[192,512]{1,0:T(8,128)(2,1)S(1)} collective-permute-done((bf16[192,512]{1,0:T(8,128)(2,1)S(1)}, bf16[192,512]{1,0:T(8,128)(2,1)S(1)}, u32[]{:S(2)}, u32[]{:S(2)}) %collective-permute-start.30) | collective-permute-done | bytes 196640 | tf_op jit(solution)/shard_map/ppermute | solution.py:1202
  239.4 7.8 %attend.3 = (bf16[4,192,512]{2,1,0:T(8,128)(2,1)}, bf16[16,64,128]{2,1,0:T(8,128)(2,1)}, f32[64,2048]{1,0:T(8,128)}, f32[1,2048]{1,0:T(1,128)}) custom-call(s32[4]{0:T(128)} %pad_add_fusion.refs_0_.place_ref, bf16[192,512]{1,0:T(8,128)(2,1)} %get-tuple-element.136.refs_0_.refs_1_, bf16[192,512]{1,0:T(8,128)(2,1)} %copy-done.109, ...), custom_call_target="tpu_custom_call" | custom-call | flops 16777216 | bytes 1572864 | tf_op jit(solution)/shard_map/attend/pallas_call | solution.py:295
  258.3 7.5 %collective-permute-done.39 = bf16[192,768]{1,0:T(8,128)(2,1)S(1)} collective-permute-done((bf16[192,768]{1,0:T(8,128)(2,1)S(1)}, bf16[192,768]{1,0:T(8,128)(2,1)S(1)}, u32[]{:S(2)}, u32[]{:S(2)}) %collective-permute-start.39) | collective-permute-done | bytes 294944 | tf_op jit(solution)/shard_map/ppermute | solution.py:63
  283.3 12.7 %collective-permute-done.44 = bf16[384,768]{1,0:T(8,128)(2,1)S(1)} collective-permute-done((bf16[384,768]{1,0:T(8,128)(2,1)}, bf16[384,768]{1,0:T(8,128)(2,1)S(1)}, u32[]{:S(2)}, u32[]{:S(2)}) %collective-permute-start.44) | collective-permute-done | bytes 589856 | tf_op jit(solution)/shard_map/ppermute | solution.py:1310
  299.4 6.6 shared.4
  307.0 13.8 %expert_both.1 = bf16[384,1536]{1,0:T(8,128)(2,1)} custom-call(bf16[384,1536]{1,0:T(8,128)(2,1)} %bitcast.207, bf16[384,1536]{1,0:T(8,128)(2,1)} %bitcast.208, bf16[2,1,768,4096]{3,2,1,0:T(8,128)(2,1)} %up_ref.9, bf16[2,1,768,4096]{3,2,1,0:T(8,128)(2,1)} %up_ref.9, bf16[2,1,2048,768]{3,2,1,0:T(8,128)(2,1)} %down_ref.9, ...), custom_call_target="tpu_custom_call" | custom-call | flops 7247757312 | bytes 11796480 | tf_op jit(solution)/shard_map/expert_both/pallas_call | solution.py:988
  334.7 13.2 %collective-permute-done.45.refs_12_ = bf16[128,1536]{1,0:T(8,128)(2,1)} collective-permute-done((bf16[128,1536]{1,0:T(8,128)(2,1)}, bf16[128,1536]{1,0:T(8,128)(2,1)}, u32[]{:S(2)}, u32[]{:S(2)}) %collective-permute-start.45) | collective-permute-done | bytes 393248 | tf_op jit(solution)/shard_map/ppermute | solution.py:60
  347.9 10.6 %collective-permute-done.47.refs_14_ = bf16[128,1536]{1,0:T(8,128)(2,1)} collective-permute-done((bf16[128,1536]{1,0:T(8,128)(2,1)}, bf16[128,1536]{1,0:T(8,128)(2,1)}, u32[]{:S(2)}, u32[]{:S(2)}) %collective-permute-start.47) | collective-permute-done | bytes 393248 | tf_op jit(solution)/shard_map/ppermute | solution.py:63
  371.0 7.5 %all-to-all-done.8.grad_ref = bf16[16,64,128]{2,1,0:T(8,128)(2,1)} async-done(((bf16[16,64,128]{2,1,0:T(8,128)(2,1)}), bf16[16,64,128]{2,1,0:T(8,128)(2,1)}, u32[]{:S(2)}, u32[]{:S(2)}) %all-to-all-start.8) | async-done | bytes 262176 | tf_op jit(solution)/shard_map/all_to_all | solution.py:52
  378.4 10.2 %attend_back.2 = (bf16[192,512]{1,0:T(8,128)(2,1)}, bf16[192,512]{1,0:T(8,128)(2,1)}, bf16[192,512]{1,0:T(8,128)(2,1)}, bf16[192,512]{1,0:T(8,128)(2,1)}) custom-call(s32[4]{0:T(128)} %pad_add_fusion.refs_0_.place_ref, bf16[4,192,512]{2,1,0:T(8,128)(2,1)} %get-tuple-element.159.rows_ref, s32[1,2048]{1,0:T(1,128)} %bitcast.286, ...), custom_call_target="tpu_custom_call" | custom-call | flops 50331648 | bytes 1572864 | tf_op jit(solution)/shard_map/attend_back/pallas_call | solution.py:322
  396.8 15.2 %expert_grads.5 = (f32[2,1,768,4096]{3,2,1,0:T(8,128)}, f32[2,1,2048,768]{3,2,1,0:T(8,128)}) custom-call(s32[4]{0:T(128)} %pad_add_fusion.refs_0_.place_ref, bf16[384,1536]{1,0:T(8,128)(2,1)} %bitcast.209, bf16[384,1536]{1,0:T(8,128)(2,1)} %bitcast.210, bf16[384,1536]{1,0:T(8,128)(2,1)} %copy-done.2, bf16[384,1536]{1,0:T(8,128)(2,1)} %copy-done.2, ...), custom_call_target="tpu_custom_call" | custom-call | flops 7247757312 | bytes 14155776 | tf_op jit(solution)/shard_map/expert_grads/pallas_call | solution.py:1065
  440.1 5.5 all-to-all-start.9
  448.8 8.6 %expert_grads.6 = (f32[2,1,768,4096]{3,2,1,0:T(8,128)}, f32[2,1,2048,768]{3,2,1,0:T(8,128)}) custom-call(s32[4]{0:T(128)} %pad_add_fusion.refs_0_.place_ref, bf16[384,1536]{1,0:T(8,128)(2,1)} %bitcast.211, bf16[384,1536]{1,0:T(8,128)(2,1)} %bitcast.212, bf16[384,1536]{1,0:T(8,128)(2,1)} %copy-done.2, ...), custom_call_target="tpu_custom_call", output_to_operand_aliasing={{0}: (8, {}), {1}: (9, {})} | custom-call | flops 3623878656 | bytes 7077888 | tf_op jit(solution)/shard_map/expert_grads/pallas_call | solution.py:1065
  459.5 6.0 shared.5
  471.9 11.8 %expert_back.1 = bf16[384,768]{1,0:T(8,128)(2,1)} custom-call(bf16[384,768]{1,0:T(8,128)(2,1)} %bitcast.217, bf16[384,768]{1,0:T(8,128)(2,1)} %bitcast.227, bf16[2,1,768,4096]{3,2,1,0:T(8,128)(2,1)} %up_ref.9, bf16[2,1,768,4096]{3,2,1,0:T(8,128)(2,1)} %up_ref.9, bf16[2,1,2048,768]{3,2,1,0:T(8,128)(2,1)} %down_ref.9, ...), custom_call_target="tpu_custom_call" | custom-call | flops 6039797760 | bytes 10616832 | tf_op jit(solution)/shard_map/expert_back/pallas_call | solution.py:988
  483.7 10.9 %all-to-all-start.10 = ((bf16[16,24,768]{2,1,0:T(8,128)(2,1)}), bf16[16,24,768]{2,1,0:T(8,128)(2,1)S(1)}, u32[]{:S(2)}, u32[]{:S(2)}) async-start(bf16[16,24,768]{2,1,0:T(8,128)(2,1)} %bitcast.245), calls=%async_computation.10 | async-start | bytes 1179648 | tf_op jit(solution)/shard_map/all_to_all | solution.py:52
  509.9 5.8 collective-permute-done.63.refs_14_
  529.6 8.6 %expert_grads.7 = (f32[2,1,768,4096]{3,2,1,0:T(8,128)}, f32[2,1,2048,768]{3,2,1,0:T(8,128)}) custom-call(s32[4]{0:T(128)} %pad_add_fusion.refs_0_.place_ref, bf16[384,1536]{1,0:T(8,128)(2,1)} %bitcast.213, bf16[384,1536]{1,0:T(8,128)(2,1)} %bitcast.214, bf16[384,1536]{1,0:T(8,128)(2,1)} %copy-done.2, ...), custom_call_target="tpu_custom_call", output_to_operand_aliasing={{0}: (8, {}), {1}: (9, {})} | custom-call | flops 3623878656 | bytes 7077888 | tf_op jit(solution)/shard_map/expert_grads/pallas_call | solution.py:1065
  539.2 10.1 %attend_back.3 = (bf16[192,512]{1,0:T(8,128)(2,1)}, bf16[192,512]{1,0:T(8,128)(2,1)}, bf16[192,512]{1,0:T(8,128)(2,1)}, bf16[192,512]{1,0:T(8,128)(2,1)}) custom-call(s32[4]{0:T(128)} %pad_add_fusion.refs_0_.place_ref, bf16[4,192,512]{2,1,0:T(8,128)(2,1)} %get-tuple-element.197.rows_ref, s32[1,2048]{1,0:T(1,128)} %bitcast.287, ...), custom_call_target="tpu_custom_call" | custom-call | flops 50331648 | bytes 1572864 | tf_op jit(solution)/shard_map/attend_back/pallas_call | solution.py:322
  567.4 15.3 %expert_grads.8 = (f32[2,1,768,4096]{3,2,1,0:T(8,128)}, f32[2,1,2048,768]{3,2,1,0:T(8,128)}) custom-call(s32[4]{0:T(128)} %pad_add_fusion.refs_0_.place_ref, bf16[384,768]{1,0:T(8,128)(2,1)} %bitcast.218, bf16[384,768]{1,0:T(8,128)(2,1)} %bitcast.228, bf16[384,768]{1,0:T(8,128)(2,1)} %copy-done.24, ...), custom_call_target="tpu_custom_call", output_to_operand_aliasing={{0}: (8, {}), {1}: (9, {})} | custom-call | flops 7247757312 | bytes 14155776 | tf_op jit(solution)/shard_map/expert_grads/pallas_call | solution.py:1065
  600.3 15.2 %expert_grads.9 = (f32[2,1,768,4096]{3,2,1,0:T(8,128)}, f32[2,1,2048,768]{3,2,1,0:T(8,128)}) custom-call(s32[4]{0:T(128)} %pad_add_fusion.refs_0_.place_ref, bf16[384,768]{1,0:T(8,128)(2,1)} %bitcast.219, bf16[384,768]{1,0:T(8,128)(2,1)} %bitcast.229, bf16[384,768]{1,0:T(8,128)(2,1)} %copy-done.24, ...), custom_call_target="tpu_custom_call", output_to_operand_aliasing={{0}: (8, {}), {1}: (9, {})} | custom-call | flops 7247757312 | bytes 14155776 | tf_op jit(solution)/shard_map/expert_grads/pallas_call | solution.py:1065
  618.9 6.9 %collective-permute-start.76 = (bf16[96,640]{1,0:T(8,128)(2,1)S(1)}, bf16[96,640]{1,0:T(8,128)(2,1)S(1)}, u32[]{:S(2)}, u32[]{:S(2)}) collective-permute-start(bf16[96,640]{1,0:T(8,128)(2,1)S(1)} %get-tuple-element.292), channel_id=1, source_target_pairs={{0,4},{4,8},{8,12},{12,0},{1,5},{5,9},{9,13},{13,1},{2,6},{6,10},{... | collective-permute-start | bytes 368648 | tf_op jit(solution)/shard_map/ppermute | solution.py:1290
  (608 shorter events, 346.4 us)
Async XLA Ops:
  7.2 59.1 %collective-permute-start = (bf16[128,768]{1,0:T(8,128)(2,1)}, bf16[128,768]{1,0:T(8,128)(2,1)S(1)}, u32[]{:S(2)}, u32[]{:S(2)}) collective-permute-start(bf16[128,768]{1,0:T(8,128)(2,1)} %bitcast.248), channel_id=1, source_target_pairs={{0,1},{1,0},{2,3},{3,2},{4,5},{5,4},{6,7},{7,6},{8,9},{9,8},{10,11... | collective-permute-start | bytes 589832 | tf_op jit(solution)/shard_map/ppermute | solution.py:60
  10.3 56.1 %collective-permute-start.1 = (bf16[128,768]{1,0:T(8,128)(2,1)}, bf16[128,768]{1,0:T(8,128)(2,1)}, u32[]{:S(2)}, u32[]{:S(2)}) collective-permute-start(bf16[128,768]{1,0:T(8,128)(2,1)} %bitcast.249), channel_id=1, source_target_pairs={{0,2},{2,0},{1,3},{3,1},{4,6},{6,4},{5,7},{7,5},{8,10},{10,8},{9,1... | collective-permute-start | bytes 589832 | tf_op jit(solution)/shard_map/ppermute | solution.py:62
  20.3 29.5 %collective-permute-start.22 = (bf16[24,1600]{1,0:T(8,128)(2,1)S(1)}, bf16[24,1600]{1,0:T(8,128)(2,1)S(1)}, u32[]{:S(2)}, u32[]{:S(2)}) collective-permute-start(bf16[24,1600]{1,0:T(8,128)(2,1)S(1)} %get-tuple-element.301), channel_id=1, source_target_pairs={{0,2},{2,0},{1,3},{3,1},{4,6},{6,4},{5,7},{7,5},{8,10},{10,8},{9,1... | collective-permute-start | bytes 230408 | tf_op jit(solution)/shard_map/ppermute | solution.py:62
  21.1 28.8 %collective-permute-start.23 = (bf16[24,1600]{1,0:T(8,128)(2,1)S(1)}, bf16[24,1600]{1,0:T(8,128)(2,1)S(1)}, u32[]{:S(2)}, u32[]{:S(2)}) collective-permute-start(bf16[24,1600]{1,0:T(8,128)(2,1)S(1)} %get-tuple-element.302), channel_id=1, source_target_pairs={{0,1},{1,0},{2,3},{3,2},{4,5},{5,4},{6,7},{7,6},{8,9},{9,8},{10,11... | collective-permute-start | bytes 230408 | tf_op jit(solution)/shard_map/ppermute | solution.py:60
  22.6 28.9 %collective-permute-start.24 = (bf16[24,1600]{1,0:T(8,128)(2,1)S(1)}, bf16[24,1600]{1,0:T(8,128)(2,1)S(1)}, u32[]{:S(2)}, u32[]{:S(2)}) collective-permute-start(bf16[24,1600]{1,0:T(8,128)(2,1)S(1)} %get-tuple-element.300), channel_id=1, source_target_pairs={{0,3},{1,2},{2,1},{3,0},{4,7},{5,6},{6,5},{7,4},{8,11},{9,10},{10,... | collective-permute-start | bytes 230408 | tf_op jit(solution)/shard_map/ppermute | solution.py:63
  30.1 53.3 %all-gather.3.cloned.1.call-start = ((), (), s32[]{:S(2)}) async-start(), calls=%async_computation.16 | async-start | bytes 1966080 | tf_op jit(solution)/shard_map/all_gather | solution.py:1379
  44.2 129.7 %all-gather.5.cloned.1.call-start = ((), (), s32[]{:S(2)}) async-start(), calls=%async_computation.17 | async-start | bytes 2457600 | tf_op jit(solution)/shard_map/all_gather | solution.py:1379
  126.0 31.1 %all-to-all-start.3 = ((bf16[16,24,768]{2,1,0:T(8,128)(2,1)}), bf16[16,24,768]{2,1,0:T(8,128)(2,1)S(1)}, u32[]{:S(2)}, u32[]{:S(2)}) async-start(bf16[16,24,768]{2,1,0:T(8,128)(2,1)} %bitcast.38), calls=%async_computation.3 | async-start | bytes 1179648 | tf_op jit(solution)/shard_map/all_to_all | solution.py:52
  136.6 40.2 %collective-permute-start.18 = (bf16[384,768]{1,0:T(8,128)(2,1)}, bf16[384,768]{1,0:T(8,128)(2,1)}, u32[]{:S(2)}, u32[]{:S(2)}) collective-permute-start(bf16[384,768]{1,0:T(8,128)(2,1)} %later.18), channel_id=1, source_target_pairs={{0,16},{16,0},{1,17},{17,1},{2,18},{18,2},{3,19},{19,3},{4,20},{20... | collective-permute-start | bytes 1769480 | tf_op jit(solution)/shard_map/ppermute | solution.py:1310
  166.5 29.3 %all-to-all-start.4 = ((bf16[16,24,768]{2,1,0:T(8,128)(2,1)}), bf16[16,24,768]{2,1,0:T(8,128)(2,1)S(1)}, u32[]{:S(2)}, u32[]{:S(2)}) async-start(bf16[16,24,768]{2,1,0:T(8,128)(2,1)} %bitcast.225), calls=%async_computation.4 | async-start | bytes 1179648 | tf_op jit(solution)/shard_map/all_to_all | solution.py:52
  201.7 26.0 %collective-permute-start.35 = (bf16[384,768]{1,0:T(8,128)(2,1)S(1)}, bf16[384,768]{1,0:T(8,128)(2,1)S(1)}, u32[]{:S(2)}, u32[]{:S(2)}) collective-permute-start(bf16[384,768]{1,0:T(8,128)(2,1)S(1)} %bitcast.220), channel_id=1, source_target_pairs={{0,16},{16,0},{1,17},{17,1},{2,18},{18,2},{3,19},{19,3},{4,20},{20... | collective-permute-start | bytes 1769480 | tf_op jit(solution)/shard_map/ppermute | solution.py:1268
  273.9 32.0 %all-to-all-start.6 = ((bf16[16,24,1536]{2,1,0:T(8,128)(2,1)}), bf16[16,24,1536]{2,1,0:T(8,128)(2,1)S(1)}, u32[]{:S(2)}, u32[]{:S(2)}) async-start(bf16[16,24,1536]{2,1,0:T(8,128)(2,1)} %bitcast.268), calls=%async_computation.6 | async-start | bytes 2359296 | tf_op jit(solution)/shard_map/all_to_all | solution.py:52
  320.8 37.7 %all-to-all-start.7 = ((bf16[16,24,1536]{2,1,0:T(8,128)(2,1)}), bf16[16,24,1536]{2,1,0:T(8,128)(2,1)}, u32[]{:S(2)}, u32[]{:S(2)}) async-start(bf16[16,24,1536]{2,1,0:T(8,128)(2,1)} %bitcast.232), calls=%async_computation.7 | async-start | bytes 2359296 | tf_op jit(solution)/shard_map/all_to_all | solution.py:52
  326.3 68.5 %collective-permute-start.51 = (bf16[384,1536]{1,0:T(8,128)(2,1)S(1)}, bf16[384,1536]{1,0:T(8,128)(2,1)S(1)}, u32[]{:S(2)}, u32[]{:S(2)}) collective-permute-start(bf16[384,1536]{1,0:T(8,128)(2,1)S(1)} %bitcast.215), channel_id=1, source_target_pairs={{0,16},{16,0},{1,17},{17,1},{2,18},{18,2},{3,19},{19,3},{4,20},{20... | collective-permute-start | bytes 3538952 | tf_op jit(solution)/shard_map/ppermute | solution.py:1268
  329.3 29.3 %collective-permute-start.47 = (bf16[128,1536]{1,0:T(8,128)(2,1)}, bf16[128,1536]{1,0:T(8,128)(2,1)}, u32[]{:S(2)}, u32[]{:S(2)}) collective-permute-start(bf16[128,1536]{1,0:T(8,128)(2,1)} %get-tuple-element.150), channel_id=1, source_target_pairs={{0,3},{1,2},{2,1},{3,0},{4,7},{5,6},{6,5},{7,4},{8,11},{9,10},{10,... | collective-permute-start | bytes 1179656 | tf_op jit(solution)/shard_map/ppermute | solution.py:63
  368.4 137.6 %reduce-scatter.5.cloned.1.call-start = ((), (), s32[]{:S(2)}) async-start(), calls=%async_computation.18 | async-start | bytes 2457600 | tf_op jit(solution)/shard_map/reduce_scatter | solution.py:1278
  368.9 46.6 %collective-permute-start.53 = (bf16[384,1024]{1,0:T(8,128)(2,1)}, bf16[384,1024]{1,0:T(8,128)(2,1)}, u32[]{:S(2)}, u32[]{:S(2)}) collective-permute-start(bf16[384,1024]{1,0:T(8,128)(2,1)} %get-tuple-element.155.refs_15_), channel_id=1, source_target_pairs={{0,16},{16,0},{1,17},{17,1},{2,18},{18,2},{3,19},{19,3},{4,20},{20... | collective-permute-start | bytes 2359304 | tf_op jit(solution)/shard_map/ppermute | solution.py:1268
  369.9 45.6 %collective-permute-start.52 = (bf16[384,768]{1,0:T(8,128)(2,1)}, bf16[384,768]{1,0:T(8,128)(2,1)S(1)}, u32[]{:S(2)}, u32[]{:S(2)}) collective-permute-start(bf16[384,768]{1,0:T(8,128)(2,1)} %get-tuple-element.156.refs_16_), channel_id=1, source_target_pairs={{0,16},{16,0},{1,17},{17,1},{2,18},{18,2},{3,19},{19,3},{4,20},{20... | collective-permute-start | bytes 1769480 | tf_op jit(solution)/shard_map/ppermute | solution.py:1268
  388.6 23.5 %collective-permute-start.48 = (bf16[192,512]{1,0:T(8,128)(2,1)}, bf16[192,512]{1,0:T(8,128)(2,1)}, u32[]{:S(2)}, u32[]{:S(2)}) collective-permute-start(bf16[192,512]{1,0:T(8,128)(2,1)} %get-tuple-element.163), channel_id=1, source_target_pairs={{0,4},{4,8},{6,10},{8,12},{10,14},{14,2},{1,5},{5,9},{7,11},{9,13}... | collective-permute-start | bytes 589832 | tf_op jit(solution)/shard_map/ppermute | solution.py:1202
  440.1 30.0 %all-to-all-start.9 = ((bf16[16,24,768]{2,1,0:T(8,128)(2,1)}), bf16[16,24,768]{2,1,0:T(8,128)(2,1)S(1)}, u32[]{:S(2)}, u32[]{:S(2)}) async-start(bf16[16,24,768]{2,1,0:T(8,128)(2,1)} %bitcast.75), calls=%async_computation.9 | async-start | bytes 1179648 | tf_op jit(solution)/shard_map/all_to_all | solution.py:52
  445.6 25.5 %collective-permute-start.60 = (bf16[384,640]{1,0:T(8,128)(2,1)S(1)}, bf16[384,640]{1,0:T(8,128)(2,1)S(1)}, u32[]{:S(2)}, u32[]{:S(2)}) collective-permute-start(bf16[384,640]{1,0:T(8,128)(2,1)S(1)} %copy-done.94), channel_id=1, source_target_pairs={{0,16},{16,0},{1,17},{17,1},{2,18},{18,2},{3,19},{19,3},{4,20},{20... | collective-permute-start | bytes 1474568 | tf_op jit(solution)/shard_map/ppermute | solution.py:1268
  470.1 26.8 %collective-permute-start.64 = (bf16[384,768]{1,0:T(8,128)(2,1)S(1)}, bf16[384,768]{1,0:T(8,128)(2,1)S(1)}, u32[]{:S(2)}, u32[]{:S(2)}) collective-permute-start(bf16[384,768]{1,0:T(8,128)(2,1)S(1)} %bitcast.226), channel_id=1, source_target_pairs={{0,16},{16,0},{1,17},{17,1},{2,18},{18,2},{3,19},{19,3},{4,20},{20... | collective-permute-start | bytes 1769480 | tf_op jit(solution)/shard_map/ppermute | solution.py:1268
  483.7 32.0 %all-to-all-start.10 = ((bf16[16,24,768]{2,1,0:T(8,128)(2,1)}), bf16[16,24,768]{2,1,0:T(8,128)(2,1)S(1)}, u32[]{:S(2)}, u32[]{:S(2)}) async-start(bf16[16,24,768]{2,1,0:T(8,128)(2,1)} %bitcast.245), calls=%async_computation.10 | async-start | bytes 1179648 | tf_op jit(solution)/shard_map/all_to_all | solution.py:52
  494.6 43.7 %reduce-scatter.7.cloned.1.call-start = ((), (), s32[]{:S(2)}) async-start(), calls=%async_computation.19 | async-start | bytes 614400 | tf_op jit(solution)/shard_map/reduce_scatter | solution.py:1278
  502.2 23.6 %collective-permute-start.67 = (bf16[384,768]{1,0:T(8,128)(2,1)}, bf16[384,768]{1,0:T(8,128)(2,1)S(1)}, u32[]{:S(2)}, u32[]{:S(2)}) collective-permute-start(bf16[384,768]{1,0:T(8,128)(2,1)} %get-tuple-element.189.refs_17_), channel_id=1, source_target_pairs={{0,16},{16,0},{1,17},{17,1},{2,18},{18,2},{3,19},{19,3},{4,20},{20... | collective-permute-start | bytes 1769480 | tf_op jit(solution)/shard_map/ppermute | solution.py:1268
  508.8 29.5 %collective-permute-start.66 = (bf16[384,1024]{1,0:T(8,128)(2,1)S(1)}, bf16[384,1024]{1,0:T(8,128)(2,1)S(1)}, u32[]{:S(2)}, u32[]{:S(2)}) collective-permute-start(bf16[384,1024]{1,0:T(8,128)(2,1)S(1)} %copy-done.40), channel_id=1, source_target_pairs={{0,16},{16,0},{1,17},{17,1},{2,18},{18,2},{3,19},{19,3},{4,20},{20... | collective-permute-start | bytes 2359304 | tf_op jit(solution)/shard_map/ppermute | solution.py:1268
  525.5 74.8 %reduce-scatter.9.cloned.1.call-start = ((), (), s32[]{:S(2)}) async-start(), calls=%async_computation.20 | async-start | bytes 1720320 | tf_op jit(solution)/shard_map/reduce_scatter | solution.py:1278
  553.2 75.9 %reduce-scatter.11.cloned.1.call-start = ((), (), s32[]{:S(2)}) async-start(), calls=%async_computation.21 | async-start | bytes 737280 | tf_op jit(solution)/shard_map/reduce_scatter | solution.py:1278
  553.3 30.0 %collective-permute-start.71 = (bf16[384,768]{1,0:T(8,128)(2,1)S(1)}, bf16[384,768]{1,0:T(8,128)(2,1)S(1)}, u32[]{:S(2)}, u32[]{:S(2)}) collective-permute-start(bf16[384,768]{1,0:T(8,128)(2,1)S(1)} %copy-done.47), channel_id=1, source_target_pairs={{0,16},{16,0},{1,17},{17,1},{2,18},{18,2},{3,19},{19,3},{4,20},{20... | collective-permute-start | bytes 1769480 | tf_op jit(solution)/shard_map/ppermute | solution.py:1268
  555.0 74.1 %collective-permute-start.94 = (bf16[24,768]{1,0:T(8,128)(2,1)S(1)}, bf16[24,768]{1,0:T(8,128)(2,1)S(1)}, u32[]{:S(2)}, u32[]{:S(2)}) collective-permute-start(bf16[24,768]{1,0:T(8,128)(2,1)S(1)} %get-tuple-element.325), channel_id=1, source_target_pairs={{0,1},{1,0},{2,3},{3,2},{4,5},{5,4},{6,7},{7,6},{8,9},{9,8},{10,11... | collective-permute-start | bytes 110600 | tf_op jit(solution)/shard_map/ppermute | solution.py:60
  557.6 25.8 %collective-permute-start.68 = (bf16[192,512]{1,0:T(8,128)(2,1)S(1)}, bf16[192,512]{1,0:T(8,128)(2,1)S(1)}, u32[]{:S(2)}, u32[]{:S(2)}) collective-permute-start(bf16[192,512]{1,0:T(8,128)(2,1)S(1)} %copy-done.101), channel_id=1, source_target_pairs={{0,4},{4,8},{6,10},{8,12},{10,14},{14,2},{1,5},{5,9},{7,11},{9,13}... | collective-permute-start | bytes 589832 | tf_op jit(solution)/shard_map/ppermute | solution.py:1202
  565.3 24.4 %collective-permute-start.70 = (bf16[192,512]{1,0:T(8,128)(2,1)S(1)}, bf16[192,512]{1,0:T(8,128)(2,1)S(1)}, u32[]{:S(2)}, u32[]{:S(2)}) collective-permute-start(bf16[192,512]{1,0:T(8,128)(2,1)S(1)} %copy-done.99), channel_id=1, source_target_pairs={{0,12},{4,0},{6,2},{8,4},{10,6},{14,10},{1,13},{5,1},{7,3},{9,5},{... | collective-permute-start | bytes 589832 | tf_op jit(solution)/shard_map/ppermute | solution.py:1202
  (202 other events, 1708.0 us)
Sparse Core Ops, SparseCore 0:
  44.3 39.0 all-gather.2
  98.9 62.1 all-gather.4
  440.2 50.9 reduce-scatter.4
  508.8 20.6 reduce-scatter.6
  553.3 43.3 reduce-scatter.8
  600.4 24.9 reduce-scatter.10

commit v6 on v5

--- a/solution.py
+++ b/solution.py
@@ -826,7 +826,7 @@
     )
 
 
-def shared_grads_kernel(unit, place_ref, *refs):
+def shared_grads_kernel(place_ref, *refs):
     team_ref, joint_ref, hidden_ref, grads_ref = refs[:4]
     joint_outs, down_outs = refs[4:6], refs[6:8]
     half = D // 2
@@ -836,19 +836,15 @@
             team_ref[:, rows_at(dp, half)], joint_ref[...], 0, 0
         ).astype(BF16)
         down = contract(hidden_ref[:, rows_at(dp, units)], grads_ref[...], 0, 0).astype(BF16)
-        out = down_outs[place]
-        for block in range(units // unit):
-            low, high = block * unit, (block + 1) * unit
-            at, end = block * half * unit // units, (block + 1) * half * unit // units
-            out[at : at + unit] = down[low:high]
-            out[at + unit : end] = jnp.zeros((end - at - unit, D), BF16)
+        down_outs[place][...] = down
 
 
 def shared_grads_step(team, joint_grad, hidden, grad_team, after, context):
     return run_kernel(
-        functools.partial(shared_grads_kernel, FF // lax.axis_size(ALL)),
+        shared_grads_kernel,
         [context["place"], team, joint_grad, hidden, grad_team],
-        [((D // 2, joint_grad.shape[1]), BF16)] * 2 + [((D // 2, D), BF16)] * 2,
+        [((D // 2, joint_grad.shape[1]), BF16)] * 2
+        + [((hidden.shape[1] // 2, D), BF16)] * 2,
         (),
         after,
         flops=2 * team.shape[0] * D * (joint_grad.shape[1] + D),
@@ -858,7 +854,8 @@
 
 def shared_grads(shared, after, context):
     team, grads, hidden, joint_grad = shared[-4:]
-    return shared_grads_step(team, joint_grad, hidden, grads, after, context)
+    *joints, own, other = shared_grads_step(team, joint_grad, hidden, grads, after, context)
+    return [*joints, own.reshape(D // 2, -1), other.reshape(D // 2, -1)]
 
 
 def out_grads_kernel(place_ref, mixed_ref, attn_ref, own_ref, other_ref):
@@ -1346,18 +1343,16 @@
     return blocks.transpose(3, 0, 1, 2, 4).reshape(TEAM_SIZE, width, -1)
 
 
-def padded_rows(shared_down):
-    total = lax.axis_size(ALL)
-    return jnp.pad(shared_down, ((0, TEAM_SIZE * D // total - shared_down.shape[0]), (0, 0)))
-
-
-def down_rows(padded):
-    total = lax.axis_size(ALL)
-    return padded.reshape(total // TEAM_SIZE, -1, D)[:, : FF // total].reshape(-1, D)
+def down_rows(rows):
+    return rows.reshape(-1, D)
 
 
 def folded(w_out):
     return w_out.reshape(TEAM_SIZE * w_out.shape[0], -1)
+
+
+def folded_down(shared_down):
+    return shared_down.reshape(TEAM_SIZE * D // lax.axis_size(ALL), -1)
 
 
 def out_rows(rows, member):
@@ -1417,7 +1412,7 @@
     rows = team_turn(rows, member).reshape(TEAM_SIZE * width, -1)
     first_rows = spread(rows, "z")
     rows = exchange(joint_columns(shared_gate_up[0]), TEAM).reshape(TEAM_SIZE * width, -1)
-    main_rows = jnp.concatenate([folded(w_out[0]), rows, padded_rows(shared_down[0])], axis=1)
+    main_rows = jnp.concatenate([folded(w_out[0]), rows, folded_down(shared_down[0])], axis=1)
     main_rows = z_gather(later(main_rows, first_rows))
     if LAYERS > 1:
         rows = side_by_side(
@@ -1435,7 +1430,7 @@
                 rows[:, :edge],
                 *[folded(w_out[layer]) for layer in range(1, LAYERS)],
                 rows[:, edge:],
-                *[padded_rows(shared_down[layer]) for layer in range(1, LAYERS)],
+                *[folded_down(shared_down[layer]) for layer in range(1, LAYERS)],
             ],
             axis=1,
         )
@@ -1464,7 +1459,7 @@
             at, held_rows, edges = layer - 1, more_rows, more_edges
         columns = [
             held_rows[:, low + at * size : low + (at + 1) * size]
-            for low, size in zip(edges, (D // TEAM_SIZE, joint_width, D))
+            for low, size in zip(edges, (D // TEAM_SIZE, joint_width, FF // TEAM_SIZE))
         ]
         after = grad_rows[1:] if layer == last else []
         if layer > 0:
@@ -1659,12 +1654,12 @@
         if layer < last:
             head_parts[layer + 1] = team_pieces(waiting_sum, member)
             feed_parts[layer + 1][1] = team_pieces(waited_sum[:, :D], member)
-            feed_parts[layer + 1][2] = waited_sum[:unit, D : 2 * D]
-            feed_parts[layer + 1][0] = team_pieces(waited_sum[:, 2 * D :], member)
+            feed_parts[layer + 1][2] = waited_sum[:, D : D + FF // TEAM_SIZE].reshape(unit, D)
+            feed_parts[layer + 1][0] = team_pieces(waited_sum[:, D + FF // TEAM_SIZE :], member)
         feed_parts[layer] = [None] * 3
         if layer == 0:
             feed_parts[0][0] = team_pieces(shared_sum[:, :joint_width], member)
-            feed_parts[0][2] = shared_sum[:unit, joint_width:]
+            feed_parts[0][2] = shared_sum[:, joint_width:].reshape(unit, D)
         if layer == 0:
             terms = expert_grads(
                 layer, (2, 2), *held, joint, down, terms, [packed[0], shared_sum], context

time: 675 us -> 668 us (0.990)
  local copies, waits for them, and re-layouts: 61.5 us -> 70.8 us
    all_to_all x12, waiting for transfers between devices: 35.8 us -> 27 us  [exchange(): return lax.all_to_all(rows, axes, split_axis=0, concat_axis=0, tiled=True)]
    reshape x0 -> x6, local copies, waits for them, and re-layouts: none -> 7.4 us  [the longest x2 3.27 us: shared_grads(): return [*joints, own.reshape(D // 2, -1), other.reshape(D // 2, -1)]]
  transfers between devices with their start and end apart: 115 -> 115, of which waited for: 34 -> 35; matrix products, arithmetic and copies ran while one was open for 10% -> 11% of each run, Pallas kernels for 25% -> 26%
where the time goes in v6:
time: 668 us; the launch traced here: 657 us
  Pallas kernels  209 us (31%)
  starting transfers between devices  170 us (25%)
  waiting for transfers between devices  161 us (24%)
  local copies, waits for them, and re-layouts  70.8 us (11%)
  other arithmetic  29.9 us (4%)
  between operations  16.4 us (2%)
    pallas_call x20, Pallas kernels, run_kernel(): pl.pallas_call(lambda *refs: kernel(*refs[:given], *refs[kept:]), grid=(1...  76.2 us
    all_to_all x12, starting transfers between devices, exchange(): return lax.all_to_all(rows, axes, split_axis=0, concat_axis=0, tiled=True)  63.4 us
    pallas_call x5, Pallas kernels, expert_grads(): pl.pallas_call(expert_grad_kernel, grid=(steps, 2), in_specs=in_specs, ou...  63 us
    ppermute x21, waiting for transfers between devices, from_member(): return lax.ppermute(rows, TEAM, [(i, 3 - i) for i in range(4)])  44.3 us
    pallas_call x3, Pallas kernels, run_expert(): pl.pallas_call(lambda *refs: body(*refs[:drop], *refs[drop + len(after):]...  34.2 us
    ppermute x8, waiting for transfers between devices, dp_rows(): other = lax.ppermute(rows, 'dp', SWAP)  31.9 us
    ppermute x21, starting transfers between devices, from_member(): return lax.ppermute(rows, 'ulysses', SWAP)  31.7 us
    ppermute x12, starting transfers between devices, z_turn(): arrived.append(lax.ppermute(pieces[turn], ('z', 'core'), pairs))  30 us
  transfers between devices with their start and end apart: 115, of which 35 were waited for; matrix products, arithmetic and copies ran while one was open for 11% of the time, Pallas kernels for 26%

profile of v6, /device:TPU:0, one launch (start us, length us, event | category | flops | bytes accessed | tf_op | source)
XLA Modules:
  0.0 657.2 jit_solution(3565812392632559217)
XLA Ops:
  34.5 9.5 %all-to-all-done = bf16[4,96,612]{2,1,0:T(8,128)(2,1)S(1)} async-done(((bf16[4,96,612]{2,1,0:T(8,128)(2,1)}), bf16[4,96,612]{2,1,0:T(8,128)(2,1)S(1)}, u32[]{:S(2)}, u32[]{:S(2)}) %all-to-all-start) | async-done | bytes 470048 | tf_op jit(solution)/shard_map/all_to_all | solution.py:52
  49.7 11.8 %collective-permute-done.6 = bf16[384,612]{0,1:T(8,128)(2,1)S(1)} collective-permute-done((bf16[384,612]{0,1:T(8,128)(2,1)S(1)}, bf16[384,612]{0,1:T(8,128)(2,1)S(1)}, u32[]{:S(2)}, u32[]{:S(2)}) %collective-permute-start.6) | collective-permute-done | bytes 470048 | tf_op jit(solution)/shard_map/ppermute | solution.py:1307
  73.4 7.7 %all-gather.3.cloned.1.call-done = bf16[384,1728]{1,0:T(8,128)(2,1)} async-done(((bf16[96,1728]{1,0:T(8,128)(2,1)}), bf16[384,1728]{1,0:T(8,128)(2,1)}) %all-gather.3.cloned.1.call-update) | async-done | bytes 1327120 | tf_op jit(solution)/shard_map/all_gather | solution.py:1374
  88.6 7.8 %attend.2 = (bf16[4,192,512]{2,1,0:T(8,128)(2,1)}, bf16[16,64,128]{2,1,0:T(8,128)(2,1)}, f32[64,2048]{1,0:T(8,128)}, f32[1,2048]{1,0:T(1,128)}) custom-call(s32[4]{0:T(128)} %pad_add_fusion.refs_0_.place_ref, bf16[192,512]{1,0:T(8,128)(2,1)} %get-tuple-element.121.refs_0_.refs_1_, bf16[192,512]{1,0:T(8,128)(2,1)} %copy-done.103, ...), custom_call_target="tpu_custom_call" | custom-call | flops 16777216 | bytes 1572864 | tf_op jit(solution)/shard_map/attend/pallas_call | solution.py:295
  107.8 6.9 %collective-permute-done.13 = bf16[192,768]{1,0:T(8,128)(2,1)} collective-permute-done((bf16[192,768]{1,0:T(8,128)(2,1)}, bf16[192,768]{1,0:T(8,128)(2,1)}, u32[]{:S(2)}, u32[]{:S(2)}) %collective-permute-start.13) | collective-permute-done | bytes 294944 | tf_op jit(solution)/shard_map/ppermute | solution.py:63
  124.0 6.0 all-to-all-start.3
  134.7 7.7 %collective-permute-done.17 = bf16[384,1024]{1,0:T(8,128)(2,1)S(1)} collective-permute-done((bf16[384,1024]{1,0:T(8,128)(2,1)}, bf16[384,1024]{1,0:T(8,128)(2,1)S(1)}, u32[]{:S(2)}, u32[]{:S(2)}) %collective-permute-start.17) | collective-permute-done | bytes 786464 | tf_op jit(solution)/shard_map/ppermute | solution.py:1307
  145.3 7.9 %all-to-all-done.3 = bf16[16,24,768]{2,1,0:T(8,128)(2,1)S(1)} async-done(((bf16[16,24,768]{2,1,0:T(8,128)(2,1)}), bf16[16,24,768]{2,1,0:T(8,128)(2,1)S(1)}, u32[]{:S(2)}, u32[]{:S(2)}) %all-to-all-start.3) | async-done | bytes 589856 | tf_op jit(solution)/shard_map/all_to_all | solution.py:52
  154.0 8.5 %expert_forward.1.refs_7_.refs_1_ = bf16[384,768]{1,0:T(8,128)(2,1)} custom-call(bf16[384,768]{1,0:T(8,128)(2,1)} %bitcast.208, bf16[2,1,768,4096]{3,2,1,0:T(8,128)(2,1)} %up_ref.9, bf16[2,1,768,4096]{3,2,1,0:T(8,128)(2,1)} %up_ref.9, bf16[2,1,2048,768]{3,2,1,0:T(8,128)(2,1)} %down_ref.9, bf16[128,768]{1,0:T(8,128)(2,1)} %copy-done.24, ...), custom_call_target="tpu_custom_call" | custom-call | flops 3623878656 | bytes 10616832 | tf_op jit(solution)/shard_map/expert_forward/pallas_call | solution.py:985
  162.5 5.3 all-to-all-start.4
  225.5 8.0 %collective-permute-done.30.refs_2_ = bf16[192,512]{1,0:T(8,128)(2,1)S(1)} collective-permute-done((bf16[192,512]{1,0:T(8,128)(2,1)S(1)}, bf16[192,512]{1,0:T(8,128)(2,1)S(1)}, u32[]{:S(2)}, u32[]{:S(2)}) %collective-permute-start.30) | collective-permute-done | bytes 196640 | tf_op jit(solution)/shard_map/ppermute | solution.py:1199
  234.2 7.8 %attend.3 = (bf16[4,192,512]{2,1,0:T(8,128)(2,1)}, bf16[16,64,128]{2,1,0:T(8,128)(2,1)}, f32[64,2048]{1,0:T(8,128)}, f32[1,2048]{1,0:T(1,128)}) custom-call(s32[4]{0:T(128)} %pad_add_fusion.refs_0_.place_ref, bf16[192,512]{1,0:T(8,128)(2,1)} %get-tuple-element.136.refs_0_.refs_1_, bf16[192,512]{1,0:T(8,128)(2,1)} %copy-done.109, ...), custom_call_target="tpu_custom_call" | custom-call | flops 16777216 | bytes 1572864 | tf_op jit(solution)/shard_map/attend/pallas_call | solution.py:295
  253.7 7.5 %collective-permute-done.39 = bf16[192,768]{1,0:T(8,128)(2,1)S(1)} collective-permute-done((bf16[192,768]{1,0:T(8,128)(2,1)S(1)}, bf16[192,768]{1,0:T(8,128)(2,1)S(1)}, u32[]{:S(2)}, u32[]{:S(2)}) %collective-permute-start.39) | collective-permute-done | bytes 294944 | tf_op jit(solution)/shard_map/ppermute | solution.py:63
  277.9 8.9 %collective-permute-done.44 = bf16[384,512]{1,0:T(8,128)(2,1)S(1)} collective-permute-done((bf16[384,512]{1,0:T(8,128)(2,1)}, bf16[384,512]{1,0:T(8,128)(2,1)S(1)}, u32[]{:S(2)}, u32[]{:S(2)}) %collective-permute-start.44) | collective-permute-done | bytes 393248 | tf_op jit(solution)/shard_map/ppermute | solution.py:1307
  294.5 6.6 shared.4
  302.1 13.8 %expert_both.1 = bf16[384,1536]{1,0:T(8,128)(2,1)} custom-call(bf16[384,1536]{1,0:T(8,128)(2,1)} %bitcast.199, bf16[384,1536]{1,0:T(8,128)(2,1)} %bitcast.200, bf16[2,1,768,4096]{3,2,1,0:T(8,128)(2,1)} %up_ref.9, bf16[2,1,768,4096]{3,2,1,0:T(8,128)(2,1)} %up_ref.9, bf16[2,1,2048,768]{3,2,1,0:T(8,128)(2,1)} %down_ref.9, ...), custom_call_target="tpu_custom_call" | custom-call | flops 7247757312 | bytes 11796480 | tf_op jit(solution)/shard_map/expert_both/pallas_call | solution.py:985
  315.9 5.6 all-to-all-start.7
  330.9 12.2 %collective-permute-done.45.refs_12_ = bf16[128,1536]{1,0:T(8,128)(2,1)} collective-permute-done((bf16[128,1536]{1,0:T(8,128)(2,1)}, bf16[128,1536]{1,0:T(8,128)(2,1)}, u32[]{:S(2)}, u32[]{:S(2)}) %collective-permute-start.45) | collective-permute-done | bytes 393248 | tf_op jit(solution)/shard_map/ppermute | solution.py:60
  343.1 10.6 %collective-permute-done.47.refs_14_ = bf16[128,1536]{1,0:T(8,128)(2,1)} collective-permute-done((bf16[128,1536]{1,0:T(8,128)(2,1)}, bf16[128,1536]{1,0:T(8,128)(2,1)}, u32[]{:S(2)}, u32[]{:S(2)}) %collective-permute-start.47) | collective-permute-done | bytes 393248 | tf_op jit(solution)/shard_map/ppermute | solution.py:63
  368.3 5.3 all-to-all-done.8.grad_ref
  374.3 10.2 %attend_back.2 = (bf16[192,512]{1,0:T(8,128)(2,1)}, bf16[192,512]{1,0:T(8,128)(2,1)}, bf16[192,512]{1,0:T(8,128)(2,1)}, bf16[192,512]{1,0:T(8,128)(2,1)}) custom-call(s32[4]{0:T(128)} %pad_add_fusion.refs_0_.place_ref, bf16[4,192,512]{2,1,0:T(8,128)(2,1)} %get-tuple-element.159.rows_ref, s32[1,2048]{1,0:T(1,128)} %bitcast.273, ...), custom_call_target="tpu_custom_call" | custom-call | flops 50331648 | bytes 1572864 | tf_op jit(solution)/shard_map/attend_back/pallas_call | solution.py:322
  392.7 15.2 %expert_grads.5 = (f32[2,1,768,4096]{3,2,1,0:T(8,128)}, f32[2,1,2048,768]{3,2,1,0:T(8,128)}) custom-call(s32[4]{0:T(128)} %pad_add_fusion.refs_0_.place_ref, bf16[384,1536]{1,0:T(8,128)(2,1)} %bitcast.201, bf16[384,1536]{1,0:T(8,128)(2,1)} %bitcast.202, bf16[384,1536]{1,0:T(8,128)(2,1)} %copy-done.2, bf16[384,1536]{1,0:T(8,128)(2,1)} %copy-done.2, ...), custom_call_target="tpu_custom_call" | custom-call | flops 7247757312 | bytes 14155776 | tf_op jit(solution)/shard_map/expert_grads/pallas_call | solution.py:1062
  434.8 5.7 all-to-all-start.9
  444.5 8.6 %expert_grads.6 = (f32[2,1,768,4096]{3,2,1,0:T(8,128)}, f32[2,1,2048,768]{3,2,1,0:T(8,128)}) custom-call(s32[4]{0:T(128)} %pad_add_fusion.refs_0_.place_ref, bf16[384,1536]{1,0:T(8,128)(2,1)} %bitcast.203, bf16[384,1536]{1,0:T(8,128)(2,1)} %bitcast.204, bf16[384,1536]{1,0:T(8,128)(2,1)} %copy-done.2, ...), custom_call_target="tpu_custom_call", output_to_operand_aliasing={{0}: (8, {}), {1}: (9, {})} | custom-call | flops 3623878656 | bytes 7077888 | tf_op jit(solution)/shard_map/expert_grads/pallas_call | solution.py:1062
  456.1 5.9 shared.5
  466.9 11.8 %expert_back.1 = bf16[384,768]{1,0:T(8,128)(2,1)} custom-call(bf16[384,768]{1,0:T(8,128)(2,1)} %bitcast.209, bf16[384,768]{1,0:T(8,128)(2,1)} %bitcast.219, bf16[2,1,768,4096]{3,2,1,0:T(8,128)(2,1)} %up_ref.9, bf16[2,1,768,4096]{3,2,1,0:T(8,128)(2,1)} %up_ref.9, bf16[2,1,2048,768]{3,2,1,0:T(8,128)(2,1)} %down_ref.9, ...), custom_call_target="tpu_custom_call" | custom-call | flops 6039797760 | bytes 10616832 | tf_op jit(solution)/shard_map/expert_back/pallas_call | solution.py:985
  478.8 10.8 %all-to-all-start.10 = ((bf16[16,24,768]{2,1,0:T(8,128)(2,1)}), bf16[16,24,768]{2,1,0:T(8,128)(2,1)S(1)}, u32[]{:S(2)}, u32[]{:S(2)}) async-start(bf16[16,24,768]{2,1,0:T(8,128)(2,1)} %bitcast.233), calls=%async_computation.10 | async-start | bytes 1179648 | tf_op jit(solution)/shard_map/all_to_all | solution.py:52
  524.1 8.6 %expert_grads.7 = (f32[2,1,768,4096]{3,2,1,0:T(8,128)}, f32[2,1,2048,768]{3,2,1,0:T(8,128)}) custom-call(s32[4]{0:T(128)} %pad_add_fusion.refs_0_.place_ref, bf16[384,1536]{1,0:T(8,128)(2,1)} %bitcast.205, bf16[384,1536]{1,0:T(8,128)(2,1)} %bitcast.206, bf16[384,1536]{1,0:T(8,128)(2,1)} %copy-done.2, ...), custom_call_target="tpu_custom_call", output_to_operand_aliasing={{0}: (8, {}), {1}: (9, {})} | custom-call | flops 3623878656 | bytes 7077888 | tf_op jit(solution)/shard_map/expert_grads/pallas_call | solution.py:1062
  533.6 10.1 %attend_back.3 = (bf16[192,512]{1,0:T(8,128)(2,1)}, bf16[192,512]{1,0:T(8,128)(2,1)}, bf16[192,512]{1,0:T(8,128)(2,1)}, bf16[192,512]{1,0:T(8,128)(2,1)}) custom-call(s32[4]{0:T(128)} %pad_add_fusion.refs_0_.place_ref, bf16[4,192,512]{2,1,0:T(8,128)(2,1)} %get-tuple-element.197.rows_ref, s32[1,2048]{1,0:T(1,128)} %bitcast.274, ...), custom_call_target="tpu_custom_call" | custom-call | flops 50331648 | bytes 1572864 | tf_op jit(solution)/shard_map/attend_back/pallas_call | solution.py:322
  561.1 15.3 %expert_grads.8 = (f32[2,1,768,4096]{3,2,1,0:T(8,128)}, f32[2,1,2048,768]{3,2,1,0:T(8,128)}) custom-call(s32[4]{0:T(128)} %pad_add_fusion.refs_0_.place_ref, bf16[384,768]{1,0:T(8,128)(2,1)} %bitcast.210, bf16[384,768]{1,0:T(8,128)(2,1)} %bitcast.220, bf16[384,768]{1,0:T(8,128)(2,1)} %copy-done.22, ...), custom_call_target="tpu_custom_call", output_to_operand_aliasing={{0}: (8, {}), {1}: (9, {})} | custom-call | flops 7247757312 | bytes 14155776 | tf_op jit(solution)/shard_map/expert_grads/pallas_call | solution.py:1062
  593.8 15.3 %expert_grads.9 = (f32[2,1,768,4096]{3,2,1,0:T(8,128)}, f32[2,1,2048,768]{3,2,1,0:T(8,128)}) custom-call(s32[4]{0:T(128)} %pad_add_fusion.refs_0_.place_ref, bf16[384,768]{1,0:T(8,128)(2,1)} %bitcast.211, bf16[384,768]{1,0:T(8,128)(2,1)} %bitcast.221, bf16[384,768]{1,0:T(8,128)(2,1)} %copy-done.22, ...), custom_call_target="tpu_custom_call", output_to_operand_aliasing={{0}: (8, {}), {1}: (9, {})} | custom-call | flops 7247757312 | bytes 14155776 | tf_op jit(solution)/shard_map/expert_grads/pallas_call | solution.py:1062
  612.3 6.0 collective-permute-start.76
  (616 shorter events, 351.6 us)
Async XLA Ops:
  7.2 56.5 %collective-permute-start = (bf16[128,768]{1,0:T(8,128)(2,1)}, bf16[128,768]{1,0:T(8,128)(2,1)S(1)}, u32[]{:S(2)}, u32[]{:S(2)}) collective-permute-start(bf16[128,768]{1,0:T(8,128)(2,1)} %bitcast.236), channel_id=1, source_target_pairs={{0,1},{1,0},{2,3},{3,2},{4,5},{5,4},{6,7},{7,6},{8,9},{9,8},{10,11... | collective-permute-start | bytes 589832 | tf_op jit(solution)/shard_map/ppermute | solution.py:60
  10.3 53.5 %collective-permute-start.1 = (bf16[128,768]{1,0:T(8,128)(2,1)}, bf16[128,768]{1,0:T(8,128)(2,1)}, u32[]{:S(2)}, u32[]{:S(2)}) collective-permute-start(bf16[128,768]{1,0:T(8,128)(2,1)} %bitcast.237), channel_id=1, source_target_pairs={{0,2},{2,0},{1,3},{3,1},{4,6},{6,4},{5,7},{7,5},{8,10},{10,8},{9,1... | collective-permute-start | bytes 589832 | tf_op jit(solution)/shard_map/ppermute | solution.py:62
  21.2 26.4 %collective-permute-start.22 = (bf16[24,1600]{1,0:T(8,128)(2,1)S(1)}, bf16[24,1600]{1,0:T(8,128)(2,1)S(1)}, u32[]{:S(2)}, u32[]{:S(2)}) collective-permute-start(bf16[24,1600]{1,0:T(8,128)(2,1)S(1)} %get-tuple-element.301), channel_id=1, source_target_pairs={{0,2},{2,0},{1,3},{3,1},{4,6},{6,4},{5,7},{7,5},{8,10},{10,8},{9,1... | collective-permute-start | bytes 230408 | tf_op jit(solution)/shard_map/ppermute | solution.py:62
  22.0 26.1 %collective-permute-start.23 = (bf16[24,1600]{1,0:T(8,128)(2,1)S(1)}, bf16[24,1600]{1,0:T(8,128)(2,1)S(1)}, u32[]{:S(2)}, u32[]{:S(2)}) collective-permute-start(bf16[24,1600]{1,0:T(8,128)(2,1)S(1)} %get-tuple-element.302), channel_id=1, source_target_pairs={{0,1},{1,0},{2,3},{3,2},{4,5},{5,4},{6,7},{7,6},{8,9},{9,8},{10,11... | collective-permute-start | bytes 230408 | tf_op jit(solution)/shard_map/ppermute | solution.py:60
  23.4 26.2 %collective-permute-start.24 = (bf16[24,1600]{1,0:T(8,128)(2,1)S(1)}, bf16[24,1600]{1,0:T(8,128)(2,1)S(1)}, u32[]{:S(2)}, u32[]{:S(2)}) collective-permute-start(bf16[24,1600]{1,0:T(8,128)(2,1)S(1)} %get-tuple-element.300), channel_id=1, source_target_pairs={{0,3},{1,2},{2,1},{3,0},{4,7},{5,6},{6,5},{7,4},{8,11},{9,10},{10,... | collective-permute-start | bytes 230408 | tf_op jit(solution)/shard_map/ppermute | solution.py:63
  29.8 51.3 %all-gather.3.cloned.1.call-start = ((), (), s32[]{:S(2)}) async-start(), calls=%async_computation.16 | async-start | bytes 1720320 | tf_op jit(solution)/shard_map/all_gather | solution.py:1374
  44.7 123.8 %all-gather.5.cloned.1.call-start = ((), (), s32[]{:S(2)}) async-start(), calls=%async_computation.17 | async-start | bytes 2211840 | tf_op jit(solution)/shard_map/all_gather | solution.py:1374
  124.0 29.2 %all-to-all-start.3 = ((bf16[16,24,768]{2,1,0:T(8,128)(2,1)}), bf16[16,24,768]{2,1,0:T(8,128)(2,1)S(1)}, u32[]{:S(2)}, u32[]{:S(2)}) async-start(bf16[16,24,768]{2,1,0:T(8,128)(2,1)} %bitcast.37), calls=%async_computation.3 | async-start | bytes 1179648 | tf_op jit(solution)/shard_map/all_to_all | solution.py:52
  134.1 37.7 %collective-permute-start.18 = (bf16[384,512]{1,0:T(8,128)(2,1)}, bf16[384,512]{1,0:T(8,128)(2,1)}, u32[]{:S(2)}, u32[]{:S(2)}) collective-permute-start(bf16[384,512]{1,0:T(8,128)(2,1)} %later.18), channel_id=1, source_target_pairs={{0,16},{16,0},{1,17},{17,1},{2,18},{18,2},{3,19},{19,3},{4,20},{20... | collective-permute-start | bytes 1179656 | tf_op jit(solution)/shard_map/ppermute | solution.py:1307
  162.5 28.3 %all-to-all-start.4 = ((bf16[16,24,768]{2,1,0:T(8,128)(2,1)}), bf16[16,24,768]{2,1,0:T(8,128)(2,1)S(1)}, u32[]{:S(2)}, u32[]{:S(2)}) async-start(bf16[16,24,768]{2,1,0:T(8,128)(2,1)} %bitcast.217), calls=%async_computation.4 | async-start | bytes 1179648 | tf_op jit(solution)/shard_map/all_to_all | solution.py:52
  196.8 25.8 %collective-permute-start.35 = (bf16[384,768]{1,0:T(8,128)(2,1)S(1)}, bf16[384,768]{1,0:T(8,128)(2,1)S(1)}, u32[]{:S(2)}, u32[]{:S(2)}) collective-permute-start(bf16[384,768]{1,0:T(8,128)(2,1)S(1)} %bitcast.212), channel_id=1, source_target_pairs={{0,16},{16,0},{1,17},{17,1},{2,18},{18,2},{3,19},{19,3},{4,20},{20... | collective-permute-start | bytes 1769480 | tf_op jit(solution)/shard_map/ppermute | solution.py:1265
  269.4 31.7 %all-to-all-start.6 = ((bf16[16,24,1536]{2,1,0:T(8,128)(2,1)}), bf16[16,24,1536]{2,1,0:T(8,128)(2,1)S(1)}, u32[]{:S(2)}, u32[]{:S(2)}) async-start(bf16[16,24,1536]{2,1,0:T(8,128)(2,1)} %bitcast.256), calls=%async_computation.6 | async-start | bytes 2359296 | tf_op jit(solution)/shard_map/all_to_all | solution.py:52
  315.9 37.8 %all-to-all-start.7 = ((bf16[16,24,1536]{2,1,0:T(8,128)(2,1)}), bf16[16,24,1536]{2,1,0:T(8,128)(2,1)}, u32[]{:S(2)}, u32[]{:S(2)}) async-start(bf16[16,24,1536]{2,1,0:T(8,128)(2,1)} %bitcast.222), calls=%async_computation.7 | async-start | bytes 2359296 | tf_op jit(solution)/shard_map/all_to_all | solution.py:52
  321.6 69.2 %collective-permute-start.51 = (bf16[384,1536]{1,0:T(8,128)(2,1)S(1)}, bf16[384,1536]{1,0:T(8,128)(2,1)S(1)}, u32[]{:S(2)}, u32[]{:S(2)}) collective-permute-start(bf16[384,1536]{1,0:T(8,128)(2,1)S(1)} %bitcast.207), channel_id=1, source_target_pairs={{0,16},{16,0},{1,17},{17,1},{2,18},{18,2},{3,19},{19,3},{4,20},{20... | collective-permute-start | bytes 3538952 | tf_op jit(solution)/shard_map/ppermute | solution.py:1265
  323.8 30.0 %collective-permute-start.47 = (bf16[128,1536]{1,0:T(8,128)(2,1)}, bf16[128,1536]{1,0:T(8,128)(2,1)}, u32[]{:S(2)}, u32[]{:S(2)}) collective-permute-start(bf16[128,1536]{1,0:T(8,128)(2,1)} %get-tuple-element.150), channel_id=1, source_target_pairs={{0,3},{1,2},{2,1},{3,0},{4,7},{5,6},{6,5},{7,4},{8,11},{9,10},{10,... | collective-permute-start | bytes 1179656 | tf_op jit(solution)/shard_map/ppermute | solution.py:63
  363.6 137.4 %reduce-scatter.5.cloned.1.call-start = ((), (), s32[]{:S(2)}) async-start(), calls=%async_computation.18 | async-start | bytes 2211840 | tf_op jit(solution)/shard_map/reduce_scatter | solution.py:1275
  364.1 46.9 %collective-permute-start.53 = (bf16[384,1024]{1,0:T(8,128)(2,1)}, bf16[384,1024]{1,0:T(8,128)(2,1)}, u32[]{:S(2)}, u32[]{:S(2)}) collective-permute-start(bf16[384,1024]{1,0:T(8,128)(2,1)} %get-tuple-element.155.refs_15_), channel_id=1, source_target_pairs={{0,16},{16,0},{1,17},{17,1},{2,18},{18,2},{3,19},{19,3},{4,20},{20... | collective-permute-start | bytes 2359304 | tf_op jit(solution)/shard_map/ppermute | solution.py:1265
  364.2 46.8 %collective-permute-start.52 = (bf16[384,512]{1,0:T(8,128)(2,1)S(1)}, bf16[384,512]{1,0:T(8,128)(2,1)}, u32[]{:S(2)}, u32[]{:S(2)}) collective-permute-start(bf16[384,512]{1,0:T(8,128)(2,1)S(1)} %copy-done.29), channel_id=1, source_target_pairs={{0,16},{16,0},{1,17},{17,1},{2,18},{18,2},{3,19},{19,3},{4,20},{20... | collective-permute-start | bytes 1179656 | tf_op jit(solution)/shard_map/ppermute | solution.py:1265
  384.5 23.4 %collective-permute-start.48 = (bf16[192,512]{1,0:T(8,128)(2,1)}, bf16[192,512]{1,0:T(8,128)(2,1)S(1)}, u32[]{:S(2)}, u32[]{:S(2)}) collective-permute-start(bf16[192,512]{1,0:T(8,128)(2,1)} %get-tuple-element.163), channel_id=1, source_target_pairs={{0,4},{4,8},{6,10},{8,12},{10,14},{14,2},{1,5},{5,9},{7,11},{9,13}... | collective-permute-start | bytes 589832 | tf_op jit(solution)/shard_map/ppermute | solution.py:1199
  387.4 23.7 %collective-permute-start.49 = (bf16[192,512]{1,0:T(8,128)(2,1)}, bf16[192,512]{1,0:T(8,128)(2,1)}, u32[]{:S(2)}, u32[]{:S(2)}) collective-permute-start(bf16[192,512]{1,0:T(8,128)(2,1)} %get-tuple-element.164), channel_id=1, source_target_pairs={{0,8},{4,12},{6,14},{8,0},{10,2},{14,6},{1,9},{5,13},{7,15},{9,1},... | collective-permute-start | bytes 589832 | tf_op jit(solution)/shard_map/ppermute | solution.py:1199
  434.8 29.9 %all-to-all-start.9 = ((bf16[16,24,768]{2,1,0:T(8,128)(2,1)}), bf16[16,24,768]{2,1,0:T(8,128)(2,1)S(1)}, u32[]{:S(2)}, u32[]{:S(2)}) async-start(bf16[16,24,768]{2,1,0:T(8,128)(2,1)} %bitcast.69), calls=%async_computation.9 | async-start | bytes 1179648 | tf_op jit(solution)/shard_map/all_to_all | solution.py:52
  440.5 25.6 %collective-permute-start.60 = (bf16[384,640]{1,0:T(8,128)(2,1)S(1)}, bf16[384,640]{1,0:T(8,128)(2,1)S(1)}, u32[]{:S(2)}, u32[]{:S(2)}) collective-permute-start(bf16[384,640]{1,0:T(8,128)(2,1)S(1)} %copy-done.93), channel_id=1, source_target_pairs={{0,16},{16,0},{1,17},{17,1},{2,18},{18,2},{3,19},{19,3},{4,20},{20... | collective-permute-start | bytes 1474568 | tf_op jit(solution)/shard_map/ppermute | solution.py:1265
  464.7 27.1 %collective-permute-start.64 = (bf16[384,768]{1,0:T(8,128)(2,1)S(1)}, bf16[384,768]{1,0:T(8,128)(2,1)S(1)}, u32[]{:S(2)}, u32[]{:S(2)}) collective-permute-start(bf16[384,768]{1,0:T(8,128)(2,1)S(1)} %bitcast.218), channel_id=1, source_target_pairs={{0,16},{16,0},{1,17},{17,1},{2,18},{18,2},{3,19},{19,3},{4,20},{20... | collective-permute-start | bytes 1769480 | tf_op jit(solution)/shard_map/ppermute | solution.py:1265
  478.8 31.9 %all-to-all-start.10 = ((bf16[16,24,768]{2,1,0:T(8,128)(2,1)}), bf16[16,24,768]{2,1,0:T(8,128)(2,1)S(1)}, u32[]{:S(2)}, u32[]{:S(2)}) async-start(bf16[16,24,768]{2,1,0:T(8,128)(2,1)} %bitcast.233), calls=%async_computation.10 | async-start | bytes 1179648 | tf_op jit(solution)/shard_map/all_to_all | solution.py:52
  489.6 43.2 %reduce-scatter.7.cloned.1.call-start = ((), (), s32[]{:S(2)}) async-start(), calls=%async_computation.19 | async-start | bytes 614400 | tf_op jit(solution)/shard_map/reduce_scatter | solution.py:1275
  503.8 29.0 %collective-permute-start.66 = (bf16[384,1024]{1,0:T(8,128)(2,1)}, bf16[384,1024]{1,0:T(8,128)(2,1)S(1)}, u32[]{:S(2)}, u32[]{:S(2)}) collective-permute-start(bf16[384,1024]{1,0:T(8,128)(2,1)} %get-tuple-element.188.refs_16_), channel_id=1, source_target_pairs={{0,16},{16,0},{1,17},{17,1},{2,18},{18,2},{3,19},{19,3},{4,20},{20... | collective-permute-start | bytes 2359304 | tf_op jit(solution)/shard_map/ppermute | solution.py:1265
  521.3 72.5 %reduce-scatter.9.cloned.1.call-start = ((), (), s32[]{:S(2)}) async-start(), calls=%async_computation.20 | async-start | bytes 1474560 | tf_op jit(solution)/shard_map/reduce_scatter | solution.py:1275
  547.5 74.2 %reduce-scatter.11.cloned.1.call-start = ((), (), s32[]{:S(2)}) async-start(), calls=%async_computation.21 | async-start | bytes 737280 | tf_op jit(solution)/shard_map/reduce_scatter | solution.py:1275
  547.6 29.4 %collective-permute-start.71 = (bf16[384,768]{1,0:T(8,128)(2,1)S(1)}, bf16[384,768]{1,0:T(8,128)(2,1)S(1)}, u32[]{:S(2)}, u32[]{:S(2)}) collective-permute-start(bf16[384,768]{1,0:T(8,128)(2,1)S(1)} %copy-done.47), channel_id=1, source_target_pairs={{0,16},{16,0},{1,17},{17,1},{2,18},{18,2},{3,19},{19,3},{4,20},{20... | collective-permute-start | bytes 1769480 | tf_op jit(solution)/shard_map/ppermute | solution.py:1265
  548.7 73.0 %collective-permute-start.94 = (bf16[24,768]{1,0:T(8,128)(2,1)S(1)}, bf16[24,768]{1,0:T(8,128)(2,1)S(1)}, u32[]{:S(2)}, u32[]{:S(2)}) collective-permute-start(bf16[24,768]{1,0:T(8,128)(2,1)S(1)} %get-tuple-element.325), channel_id=1, source_target_pairs={{0,1},{1,0},{2,3},{3,2},{4,5},{5,4},{6,7},{7,6},{8,9},{9,8},{10,11... | collective-permute-start | bytes 110600 | tf_op jit(solution)/shard_map/ppermute | solution.py:60
  551.2 25.8 %collective-permute-start.68 = (bf16[192,512]{1,0:T(8,128)(2,1)S(1)}, bf16[192,512]{1,0:T(8,128)(2,1)S(1)}, u32[]{:S(2)}, u32[]{:S(2)}) collective-permute-start(bf16[192,512]{1,0:T(8,128)(2,1)S(1)} %copy-done.100), channel_id=1, source_target_pairs={{0,4},{4,8},{6,10},{8,12},{10,14},{14,2},{1,5},{5,9},{7,11},{9,13}... | collective-permute-start | bytes 589832 | tf_op jit(solution)/shard_map/ppermute | solution.py:1199
  558.9 23.8 %collective-permute-start.70 = (bf16[192,512]{1,0:T(8,128)(2,1)S(1)}, bf16[192,512]{1,0:T(8,128)(2,1)S(1)}, u32[]{:S(2)}, u32[]{:S(2)}) collective-permute-start(bf16[192,512]{1,0:T(8,128)(2,1)S(1)} %copy-done.98), channel_id=1, source_target_pairs={{0,12},{4,0},{6,2},{8,4},{10,6},{14,10},{1,13},{5,1},{7,3},{9,5},{... | collective-permute-start | bytes 589832 | tf_op jit(solution)/shard_map/ppermute | solution.py:1199
  (204 other events, 1704.4 us)
Sparse Core Ops, SparseCore 0:
  44.8 36.2 all-gather.2
  96.5 57.8 all-gather.4
  434.9 48.6 reduce-scatter.4
  503.8 20.1 reduce-scatter.6
  547.6 38.9 reduce-scatter.8
  593.8 24.4 reduce-scatter.10
